TPU v7x, 128 devices: a whole 4x4x4 slice. The times are simulated.
128 devices in a mesh: ctx: 16 (over y, x), tp: 8 (over z, core).
Axes of the slice: x: 4, y: 4, z: 4, core: 2. Of those that a mesh axis runs over, the one named last changes fastest.
Arguments:
- query_heads: bfloat16 [8192, 4096], P('ctx', 'tp'), may hold values from -6 to 6
- key_heads: bfloat16 [8192, 2048], P('ctx', 'tp'), may hold values from -6 to 6
- value_heads: bfloat16 [8192, 2048], P('ctx', 'tp'), may hold values from -6 to 6
- doc_ids: int32 [8192], replicated, may hold values from 0 to 7, never falling along the last dimension, each value on 1 to 4096 neighbouring positions
- out_weight: bfloat16 [4096, 5376], P('tp'), may hold values from -0.75 to 0.75
- residual: bfloat16 [8192, 5376], P('ctx', 'tp'), may hold values from -32 to 32
- post_gain: float32 [5376], P('tp'), may hold values from 0.25 to 1.75
- pre_gain: float32 [5376], P('tp'), may hold values from 0.25 to 1.75
- gate_weight: bfloat16 [5376, 10752], P('ctx', 'tp'), may hold values from -0.078125 to 0.078125
- up_weight: bfloat16 [5376, 10752], P('ctx', 'tp'), may hold values from -0.078125 to 0.078125
Outputs:
- new_residual: bfloat16 [8192, 5376], P('ctx', 'tp')
- activated: bfloat16 [8192, 10752], P('ctx', 'tp')
Inputs may be any that keep to these rules, and one draw needn't show every extreme that they name: doc_ids never fall along the span; a document is a run of equal ids.
All inputs are finite; a program needn't handle non-finite values.
Results may differ from a plain program's by a relative error of at most 0.03.
Values may be sent and summed in bfloat16 or wider, within the bound.
No kernel may reach another device: no remote copies, remote signals or barrier semaphores. Data moves between devices by JAX's collectives and lax.ppermute only.
A program may use at most 128 MiB of HBM per device.

v0:
```python
import jax
import jax.numpy as jnp
from jax import lax
from jax.sharding import PartitionSpec as P

D = 5376
H = 32
HD = 128
WINDOW = 1024


epsilon = 1e-06


def from_behind(value, axis, by):
    length = lax.axis_size(axis)
    pairs = [(i, i + by) for i in range(length) if 0 <= i + by < length]
    return lax.ppermute(value, axis, pairs)


def accumulate(gathered, piece):
    return jnp.dot(gathered, piece, preferred_element_type=jnp.float32)


def per_device(
    query_heads,
    key_heads,
    value_heads,
    doc_ids,
    out_weight,
    residual,
    post_gain,
    pre_gain,
    gate_weight,
    up_weight,
):
    tok_rows = query_heads.shape[0]
    key_groups = key_heads.shape[1] // HD
    head_count = query_heads.shape[1] // HD
    group_size = head_count // key_groups
    reach_shards = -(-WINDOW // tok_rows)
    span_rows = reach_shards * tok_rows
    row_start = lax.axis_index("ctx") * tok_rows
    local_pairs = jnp.concatenate([key_heads, value_heads], axis=1)
    earlier = [from_behind(local_pairs, "ctx", shift_by) for shift_by in range(reach_shards, 0, -1)]
    keyed = jnp.concatenate(earlier + [local_pairs], axis=0)
    padded_ids = jnp.concatenate([jnp.full((span_rows,), -1, jnp.int32), doc_ids])
    key_ids_all = lax.dynamic_slice_in_dim(padded_ids, row_start, span_rows + tok_rows, 0)
    query_ids_all = lax.dynamic_slice_in_dim(doc_ids, row_start, tok_rows, 0)
    block_rows = min(tok_rows, 512)
    block_count = tok_rows // block_rows
    score_scale = float(D // H) ** (-0.5)
    pair_width = key_groups * HD

    def attend(block_index):
        offset = block_index * block_rows
        queries = query_heads.reshape(block_rows, key_groups, group_size, HD)
        key_rows = keyed[:, :pair_width].reshape(span_rows + block_rows, key_groups, HD)
        value_rows = keyed[:, pair_width:].reshape(span_rows + block_rows, key_groups, HD)
        query_pos = offset + jnp.arange(block_rows, dtype=jnp.int32)
        key_pos = offset - span_rows + jnp.arange(span_rows + block_rows, dtype=jnp.int32)
        allowed = (
            (query_ids_all[:, None] == key_ids_all[None, :])
            & (key_pos[None, :] <= query_pos[:, None])
            & (key_pos[None, :] > query_pos[:, None] - WINDOW)
        )
        scores = (
            jnp.einsum("qhgd,khd->hgqk", queries, key_rows, preferred_element_type=jnp.float32)
            * score_scale
        )
        scores = jnp.where(allowed[None, None], scores, -1e30)
        row_max = jnp.max(scores, axis=-1, keepdims=True)
        weights = jnp.exp(scores - row_max)
        row_total = jnp.sum(weights, axis=-1, keepdims=True)
        attn_probs = (weights / row_total).astype(jnp.bfloat16)
        mixture = jnp.einsum(
            "hgqk,khd->qhgd", attn_probs, value_rows, preferred_element_type=jnp.float32
        )
        return mixture.astype(jnp.bfloat16).reshape(block_rows, head_count * HD)

    attended = lax.map(attend, jnp.arange(block_count, dtype=jnp.int32)).reshape(
        tok_rows, head_count * HD
    )
    partial_value = jnp.dot(attended, out_weight, preferred_element_type=jnp.float32)
    owned = lax.psum_scatter(
        partial_value.astype(jnp.bfloat16), "tp", scatter_dimension=1, tiled=True
    ).astype(jnp.float32)
    stream_in = residual.astype(jnp.float32)
    first_sum = lax.psum(jnp.sum(owned * owned, axis=1), "tp")
    factor = lax.rsqrt(first_sum / D + epsilon)
    branch = owned * factor[:, None] * post_gain[None, :]
    new_residual = (stream_in + branch).astype(jnp.bfloat16)
    stream = new_residual.astype(jnp.float32)
    second_sum = lax.psum(jnp.sum(stream * stream, axis=1), "tp")
    second = lax.rsqrt(second_sum / D + epsilon)
    normed = (stream * second[:, None] * pre_gain[None, :]).astype(jnp.bfloat16)
    gathered = lax.all_gather(normed, "tp", axis=1, tiled=True)

    def add_single(piece):
        return accumulate(gathered, piece)

    gate_sums = add_single(lax.all_gather(gate_weight, "ctx", axis=0, tiled=True))
    up_sums = add_single(lax.all_gather(up_weight, "ctx", axis=0, tiled=True))
    activated = (jax.nn.gelu(gate_sums, approximate=True) * up_sums).astype(jnp.bfloat16)
    return (new_residual, activated)


def solution(mesh):
    in_specs = (
        P("ctx", "tp"),
        P("ctx", "tp"),
        P("ctx", "tp"),
        P(),
        P("tp", None),
        P("ctx", "tp"),
        P("tp"),
        P("tp"),
        P("ctx", "tp"),
        P("ctx", "tp"),
    )
    out_specs = (P("ctx", "tp"), P("ctx", "tp"))
    return jax.shard_map(
        per_device, mesh=mesh, in_specs=in_specs, out_specs=out_specs, check_vma=False
    )
```

profile of v0, /device:TPU:1, one launch (start us, length us, event | category | flops | bytes accessed | tf_op | source)
XLA Modules:
  0.0 406.2 jit_solution(6202778815302964050)
XLA Ops:
  7.2 0.0 reduce-scatter.2.cloned.1.call-start
  7.2 1.1 copy.15
  8.3 1.1 copy.16
  9.4 5.5 %collective-permute-start = (bf16[512,512]{0,1:T(8,128)(2,1)S(1)}, bf16[512,512]{0,1:T(8,128)(2,1)S(1)}, u32[]{:S(2)}, u32[]{:S(2)}) collective-permute-start(bf16[512,512]{0,1:T(8,128)(2,1)S(1)} %pad_maximum_fusion), channel_id=1, source_target_pairs={{0,16},{8,24},{16,32},{24,40},{32,48},{40,56},{48,64},{56,72},{64,... | collective-permute-start | bytes 1572872 | tf_op jit(solution)/shard_map/ppermute | solution.py:18
  15.0 2.2 collective-permute-start.1
  17.2 0.8 pad_dynamic-slice_fusion
  18.0 0.8 dynamic_slice.9
  18.8 1.2 reshape.121
  19.9 3.4 fusion.7
  23.4 2.2 collective-permute-done
  25.6 11.2 %collective-permute-done.1 = bf16[512,512]{0,1:T(8,128)(2,1)S(1)} collective-permute-done((bf16[512,512]{0,1:T(8,128)(2,1)S(1)}, bf16[512,512]{0,1:T(8,128)(2,1)S(1)}, u32[]{:S(2)}, u32[]{:S(2)}) %collective-permute-start.1) | collective-permute-done | bytes 524320 | tf_op jit(solution)/shard_map/ppermute | solution.py:18
  36.8 0.1 maximum_maximum_fusion
  36.9 0.1 fusion.36
  37.0 8.1 %fusion.37 = (f32[2,2,512]{2,1,0:T(2,128)S(1)}, f32[2,2,512,1536]{2,3,1,0:T(8,128)}) fusion(pred[512,1536]{0,1:T(8,128)(4,1)S(1)} %fusion.7, bf16[1536,2,128,1]{0,2,3,1:T(8,128)(2,1)S(1)} %bitcast.34, bf16[512,2,2,128]{3,2,1,0:T(2,128)(2,1)S(1)} %reshape.121), kind=kOutput, calls=%fused_computation.49 | convolution fusion | flops 817890816 | bytes 14688256 | tf_op jit(solution)/shard_map/while/body/eval_jaxpr/sub | solution.py:73
  45.1 5.6 %fusion.25 = bf16[2,128,2,512]{3,1,2,0:T(8,128)(2,1)S(1)} fusion(bf16[1536,2,128,1]{0,2,3,1:T(8,128)(2,1)S(1)} %bitcast.33, f32[2,2,512,1536]{2,3,1,0:T(8,128)} %get-tuple-element.25, f32[2,2,512]{2,1,0:T(2,128)S(1)} %get-tuple-element.24), kind=kOutput, calls=%fused_computation.36 | convolution fusion | flops 811859968 | bytes 13901824 | tf_op jit(solution)/shard_map/while/body/eval_jaxpr/hgqk,khd->qhgd/dot_general | solution.py:76
  50.6 8.6 %convolution_convert_fusion = bf16[512,5376]{0,1:T(8,128)(2,1)} fusion(bf16[512,512]{0,1:T(8,128)(2,1)S(1)} %bitcast.35, bf16[512,5376]{1,0:T(8,128)(2,1)} %param.14), kind=kOutput, calls=%fused_computation.5 | convolution fusion | flops 2821324800 | bytes 11534336 | tf_op jit(solution)/shard_map/dot_general | solution.py:84
  59.3 0.0 copy-start.1
  59.3 0.0 copy-start.2
  59.3 0.0 copy-start.3
  59.3 0.0 reduce-scatter.2.cloned.1.call-update
  59.3 0.0 all-gather.4.cloned.1.call-start
  59.4 42.4 %reduce-scatter.2.cloned.1.call-done = bf16[512,672]{0,1:T(8,128)(2,1)} async-done(((bf16[512,5376]{0,1:T(8,128)(2,1)}), bf16[512,672]{0,1:T(8,128)(2,1)}) %reduce-scatter.2.cloned.1.call-update) | async-done | bytes 688144 | tf_op jit(solution)/shard_map/reduce_scatter | solution.py:85
  101.8 1.3 fusion.16
  103.1 15.2 %psum.14 = f32[512]{0:T(512)S(1)} all-reduce(f32[512]{0:T(512)S(1)} %fusion.16), channel_id=1, replica_groups=mesh['ctx'=16,'tp'=8] {'tp'}, use_global_device_ids=true, to_apply=%region_4.5 | all-reduce | flops 512 | bytes 4096 | tf_op jit(solution)/shard_map/psum | solution.py:89
  118.3 0.0 copy-done.1
  118.3 0.0 copy-done.2
  118.3 1.5 fusion.20
  119.9 0.0 copy-start
  119.9 13.4 %psum.15 = f32[512]{0:T(512)S(1)} all-reduce(f32[512]{0:T(512)S(1)} %get-tuple-element.14), channel_id=1, replica_groups=mesh['ctx'=16,'tp'=8] {'tp'}, use_global_device_ids=true, to_apply=%region_6.7 | all-reduce | flops 512 | bytes 4096 | tf_op jit(solution)/shard_map/psum | solution.py:94
  133.3 0.0 copy-done.3
  133.3 1.1 fusion.22
  134.4 0.0 all-gather.4.cloned.1.call-update
  134.4 0.0 all-gather.6.cloned.1.call-start
  134.5 0.7 all-gather.6.cloned.1.call-update
  135.2 0.2 all-gather.8.cloned.1.call-start
  135.4 0.3 all-gather.8.cloned.1.call-update
  135.7 35.7 %all-gather.4.cloned.1.call-done = bf16[512,5376]{0,1:T(8,128)(2,1)} async-done(((bf16[512,672]{0,1:T(8,128)(2,1)}), bf16[512,5376]{0,1:T(8,128)(2,1)}) %all-gather.4.cloned.1.call-update) | async-done | bytes 5505040 | tf_op jit(solution)/shard_map/all_gather | solution.py:97
  171.5 104.4 %all-gather.6.cloned.1.call-done = bf16[5376,1344]{1,0:T(8,128)(2,1)} async-done(((bf16[336,1344]{1,0:T(8,128)(2,1)}), bf16[5376,1344]{1,0:T(8,128)(2,1)}) %all-gather.6.cloned.1.call-update) | async-done | bytes 14450704 | tf_op jit(solution)/shard_map/all_gather | solution.py:102
  275.9 12.3 %fusion.42 = f32[512,1344]{0,1:T(8,128)S(1)} fusion(bf16[512,5376]{0,1:T(8,128)(2,1)} %all-gather.4.cloned.1.call-done, bf16[5376,1344]{1,0:T(8,128)(2,1)} %all-gather.6.cloned.1.call-done), kind=kOutput, calls=%fused_computation.50 | convolution fusion | flops 7398752256 | bytes 22708224 | tf_op jit(solution)/shard_map/dot_general | solution.py:22
  288.2 0.0 copy-done
  288.2 92.3 %all-gather.8.cloned.1.call-done = bf16[5376,1344]{1,0:T(8,128)(2,1)} async-done(((bf16[336,1344]{1,0:T(8,128)(2,1)}), bf16[5376,1344]{1,0:T(8,128)(2,1)}) %all-gather.8.cloned.1.call-update) | async-done | bytes 14450704 | tf_op jit(solution)/shard_map/all_gather | solution.py:103
  380.5 19.1 %fusion.8 = bf16[512,1344]{0,1:T(8,128)(2,1)} fusion(bf16[512,5376]{0,1:T(8,128)(2,1)} %all-gather.4.cloned.1.call-done, bf16[5376,1344]{1,0:T(8,128)(2,1)} %all-gather.8.cloned.1.call-done, f32[512,1344]{0,1:T(8,128)S(1)} %fusion.42), kind=kOutput, calls=%fused_computation.15 | convolution fusion | flops 7405633536 | bytes 24084480 | tf_op jit(solution)/shard_map/dot_general | solution.py:22
  (4 shorter events, 0.1 us)
Async XLA Ops:
  7.2 94.6 %reduce-scatter.2.cloned.1.call-start = ((), (), s32[]{:S(2)}) async-start(), calls=%async_computation.1 | async-start | bytes 6193152 | tf_op jit(solution)/shard_map/reduce_scatter | solution.py:85
  9.4 16.1 %collective-permute-start = (bf16[512,512]{0,1:T(8,128)(2,1)S(1)}, bf16[512,512]{0,1:T(8,128)(2,1)S(1)}, u32[]{:S(2)}, u32[]{:S(2)}) collective-permute-start(bf16[512,512]{0,1:T(8,128)(2,1)S(1)} %pad_maximum_fusion), channel_id=1, source_target_pairs={{0,16},{8,24},{16,32},{24,40},{32,48},{40,56},{48,64},{56,72},{64,... | collective-permute-start | bytes 1572872 | tf_op jit(solution)/shard_map/ppermute | solution.py:18
  15.0 21.8 %collective-permute-start.1 = (bf16[512,512]{0,1:T(8,128)(2,1)S(1)}, bf16[512,512]{0,1:T(8,128)(2,1)S(1)}, u32[]{:S(2)}, u32[]{:S(2)}) collective-permute-start(bf16[512,512]{0,1:T(8,128)(2,1)S(1)} %pad_maximum_fusion), channel_id=1, source_target_pairs={{0,8},{8,16},{16,24},{24,32},{32,40},{40,48},{48,56},{56,64},{64,7... | collective-permute-start | bytes 1572872 | tf_op jit(solution)/shard_map/ppermute | solution.py:18
  59.3 59.1 %copy-start.1 = (bf16[512,672]{0,1:T(8,128)(2,1)S(1)}, bf16[512,672]{0,1:T(8,128)(2,1)}, u32[]{:S(2)}) copy-start(bf16[512,672]{0,1:T(8,128)(2,1)} %param.15) | copy-start | bytes 2064388
  59.3 59.1 %copy-start.2 = (f32[672]{0:T(1024)S(1)}, f32[672]{0:T(1024)}, u32[]{:S(2)}) copy-start(f32[672]{0:T(1024)} %param.16) | copy-start | bytes 8068
  59.3 74.0 %copy-start.3 = (f32[672]{0:T(1024)S(1)}, f32[672]{0:T(1024)}, u32[]{:S(2)}) copy-start(f32[672]{0:T(1024)} %param.17) | copy-start | bytes 8068
  59.3 112.2 %all-gather.4.cloned.1.call-start = ((), (), s32[]{:S(2)}) async-start(), calls=%async_computation.2 | async-start | bytes 6193152 | tf_op jit(solution)/shard_map/all_gather | solution.py:97
  119.9 168.3 %copy-start = (bf16[512,672]{0,1:T(8,128)(2,1)}, bf16[512,672]{0,1:T(8,128)(2,1)S(1)}, u32[]{:S(2)}) copy-start(bf16[512,672]{0,1:T(8,128)(2,1)S(1)} %get-tuple-element.15) | copy-start | bytes 2064388
  134.4 141.5 %all-gather.6.cloned.1.call-start = ((), (), s32[]{:S(2)}) async-start(), calls=%async_computation.3 | async-start | bytes 16084992 | tf_op jit(solution)/shard_map/all_gather | solution.py:102
  135.2 245.3 %all-gather.8.cloned.1.call-start = ((), (), s32[]{:S(2)}) async-start(), calls=%async_computation.4 | async-start | bytes 16084992 | tf_op jit(solution)/shard_map/all_gather | solution.py:103
Sparse Core Ops, SparseCore 0:
  59.4 42.3 reduce-scatter.1
  134.5 36.8 all-gather.3
  173.6 102.2 all-gather.5
  277.9 102.5 all-gather.7
where the time goes:
time: 407 us; the launch traced here: 406 us
  waiting for transfers between devices  289 us (71%)
  matrix products  53.7 us (13%)
  blocking collectives  28.7 us (7%)
  between operations  13.9 us (3%)
  other arithmetic  8.23 us (2%)
  starting transfers between devices  8.1 us (2%)
  local copies, waits for them, and re-layouts  4.23 us (1%)
    all_gather x1, waiting for transfers between devices, per_device(): lax.all_gather(gate_weight, 'ctx', axis=0, tiled=True)  104 us
    all_gather x1, waiting for transfers between devices, per_device(): up_sums = add_single(lax.all_gather(up_weight, 'ctx', axis=0, tiled=True))  92.3 us
    reduce_scatter x1, waiting for transfers between devices, per_device(): lax.psum_scatter(partial_value.astype(jnp.bfloat16), 'tp', scatter_dimens...  42.4 us
    all_gather x1, waiting for transfers between devices, per_device(): gathered = lax.all_gather(normed, 'tp', axis=1, tiled=True)  35.7 us
    dot_general x2, matrix products, accumulate(): return jnp.dot(gathered, piece, preferred_element_type=jnp.float32)  31.4 us
    psum x1, blocking collectives, per_device(): first_sum = lax.psum(jnp.sum(owned * owned, axis=1), 'tp')  15.2 us
    psum x1, blocking collectives, per_device(): second_sum = lax.psum(jnp.sum(stream * stream, axis=1), 'tp')  13.4 us
    ppermute x2, waiting for transfers between devices, from_behind(): return lax.ppermute(value, axis, pairs)  13.4 us
  transfers between devices with their start and end apart: 6, of which 6 were waited for; matrix products, arithmetic and copies ran while one was open for 5% of the time, Pallas kernels for 0%

commit v1 on v0

v1 whole, which is shorter than its diff:
```python
import jax
import jax.numpy as jnp
from jax import lax
from jax.experimental import pallas as pl
from jax.experimental.pallas import tpu as pltpu
from jax.sharding import Mesh, PartitionSpec as P

D = 5376
HD = 128
WINDOW = 1024
EPS = 1e-06
LOG2E = 1.4426950408889634
SCALE = float(168) ** -0.5
TOK = 512
PER = 64
BF = jnp.bfloat16
F32 = jnp.float32
VM = pl.BlockSpec(memory_space=pltpu.VMEM)
SM = pl.BlockSpec(memory_space=pltpu.SMEM)
HB = pl.BlockSpec(memory_space=pl.ANY)
MB = 1 << 20


def params(mb):
    return pltpu.CompilerParams(vmem_limit_bytes=mb * MB)


def cost(flops, nbytes, trans=0):
    return pl.CostEstimate(flops=int(flops), bytes_accessed=int(nbytes), transcendentals=int(trans))


def shift(value, axis, by):
    n = lax.axis_size(axis)
    return lax.ppermute(value, axis, [(i, (i + by) % n) for i in range(n)])


def behind(value):
    n = 16
    return lax.ppermute(value, ("y", "x"), [(i, i + 1) for i in range(n - 1)])


def pack_kernel(g_ref, u_ref, o_ref):
    g, u = g_ref[...], u_ref[...]
    for j in range(7):
        lo = 192 * j
        o_ref[:, 384 * j:384 * j + 384] = jnp.concatenate(
            [g[:, lo:lo + 128], u[:, lo:lo + 128], g[:, lo + 128:lo + 192], u[:, lo + 128:lo + 192]], axis=1
        )


def pack(gate, up):
    return pl.pallas_call(
        pack_kernel,
        out_shape=jax.ShapeDtypeStruct((336, 2688), BF),
        in_specs=[VM, VM],
        out_specs=VM,
        compiler_params=params(24),
        cost_estimate=cost(0, 4 * 336 * 2688),
        name="pack",
    )(gate, up)


def attend_kernel(at_ref, q_ref, kv2_ref, kv1_ref, kv0_ref, qid_ref, kid_ref, o_ref):
    z, c = at_ref[0], at_ref[1]
    k = jnp.concatenate([kv2_ref[:, :HD], kv1_ref[:, :HD], kv0_ref[:, :HD]], axis=0)
    v = jnp.concatenate([kv2_ref[:, HD:], kv1_ref[:, HD:], kv0_ref[:, HD:]], axis=0)
    for b in range(2):
        lo = 256 * b
        qid = qid_ref[lo:lo + 256, :]
        kid = kid_ref[:, lo:lo + 1280]
        row = lax.broadcasted_iota(jnp.int32, (256, 1280), 0)
        col = lax.broadcasted_iota(jnp.int32, (256, 1280), 1)
        allowed = (qid == kid) & (col > row) & (col <= row + 1024)
        outs = []
        for h in range(2):
            q = q_ref[lo:lo + 256, HD * h:HD * h + HD]
            s = lax.dot_general(q, k[lo:lo + 1280], (((1,), (1,)), ((), ())), preferred_element_type=F32)
            s = jnp.where(allowed, s * (SCALE * LOG2E), -1e30)
            top = jnp.max(s, axis=1, keepdims=True)
            e = jnp.exp2(s - top)
            total = jnp.sum(e, axis=1, keepdims=True)
            mix = jnp.dot(e.astype(BF), v[lo:lo + 1280], preferred_element_type=F32)
            outs.append(mix / total)
        out = jnp.concatenate(outs, axis=1).astype(BF)
        for i in range(4):
            zz, cc = 2 * b + i // 2, i % 2
            o_ref[(cc + c) % 2, (zz - z + 4) % 4] = out[PER * i:PER * i + PER]


def attend(at, q, kv2, kv1, kv0, qid, kid):
    return pl.pallas_call(
        attend_kernel,
        out_shape=jax.ShapeDtypeStruct((2, 4, PER, 256), BF),
        in_specs=[SM] + [VM] * 6,
        out_specs=VM,
        compiler_params=params(32),
        cost_estimate=cost(4 * 1024 * 1280 * 128 * 1.5, 2 * MB, 1024 * 1280),
        name="attend",
    )(at, q, kv2, kv1, kv0, qid, kid)


def project_kernel(a0, a1, s0, s1, w_ref, ws_ref, p0, p1t, p1b, p2t, p2b, p3t, p3b):
    acc = jnp.dot(a0[...], w_ref[:256], preferred_element_type=F32)
    acc += jnp.dot(a1[...], w_ref[256:], preferred_element_type=F32)
    acc += jnp.dot(s0[...], ws_ref[:256], preferred_element_type=F32)
    acc += jnp.dot(s1[...], ws_ref[256:], preferred_element_type=F32)
    out = acc.astype(BF)
    p0[...] = out[:64]
    for i, ref in enumerate((p1t, p1b, p2t, p2b, p3t, p3b)):
        ref[...] = out[64 + 32 * i:96 + 32 * i]


def project(a0, a1, s0, s1, w, ws):
    width = 768
    row = lambda r: pl.BlockSpec((r, width), lambda j: (0, j))
    full = pl.BlockSpec((256, 256), lambda j: (0, 0))
    return pl.pallas_call(
        project_kernel,
        out_shape=[jax.ShapeDtypeStruct((64, D), BF)] + [jax.ShapeDtypeStruct((32, D), BF)] * 6,
        grid=(D // width,),
        in_specs=[full] * 4 + [row(512)] * 2,
        out_specs=[row(64)] + [row(32)] * 6,
        compiler_params=params(24),
        cost_estimate=cost(2 * 256 * 1024 * D, 2 * 1280 * D),
        name="project",
    )(a0, a1, s0, s1, w, ws)


def norm_kernel(p0, at_ref, ab_ref, bt_ref, bb_ref, res_ref, post_ref, pre_ref, new_ref, nrm_ref):
    for half, (a, b) in enumerate(((at_ref, bt_ref), (ab_ref, bb_ref))):
        rows = slice(32 * half, 32 * half + 32)
        owned = p0[rows].astype(F32) + a[...].astype(F32) + b[...].astype(F32)
        factor = lax.rsqrt(jnp.mean(owned * owned, axis=1, keepdims=True) + EPS)
        new = (res_ref[rows].astype(F32) + owned * factor * post_ref[...]).astype(BF)
        new_ref[rows] = new
        stream = new.astype(F32)
        second = lax.rsqrt(jnp.mean(stream * stream, axis=1, keepdims=True) + EPS)
        nrm_ref[rows] = (stream * second * pre_ref[...]).astype(BF)


def norm(*args):
    return pl.pallas_call(
        norm_kernel,
        out_shape=[jax.ShapeDtypeStruct((PER, D), BF)] * 2,
        in_specs=[VM] * 8,
        out_specs=[VM] * 2,
        compiler_params=params(24),
        cost_estimate=cost(20 * PER * D, 8 * PER * D),
        name="norm",
    )(*args)


def gated_kernel(tokens_at, *refs):
    pieces, (w_ref, o_ref, n_ref, sems) = refs[:len(tokens_at)], refs[len(tokens_at):][1:]
    where = refs[len(tokens_at)]

    @pl.when(pl.program_id(0) == 0)
    def _():
        z, c = where[0], where[1]
        copies = []
        for i, (ref, (dz, dc, part)) in enumerate(zip(pieces, tokens_at)):
            base = 64 * (2 * ((z + dz) % 4) + (c + dc) % 2)
            rows = 64
            if part is not None:
                base, rows = base + 32 * part, 32
            copies.append(pltpu.make_async_copy(ref, n_ref.at[pl.ds(pl.multiple_of(base, 32), rows)], sems.at[i]))
            copies[-1].start()
        for copy in copies:
            copy.wait()

    acc = jnp.dot(n_ref[...], w_ref[...], preferred_element_type=F32)
    last = acc[:, 256:]
    g = jnp.concatenate([acc[:, :128], last], axis=1)
    u = jnp.concatenate([acc[:, 128:256], pltpu.roll(last, 64, 1)], axis=1)
    act = 0.5 * g * (1 + jnp.tanh(0.7978845608028654 * (g + 0.044715 * (g * g * g)))) * u
    o_ref[...] = act.T[:192].astype(BF)


def gated(pieces, tokens_at, where, w):
    blocks = w.shape[1] // 384
    n = len(pieces)

    def body(*refs):
        gated_kernel(tokens_at, *refs)

    return pl.pallas_call(
        body,
        out_shape=jax.ShapeDtypeStruct((192 * blocks, TOK), BF),
        grid=(blocks,),
        in_specs=[HB] * n + [SM, pl.BlockSpec((D, 384), lambda j: (0, j))],
        out_specs=pl.BlockSpec((192, TOK), lambda j: (j, 0)),
        scratch_shapes=[pltpu.VMEM((TOK, D), BF), pltpu.SemaphoreType.DMA((n,))],
        compiler_params=params(48),
        cost_estimate=cost(2 * TOK * D * 384 * blocks, 2 * D * 384 * blocks + 2 * TOK * D),
        name="gated",
    )(*pieces, where, w)


def per_device(queries, keys, values, doc_ids, out_weight, residual, post_gain, pre_gain, gate_weight, up_weight):
    y, x, z, c = (lax.axis_index(a) for a in ("y", "x", "z", "c"))
    where = jnp.stack([z, c]).astype(jnp.int32)

    w = pack(gate_weight, up_weight)
    w_first = lax.all_gather(w[:, :1920], ("y", "x"), axis=0, tiled=True)
    w_last = lax.all_gather(w[:, 1920:], ("y", "x"), axis=0, tiled=True)

    start = (4 * y + x) * TOK
    padded = jnp.concatenate([jnp.full((2 * TOK,), -1, jnp.int32), doc_ids])
    kid = lax.dynamic_slice_in_dim(padded, start, 3 * TOK, 0)[None, :]
    qid = lax.dynamic_slice_in_dim(doc_ids, start, TOK, 0)[:, None]

    mixes = []
    for h in range(2):
        cols = slice(HD * h, HD * h + HD)
        kv0 = jnp.concatenate([keys[:, cols], values[:, cols]], axis=1)
        kv1 = behind(kv0)
        kv2 = behind(kv1)
        mixes.append(attend(where, queries[:, 256 * h:256 * h + 256], kv2, kv1, kv0, qid, kid))
    other_weight = shift(out_weight, "c", 1)
    own = [m[0].reshape(256, 256) for m in mixes]
    other = [shift(m[1].reshape(256, 256), "c", 1) for m in mixes]
    p0, p1t, p1b, p2t, p2b, p3t, p3b = project(*own, *other, out_weight, other_weight)

    up_t = shift(p2t, "z", 1)
    dn_b = shift(p2b, "z", -1)
    a_b = shift(p1b, "z", 1)
    b_t = shift(p3t, "z", -1)
    add = lambda p, q: (p.astype(F32) + q.astype(F32)).astype(BF)
    a_t = shift(add(p1t, up_t), "z", 1)
    b_b = shift(add(p3b, dn_b), "z", -1)

    mine = lax.all_to_all(residual, ("z", "c"), 0, 1, tiled=True)
    post = lax.all_gather(post_gain, ("z", "c"), axis=0, tiled=True)[None, :]
    pre = lax.all_gather(pre_gain, ("z", "c"), axis=0, tiled=True)[None, :]
    new, nrm = norm(p0, a_t, a_b, b_t, b_b, mine, post, pre)
    new_residual = lax.all_to_all(new, ("z", "c"), 1, 0, tiled=True)

    top, bottom = nrm[:32], nrm[32:]
    m_t, m_b = shift(top, "z", 1), shift(bottom, "z", 1)
    q_t, q_b = shift(top, "z", -1), shift(bottom, "z", -1)
    f_t, f_b = shift(m_t, "z", 1), shift(q_b, "z", -1)
    pieces = [nrm, m_t, m_b, q_t, q_b, f_t, f_b]
    places = [(0, None), (3, 0), (3, 1), (1, 0), (1, 1), (2, 0), (2, 1)]
    pieces += [shift(p, "c", 1) for p in pieces]
    tokens_at = [(dz, dc, part) for dc in range(2) for dz, part in places]
    act = jnp.concatenate([gated(pieces, tokens_at, where, w_first), gated(pieces, tokens_at, where, w_last)], axis=0)
    return new_residual, act.T


def solution(mesh):
    fine = Mesh(mesh.devices.reshape(4, 4, 4, 2), ("y", "x", "z", "c"))
    t, f = ("y", "x"), ("z", "c")
    in_specs = (P(t, f), P(t, f), P(t, f), P(), P(f, None), P(t, f), P(f), P(f), P(t, f), P(t, f))
    return jax.shard_map(per_device, mesh=fine, in_specs=in_specs, out_specs=(P(t, f), P(t, f)), check_vma=False)
```

time: 407 us -> 257 us (0.63)
  waiting for transfers between devices: 289 us -> 78.8 us
  matrix products: 53.7 us -> 0 us
  Pallas kernels: 0 us -> 49 us
  starting transfers between devices: 8.1 us -> 53.5 us
  local copies, waits for them, and re-layouts: 4.23 us -> 30.5 us
  other arithmetic: 8.23 us -> 3.43 us
    all_gather x3 -> x2, waiting for transfers between devices: 232 us -> 27.3 us  [the longest x1 27.3 us: per_device(): w_first = lax.all_gather(w[:, :1920], ('y', 'x'), axis=0, tiled=True)]
    pallas_call x0 -> x7, Pallas kernels: none -> 49 us  [the longest x2 33 us: gated(): pl.pallas_call(body, out_shape=jax.ShapeDtypeStruct((192 * blocks, TOK),...]
    dot_general x4 -> x0, matrix products: 45.6 us -> none  [the longest x2 31.4 us: accumulate(): return jnp.dot(gathered, piece, preferred_element_type=jnp.float32)]
    reduce_scatter x1 -> x0, waiting for transfers between devices: 42.4 us -> none  [per_device(): lax.psum_scatter(partial_value.astype(jnp.bfloat16), 'tp', scatter_dimens...]
    ppermute x2 -> x26, starting transfers between devices: 7.76 us -> 43.9 us  [the longest x22 29 us: shift(): return lax.ppermute(value, axis, [(i, (i + by) % n) for i in range(n)])]
    psum x2 -> x0, blocking collectives: 28.7 us -> none  [the longest x1 15.2 us: per_device(): first_sum = lax.psum(jnp.sum(owned * owned, axis=1), 'tp')]
    ppermute x2 -> x26, waiting for transfers between devices: 13.4 us -> 40.5 us  [the longest x22 26.6 us: shift(): return lax.ppermute(value, axis, [(i, (i + by) % n) for i in range(n)])]
    unnamed x0 -> x1, blocking collectives: none -> 25.3 us
  transfers between devices with their start and end apart: 6 -> 30, of which waited for: 6 -> 9; matrix products, arithmetic and copies ran while one was open for 5% -> 5% of each run, Pallas kernels for 0% -> 11%
where the time goes in v1:
time: 257 us; the launch traced here: 256 us
  waiting for transfers between devices  78.8 us (31%)
  starting transfers between devices  53.5 us (21%)
  Pallas kernels  49 us (19%)
  local copies, waits for them, and re-layouts  30.5 us (12%)
  blocking collectives  25.3 us (10%)
  between operations  15 us (6%)
  other arithmetic  3.43 us (1%)
    pallas_call x2, Pallas kernels, gated(): pl.pallas_call(body, out_shape=jax.ShapeDtypeStruct((192 * blocks, TOK),...  33 us
    ppermute x22, starting transfers between devices, shift(): return lax.ppermute(value, axis, [(i, (i + by) % n) for i in range(n)])  29 us
    all_gather x1, waiting for transfers between devices, per_device(): w_first = lax.all_gather(w[:, :1920], ('y', 'x'), axis=0, tiled=True)  27.3 us
    ppermute x22, waiting for transfers between devices, shift(): return lax.ppermute(value, axis, [(i, (i + by) % n) for i in range(n)])  26.6 us
    unnamed x1, blocking collectives  25.3 us
    unnamed x65, local copies, waits for them, and re-layouts  18.6 us
    ppermute x4, starting transfers between devices, behind(): return lax.ppermute(value, ('y', 'x'), [(i, i + 1) for i in range(n - 1)])  14.8 us
    ppermute x4, waiting for transfers between devices, behind(): return lax.ppermute(value, ('y', 'x'), [(i, i + 1) for i in range(n - 1)])  13.9 us
  transfers between devices with their start and end apart: 30, of which 9 were waited for; matrix products, arithmetic and copies ran while one was open for 5% of the time, Pallas kernels for 11%

profile of v1, /device:TPU:1, one launch (start us, length us, event | category | flops | bytes accessed | tf_op | source)
XLA Modules:
  0.0 255.5 jit_solution(10393498520209874583)
XLA Ops:
  7.2 1.2 copy-done
  8.4 1.2 copy-done.1
  11.0 1.1 slice.60
  12.1 1.5 collective-permute-start.6
  13.8 3.2 %collective-permute-start = (bf16[512,256]{1,0:T(8,128)(2,1)S(1)}, bf16[512,256]{1,0:T(8,128)(2,1)S(1)}, u32[]{:S(2)}, u32[]{:S(2)}) collective-permute-start(bf16[512,256]{1,0:T(8,128)(2,1)S(1)} %pad_maximum_fusion.kv0_ref), channel_id=1, source_target_pairs={{0,8},{8,16},{16,24},{24,32},{32,40},{40,48},{48,56},{56,64},{64,7... | collective-permute-start | bytes 786440 | tf_op jit(solution)/shard_map/ppermute | solution.py:39
  17.0 3.3 %collective-permute-start.2 = (bf16[512,256]{1,0:T(8,128)(2,1)S(1)}, bf16[512,256]{1,0:T(8,128)(2,1)S(1)}, u32[]{:S(2)}, u32[]{:S(2)}) collective-permute-start(bf16[512,256]{1,0:T(8,128)(2,1)S(1)} %pad_maximum_fusion.1.kv0_ref), channel_id=1, source_target_pairs={{0,8},{8,16},{16,24},{24,32},{32,40},{40,48},{48,56},{56,64},{64,7... | collective-permute-start | bytes 786440 | tf_op jit(solution)/shard_map/ppermute | solution.py:39
  20.4 2.2 collective-permute-done.kv1_ref
  22.7 4.1 %collective-permute-start.1 = (bf16[512,256]{1,0:T(8,128)(2,1)S(1)}, bf16[512,256]{1,0:T(8,128)(2,1)S(1)}, u32[]{:S(2)}, u32[]{:S(2)}) collective-permute-start(bf16[512,256]{1,0:T(8,128)(2,1)S(1)} %collective-permute-done.kv1_ref), channel_id=1, source_target_pairs={{0,8},{8,16},{16,24},{24,32},{32,40},{40,48},{48,56},{56,64},{64,7... | collective-permute-start | bytes 786440 | tf_op jit(solution)/shard_map/ppermute | solution.py:39
  27.1 3.9 %collective-permute-done.2.kv1_ref = bf16[512,256]{1,0:T(8,128)(2,1)S(1)} collective-permute-done((bf16[512,256]{1,0:T(8,128)(2,1)S(1)}, bf16[512,256]{1,0:T(8,128)(2,1)S(1)}, u32[]{:S(2)}, u32[]{:S(2)}) %collective-permute-start.2) | collective-permute-done | bytes 262176 | tf_op jit(solution)/shard_map/ppermute | solution.py:39
  31.0 4.3 %collective-permute-start.3 = (bf16[512,256]{1,0:T(8,128)(2,1)S(1)}, bf16[512,256]{1,0:T(8,128)(2,1)S(1)}, u32[]{:S(2)}, u32[]{:S(2)}) collective-permute-start(bf16[512,256]{1,0:T(8,128)(2,1)S(1)} %collective-permute-done.2.kv1_ref), channel_id=1, source_target_pairs={{0,8},{8,16},{16,24},{24,32},{32,40},{40,48},{48,56},{56,64},{64,7... | collective-permute-start | bytes 786440 | tf_op jit(solution)/shard_map/ppermute | solution.py:39
  35.3 6.8 %collective-permute-done.1.kv2_ref = bf16[512,256]{1,0:T(8,128)(2,1)S(1)} collective-permute-done((bf16[512,256]{1,0:T(8,128)(2,1)S(1)}, bf16[512,256]{1,0:T(8,128)(2,1)S(1)}, u32[]{:S(2)}, u32[]{:S(2)}) %collective-permute-start.1) | collective-permute-done | bytes 262176 | tf_op jit(solution)/shard_map/ppermute | solution.py:39
  42.1 3.3 %attend.2 = bf16[2,4,64,256]{3,2,1,0:T(8,128)(2,1)S(1)} custom-call(s32[2]{0:T(128)S(1)} %pad_add_fusion.at_ref.refs_14_, bf16[512,256]{1,0:T(8,128)(2,1)S(1)} %get-tuple-element.27.q_ref, bf16[512,256]{1,0:T(8,128)(2,1)S(1)} %collective-permute-done.1.kv2_ref, bf16[512,256]{1,0:T(8,128)(2,1)S(1)} %collective-permute-done.kv1_ref, ...), custom_call_target="tpu_custom_call" | custom-call | flops 1006632960 | bytes 2097152 | tf_op jit(solution)/shard_map/attend/pallas_call | solution.py:91
  45.4 1.4 collective-permute-start.4
  46.8 1.0 collective-permute-done.3.kv2_ref
  47.8 3.3 %attend.3 = bf16[2,4,64,256]{3,2,1,0:T(8,128)(2,1)S(1)} custom-call(s32[2]{0:T(128)S(1)} %pad_add_fusion.at_ref.refs_14_, bf16[512,256]{1,0:T(8,128)(2,1)S(1)} %get-tuple-element.26.q_ref, bf16[512,256]{1,0:T(8,128)(2,1)S(1)} %collective-permute-done.3.kv2_ref, bf16[512,256]{1,0:T(8,128)(2,1)S(1)} %collective-permute-done.2.kv1_ref, ...), custom_call_target="tpu_custom_call" | custom-call | flops 1006632960 | bytes 2097152 | tf_op jit(solution)/shard_map/attend/pallas_call | solution.py:91
  52.0 1.0 collective-permute-done.5.s1
  53.0 8.2 %project.1 = (bf16[64,5376]{1,0:T(8,128)(2,1)S(1)}, bf16[32,5376]{1,0:T(8,128)(2,1)S(1)}, bf16[32,5376]{1,0:T(8,128)(2,1)}, bf16[32,5376]{1,0:T(8,128)(2,1)}, bf...) custom-call(bf16[256,256]{1,0:T(8,128)(2,1)S(1)} %bitcast.17, ...), custom_call_target="tpu_custom_call" | custom-call | flops 2818572288 | bytes 13762560 | tf_op jit(solution)/shard_map/project/pallas_call | solution.py:117
  62.0 1.6 collective-permute-start.7
  63.7 1.1 copy.16
  64.8 5.4 %all-to-all-start = ((bf16[8,64,672]{2,1,0:T(8,128)(2,1)}), bf16[8,64,672]{2,1,0:T(8,128)(2,1)}, u32[]{:S(2)}, u32[]{:S(2)}) async-start(bf16[8,64,672]{2,1,0:T(8,128)(2,1)} %bitcast.7), calls=%async_computation | async-start | bytes 1572864 | tf_op jit(solution)/shard_map/all_to_all | solution.py:232
  70.2 1.4 collective-permute-start.9
  71.5 1.3 collective-permute-start.10
  72.8 1.4 collective-permute-start.11
  75.1 20.6 %collective-permute-done.11 = bf16[32,5376]{1,0:T(8,128)(2,1)S(1)} collective-permute-done((bf16[32,5376]{1,0:T(8,128)(2,1)S(1)}, bf16[32,5376]{1,0:T(8,128)(2,1)S(1)}, u32[]{:S(2)}, u32[]{:S(2)}) %collective-permute-start.11) | collective-permute-done | bytes 344096 | tf_op jit(solution)/shard_map/ppermute | solution.py:34
  95.8 1.6 collective-permute-start.12
  99.2 25.3 %all-reduce.3 = (f32[5376]{0:T(1024)S(1)}, f32[5376]{0:T(1024)S(1)}) all-reduce(f32[5376]{0:T(1024)S(1)} %dynamic-update-slice, f32[5376]{0:T(1024)S(1)} %dynamic-update-slice.1), channel_id=1, replica_groups=mesh['y'=4,'x'=4,'z'=4,'c'=2] {'z','c'}, use_global_device_ids=true, to_apply=%add.1 | all-reduce | flops 10752 | bytes 86016
  124.6 2.4 copy.17
  127.0 1.9 all_to_all.31.res_ref
  130.4 1.0 copy-done.3
  134.0 3.6 %collective-permute-start.16 = (bf16[32,5376]{1,0:T(8,128)(2,1)S(1)}, bf16[32,5376]{1,0:T(8,128)(2,1)S(1)}, u32[]{:S(2)}, u32[]{:S(2)}) collective-permute-start(bf16[32,5376]{1,0:T(8,128)(2,1)S(1)} %get-tuple-element.24), channel_id=1, source_target_pairs={{0,6},{2,0},{4,2},{6,4},{1,7},{3,1},{5,3},{7,5},{8,14},{10,8},{12,... | collective-permute-start | bytes 1032200 | tf_op jit(solution)/shard_map/ppermute | solution.py:34
  137.6 3.6 %collective-permute-start.19 = (bf16[64,5376]{1,0:T(8,128)(2,1)S(1)}, bf16[64,5376]{1,0:T(8,128)(2,1)S(1)}, u32[]{:S(2)}, u32[]{:S(2)}) collective-permute-start(bf16[64,5376]{1,0:T(8,128)(2,1)S(1)} %get-tuple-element.19.refs_0_), channel_id=1, source_target_pairs={{0,1},{1,0},{2,3},{3,2},{4,5},{5,4},{6,7},{7,6},{8,9},{9,8},{10,11... | collective-permute-start | bytes 2064392 | tf_op jit(solution)/shard_map/ppermute | solution.py:34
  141.2 2.7 %collective-permute-start.15 = (bf16[32,5376]{1,0:T(8,128)(2,1)}, bf16[32,5376]{1,0:T(8,128)(2,1)S(1)}, u32[]{:S(2)}, u32[]{:S(2)}) collective-permute-start(bf16[32,5376]{1,0:T(8,128)(2,1)} %get-tuple-element.25), channel_id=1, source_target_pairs={{0,6},{2,0},{4,2},{6,4},{1,7},{3,1},{5,3},{7,5},{8,14},{10,8},{12,... | collective-permute-start | bytes 1032200 | tf_op jit(solution)/shard_map/ppermute | solution.py:34
  143.9 3.8 %collective-permute-start.18 = (bf16[32,5376]{1,0:T(8,128)(2,1)S(1)}, bf16[32,5376]{1,0:T(8,128)(2,1)}, u32[]{:S(2)}, u32[]{:S(2)}) collective-permute-start(bf16[32,5376]{1,0:T(8,128)(2,1)S(1)} %collective-permute-done.16.refs_4_), channel_id=1, source_target_pairs={{0,6},{2,0},{4,2},{6,4},{1,7},{3,1},{5,3},{7,5},{8,14},{10,8},{12,... | collective-permute-start | bytes 1032200 | tf_op jit(solution)/shard_map/ppermute | solution.py:34
  147.7 5.0 %collective-permute-done.14.refs_2_ = bf16[32,5376]{1,0:T(8,128)(2,1)S(1)} collective-permute-done((bf16[32,5376]{1,0:T(8,128)(2,1)S(1)}, bf16[32,5376]{1,0:T(8,128)(2,1)S(1)}, u32[]{:S(2)}, u32[]{:S(2)}) %collective-permute-start.14) | collective-permute-done | bytes 344096 | tf_op jit(solution)/shard_map/ppermute | solution.py:34
  152.7 2.8 %collective-permute-start.20 = (bf16[32,5376]{1,0:T(8,128)(2,1)S(1)}, bf16[32,5376]{1,0:T(8,128)(2,1)}, u32[]{:S(2)}, u32[]{:S(2)}) collective-permute-start(bf16[32,5376]{1,0:T(8,128)(2,1)S(1)} %collective-permute-done.13.refs_1_), channel_id=1, source_target_pairs={{0,1},{1,0},{2,3},{3,2},{4,5},{5,4},{6,7},{7,6},{8,9},{9,8},{10,11... | collective-permute-start | bytes 1032200 | tf_op jit(solution)/shard_map/ppermute | solution.py:34
  155.4 2.1 all_to_all.32
  157.6 2.2 copy.18
  159.8 4.2 %all-to-all-start.1 = ((bf16[64,8,672]{2,0,1:T(8,128)(2,1)}), bf16[64,8,672]{2,0,1:T(8,128)(2,1)}, u32[]{:S(2)}, u32[]{:S(2)}) async-start(bf16[64,8,672]{2,0,1:T(8,128)(2,1)} %copy.18), calls=%async_computation.1 | async-start | bytes 1572864 | tf_op jit(solution)/shard_map/all_to_all | solution.py:236
  165.4 10.9 %all-to-all-done.1 = bf16[64,8,672]{2,0,1:T(8,128)(2,1)} async-done(((bf16[64,8,672]{2,0,1:T(8,128)(2,1)}), bf16[64,8,672]{2,0,1:T(8,128)(2,1)}, u32[]{:S(2)}, u32[]{:S(2)}) %all-to-all-start.1) | async-done | bytes 688160 | tf_op jit(solution)/shard_map/all_to_all | solution.py:236
  176.3 2.3 copy.19
  181.1 1.0 copy-done.10
  182.1 1.0 copy-done.12
  183.1 1.0 copy-done.15
  184.1 11.4 %gated.3 = bf16[384,512]{1,0:T(8,128)(2,1)S(1)} custom-call(bf16[64,5376]{1,0:T(8,128)(2,1)S(1)} %get-tuple-element.19.refs_0_, bf16[32,5376]{1,0:T(8,128)(2,1)S(1)} %collective-permute-done.13.refs_1_, bf16[32,5376]{1,0:T(8,128)(2,1)S(1)} %copy-done.7, bf16[32,5376]{1,0:T(8,128)(2,1)S(1)} %copy-done.10, ...), custom_call_target="tpu_custom_call" | custom-call | flops 4227858432 | bytes 13762560 | tf_op jit(solution)/shard_map/gated/pallas_call | solution.py:186
  195.5 27.3 %all-gather.3.cloned.1.call-done.refs_15_ = bf16[5376,1920]{1,0:T(8,128)(2,1)} async-done(((bf16[336,1920]{1,0:T(8,128)(2,1)}), bf16[5376,1920]{1,0:T(8,128)(2,1)}) %all-gather.3.cloned.1.call-update) | async-done | bytes 20643856 | tf_op jit(solution)/shard_map/all_gather | solution.py:204
  222.8 1.0 copy-done.13
  224.7 21.6 %gated.2 = bf16[960,512]{1,0:T(8,128)(2,1)} custom-call(bf16[64,5376]{1,0:T(8,128)(2,1)S(1)} %get-tuple-element.19.refs_0_, bf16[32,5376]{1,0:T(8,128)(2,1)S(1)} %collective-permute-done.13.refs_1_, bf16[32,5376]{1,0:T(8,128)(2,1)S(1)} %copy-done.8, bf16[32,5376]{1,0:T(8,128)(2,1)S(1)} %copy-done.10, bf16[32,5376]{1,0:T(8,128)(2,1)S(1)} %collective-permute-done.16.refs_4_, ...), custom_call_target="tpu_custom_call" | custom-call | flops 10569646080 | bytes 26148864 | tf_op jit(solution)/shard_map/gated/pallas_call | solution.py:186
  246.3 2.4 maximum_bitcast_fusion
  (111 shorter events, 14.9 us)
Async XLA Ops:
  7.2 172.9 %all-gather.5.cloned.1.call-start = ((), (), s32[]{:S(2)}) async-start(), calls=%async_computation.3 | async-start | bytes 8773632 | tf_op jit(solution)/shard_map/all_gather | solution.py:205
  7.2 1.2 copy-start
  8.4 1.2 copy-start.1
  10.0 3.6 %copy-start.21 = (bf16[512,256]{1,0:T(8,128)(2,1)S(1)}, bf16[512,256]{1,0:T(8,128)(2,1)}, u32[]{:S(2)}) copy-start(bf16[512,256]{1,0:T(8,128)(2,1)} %param.11) | copy-start | bytes 786436
  10.0 3.6 %copy-start.22 = (bf16[512,256]{1,0:T(8,128)(2,1)S(1)}, bf16[512,256]{1,0:T(8,128)(2,1)}, u32[]{:S(2)}) copy-start(bf16[512,256]{1,0:T(8,128)(2,1)} %param.12) | copy-start | bytes 786436
  10.9 9.4 %copy-start.23 = (s32[8192]{0:T(1024)S(1)}, s32[8192]{0:T(1024)}, u32[]{:S(2)}) copy-start(s32[8192]{0:T(1024)} %param.13) | copy-start | bytes 98308
  10.9 16.2 %copy-start.20 = (bf16[512,512]{1,0:T(8,128)(2,1)S(1)}, bf16[512,512]{1,0:T(8,128)(2,1)}, u32[]{:S(2)}) copy-start(bf16[512,512]{1,0:T(8,128)(2,1)} %param.10) | copy-start | bytes 1572868
  10.9 211.8 %all-gather.3.cloned.1.call-start = ((), (), s32[]{:S(2)}) async-start(), calls=%async_computation.2 | async-start | bytes 21934080 | tf_op jit(solution)/shard_map/all_gather | solution.py:204
  12.1 40.9 %collective-permute-start.6 = (bf16[512,5376]{1,0:T(8,128)(2,1)}, bf16[512,5376]{1,0:T(8,128)(2,1)}, u32[]{:S(2)}, u32[]{:S(2)}) collective-permute-start(bf16[512,5376]{1,0:T(8,128)(2,1)} %w_ref.1), channel_id=1, source_target_pairs={{0,1},{1,0},{2,3},{3,2},{4,5},{5,4},{6,7},{7,6},{8,9},{9,8},{10,11... | collective-permute-start | bytes 16515080 | tf_op jit(solution)/shard_map/ppermute | solution.py:34
  13.8 8.9 %collective-permute-start = (bf16[512,256]{1,0:T(8,128)(2,1)S(1)}, bf16[512,256]{1,0:T(8,128)(2,1)S(1)}, u32[]{:S(2)}, u32[]{:S(2)}) collective-permute-start(bf16[512,256]{1,0:T(8,128)(2,1)S(1)} %pad_maximum_fusion.kv0_ref), channel_id=1, source_target_pairs={{0,8},{8,16},{16,24},{24,32},{32,40},{40,48},{48,56},{56,64},{64,7... | collective-permute-start | bytes 786440 | tf_op jit(solution)/shard_map/ppermute | solution.py:39
  17.0 36.0 %slice-start = ((s8[5505024]{0:T(1024)(128)(4,1)}), s8[1310720]{0:T(1024)(128)(4,1)S(1)}, s32[]{:S(2)}) async-start(s8[5505024]{0:T(1024)(128)(4,1)} %bitcast.15), calls=%async_computation.4 | async-start | bytes 2621440
  17.0 14.0 %collective-permute-start.2 = (bf16[512,256]{1,0:T(8,128)(2,1)S(1)}, bf16[512,256]{1,0:T(8,128)(2,1)S(1)}, u32[]{:S(2)}, u32[]{:S(2)}) collective-permute-start(bf16[512,256]{1,0:T(8,128)(2,1)S(1)} %pad_maximum_fusion.1.kv0_ref), channel_id=1, source_target_pairs={{0,8},{8,16},{16,24},{24,32},{32,40},{40,48},{48,56},{56,64},{64,7... | collective-permute-start | bytes 786440 | tf_op jit(solution)/shard_map/ppermute | solution.py:39
  22.7 19.5 %collective-permute-start.1 = (bf16[512,256]{1,0:T(8,128)(2,1)S(1)}, bf16[512,256]{1,0:T(8,128)(2,1)S(1)}, u32[]{:S(2)}, u32[]{:S(2)}) collective-permute-start(bf16[512,256]{1,0:T(8,128)(2,1)S(1)} %collective-permute-done.kv1_ref), channel_id=1, source_target_pairs={{0,8},{8,16},{16,24},{24,32},{32,40},{40,48},{48,56},{56,64},{64,7... | collective-permute-start | bytes 786440 | tf_op jit(solution)/shard_map/ppermute | solution.py:39
  31.0 16.8 %collective-permute-start.3 = (bf16[512,256]{1,0:T(8,128)(2,1)S(1)}, bf16[512,256]{1,0:T(8,128)(2,1)S(1)}, u32[]{:S(2)}, u32[]{:S(2)}) collective-permute-start(bf16[512,256]{1,0:T(8,128)(2,1)S(1)} %collective-permute-done.2.kv1_ref), channel_id=1, source_target_pairs={{0,8},{8,16},{16,24},{24,32},{32,40},{40,48},{48,56},{56,64},{64,7... | collective-permute-start | bytes 786440 | tf_op jit(solution)/shard_map/ppermute | solution.py:39
  42.1 10.9 %slice-start.1 = ((s8[5505024]{0:T(1024)(128)(4,1)}), s8[4194304]{0:T(1024)(128)(4,1)S(1)}, s32[]{:S(2)}) async-start(s8[5505024]{0:T(1024)(128)(4,1)} %bitcast.15), calls=%async_computation.5 | async-start | bytes 8388608
  45.4 6.6 %collective-permute-start.4 = (bf16[256,256]{1,0:T(8,128)(2,1)S(1)}, bf16[256,256]{1,0:T(8,128)(2,1)S(1)}, u32[]{:S(2)}, u32[]{:S(2)}) collective-permute-start(bf16[256,256]{1,0:T(8,128)(2,1)S(1)} %bitcast.19), channel_id=1, source_target_pairs={{0,1},{1,0},{2,3},{3,2},{4,5},{5,4},{6,7},{7,6},{8,9},{9,8},{10,11... | collective-permute-start | bytes 393224 | tf_op jit(solution)/shard_map/ppermute | solution.py:34
  51.1 1.9 collective-permute-start.5
  53.0 10.6 %copy-start.19 = (bf16[512,672]{0,1:T(8,128)(2,1)S(1)}, bf16[512,672]{0,1:T(8,128)(2,1)}, u32[]{:S(2)}) copy-start(bf16[512,672]{0,1:T(8,128)(2,1)} %param.15) | copy-start | bytes 2064388
  62.0 35.4 %copy-start.26 = (u32[128]{0:T(128)S(1)}, u32[128]{0:T(128)}, u32[]{:S(2)}) copy-start(u32[128]{0:T(128)} %constant.31) | copy-start | bytes 1540
  62.0 36.6 %copy-start.24 = (f32[672]{0:T(1024)S(1)}, f32[672]{0:T(1024)}, u32[]{:S(2)}) copy-start(f32[672]{0:T(1024)} %param.16) | copy-start | bytes 8068
  62.0 36.9 %copy-start.25 = (f32[672]{0:T(1024)S(1)}, f32[672]{0:T(1024)}, u32[]{:S(2)}) copy-start(f32[672]{0:T(1024)} %param.17) | copy-start | bytes 8068
  62.0 10.8 %copy-start.18 = (bf16[32,5376]{1,0:T(8,128)(2,1)S(1)}, bf16[32,5376]{1,0:T(8,128)(2,1)}, u32[]{:S(2)}) copy-start(bf16[32,5376]{1,0:T(8,128)(2,1)} %copy-done.17) | copy-start | bytes 1032196
  62.0 12.2 %collective-permute-start.7 = (bf16[32,5376]{1,0:T(8,128)(2,1)}, bf16[32,5376]{1,0:T(8,128)(2,1)S(1)}, u32[]{:S(2)}, u32[]{:S(2)}) collective-permute-start(bf16[32,5376]{1,0:T(8,128)(2,1)} %get-tuple-element.13), channel_id=1, source_target_pairs={{0,2},{2,4},{4,6},{6,0},{1,3},{3,5},{5,7},{7,1},{8,10},{10,12},{12... | collective-permute-start | bytes 1032200 | tf_op jit(solution)/shard_map/ppermute | solution.py:34
  64.8 59.8 %all-to-all-start = ((bf16[8,64,672]{2,1,0:T(8,128)(2,1)}), bf16[8,64,672]{2,1,0:T(8,128)(2,1)}, u32[]{:S(2)}, u32[]{:S(2)}) async-start(bf16[8,64,672]{2,1,0:T(8,128)(2,1)} %bitcast.7), calls=%async_computation | async-start | bytes 1572864 | tf_op jit(solution)/shard_map/all_to_all | solution.py:232
  70.2 58.8 %collective-permute-start.9 = (bf16[32,5376]{1,0:T(8,128)(2,1)}, bf16[32,5376]{1,0:T(8,128)(2,1)S(1)}, u32[]{:S(2)}, u32[]{:S(2)}) collective-permute-start(bf16[32,5376]{1,0:T(8,128)(2,1)} %get-tuple-element.14), channel_id=1, source_target_pairs={{0,2},{2,4},{4,6},{6,0},{1,3},{3,5},{5,7},{7,1},{8,10},{10,12},{12... | collective-permute-start | bytes 1032200 | tf_op jit(solution)/shard_map/ppermute | solution.py:34
  71.5 57.4 %collective-permute-start.10 = (bf16[32,5376]{1,0:T(8,128)(2,1)}, bf16[32,5376]{1,0:T(8,128)(2,1)S(1)}, u32[]{:S(2)}, u32[]{:S(2)}) collective-permute-start(bf16[32,5376]{1,0:T(8,128)(2,1)} %get-tuple-element.15), channel_id=1, source_target_pairs={{0,6},{2,0},{4,2},{6,4},{1,7},{3,1},{5,3},{7,5},{8,14},{10,8},{12,... | collective-permute-start | bytes 1032200 | tf_op jit(solution)/shard_map/ppermute | solution.py:34
  72.8 22.9 %collective-permute-start.11 = (bf16[32,5376]{1,0:T(8,128)(2,1)S(1)}, bf16[32,5376]{1,0:T(8,128)(2,1)S(1)}, u32[]{:S(2)}, u32[]{:S(2)}) collective-permute-start(bf16[32,5376]{1,0:T(8,128)(2,1)S(1)} %copy-done.18), channel_id=1, source_target_pairs={{0,6},{2,0},{4,2},{6,4},{1,7},{3,1},{5,3},{7,5},{8,14},{10,8},{12,... | collective-permute-start | bytes 1032200 | tf_op jit(solution)/shard_map/ppermute | solution.py:34
  75.1 53.9 %collective-permute-start.8 = (bf16[32,5376]{1,0:T(8,128)(2,1)}, bf16[32,5376]{1,0:T(8,128)(2,1)S(1)}, u32[]{:S(2)}, u32[]{:S(2)}) collective-permute-start(bf16[32,5376]{1,0:T(8,128)(2,1)} %add_convert_fusion.1), channel_id=1, source_target_pairs={{0,2},{2,4},{4,6},{6,0},{1,3},{3,5},{5,7},{7,1},{8,10},{10,12},{12... | collective-permute-start | bytes 1032200 | tf_op jit(solution)/shard_map/ppermute | solution.py:34
  95.8 33.9 %collective-permute-start.12 = (bf16[32,5376]{1,0:T(8,128)(2,1)S(1)}, bf16[32,5376]{1,0:T(8,128)(2,1)S(1)}, u32[]{:S(2)}, u32[]{:S(2)}) collective-permute-start(bf16[32,5376]{1,0:T(8,128)(2,1)S(1)} %add_convert_fusion), channel_id=1, source_target_pairs={{0,6},{2,0},{4,2},{6,4},{1,7},{3,1},{5,3},{7,5},{8,14},{10,8},{12,... | collective-permute-start | bytes 1032200 | tf_op jit(solution)/shard_map/ppermute | solution.py:34
  134.0 9.9 %collective-permute-start.13 = (bf16[32,5376]{1,0:T(8,128)(2,1)}, bf16[32,5376]{1,0:T(8,128)(2,1)S(1)}, u32[]{:S(2)}, u32[]{:S(2)}) collective-permute-start(bf16[32,5376]{1,0:T(8,128)(2,1)} %get-tuple-element.25), channel_id=1, source_target_pairs={{0,2},{2,4},{4,6},{6,0},{1,3},{3,5},{5,7},{7,1},{8,10},{10,12},{12... | collective-permute-start | bytes 1032200 | tf_op jit(solution)/shard_map/ppermute | solution.py:34
  134.0 9.9 %collective-permute-start.16 = (bf16[32,5376]{1,0:T(8,128)(2,1)S(1)}, bf16[32,5376]{1,0:T(8,128)(2,1)S(1)}, u32[]{:S(2)}, u32[]{:S(2)}) collective-permute-start(bf16[32,5376]{1,0:T(8,128)(2,1)S(1)} %get-tuple-element.24), channel_id=1, source_target_pairs={{0,6},{2,0},{4,2},{6,4},{1,7},{3,1},{5,3},{7,5},{8,14},{10,8},{12,... | collective-permute-start | bytes 1032200 | tf_op jit(solution)/shard_map/ppermute | solution.py:34
  137.6 27.1 %collective-permute-start.19 = (bf16[64,5376]{1,0:T(8,128)(2,1)S(1)}, bf16[64,5376]{1,0:T(8,128)(2,1)S(1)}, u32[]{:S(2)}, u32[]{:S(2)}) collective-permute-start(bf16[64,5376]{1,0:T(8,128)(2,1)S(1)} %get-tuple-element.19.refs_0_), channel_id=1, source_target_pairs={{0,1},{1,0},{2,3},{3,2},{4,5},{5,4},{6,7},{7,6},{8,9},{9,8},{10,11... | collective-permute-start | bytes 2064392 | tf_op jit(solution)/shard_map/ppermute | solution.py:34
  141.2 11.5 %collective-permute-start.14 = (bf16[32,5376]{1,0:T(8,128)(2,1)S(1)}, bf16[32,5376]{1,0:T(8,128)(2,1)S(1)}, u32[]{:S(2)}, u32[]{:S(2)}) collective-permute-start(bf16[32,5376]{1,0:T(8,128)(2,1)S(1)} %get-tuple-element.24), channel_id=1, source_target_pairs={{0,2},{2,4},{4,6},{6,0},{1,3},{3,5},{5,7},{7,1},{8,10},{10,12},{12... | collective-permute-start | bytes 1032200 | tf_op jit(solution)/shard_map/ppermute | solution.py:34
  141.2 22.7 %collective-permute-start.15 = (bf16[32,5376]{1,0:T(8,128)(2,1)}, bf16[32,5376]{1,0:T(8,128)(2,1)S(1)}, u32[]{:S(2)}, u32[]{:S(2)}) collective-permute-start(bf16[32,5376]{1,0:T(8,128)(2,1)} %get-tuple-element.25), channel_id=1, source_target_pairs={{0,6},{2,0},{4,2},{6,4},{1,7},{3,1},{5,3},{7,5},{8,14},{10,8},{12,... | collective-permute-start | bytes 1032200 | tf_op jit(solution)/shard_map/ppermute | solution.py:34
  143.9 20.2 %collective-permute-start.17 = (bf16[32,5376]{1,0:T(8,128)(2,1)S(1)}, bf16[32,5376]{1,0:T(8,128)(2,1)}, u32[]{:S(2)}, u32[]{:S(2)}) collective-permute-start(bf16[32,5376]{1,0:T(8,128)(2,1)S(1)} %collective-permute-done.13.refs_1_), channel_id=1, source_target_pairs={{0,2},{2,4},{4,6},{6,0},{1,3},{3,5},{5,7},{7,1},{8,10},{10,12},{12... | collective-permute-start | bytes 1032200 | tf_op jit(solution)/shard_map/ppermute | solution.py:34
  143.9 20.6 %collective-permute-start.18 = (bf16[32,5376]{1,0:T(8,128)(2,1)S(1)}, bf16[32,5376]{1,0:T(8,128)(2,1)}, u32[]{:S(2)}, u32[]{:S(2)}) collective-permute-start(bf16[32,5376]{1,0:T(8,128)(2,1)S(1)} %collective-permute-done.16.refs_4_), channel_id=1, source_target_pairs={{0,6},{2,0},{4,2},{6,4},{1,7},{3,1},{5,3},{7,5},{8,14},{10,8},{12,... | collective-permute-start | bytes 1032200 | tf_op jit(solution)/shard_map/ppermute | solution.py:34
  152.7 25.9 %copy-start.6 = (bf16[32,5376]{1,0:T(8,128)(2,1)}, bf16[32,5376]{1,0:T(8,128)(2,1)S(1)}, u32[]{:S(2)}) copy-start(bf16[32,5376]{1,0:T(8,128)(2,1)S(1)} %collective-permute-done.14.refs_2_) | copy-start | bytes 1032196
  152.7 12.4 %collective-permute-start.20 = (bf16[32,5376]{1,0:T(8,128)(2,1)S(1)}, bf16[32,5376]{1,0:T(8,128)(2,1)}, u32[]{:S(2)}, u32[]{:S(2)}) collective-permute-start(bf16[32,5376]{1,0:T(8,128)(2,1)S(1)} %collective-permute-done.13.refs_1_), channel_id=1, source_target_pairs={{0,1},{1,0},{2,3},{3,2},{4,5},{5,4},{6,7},{7,6},{8,9},{9,8},{10,11... | collective-permute-start | bytes 1032200 | tf_op jit(solution)/shard_map/ppermute | solution.py:34
  159.8 16.5 %all-to-all-start.1 = ((bf16[64,8,672]{2,0,1:T(8,128)(2,1)}), bf16[64,8,672]{2,0,1:T(8,128)(2,1)}, u32[]{:S(2)}, u32[]{:S(2)}) async-start(bf16[64,8,672]{2,0,1:T(8,128)(2,1)} %copy.18), calls=%async_computation.1 | async-start | bytes 1572864 | tf_op jit(solution)/shard_map/all_to_all | solution.py:236
  164.0 16.1 %copy-start.9 = (bf16[32,5376]{1,0:T(8,128)(2,1)}, bf16[32,5376]{1,0:T(8,128)(2,1)S(1)}, u32[]{:S(2)}) copy-start(bf16[32,5376]{1,0:T(8,128)(2,1)S(1)} %collective-permute-done.15.refs_3_) | copy-start | bytes 1032196
  164.0 15.4 %collective-permute-start.23 = (bf16[32,5376]{1,0:T(8,128)(2,1)S(1)}, bf16[32,5376]{1,0:T(8,128)(2,1)S(1)}, u32[]{:S(2)}, u32[]{:S(2)}) collective-permute-start(bf16[32,5376]{1,0:T(8,128)(2,1)S(1)} %collective-permute-done.16.refs_4_), channel_id=1, source_target_pairs={{0,1},{1,0},{2,3},{3,2},{4,5},{5,4},{6,7},{7,6},{8,9},{9,8},{10,11... | collective-permute-start | bytes 1032200 | tf_op jit(solution)/shard_map/ppermute | solution.py:34
  164.1 14.5 %collective-permute-start.21 = (bf16[32,5376]{1,0:T(8,128)(2,1)S(1)}, bf16[32,5376]{1,0:T(8,128)(2,1)S(1)}, u32[]{:S(2)}, u32[]{:S(2)}) collective-permute-start(bf16[32,5376]{1,0:T(8,128)(2,1)S(1)} %collective-permute-done.14.refs_2_), channel_id=1, source_target_pairs={{0,1},{1,0},{2,3},{3,2},{4,5},{5,4},{6,7},{7,6},{8,9},{9,8},{10,11... | collective-permute-start | bytes 1032200 | tf_op jit(solution)/shard_map/ppermute | solution.py:34
  164.6 14.8 %collective-permute-start.22 = (bf16[32,5376]{1,0:T(8,128)(2,1)S(1)}, bf16[32,5376]{1,0:T(8,128)(2,1)}, u32[]{:S(2)}, u32[]{:S(2)}) collective-permute-start(bf16[32,5376]{1,0:T(8,128)(2,1)S(1)} %collective-permute-done.15.refs_3_), channel_id=1, source_target_pairs={{0,1},{1,0},{2,3},{3,2},{4,5},{5,4},{6,7},{7,6},{8,9},{9,8},{10,11... | collective-permute-start | bytes 1032200 | tf_op jit(solution)/shard_map/ppermute | solution.py:34
  164.7 15.4 %collective-permute-start.24 = (bf16[32,5376]{1,0:T(8,128)(2,1)}, bf16[32,5376]{1,0:T(8,128)(2,1)}, u32[]{:S(2)}, u32[]{:S(2)}) collective-permute-start(bf16[32,5376]{1,0:T(8,128)(2,1)} %collective-permute-done.17.refs_5_), channel_id=1, source_target_pairs={{0,1},{1,0},{2,3},{3,2},{4,5},{5,4},{6,7},{7,6},{8,9},{9,8},{10,11... | collective-permute-start | bytes 1032200 | tf_op jit(solution)/shard_map/ppermute | solution.py:34
  165.1 15.0 %collective-permute-start.25 = (bf16[32,5376]{1,0:T(8,128)(2,1)}, bf16[32,5376]{1,0:T(8,128)(2,1)}, u32[]{:S(2)}, u32[]{:S(2)}) collective-permute-start(bf16[32,5376]{1,0:T(8,128)(2,1)} %collective-permute-done.18.refs_6_), channel_id=1, source_target_pairs={{0,1},{1,0},{2,3},{3,2},{4,5},{5,4},{6,7},{7,6},{8,9},{9,8},{10,11... | collective-permute-start | bytes 1032200 | tf_op jit(solution)/shard_map/ppermute | solution.py:34
  182.1 1.0 copy-start.12
  183.1 1.0 copy-start.15
  184.0 38.7 %copy-start.8 = (bf16[32,5376]{1,0:T(8,128)(2,1)S(1)}, bf16[32,5376]{1,0:T(8,128)(2,1)}, u32[]{:S(2)}) copy-start(bf16[32,5376]{1,0:T(8,128)(2,1)} %copy-done.6) | copy-start | bytes 1032196
  (11 other events, 9.6 us)
Sparse Core Ops, SparseCore 0:
  11.0 78.3 all-gather.4
  92.1 130.6 all-gather.2

commit v2 on v1

v2 whole, which is shorter than its diff:
```python
import jax
import jax.numpy as jnp
from jax import lax
from jax.experimental import pallas as pl
from jax.experimental.pallas import tpu as pltpu
from jax.sharding import Mesh, PartitionSpec as P

D = 5376
HD = 128
WINDOW = 1024
EPS = 1e-06
LOG2E = 1.4426950408889634
SCALE = float(168) ** -0.5
TOK = 512
PER = 64
BF = jnp.bfloat16
F32 = jnp.float32
VM = pl.BlockSpec(memory_space=pltpu.VMEM)
SM = pl.BlockSpec(memory_space=pltpu.SMEM)
HB = pl.BlockSpec(memory_space=pltpu.HBM)
MB = 1 << 20


def params(mb):
    return pltpu.CompilerParams(vmem_limit_bytes=mb * MB)


def cost(flops, nbytes, trans=0):
    return pl.CostEstimate(flops=int(flops), bytes_accessed=int(nbytes), transcendentals=int(trans))


def shift(value, axis, by):
    n = lax.axis_size(axis)
    return lax.ppermute(value, axis, [(i, (i + by) % n) for i in range(n)])


def behind(value):
    n = 16
    return lax.ppermute(value, ("y", "x"), [(i, i + 1) for i in range(n - 1)])


SPLIT = 8
REST = 2688 - 256 * SPLIT


def pack_kernel(g_ref, u_ref, o_ref, r_ref):
    g, u = g_ref[...], u_ref[...]
    for j in range(10):
        lo = 128 * j
        pair = jnp.concatenate([g[:, lo:lo + 128], u[:, lo:lo + 128]], axis=1)
        if j < SPLIT:
            o_ref[:, 256 * j:256 * j + 256] = pair
        else:
            r_ref[:, 256 * (j - SPLIT):256 * (j - SPLIT) + 256] = pair
    r_ref[:, REST - 128:] = jnp.concatenate([g[:, 1280:], u[:, 1280:]], axis=1)


def pack(gate, up):
    return pl.pallas_call(
        pack_kernel,
        out_shape=[jax.ShapeDtypeStruct((336, 256 * SPLIT), BF), jax.ShapeDtypeStruct((336, REST), BF)],
        in_specs=[VM, VM],
        out_specs=[VM, VM],
        compiler_params=params(16),
        cost_estimate=cost(0, 4 * 336 * 2688),
        name="pack",
    )(gate, up)


def ring(value, by, phase):
    pairs = []
    for y in range(4):
        for x in range(4):
            for z in range(4):
                for c in range(2):
                    along_x = (c == 0) == (phase == 0)
                    yy, xx = (y, (x + by) % 4) if along_x else ((y + by) % 4, x)
                    pairs.append((((y * 4 + x) * 4 + z) * 2 + c, ((yy * 4 + xx) * 4 + z) * 2 + c))
    return lax.ppermute(value, ("y", "x", "z", "c"), pairs)


def ring_gather(own, cut, phase):
    m, p = ring(own, 1, phase), ring(own, -1, phase)
    top, bottom = ring(m[:cut], 1, phase), ring(p[cut:], -1, phase)
    return m, p, top, bottom


def attend_kernel(at_ref, q_ref, kv2_ref, kv1_ref, kv0_ref, qid_ref, kid_ref, o_ref):
    z, c = at_ref[0], at_ref[1]
    k = jnp.concatenate([kv2_ref[:, :HD], kv1_ref[:, :HD], kv0_ref[:, :HD]], axis=0)
    v = jnp.concatenate([kv2_ref[:, HD:], kv1_ref[:, HD:], kv0_ref[:, HD:]], axis=0)
    for b in range(2):
        lo = 256 * b
        qid = qid_ref[lo:lo + 256, :]
        kid = kid_ref[:, lo:lo + 1280]
        row = lax.broadcasted_iota(jnp.int32, (256, 1280), 0)
        col = lax.broadcasted_iota(jnp.int32, (256, 1280), 1)
        allowed = (qid == kid) & (col > row) & (col <= row + 1024)
        outs = []
        for h in range(2):
            q = q_ref[lo:lo + 256, HD * h:HD * h + HD]
            s = lax.dot_general(q, k[lo:lo + 1280], (((1,), (1,)), ((), ())), preferred_element_type=F32)
            s = jnp.where(allowed, s * (SCALE * LOG2E), -1e30)
            top = jnp.max(s, axis=1, keepdims=True)
            e = jnp.exp2(s - top)
            total = jnp.sum(e, axis=1, keepdims=True)
            mix = jnp.dot(e.astype(BF), v[lo:lo + 1280], preferred_element_type=F32)
            outs.append(mix / total)
        out = jnp.concatenate(outs, axis=1).astype(BF)
        for i in range(4):
            zz, cc = 2 * b + i // 2, i % 2
            o_ref[(cc + c) % 2, (zz - z + 4) % 4] = out[PER * i:PER * i + PER]


def attend(at, q, kv2, kv1, kv0, qid, kid):
    return pl.pallas_call(
        attend_kernel,
        out_shape=jax.ShapeDtypeStruct((2, 4, PER, 256), BF),
        in_specs=[SM] + [VM] * 6,
        out_specs=VM,
        compiler_params=params(32),
        cost_estimate=cost(4 * 1024 * 1280 * 128 * 1.5, 2 * MB, 1024 * 1280),
        name="attend",
    )(at, q, kv2, kv1, kv0, qid, kid)


def project_kernel(a0, a1, s0, s1, w_ref, ws_ref, p0, p1t, p1b, p2t, p2b, p3t, p3b):
    acc = jnp.dot(jnp.concatenate([a0[...], a1[...]], axis=1), w_ref[...], preferred_element_type=F32)
    acc += jnp.dot(jnp.concatenate([s0[...], s1[...]], axis=1), ws_ref[...], preferred_element_type=F32)
    out = acc.astype(BF)
    p0[...] = out[:64]
    for i, ref in enumerate((p1t, p1b, p2t, p2b, p3t, p3b)):
        ref[...] = out[64 + 32 * i:96 + 32 * i]


def project(a0, a1, s0, s1, w, ws):
    width = 768
    row = lambda r: pl.BlockSpec((r, width), lambda j: (0, j))
    full = pl.BlockSpec((256, 256), lambda j: (0, 0))
    return pl.pallas_call(
        project_kernel,
        out_shape=[jax.ShapeDtypeStruct((64, D), BF)] + [jax.ShapeDtypeStruct((32, D), BF)] * 6,
        grid=(D // width,),
        in_specs=[full] * 4 + [row(512)] * 2,
        out_specs=[row(64)] + [row(32)] * 6,
        compiler_params=params(24),
        cost_estimate=cost(2 * 256 * 1024 * D, 2 * 1280 * D),
        name="project",
    )(a0, a1, s0, s1, w, ws)


def norm_kernel(p0, at_ref, ab_ref, bt_ref, bb_ref, res_ref, gain_ref, new_ref, nrm_ref):
    post = gain_ref[0:1].astype(F32) + gain_ref[1:2].astype(F32)
    pre = gain_ref[2:3].astype(F32) + gain_ref[3:4].astype(F32)
    for half, (a, b) in enumerate(((at_ref, bt_ref), (ab_ref, bb_ref))):
        rows = slice(32 * half, 32 * half + 32)
        owned = p0[rows].astype(F32) + a[...].astype(F32) + b[...].astype(F32)
        factor = lax.rsqrt(jnp.mean(owned * owned, axis=1, keepdims=True) + EPS)
        new = (res_ref[rows].astype(F32) + owned * factor * post).astype(BF)
        stream = new.astype(F32)
        for j in range(8):
            new_ref[j, rows] = stream[:, 672 * j:672 * j + 672].astype(BF)
        second = lax.rsqrt(jnp.mean(stream * stream, axis=1, keepdims=True) + EPS)
        nrm_ref[rows] = (stream * second * pre).astype(BF)


def norm(*args):
    return pl.pallas_call(
        norm_kernel,
        out_shape=[jax.ShapeDtypeStruct((8, PER, 672), BF), jax.ShapeDtypeStruct((PER, D), BF)],
        in_specs=[VM] * 7,
        out_specs=[VM] * 2,
        compiler_params=params(16),
        cost_estimate=cost(20 * PER * D, 8 * PER * D),
        name="norm",
    )(*args)


def token_copies(where, pieces, tokens_at, n_ref, sems):
    z, c = where[0], where[1]
    copies = []
    for i, (ref, (dz, dc, part)) in enumerate(zip(pieces, tokens_at)):
        base, rows = 64 * (2 * ((z + dz) % 4) + (c + dc) % 2), 64
        if part is not None:
            base, rows = base + 32 * part, 32
        copies.append(pltpu.make_async_copy(ref, n_ref.at[pl.ds(pl.multiple_of(base, 32), rows)], sems.at[i]))
    return copies


def gelu(g):
    return 0.5 * g * (1 + jnp.tanh(0.7978845608028654 * (g + 0.044715 * (g * g * g))))


def gated(pieces, tokens_at, where, w):
    blocks = w.shape[1] // 256
    n = len(pieces)

    def body(*refs):
        place, w_ref, o_ref, n_ref, sems = refs[n:]

        @pl.when(pl.program_id(0) == 0)
        def _():
            copies = token_copies(place, refs[:n], tokens_at, n_ref, sems)
            for copy in copies:
                copy.start()
            for copy in copies:
                copy.wait()

        acc = jnp.dot(n_ref[...], w_ref[...], preferred_element_type=F32)
        o_ref[...] = (gelu(acc[:, :128]) * acc[:, 128:]).T.astype(BF)

    return pl.pallas_call(
        body,
        out_shape=jax.ShapeDtypeStruct((128 * blocks, TOK), BF),
        grid=(blocks,),
        in_specs=[HB] * n + [SM, pl.BlockSpec((D, 256), lambda j: (0, j))],
        out_specs=pl.BlockSpec((128, TOK), lambda j: (j, 0)),
        scratch_shapes=[pltpu.VMEM((TOK, D), BF), pltpu.SemaphoreType.DMA((n,))],
        compiler_params=params(56),
        cost_estimate=cost(2 * TOK * D * 256 * blocks, 2 * D * 256 * blocks + 2 * TOK * D),
        name="gated",
    )(*pieces, where, w)


def gated_rest(pieces, tokens_at, where, groups):
    n, m = len(pieces), len(groups)
    rel = (0, 3, 1, 2)
    parts = [(g, k, 336 * k, rel[k], rel[g]) for g in range(3) for k in range(4)]
    parts += [(3, k, 336 * k, rel[k], 2) for k in range(2)] + [(4, k, 336 * (k - 2), rel[k], 2) for k in (2, 3)]

    def body(*refs):
        place, o_ref, n_ref, w_ref, sems, wsems = refs[n + m:]
        c, y, x = place[1], place[2], place[3]
        copies = token_copies(place, refs[:n], tokens_at, n_ref, sems)
        for i, (g, _, lo, first, then) in enumerate(parts):
            dx = jnp.where(c == 0, first, then)
            dy = jnp.where(c == 0, then, first)
            row = 336 * (4 * ((y + dy) % 4) + (x + dx) % 4)
            src = refs[n + g].at[pl.ds(lo, 336)]
            copies.append(pltpu.make_async_copy(src, w_ref.at[pl.ds(pl.multiple_of(row, 16), 336)], wsems.at[i]))
        for copy in copies:
            copy.start()
        for copy in copies:
            copy.wait()
        for j in range(10 - SPLIT):
            acc = jnp.dot(n_ref[...], w_ref[:, 256 * j:256 * j + 256], preferred_element_type=F32)
            o_ref[128 * j:128 * j + 128] = (gelu(acc[:, :128]) * acc[:, 128:]).T.astype(BF)
        acc = jnp.dot(n_ref[...], w_ref[:, REST - 128:], preferred_element_type=F32)
        act = gelu(acc) * pltpu.roll(acc, 64, 1)
        o_ref[128 * (10 - SPLIT):] = act.T[:64].astype(BF)

    return pl.pallas_call(
        body,
        out_shape=jax.ShapeDtypeStruct((REST // 2, TOK), BF),
        in_specs=[HB] * (n + m) + [SM],
        out_specs=VM,
        scratch_shapes=[
            pltpu.VMEM((TOK, D), BF),
            pltpu.VMEM((D, REST), BF),
            pltpu.SemaphoreType.DMA((n,)),
            pltpu.SemaphoreType.DMA((16,)),
        ],
        compiler_params=params(56),
        cost_estimate=cost(2 * TOK * D * REST, 2 * D * REST + 2 * TOK * D),
        name="gated_rest",
    )(*pieces, *groups, where)


def per_device(queries, keys, values, doc_ids, out_weight, residual, post_gain, pre_gain, gate_weight, up_weight):
    y, x, z, c = (lax.axis_index(a) for a in ("y", "x", "z", "c"))
    where = jnp.stack([z, c, y, x]).astype(jnp.int32)

    w, rest = pack(gate_weight, up_weight)
    w_all = lax.all_gather(w, ("y", "x"), axis=0, tiled=True)
    m, p, top, bottom = ring_gather(rest, 176, 0)
    group = jnp.concatenate([rest, m, p, top, bottom], axis=0)
    queries, group = lax.optimization_barrier((queries, group))
    groups = [group, ring(group, 1, 1), ring(group, -1, 1)]

    gains = jnp.stack([post_gain, pre_gain])
    high = gains.astype(BF)
    low = (gains - high.astype(F32)).astype(BF)
    extra = jnp.stack([high[0], low[0], high[1], low[1]])
    extra = jnp.concatenate([extra, jnp.zeros((12, 672), BF)], axis=0)
    sent = jnp.concatenate([residual.reshape(8, PER, 672), jnp.broadcast_to(extra[None], (8, 16, 672))], axis=1)
    mine = lax.all_to_all(sent, ("z", "c"), 0, 0, tiled=True).transpose(1, 0, 2).reshape(PER + 16, D)

    start = (4 * y + x) * TOK
    padded = jnp.concatenate([jnp.full((2 * TOK,), -1, jnp.int32), doc_ids])
    kid = lax.dynamic_slice_in_dim(padded, start, 3 * TOK, 0)[None, :]
    qid = lax.dynamic_slice_in_dim(doc_ids, start, TOK, 0)[:, None]

    queries, mine = lax.optimization_barrier((queries, mine))
    cols = [slice(HD * h, HD * h + HD) for h in range(2)]
    kv0 = jnp.concatenate([keys[:, cols[0]], values[:, cols[0]], keys[:, cols[1]], values[:, cols[1]]], axis=1)
    kv1 = behind(kv0)
    kv2 = behind(kv1)
    mixes = []
    for h in range(2):
        two = slice(256 * h, 256 * h + 256)
        mixes.append(attend(where, queries[:, two], kv2[:, two], kv1[:, two], kv0[:, two], qid, kid))
    other_weight = shift(out_weight, "c", 1)
    own = [m[0].reshape(256, 256) for m in mixes]
    other = [shift(m[1].reshape(256, 256), "c", 1) for m in mixes]
    p0, p1t, p1b, p2t, p2b, p3t, p3b = project(*own, *other, out_weight, other_weight)

    up_t = shift(p2t, "z", 1)
    dn_b = shift(p2b, "z", -1)
    a_b = shift(p1b, "z", 1)
    b_t = shift(p3t, "z", -1)
    add = lambda p, q: (p.astype(F32) + q.astype(F32)).astype(BF)
    a_t = shift(add(p1t, up_t), "z", 1)
    b_b = shift(add(p3b, dn_b), "z", -1)

    new, nrm = norm(p0, a_t, a_b, b_t, b_b, mine[:PER], mine[PER:PER + 4])

    m, q = shift(nrm, "z", 1), shift(nrm, "z", -1)
    m, q, groups = lax.optimization_barrier((m, q, groups))
    pieces = [nrm, m, q, shift(m[:32], "z", 1), shift(q[32:], "z", -1)]
    places = [(0, None), (3, None), (1, None), (2, 0), (2, 1)]
    pieces += [shift(p, "c", 1) for p in pieces]
    tokens_at = [(dz, dc, part) for dc in range(2) for dz, part in places]
    groups = groups + [ring(groups[1][:672], 1, 1), ring(groups[2][672:], -1, 1)]
    new, pieces = lax.optimization_barrier((new, pieces))
    new_residual = lax.all_to_all(new, ("z", "c"), 0, 0, tiled=True).reshape(TOK, 672)
    act = jnp.concatenate(
        [gated(pieces, tokens_at, where, w_all), gated_rest(pieces, tokens_at, where, groups)], axis=0
    )
    return new_residual, act.T


def solution(mesh):
    fine = Mesh(mesh.devices.reshape(4, 4, 4, 2), ("y", "x", "z", "c"))
    t, f = ("y", "x"), ("z", "c")
    in_specs = (P(t, f), P(t, f), P(t, f), P(), P(f, None), P(t, f), P(f), P(f), P(t, f), P(t, f))
    return jax.shard_map(per_device, mesh=fine, in_specs=in_specs, out_specs=(P(t, f), P(t, f)), check_vma=False)
```

time: 257 us -> 238 us (0.926)
  blocking collectives: 25.3 us -> 0 us
  waiting for transfers between devices: 78.8 us -> 101 us
  local copies, waits for them, and re-layouts: 30.5 us -> 13.4 us
  starting transfers between devices: 53.5 us -> 56.4 us
    ppermute x0 -> x8, waiting for transfers between devices: none -> 44.7 us  [ring(): return lax.ppermute(value, ('y', 'x', 'z', 'c'), pairs)]
    all_gather x2 -> x1, waiting for transfers between devices: 27.3 us -> 0.01 us  [per_device(): w_all = lax.all_gather(w, ('y', 'x'), axis=0, tiled=True)]
    unnamed x1 -> x0, blocking collectives: 25.3 us -> none
    ppermute x4 -> x2, waiting for transfers between devices: 13.9 us -> 28.9 us  [behind(): return lax.ppermute(value, ('y', 'x'), [(i, i + 1) for i in range(n - 1)])]
    unnamed x65 -> x56, local copies, waits for them, and re-layouts: 18.6 us -> 7.24 us
    all_to_all x2, waiting for transfers between devices: 10.9 us -> 0.01 us  [the longest x1 0.01 us: per_device(): lax.all_to_all(sent, ('z', 'c'), 0, 0, tiled=True).transpose(1, 0, 2)]
    ppermute x0 -> x8, starting transfers between devices: none -> 10 us  [ring(): return lax.ppermute(value, ('y', 'x', 'z', 'c'), pairs)]
    all_to_all x4 -> x0, local copies, waits for them, and re-layouts: 8.64 us -> none  [the longest x2 4.33 us: per_device(): mine = lax.all_to_all(residual, ('z', 'c'), 0, 1, tiled=True)]
  transfers between devices with their start and end apart: 30 -> 31, of which waited for: 9 -> 12; matrix products, arithmetic and copies ran while one was open for 5% -> 5% of each run, Pallas kernels for 11% -> 11%
where the time goes in v2:
time: 238 us
  waiting for transfers between devices  101 us (42%)
  starting transfers between devices  56.4 us (24%)
  Pallas kernels  47.2 us (20%)
  between operations  14.5 us (6%)
  local copies, waits for them, and re-layouts  13.4 us (6%)
  other arithmetic  4.6 us (2%)
    ppermute x8, waiting for transfers between devices, ring(): return lax.ppermute(value, ('y', 'x', 'z', 'c'), pairs)  44.7 us
    ppermute x2, waiting for transfers between devices, behind(): return lax.ppermute(value, ('y', 'x'), [(i, i + 1) for i in range(n - 1)])  28.9 us
    ppermute x18, starting transfers between devices, shift(): return lax.ppermute(value, axis, [(i, (i + by) % n) for i in range(n)])  28.2 us
    ppermute x18, waiting for transfers between devices, shift(): return lax.ppermute(value, axis, [(i, (i + by) % n) for i in range(n)])  27.8 us
    pallas_call x1, Pallas kernels, gated(): pl.pallas_call(body, out_shape=jax.ShapeDtypeStruct((128 * blocks, TOK),...  19.3 us
    pallas_call x1, Pallas kernels, gated_rest(): pl.pallas_call(body, out_shape=jax.ShapeDtypeStruct((REST // 2, TOK), BF)...  10.8 us
    ppermute x8, starting transfers between devices, ring(): return lax.ppermute(value, ('y', 'x', 'z', 'c'), pairs)  10 us
    ppermute x2, starting transfers between devices, behind(): return lax.ppermute(value, ('y', 'x'), [(i, i + 1) for i in range(n - 1)])  8.38 us
  transfers between devices with their start and end apart: 31, of which 12 were waited for; matrix products, arithmetic and copies ran while one was open for 5% of the time, Pallas kernels for 11%

profile of v2, /device:TPU:1, one launch (start us, length us, event | category | flops | bytes accessed | tf_op | source)
XLA Modules:
  0.0 237.6 jit_solution(7700024054399862176)
XLA Ops:
  7.2 1.2 copy-done
  8.4 1.2 copy-done.1
  9.6 1.3 pack.1
  10.9 1.5 collective-permute-start.8
  12.4 1.4 collective-permute-start
  13.8 1.4 collective-permute-start.1
  15.8 1.0 pad_maximum_fusion
  16.9 6.0 %all-to-all-start = ((bf16[8,80,672]{2,1,0:T(8,128)(2,1)}), bf16[8,80,672]{2,1,0:T(8,128)(2,1)S(1)}, u32[]{:S(2)}, u32[]{:S(2)}) async-start(bf16[8,80,672]{2,1,0:T(8,128)(2,1)} %pad_maximum_fusion), calls=%async_computation | async-start | bytes 1966080 | tf_op jit(solution)/shard_map/all_to_all | solution.py:286
  23.8 3.5 %collective-permute-start.4 = (bf16[512,512]{1,0:T(8,128)(2,1)}, bf16[512,512]{1,0:T(8,128)(2,1)}, u32[]{:S(2)}, u32[]{:S(2)}) collective-permute-start(bf16[512,512]{1,0:T(8,128)(2,1)} %pad_maximum_fusion.1), channel_id=1, source_target_pairs={{0,8},{8,16},{16,24},{24,32},{32,40},{40,48},{48,56},{56,64},{64,7... | collective-permute-start | bytes 1572872 | tf_op jit(solution)/shard_map/ppermute | solution.py:39
  28.7 2.7 %collective-permute-start.3 = (bf16[160,640]{1,0:T(8,128)(2,1)S(1)}, bf16[160,640]{1,0:T(8,128)(2,1)S(1)}, u32[]{:S(2)}, u32[]{:S(2)}) collective-permute-start(bf16[160,640]{1,0:T(8,128)(2,1)S(1)} %slice.109), channel_id=1, source_target_pairs={{0,24},{1,97},{2,26},{3,99},{4,28},{5,101},{6,30},{7,103},{8,0},{9... | collective-permute-start | bytes 614408 | tf_op jit(solution)/shard_map/ppermute | solution.py:79
  33.1 16.2 %collective-permute-done.4 = bf16[512,512]{1,0:T(8,128)(2,1)} collective-permute-done((bf16[512,512]{1,0:T(8,128)(2,1)}, bf16[512,512]{1,0:T(8,128)(2,1)}, u32[]{:S(2)}, u32[]{:S(2)}) %collective-permute-start.4) | collective-permute-done | bytes 524320 | tf_op jit(solution)/shard_map/ppermute | solution.py:39
  49.3 4.9 %collective-permute-start.5 = (bf16[512,512]{1,0:T(8,128)(2,1)}, bf16[512,512]{1,0:T(8,128)(2,1)}, u32[]{:S(2)}, u32[]{:S(2)}) collective-permute-start(bf16[512,512]{1,0:T(8,128)(2,1)} %collective-permute-done.4), channel_id=1, source_target_pairs={{0,8},{8,16},{16,24},{24,32},{32,40},{40,48},{48,56},{56,64},{64,7... | collective-permute-start | bytes 1572872 | tf_op jit(solution)/shard_map/ppermute | solution.py:39
  54.2 1.1 fusion.1
  58.0 1.2 fusion.3
  59.2 12.7 %collective-permute-done.5 = bf16[512,512]{1,0:T(8,128)(2,1)} collective-permute-done((bf16[512,512]{1,0:T(8,128)(2,1)}, bf16[512,512]{1,0:T(8,128)(2,1)}, u32[]{:S(2)}, u32[]{:S(2)}) %collective-permute-start.5) | collective-permute-done | bytes 524320 | tf_op jit(solution)/shard_map/ppermute | solution.py:39
  71.9 1.1 fusion.2
  73.0 3.3 %attend.2 = bf16[2,4,64,256]{3,2,1,0:T(8,128)(2,1)S(1)} custom-call(s32[4]{0:T(128)S(1)} %pad_add_fusion.at_ref.refs_10_.refs_15_, bf16[512,256]{1,0:T(8,128)(2,1)S(1)} %get-tuple-element.73.q_ref, bf16[512,256]{1,0:T(8,128)(2,1)S(1)} %get-tuple-element.71.kv2_ref, bf16[512,256]{1,0:T(8,128)(2,1)S(1)} %get-tuple-element.69.kv1_ref, ...), custom_call_target="tpu_custom_call" | custom-call | flops 1006632960 | bytes 2097152 | tf_op jit(solution)/shard_map/attend/pallas_call | solution.py:116
  76.3 1.5 collective-permute-start.6
  77.8 3.3 %attend.3 = bf16[2,4,64,256]{3,2,1,0:T(8,128)(2,1)S(1)} custom-call(s32[4]{0:T(128)S(1)} %pad_add_fusion.at_ref.refs_10_.refs_15_, bf16[512,256]{1,0:T(8,128)(2,1)S(1)} %get-tuple-element.72.q_ref, bf16[512,256]{1,0:T(8,128)(2,1)S(1)} %get-tuple-element.70.kv2_ref, bf16[512,256]{1,0:T(8,128)(2,1)S(1)} %get-tuple-element.68.kv1_ref, ...), custom_call_target="tpu_custom_call" | custom-call | flops 1006632960 | bytes 2097152 | tf_op jit(solution)/shard_map/attend/pallas_call | solution.py:116
  81.2 1.3 collective-permute-done.7.s1
  82.6 7.4 %project.1 = (bf16[64,5376]{1,0:T(8,128)(2,1)S(1)}, bf16[32,5376]{1,0:T(8,128)(2,1)S(1)}, bf16[32,5376]{1,0:T(8,128)(2,1)S(1)}, bf16[32,5376]{1,0:T(8,128)(2,1)S...) custom-call(bf16[256,256]{1,0:T(8,128)(2,1)S(1)} %bitcast.16, ...), custom_call_target="tpu_custom_call" | custom-call | flops 2818572288 | bytes 13762560 | tf_op jit(solution)/shard_map/project/pallas_call | solution.py:140
  90.0 1.6 collective-permute-start.9
  91.6 2.2 collective-permute-start.17
  93.8 1.5 collective-permute-start.18
  95.3 1.3 collective-permute-start.11
  96.6 1.4 collective-permute-start.12
  98.0 3.4 %collective-permute-done.9 = bf16[32,5376]{1,0:T(8,128)(2,1)S(1)} collective-permute-done((bf16[32,5376]{1,0:T(8,128)(2,1)S(1)}, bf16[32,5376]{1,0:T(8,128)(2,1)S(1)}, u32[]{:S(2)}, u32[]{:S(2)}) %collective-permute-start.9) | collective-permute-done | bytes 344096 | tf_op jit(solution)/shard_map/ppermute | solution.py:34
  101.4 1.2 collective-permute-start.13
  102.7 8.9 %collective-permute-done.13 = bf16[32,5376]{1,0:T(8,128)(2,1)S(1)} collective-permute-done((bf16[32,5376]{1,0:T(8,128)(2,1)S(1)}, bf16[32,5376]{1,0:T(8,128)(2,1)S(1)}, u32[]{:S(2)}, u32[]{:S(2)}) %collective-permute-start.13) | collective-permute-done | bytes 344096 | tf_op jit(solution)/shard_map/ppermute | solution.py:34
  111.7 2.7 %collective-permute-start.14 = (bf16[32,5376]{1,0:T(8,128)(2,1)S(1)}, bf16[32,5376]{1,0:T(8,128)(2,1)S(1)}, u32[]{:S(2)}, u32[]{:S(2)}) collective-permute-start(bf16[32,5376]{1,0:T(8,128)(2,1)S(1)} %add_convert_fusion), channel_id=1, source_target_pairs={{0,6},{2,0},{4,2},{6,4},{1,7},{3,1},{5,3},{7,5},{8,14},{10,8},{12,... | collective-permute-start | bytes 1032200 | tf_op jit(solution)/shard_map/ppermute | solution.py:34
  114.5 5.1 %collective-permute-done.10.at_ref = bf16[32,5376]{1,0:T(8,128)(2,1)S(1)} collective-permute-done((bf16[32,5376]{1,0:T(8,128)(2,1)S(1)}, bf16[32,5376]{1,0:T(8,128)(2,1)S(1)}, u32[]{:S(2)}, u32[]{:S(2)}) %collective-permute-start.10) | collective-permute-done | bytes 344096 | tf_op jit(solution)/shard_map/ppermute | solution.py:34
  119.6 1.8 norm.1
  122.0 2.2 collective-permute-start.16
  124.2 4.2 %collective-permute-start.21 = (bf16[64,5376]{1,0:T(8,128)(2,1)S(1)}, bf16[64,5376]{1,0:T(8,128)(2,1)S(1)}, u32[]{:S(2)}, u32[]{:S(2)}) collective-permute-start(bf16[64,5376]{1,0:T(8,128)(2,1)S(1)} %get-tuple-element.50.refs_0_), channel_id=1, source_target_pairs={{0,1},{1,0},{2,3},{3,2},{4,5},{5,4},{6,7},{7,6},{8,9},{9,8},{10,11... | collective-permute-start | bytes 2064392 | tf_op jit(solution)/shard_map/ppermute | solution.py:34
  128.4 23.6 %collective-permute-done.17.refs_11_ = bf16[1344,640]{1,0:T(8,128)(2,1)S(1)} collective-permute-done((bf16[1344,640]{1,0:T(8,128)(2,1)S(1)}, bf16[1344,640]{1,0:T(8,128)(2,1)S(1)}, u32[]{:S(2)}, u32[]{:S(2)}) %collective-permute-start.17) | collective-permute-done | bytes 1720352 | tf_op jit(solution)/shard_map/ppermute | solution.py:79
  152.0 3.6 %collective-permute-start.22 = (bf16[64,5376]{1,0:T(8,128)(2,1)S(1)}, bf16[64,5376]{1,0:T(8,128)(2,1)S(1)}, u32[]{:S(2)}, u32[]{:S(2)}) collective-permute-start(bf16[64,5376]{1,0:T(8,128)(2,1)S(1)} %collective-permute-done.15.refs_1_), channel_id=1, source_target_pairs={{0,1},{1,0},{2,3},{3,2},{4,5},{5,4},{6,7},{7,6},{8,9},{9,8},{10,11... | collective-permute-start | bytes 2064392 | tf_op jit(solution)/shard_map/ppermute | solution.py:34
  155.6 1.3 collective-permute-start.19
  157.0 1.5 collective-permute-start.20
  159.4 7.3 %collective-permute-done.19.refs_3_ = bf16[32,5376]{1,0:T(8,128)(2,1)S(1)} collective-permute-done((bf16[32,5376]{1,0:T(8,128)(2,1)S(1)}, bf16[32,5376]{1,0:T(8,128)(2,1)S(1)}, u32[]{:S(2)}, u32[]{:S(2)}) %collective-permute-start.19) | collective-permute-done | bytes 344096 | tf_op jit(solution)/shard_map/ppermute | solution.py:34
  167.3 2.9 %collective-permute-start.24 = (bf16[32,5376]{1,0:T(8,128)(2,1)S(1)}, bf16[32,5376]{1,0:T(8,128)(2,1)S(1)}, u32[]{:S(2)}, u32[]{:S(2)}) collective-permute-start(bf16[32,5376]{1,0:T(8,128)(2,1)S(1)} %collective-permute-done.19.refs_3_), channel_id=1, source_target_pairs={{0,1},{1,0},{2,3},{3,2},{4,5},{5,4},{6,7},{7,6},{8,9},{9,8},{10,11... | collective-permute-start | bytes 1032200 | tf_op jit(solution)/shard_map/ppermute | solution.py:34
  170.3 1.2 collective-permute-done.24.refs_8_
  172.2 3.8 %all-to-all-start.1 = ((bf16[8,64,672]{2,1,0:T(8,128)(2,1)}), bf16[8,64,672]{2,1,0:T(8,128)(2,1)S(1)}, u32[]{:S(2)}, u32[]{:S(2)}) async-start(bf16[8,64,672]{2,1,0:T(8,128)(2,1)} %get-tuple-element.49), calls=%async_computation.1 | async-start | bytes 1572864 | tf_op jit(solution)/shard_map/all_to_all | solution.py:325
  176.0 15.0 %collective-permute-done.26.refs_13_ = bf16[672,640]{1,0:T(8,128)(2,1)} collective-permute-done((bf16[672,640]{1,0:T(8,128)(2,1)S(1)}, bf16[672,640]{1,0:T(8,128)(2,1)}, u32[]{:S(2)}, u32[]{:S(2)}) %collective-permute-start.26) | collective-permute-done | bytes 860192 | tf_op jit(solution)/shard_map/ppermute | solution.py:79
  191.0 6.1 %collective-permute-done.27.refs_14_ = bf16[672,640]{1,0:T(8,128)(2,1)} collective-permute-done((bf16[672,640]{1,0:T(8,128)(2,1)S(1)}, bf16[672,640]{1,0:T(8,128)(2,1)}, u32[]{:S(2)}, u32[]{:S(2)}) %collective-permute-start.27) | collective-permute-done | bytes 860192 | tf_op jit(solution)/shard_map/ppermute | solution.py:79
  197.1 10.8 %gated_rest.1 = bf16[320,512]{1,0:T(8,128)(2,1)} custom-call(bf16[64,5376]{1,0:T(8,128)(2,1)} %copy-done.3, bf16[64,5376]{1,0:T(8,128)(2,1)} %copy-done.10, bf16[64,5376]{1,0:T(8,128)(2,1)} %copy-done.11, bf16[32,5376]{1,0:T(8,128)(2,1)} %copy-done.19, bf16[32,5376]{1,0:T(8,128)(2,1)} %copy-done.20, bf16[64,5376]{1,0:T(8,128)(2,1)} %copy-done.16, ...), custom_call_target="tpu_custom_call" | custom-call | flops 3523215360 | bytes 12386304 | tf_op jit(solution)/shard_map/gated_rest/pallas_call | solution.py:252
  207.9 1.1 copy.18
  209.0 19.3 %gated.1 = bf16[1024,512]{1,0:T(8,128)(2,1)} custom-call(bf16[64,5376]{1,0:T(8,128)(2,1)} %copy-done.3, bf16[64,5376]{1,0:T(8,128)(2,1)} %copy-done.10, bf16[64,5376]{1,0:T(8,128)(2,1)} %copy-done.11, bf16[32,5376]{1,0:T(8,128)(2,1)} %copy-done.19, bf16[32,5376]{1,0:T(8,128)(2,1)} %copy-done.20, bf16[64,5376]{1,0:T(8,128)(2,1)} %copy-done.16, ...), custom_call_target="tpu_custom_call" | custom-call | flops 11274289152 | bytes 27525120 | tf_op jit(solution)/shard_map/gated/pallas_call | solution.py:212
  228.3 2.4 %maximum_bitcast_fusion = bf16[512,1344]{0,1:T(8,128)(2,1)} fusion(bf16[320,512]{1,0:T(8,128)(2,1)S(1)} %copy-done.7, bf16[1024,512]{1,0:T(8,128)(2,1)} %gated.1), kind=kLoop, calls=%fused_computation | loop fusion | flops 2752512 | bytes 2752512 | tf_op jit(solution)/shard_map/transpose | solution.py:329
  (116 shorter events, 10.4 us)
Async XLA Ops:
  7.2 201.9 %all-gather.2.cloned.1.call-start = ((), (), s32[]{:S(2)}) async-start(), calls=%async_computation.2 | async-start | bytes 23396352 | tf_op jit(solution)/shard_map/all_gather | solution.py:274
  9.6 5.7 %copy-start.15 = (f32[672]{0:T(1024)S(1)}, f32[672]{0:T(1024)}, u32[]{:S(2)}) copy-start(f32[672]{0:T(1024)} %param.16) | copy-start | bytes 8068
  9.6 5.7 %copy-start.4 = (bf16[512,672]{0,1:T(8,128)(2,1)S(1)}, bf16[512,672]{0,1:T(8,128)(2,1)}, u32[]{:S(2)}) copy-start(bf16[512,672]{0,1:T(8,128)(2,1)} %param.15) | copy-start | bytes 2064388
  10.9 71.6 %collective-permute-start.8 = (bf16[512,5376]{1,0:T(8,128)(2,1)}, bf16[512,5376]{1,0:T(8,128)(2,1)}, u32[]{:S(2)}, u32[]{:S(2)}) collective-permute-start(bf16[512,5376]{1,0:T(8,128)(2,1)} %w_ref.1), channel_id=1, source_target_pairs={{0,1},{1,0},{2,3},{3,2},{4,5},{5,4},{6,7},{7,6},{8,9},{9,8},{10,11... | collective-permute-start | bytes 16515080 | tf_op jit(solution)/shard_map/ppermute | solution.py:34
  12.4 16.1 %collective-permute-start = (bf16[336,640]{1,0:T(8,128)(2,1)S(1)}, bf16[336,640]{1,0:T(8,128)(2,1)S(1)}, u32[]{:S(2)}, u32[]{:S(2)}) collective-permute-start(bf16[336,640]{1,0:T(8,128)(2,1)S(1)} %get-tuple-element.33), channel_id=1, source_target_pairs={{0,8},{1,33},{2,10},{3,35},{4,12},{5,37},{6,14},{7,39},{8,16},{9,4... | collective-permute-start | bytes 1290248 | tf_op jit(solution)/shard_map/ppermute | solution.py:79
  13.8 14.9 %collective-permute-start.1 = (bf16[336,640]{1,0:T(8,128)(2,1)S(1)}, bf16[336,640]{1,0:T(8,128)(2,1)S(1)}, u32[]{:S(2)}, u32[]{:S(2)}) collective-permute-start(bf16[336,640]{1,0:T(8,128)(2,1)S(1)} %get-tuple-element.33), channel_id=1, source_target_pairs={{0,24},{1,97},{2,26},{3,99},{4,28},{5,101},{6,30},{7,103},{8,0},{9... | collective-permute-start | bytes 1290248 | tf_op jit(solution)/shard_map/ppermute | solution.py:79
  16.9 6.0 %copy-start.8 = (bf16[512,256]{1,0:T(8,128)(2,1)S(1)}, bf16[512,256]{1,0:T(8,128)(2,1)}, u32[]{:S(2)}) copy-start(bf16[512,256]{1,0:T(8,128)(2,1)} %param.12) | copy-start | bytes 786436
  16.9 6.1 %copy-start.9 = (bf16[512,256]{1,0:T(8,128)(2,1)S(1)}, bf16[512,256]{1,0:T(8,128)(2,1)}, u32[]{:S(2)}) copy-start(bf16[512,256]{1,0:T(8,128)(2,1)} %param.11) | copy-start | bytes 786436
  16.9 39.8 %all-to-all-start = ((bf16[8,80,672]{2,1,0:T(8,128)(2,1)}), bf16[8,80,672]{2,1,0:T(8,128)(2,1)S(1)}, u32[]{:S(2)}, u32[]{:S(2)}) async-start(bf16[8,80,672]{2,1,0:T(8,128)(2,1)} %pad_maximum_fusion), calls=%async_computation | async-start | bytes 1966080 | tf_op jit(solution)/shard_map/all_to_all | solution.py:286
  23.8 25.5 %collective-permute-start.4 = (bf16[512,512]{1,0:T(8,128)(2,1)}, bf16[512,512]{1,0:T(8,128)(2,1)}, u32[]{:S(2)}, u32[]{:S(2)}) collective-permute-start(bf16[512,512]{1,0:T(8,128)(2,1)} %pad_maximum_fusion.1), channel_id=1, source_target_pairs={{0,8},{8,16},{16,24},{24,32},{32,40},{40,48},{48,56},{56,64},{64,7... | collective-permute-start | bytes 1572872 | tf_op jit(solution)/shard_map/ppermute | solution.py:39
  28.3 49.5 %copy-start.2 = (s32[4]{0:T(128)}, s32[4]{0:T(128)S(1)}, u32[]{:S(2)}) copy-start(s32[4]{0:T(128)S(1)} %pad_add_fusion.at_ref.refs_10_.refs_15_) | copy-start | bytes 52
  28.6 26.7 %collective-permute-start.2 = (bf16[176,640]{1,0:T(8,128)(2,1)S(1)}, bf16[176,640]{1,0:T(8,128)(2,1)S(1)}, u32[]{:S(2)}, u32[]{:S(2)}) collective-permute-start(bf16[176,640]{1,0:T(8,128)(2,1)S(1)} %slice.108), channel_id=1, source_target_pairs={{0,8},{1,33},{2,10},{3,35},{4,12},{5,37},{6,14},{7,39},{8,16},{9,4... | collective-permute-start | bytes 675848 | tf_op jit(solution)/shard_map/ppermute | solution.py:79
  28.7 27.3 %collective-permute-start.3 = (bf16[160,640]{1,0:T(8,128)(2,1)S(1)}, bf16[160,640]{1,0:T(8,128)(2,1)S(1)}, u32[]{:S(2)}, u32[]{:S(2)}) collective-permute-start(bf16[160,640]{1,0:T(8,128)(2,1)S(1)} %slice.109), channel_id=1, source_target_pairs={{0,24},{1,97},{2,26},{3,99},{4,28},{5,101},{6,30},{7,103},{8,0},{9... | collective-permute-start | bytes 614408 | tf_op jit(solution)/shard_map/ppermute | solution.py:79
  49.3 22.6 %collective-permute-start.5 = (bf16[512,512]{1,0:T(8,128)(2,1)}, bf16[512,512]{1,0:T(8,128)(2,1)}, u32[]{:S(2)}, u32[]{:S(2)}) collective-permute-start(bf16[512,512]{1,0:T(8,128)(2,1)} %collective-permute-done.4), channel_id=1, source_target_pairs={{0,8},{8,16},{16,24},{24,32},{32,40},{40,48},{48,56},{56,64},{64,7... | collective-permute-start | bytes 1572872 | tf_op jit(solution)/shard_map/ppermute | solution.py:39
  58.0 24.6 %slice-start = ((s8[5505024]{0:T(1024)(128)(4,1)}), s8[4194304]{0:T(1024)(128)(4,1)S(1)}, s32[]{:S(2)}) async-start(s8[5505024]{0:T(1024)(128)(4,1)} %bitcast.14), calls=%async_computation.3 | async-start | bytes 8388608
  73.0 9.6 %slice-start.1 = ((s8[5505024]{0:T(1024)(128)(4,1)}), s8[1310720]{0:T(1024)(128)(4,1)S(1)}, s32[]{:S(2)}) async-start(s8[5505024]{0:T(1024)(128)(4,1)} %bitcast.14), calls=%async_computation.4 | async-start | bytes 2621440
  76.3 4.9 %collective-permute-start.6 = (bf16[256,256]{1,0:T(8,128)(2,1)S(1)}, bf16[256,256]{1,0:T(8,128)(2,1)S(1)}, u32[]{:S(2)}, u32[]{:S(2)}) collective-permute-start(bf16[256,256]{1,0:T(8,128)(2,1)S(1)} %bitcast.21), channel_id=1, source_target_pairs={{0,1},{1,0},{2,3},{3,2},{4,5},{5,4},{6,7},{7,6},{8,9},{9,8},{10,11... | collective-permute-start | bytes 393224 | tf_op jit(solution)/shard_map/ppermute | solution.py:34
  81.1 1.4 collective-permute-start.7
  82.6 9.0 %copy-start.12 = (bf16[1344,640]{1,0:T(8,128)(2,1)S(1)}, bf16[1344,640]{1,0:T(8,128)(2,1)}, u32[]{:S(2)}) copy-start(bf16[1344,640]{1,0:T(8,128)(2,1)} %constant_dynamic-update-slice_fusion.refs_10_) | copy-start | bytes 5160964
  90.0 11.4 %collective-permute-start.9 = (bf16[32,5376]{1,0:T(8,128)(2,1)S(1)}, bf16[32,5376]{1,0:T(8,128)(2,1)S(1)}, u32[]{:S(2)}, u32[]{:S(2)}) collective-permute-start(bf16[32,5376]{1,0:T(8,128)(2,1)S(1)} %get-tuple-element.38), channel_id=1, source_target_pairs={{0,2},{2,4},{4,6},{6,0},{1,3},{3,5},{5,7},{7,1},{8,10},{10,12},{12... | collective-permute-start | bytes 1032200 | tf_op jit(solution)/shard_map/ppermute | solution.py:34
  91.6 60.3 %collective-permute-start.17 = (bf16[1344,640]{1,0:T(8,128)(2,1)S(1)}, bf16[1344,640]{1,0:T(8,128)(2,1)S(1)}, u32[]{:S(2)}, u32[]{:S(2)}) collective-permute-start(bf16[1344,640]{1,0:T(8,128)(2,1)S(1)} %copy-done.12), channel_id=1, source_target_pairs={{0,32},{1,9},{2,34},{3,11},{4,36},{5,13},{6,38},{7,15},{8,40},{9,1... | collective-permute-start | bytes 5160968 | tf_op jit(solution)/shard_map/ppermute | solution.py:79
  93.8 58.2 %collective-permute-start.18 = (bf16[1344,640]{1,0:T(8,128)(2,1)S(1)}, bf16[1344,640]{1,0:T(8,128)(2,1)S(1)}, u32[]{:S(2)}, u32[]{:S(2)}) collective-permute-start(bf16[1344,640]{1,0:T(8,128)(2,1)S(1)} %copy-done.12), channel_id=1, source_target_pairs={{0,96},{1,25},{2,98},{3,27},{4,100},{5,29},{6,102},{7,31},{8,104},... | collective-permute-start | bytes 5160968 | tf_op jit(solution)/shard_map/ppermute | solution.py:79
  95.3 16.4 %collective-permute-start.11 = (bf16[32,5376]{1,0:T(8,128)(2,1)S(1)}, bf16[32,5376]{1,0:T(8,128)(2,1)S(1)}, u32[]{:S(2)}, u32[]{:S(2)}) collective-permute-start(bf16[32,5376]{1,0:T(8,128)(2,1)S(1)} %get-tuple-element.39), channel_id=1, source_target_pairs={{0,2},{2,4},{4,6},{6,0},{1,3},{3,5},{5,7},{7,1},{8,10},{10,12},{12... | collective-permute-start | bytes 1032200 | tf_op jit(solution)/shard_map/ppermute | solution.py:34
  96.6 17.9 %collective-permute-start.12 = (bf16[32,5376]{1,0:T(8,128)(2,1)S(1)}, bf16[32,5376]{1,0:T(8,128)(2,1)S(1)}, u32[]{:S(2)}, u32[]{:S(2)}) collective-permute-start(bf16[32,5376]{1,0:T(8,128)(2,1)S(1)} %get-tuple-element.40), channel_id=1, source_target_pairs={{0,6},{2,0},{4,2},{6,4},{1,7},{3,1},{5,3},{7,5},{8,14},{10,8},{12,... | collective-permute-start | bytes 1032200 | tf_op jit(solution)/shard_map/ppermute | solution.py:34
  101.4 10.2 %collective-permute-start.13 = (bf16[32,5376]{1,0:T(8,128)(2,1)S(1)}, bf16[32,5376]{1,0:T(8,128)(2,1)S(1)}, u32[]{:S(2)}, u32[]{:S(2)}) collective-permute-start(bf16[32,5376]{1,0:T(8,128)(2,1)S(1)} %get-tuple-element.42), channel_id=1, source_target_pairs={{0,6},{2,0},{4,2},{6,4},{1,7},{3,1},{5,3},{7,5},{8,14},{10,8},{12,... | collective-permute-start | bytes 1032200 | tf_op jit(solution)/shard_map/ppermute | solution.py:34
  111.6 8.0 %collective-permute-start.10 = (bf16[32,5376]{1,0:T(8,128)(2,1)S(1)}, bf16[32,5376]{1,0:T(8,128)(2,1)S(1)}, u32[]{:S(2)}, u32[]{:S(2)}) collective-permute-start(bf16[32,5376]{1,0:T(8,128)(2,1)S(1)} %add_convert_fusion.1), channel_id=1, source_target_pairs={{0,2},{2,4},{4,6},{6,0},{1,3},{3,5},{5,7},{7,1},{8,10},{10,12},{12... | collective-permute-start | bytes 1032200 | tf_op jit(solution)/shard_map/ppermute | solution.py:34
  111.7 7.9 %collective-permute-start.14 = (bf16[32,5376]{1,0:T(8,128)(2,1)S(1)}, bf16[32,5376]{1,0:T(8,128)(2,1)S(1)}, u32[]{:S(2)}, u32[]{:S(2)}) collective-permute-start(bf16[32,5376]{1,0:T(8,128)(2,1)S(1)} %add_convert_fusion), channel_id=1, source_target_pairs={{0,6},{2,0},{4,2},{6,4},{1,7},{3,1},{5,3},{7,5},{8,14},{10,8},{12,... | collective-permute-start | bytes 1032200 | tf_op jit(solution)/shard_map/ppermute | solution.py:34
  121.5 37.8 %copy-start.3 = (bf16[64,5376]{1,0:T(8,128)(2,1)}, bf16[64,5376]{1,0:T(8,128)(2,1)S(1)}, u32[]{:S(2)}) copy-start(bf16[64,5376]{1,0:T(8,128)(2,1)S(1)} %get-tuple-element.50.refs_0_) | copy-start | bytes 2064388
  121.5 30.5 %collective-permute-start.15 = (bf16[64,5376]{1,0:T(8,128)(2,1)S(1)}, bf16[64,5376]{1,0:T(8,128)(2,1)S(1)}, u32[]{:S(2)}, u32[]{:S(2)}) collective-permute-start(bf16[64,5376]{1,0:T(8,128)(2,1)S(1)} %get-tuple-element.50.refs_0_), channel_id=1, source_target_pairs={{0,2},{2,4},{4,6},{6,0},{1,3},{3,5},{5,7},{7,1},{8,10},{10,12},{12... | collective-permute-start | bytes 2064392 | tf_op jit(solution)/shard_map/ppermute | solution.py:34
  122.0 30.0 %collective-permute-start.16 = (bf16[64,5376]{1,0:T(8,128)(2,1)S(1)}, bf16[64,5376]{1,0:T(8,128)(2,1)S(1)}, u32[]{:S(2)}, u32[]{:S(2)}) collective-permute-start(bf16[64,5376]{1,0:T(8,128)(2,1)S(1)} %get-tuple-element.50.refs_0_), channel_id=1, source_target_pairs={{0,6},{2,0},{4,2},{6,4},{1,7},{3,1},{5,3},{7,5},{8,14},{10,8},{12,... | collective-permute-start | bytes 2064392 | tf_op jit(solution)/shard_map/ppermute | solution.py:34
  124.2 35.1 %collective-permute-start.21 = (bf16[64,5376]{1,0:T(8,128)(2,1)S(1)}, bf16[64,5376]{1,0:T(8,128)(2,1)S(1)}, u32[]{:S(2)}, u32[]{:S(2)}) collective-permute-start(bf16[64,5376]{1,0:T(8,128)(2,1)S(1)} %get-tuple-element.50.refs_0_), channel_id=1, source_target_pairs={{0,1},{1,0},{2,3},{3,2},{4,5},{5,4},{6,7},{7,6},{8,9},{9,8},{10,11... | collective-permute-start | bytes 2064392 | tf_op jit(solution)/shard_map/ppermute | solution.py:34
  151.9 7.3 %copy-start.5 = (bf16[1344,640]{1,0:T(8,128)(2,1)}, bf16[1344,640]{1,0:T(8,128)(2,1)S(1)}, u32[]{:S(2)}) copy-start(bf16[1344,640]{1,0:T(8,128)(2,1)S(1)} %collective-permute-done.17.refs_11_) | copy-start | bytes 5160964
  151.9 7.3 %copy-start.6 = (bf16[1344,640]{1,0:T(8,128)(2,1)}, bf16[1344,640]{1,0:T(8,128)(2,1)S(1)}, u32[]{:S(2)}) copy-start(bf16[1344,640]{1,0:T(8,128)(2,1)S(1)} %collective-permute-done.18.refs_12_) | copy-start | bytes 5160964
  151.9 7.3 %copy-start.10 = (bf16[64,5376]{1,0:T(8,128)(2,1)}, bf16[64,5376]{1,0:T(8,128)(2,1)S(1)}, u32[]{:S(2)}) copy-start(bf16[64,5376]{1,0:T(8,128)(2,1)S(1)} %collective-permute-done.15.refs_1_) | copy-start | bytes 2064388
  152.0 18.2 %copy-start.11 = (bf16[64,5376]{1,0:T(8,128)(2,1)}, bf16[64,5376]{1,0:T(8,128)(2,1)S(1)}, u32[]{:S(2)}) copy-start(bf16[64,5376]{1,0:T(8,128)(2,1)S(1)} %collective-permute-done.16.refs_2_) | copy-start | bytes 2064388
  152.0 18.2 %collective-permute-start.22 = (bf16[64,5376]{1,0:T(8,128)(2,1)S(1)}, bf16[64,5376]{1,0:T(8,128)(2,1)S(1)}, u32[]{:S(2)}, u32[]{:S(2)}) collective-permute-start(bf16[64,5376]{1,0:T(8,128)(2,1)S(1)} %collective-permute-done.15.refs_1_), channel_id=1, source_target_pairs={{0,1},{1,0},{2,3},{3,2},{4,5},{5,4},{6,7},{7,6},{8,9},{9,8},{10,11... | collective-permute-start | bytes 2064392 | tf_op jit(solution)/shard_map/ppermute | solution.py:34
  155.6 11.1 %collective-permute-start.19 = (bf16[32,5376]{1,0:T(8,128)(2,1)S(1)}, bf16[32,5376]{1,0:T(8,128)(2,1)S(1)}, u32[]{:S(2)}, u32[]{:S(2)}) collective-permute-start(bf16[32,5376]{1,0:T(8,128)(2,1)S(1)} %slice.104), channel_id=1, source_target_pairs={{0,2},{2,4},{4,6},{6,0},{1,3},{3,5},{5,7},{7,1},{8,10},{10,12},{12... | collective-permute-start | bytes 1032200 | tf_op jit(solution)/shard_map/ppermute | solution.py:34
  157.0 10.3 %collective-permute-start.20 = (bf16[32,5376]{1,0:T(8,128)(2,1)S(1)}, bf16[32,5376]{1,0:T(8,128)(2,1)S(1)}, u32[]{:S(2)}, u32[]{:S(2)}) collective-permute-start(bf16[32,5376]{1,0:T(8,128)(2,1)S(1)} %slice.105), channel_id=1, source_target_pairs={{0,6},{2,0},{4,2},{6,4},{1,7},{3,1},{5,3},{7,5},{8,14},{10,8},{12,... | collective-permute-start | bytes 1032200 | tf_op jit(solution)/shard_map/ppermute | solution.py:34
  158.5 11.8 %collective-permute-start.23 = (bf16[64,5376]{1,0:T(8,128)(2,1)S(1)}, bf16[64,5376]{1,0:T(8,128)(2,1)S(1)}, u32[]{:S(2)}, u32[]{:S(2)}) collective-permute-start(bf16[64,5376]{1,0:T(8,128)(2,1)S(1)} %collective-permute-done.16.refs_2_), channel_id=1, source_target_pairs={{0,1},{1,0},{2,3},{3,2},{4,5},{5,4},{6,7},{7,6},{8,9},{9,8},{10,11... | collective-permute-start | bytes 2064392 | tf_op jit(solution)/shard_map/ppermute | solution.py:34
  159.3 11.0 %copy-start.16 = (bf16[64,5376]{1,0:T(8,128)(2,1)}, bf16[64,5376]{1,0:T(8,128)(2,1)S(1)}, u32[]{:S(2)}) copy-start(bf16[64,5376]{1,0:T(8,128)(2,1)S(1)} %collective-permute-done.21.refs_5_) | copy-start | bytes 2064388
  159.3 31.7 %collective-permute-start.26 = (bf16[672,640]{1,0:T(8,128)(2,1)S(1)}, bf16[672,640]{1,0:T(8,128)(2,1)}, u32[]{:S(2)}, u32[]{:S(2)}) collective-permute-start(bf16[672,640]{1,0:T(8,128)(2,1)S(1)} %slice.106), channel_id=1, source_target_pairs={{0,32},{1,9},{2,34},{3,11},{4,36},{5,13},{6,38},{7,15},{8,40},{9,1... | collective-permute-start | bytes 2580488 | tf_op jit(solution)/shard_map/ppermute | solution.py:79
  166.7 30.4 %copy-start.19 = (bf16[32,5376]{1,0:T(8,128)(2,1)}, bf16[32,5376]{1,0:T(8,128)(2,1)S(1)}, u32[]{:S(2)}) copy-start(bf16[32,5376]{1,0:T(8,128)(2,1)S(1)} %collective-permute-done.19.refs_3_) | copy-start | bytes 1032196
  166.7 30.4 %collective-permute-start.27 = (bf16[672,640]{1,0:T(8,128)(2,1)S(1)}, bf16[672,640]{1,0:T(8,128)(2,1)}, u32[]{:S(2)}, u32[]{:S(2)}) collective-permute-start(bf16[672,640]{1,0:T(8,128)(2,1)S(1)} %slice.107), channel_id=1, source_target_pairs={{0,96},{1,25},{2,98},{3,27},{4,100},{5,29},{6,102},{7,31},{8,104},... | collective-permute-start | bytes 2580488 | tf_op jit(solution)/shard_map/ppermute | solution.py:79
  167.3 4.2 %collective-permute-start.24 = (bf16[32,5376]{1,0:T(8,128)(2,1)S(1)}, bf16[32,5376]{1,0:T(8,128)(2,1)S(1)}, u32[]{:S(2)}, u32[]{:S(2)}) collective-permute-start(bf16[32,5376]{1,0:T(8,128)(2,1)S(1)} %collective-permute-done.19.refs_3_), channel_id=1, source_target_pairs={{0,1},{1,0},{2,3},{3,2},{4,5},{5,4},{6,7},{7,6},{8,9},{9,8},{10,11... | collective-permute-start | bytes 1032200 | tf_op jit(solution)/shard_map/ppermute | solution.py:34
  170.2 1.8 collective-permute-start.25
  172.2 24.9 %copy-start.22 = (bf16[32,5376]{1,0:T(8,128)(2,1)}, bf16[32,5376]{1,0:T(8,128)(2,1)S(1)}, u32[]{:S(2)}) copy-start(bf16[32,5376]{1,0:T(8,128)(2,1)S(1)} %collective-permute-done.25.refs_9_) | copy-start | bytes 1032196
  172.2 35.7 %all-to-all-start.1 = ((bf16[8,64,672]{2,1,0:T(8,128)(2,1)}), bf16[8,64,672]{2,1,0:T(8,128)(2,1)S(1)}, u32[]{:S(2)}, u32[]{:S(2)}) async-start(bf16[8,64,672]{2,1,0:T(8,128)(2,1)} %get-tuple-element.49), calls=%async_computation.1 | async-start | bytes 1572864 | tf_op jit(solution)/shard_map/all_to_all | solution.py:325
  209.0 19.3 %copy-start.7 = (bf16[320,512]{1,0:T(8,128)(2,1)S(1)}, bf16[320,512]{1,0:T(8,128)(2,1)}, u32[]{:S(2)}) copy-start(bf16[320,512]{1,0:T(8,128)(2,1)} %gated_rest.1) | copy-start | bytes 983044
  (8 other events, 21.5 us)
Sparse Core Ops, SparseCore 0:
  11.0 187.5 all-gather.1

commit v3 on v1

v3 whole, which is shorter than its diff:
```python
import jax
import jax.numpy as jnp
from jax import lax
from jax.experimental import pallas as pl
from jax.experimental.pallas import tpu as pltpu
from jax.sharding import Mesh, PartitionSpec as P

D = 5376
HD = 128
WINDOW = 1024
EPS = 1e-06
LOG2E = 1.4426950408889634
SCALE = float(168) ** -0.5
TOK = 512
PER = 64
BF = jnp.bfloat16
F32 = jnp.float32
VM = pl.BlockSpec(memory_space=pltpu.VMEM)
SM = pl.BlockSpec(memory_space=pltpu.SMEM)
HB = pl.BlockSpec(memory_space=pltpu.HBM)
MB = 1 << 20


def params(mb):
    return pltpu.CompilerParams(vmem_limit_bytes=mb * MB)


def cost(flops, nbytes, trans=0):
    return pl.CostEstimate(flops=int(flops), bytes_accessed=int(nbytes), transcendentals=int(trans))


def shift(value, axis, by):
    n = lax.axis_size(axis)
    return lax.ppermute(value, axis, [(i, (i + by) % n) for i in range(n)])


def behind(value):
    n = 16
    return lax.ppermute(value, ("y", "x"), [(i, i + 1) for i in range(n - 1)])


def pair_kernel(k_ref, v_ref, kv_ref):
    for h in range(2):
        kv_ref[:, 256 * h:256 * h + 128] = k_ref[:, 128 * h:128 * h + 128]
        kv_ref[:, 256 * h + 128:256 * h + 256] = v_ref[:, 128 * h:128 * h + 128]


def pair(keys, values):
    return pl.pallas_call(
        pair_kernel,
        out_shape=jax.ShapeDtypeStruct((TOK, 512), BF),
        in_specs=[VM] * 2,
        out_specs=VM,
        compiler_params=params(16),
        cost_estimate=cost(0, 1000),
        name="pair",
    )(keys, values)


def pack_kernel(g_ref, u_ref, o_ref):
    g, u = g_ref[...], u_ref[...]
    for j in range(7):
        lo = 192 * j
        o_ref[:, 384 * j:384 * j + 384] = jnp.concatenate(
            [g[:, lo:lo + 128], u[:, lo:lo + 128], g[:, lo + 128:lo + 192], u[:, lo + 128:lo + 192]], axis=1
        )


def pack(gate, up):
    return pl.pallas_call(
        pack_kernel,
        out_shape=jax.ShapeDtypeStruct((336, 2688), BF),
        in_specs=[VM, VM],
        out_specs=VM,
        compiler_params=params(24),
        cost_estimate=cost(0, 1000),
        name="pack",
    )(gate, up)


def ring(value, by, phase):
    pairs = []
    for y in range(4):
        for x in range(4):
            for z in range(4):
                for c in range(2):
                    along_x = (c == 0) == (phase == 0)
                    yy, xx = (y, (x + by) % 4) if along_x else ((y + by) % 4, x)
                    pairs.append((((y * 4 + x) * 4 + z) * 2 + c, ((yy * 4 + xx) * 4 + z) * 2 + c))
    return lax.ppermute(value, ("y", "x", "z", "c"), pairs)


def attend_kernel(at_ref, q_ref, kv2_ref, kv1_ref, kv0_ref, qid_ref, kid_ref, o_ref):
    z, c = at_ref[0], at_ref[1]
    for b in range(2):
        lo = 256 * b
        qid = qid_ref[lo:lo + 256, :]
        kid = kid_ref[:, lo:lo + 1280]
        row = lax.broadcasted_iota(jnp.int32, (256, 1280), 0)
        col = lax.broadcasted_iota(jnp.int32, (256, 1280), 1)
        allowed = (qid == kid) & (col > row) & (col <= row + 1024)
        outs = []
        for h in range(4):
            kc = slice(256 * (h // 2), 256 * (h // 2) + HD)
            vc = slice(256 * (h // 2) + HD, 256 * (h // 2) + 2 * HD)
            near = slice(0, 512 if b else 256)
            k = jnp.concatenate([kv2_ref[lo:, kc], kv1_ref[:, kc], kv0_ref[near, kc]], axis=0)
            v = jnp.concatenate([kv2_ref[lo:, vc], kv1_ref[:, vc], kv0_ref[near, vc]], axis=0)
            q = q_ref[lo:lo + 256, HD * h:HD * h + HD]
            s = lax.dot_general(q, k, (((1,), (1,)), ((), ())), preferred_element_type=F32)
            s = jnp.where(allowed, s * (SCALE * LOG2E), -1e30)
            top = jnp.max(s, axis=1, keepdims=True)
            e = jnp.exp2(s - top)
            total = jnp.sum(e, axis=1, keepdims=True)
            outs.append(jnp.dot(e.astype(BF), v, preferred_element_type=F32) / total)
        out = jnp.concatenate(outs, axis=1).astype(BF)
        for i in range(4):
            zz, cc = 2 * b + i // 2, i % 2
            o_ref[(cc + c) % 2, (zz - z + 4) % 4] = out[PER * i:PER * i + PER]


def attend(at, q, kv2, kv1, kv0, qid, kid):
    return pl.pallas_call(
        attend_kernel,
        out_shape=jax.ShapeDtypeStruct((2, 4, PER, 512), BF),
        in_specs=[SM] + [VM] * 6,
        out_specs=VM,
        compiler_params=params(32),
        cost_estimate=cost(0, 1000),
        name="attend",
    )(at, q, kv2, kv1, kv0, qid, kid)


def project_kernel(a, s, w_ref, ws_ref, p0, p1t, p1b, p2t, p2b, p3t, p3b):
    acc = jnp.dot(a[...], w_ref[...], preferred_element_type=F32)
    acc += jnp.dot(s[...], ws_ref[...], preferred_element_type=F32)
    out = acc.astype(BF)
    p0[...] = out[:64]
    for i, ref in enumerate((p1t, p1b, p2t, p2b, p3t, p3b)):
        ref[...] = out[64 + 32 * i:96 + 32 * i]


def project(a, s, w, ws):
    width = 768
    row = lambda r: pl.BlockSpec((r, width), lambda j: (0, j))
    full = pl.BlockSpec((256, 512), lambda j: (0, 0))
    return pl.pallas_call(
        project_kernel,
        out_shape=[jax.ShapeDtypeStruct((64, D), BF)] + [jax.ShapeDtypeStruct((32, D), BF)] * 6,
        grid=(D // width,),
        in_specs=[full] * 2 + [row(512)] * 2,
        out_specs=[row(64)] + [row(32)] * 6,
        compiler_params=params(24),
        cost_estimate=cost(0, 1000),
        name="project",
    )(a, s, w, ws)


def norm_kernel(p0, at_ref, ab_ref, bt_ref, bb_ref, res_ref, new_ref, nrm_ref):
    gain = jnp.concatenate([res_ref[j, 64:80].astype(F32) for j in range(8)], axis=1)
    post, pre = gain[0:1] + gain[1:2], gain[2:3] + gain[3:4]
    for half, (a, b) in enumerate(((at_ref, bt_ref), (ab_ref, bb_ref))):
        rows = slice(32 * half, 32 * half + 32)
        owned = p0[rows].astype(F32) + a[...].astype(F32) + b[...].astype(F32)
        factor = lax.rsqrt(jnp.mean(owned * owned, axis=1, keepdims=True) + EPS)
        res = jnp.concatenate([res_ref[j, rows].astype(F32) for j in range(8)], axis=1)
        new = (res + owned * factor * post).astype(BF)
        stream = new.astype(F32)
        for j in range(8):
            new_ref[j, rows] = stream[:, 672 * j:672 * j + 672].astype(BF)
        second = lax.rsqrt(jnp.mean(stream * stream, axis=1, keepdims=True) + EPS)
        nrm_ref[rows] = (stream * second * pre).astype(BF)


def norm(*args):
    return pl.pallas_call(
        norm_kernel,
        out_shape=[jax.ShapeDtypeStruct((8, PER, 672), BF), jax.ShapeDtypeStruct((PER, D), BF)],
        in_specs=[VM] * 6,
        out_specs=[VM] * 2,
        compiler_params=params(16),
        cost_estimate=cost(0, 1000),
        name="norm",
    )(*args)


def token_copies(where, pieces, tokens_at, n_ref, sems):
    z, c = where[0], where[1]
    copies = []
    for i, (ref, (dz, dc, part)) in enumerate(zip(pieces, tokens_at)):
        base, rows = 64 * (2 * ((z + dz) % 4) + (c + dc) % 2), 64
        if part is not None:
            base, rows = base + 32 * part, 32
        copies.append(pltpu.make_async_copy(ref, n_ref.at[pl.ds(pl.multiple_of(base, 32), rows)], sems.at[i]))
    return copies


def gelu(g):
    return 0.5 * g * (1 + jnp.tanh(0.7978845608028654 * (g + 0.044715 * (g * g * g))))


REL = (0, 3, 1, 2)


REL = (0, 3, 1, 2)
GROUP = 1408


def order(pieces, tokens_at, where):
    n = len(pieces)

    def body(*refs):
        place, o_ref, n_ref, sems = refs[n:]
        copies = token_copies(place, refs[:n], tokens_at, n_ref, sems)
        for copy in copies:
            copy.start()
        for copy in copies:
            copy.wait()
        c, y, x = place[1], place[2], place[3]

        def put(i, me, value, rows):
            rel = (i - me + 4) % 4
            slot = jnp.where(rel == 0, 0, jnp.where(rel == 3, 1, rel + 1))
            o_ref[rows, pl.ds(pl.multiple_of(GROUP * slot, 128), 1344)] = value

        @pl.loop(0, 8)
        def _(r):
            rows = pl.ds(pl.multiple_of(64 * r, 64), 64)

            @pl.when(c == 0)
            def _():
                for i in range(4):
                    put(i, y, n_ref[rows, 1344 * i:1344 * i + 1344], rows)

            @pl.when(c == 1)
            def _():
                for i in range(4):
                    cols = [1344 * k + 336 * i for k in range(4)]
                    put(i, x, jnp.concatenate([n_ref[rows, lo:lo + 336] for lo in cols], axis=1), rows)

    return pl.pallas_call(
        body,
        out_shape=jax.ShapeDtypeStruct((TOK, 4 * GROUP), BF),
        in_specs=[HB] * n + [SM],
        out_specs=VM,
        scratch_shapes=[pltpu.VMEM((TOK, D), BF), pltpu.SemaphoreType.DMA((n,))],
        compiler_params=params(40),
        cost_estimate=cost(0, 1000),
        name="order",
    )(*pieces, where)


def weight_copies(parts, where, arrays, block, w_ref, sems):
    c, y, x = where[1], where[2], where[3]
    first = jnp.where(c == 0, x, y)
    cols = pl.ds(pl.multiple_of(384 * block, 128), 384)
    copies = []
    for i, (array, slot, rel) in enumerate(parts):
        row = pl.multiple_of(1344 * slot + 336 * ((first + rel) % 4), 16)
        copies.append(
            pltpu.make_async_copy(arrays[array].at[:, cols], w_ref.at[pl.ds(row, 336)], sems.at[i])
        )
    return copies


def fetch_block(parts, place, arrays, w_ref, sems):
    j = pl.program_id(0)
    slot = lax.rem(j, 2)

    @pl.when(j == 0)
    def _():
        for copy in weight_copies(parts, place, arrays, 0, w_ref.at[0], sems.at[0]):
            copy.start()

    @pl.when(j + 1 < 7)
    def _():
        for copy in weight_copies(parts, place, arrays, j + 1, w_ref.at[1 - slot], sems.at[1 - slot]):
            copy.start()

    for copy in weight_copies(parts, place, arrays, j, w_ref.at[slot], sems.at[slot]):
        copy.wait()
    return slot


def near(rows, where, blocks):
    m = len(blocks)
    parts = [(4 * g + k, g, REL[k]) for g in range(3) for k in range(4)]

    def body(*refs):
        place, n_ref, o_ref, w_ref, sems = refs[m:]
        slot = fetch_block(parts, place, refs[:m], w_ref, sems)
        acc = jnp.dot(n_ref[:, :1344], w_ref[slot, :1344], preferred_element_type=F32)
        for g in (1, 2):
            lhs = n_ref[:, GROUP * g:GROUP * g + 1344]
            acc += jnp.dot(lhs, w_ref[slot, 1344 * g:1344 * g + 1344], preferred_element_type=F32)
        o_ref[...] = acc

    return pl.pallas_call(
        body,
        out_shape=jax.ShapeDtypeStruct((TOK, 2688), F32),
        grid=(7,),
        in_specs=[HB] * m + [SM, pl.BlockSpec((TOK, 3 * GROUP), lambda j: (0, 0))],
        out_specs=pl.BlockSpec((TOK, 384), lambda j: (0, j)),
        scratch_shapes=[pltpu.VMEM((2, 3 * 1344, 384), BF), pltpu.SemaphoreType.DMA((2, len(parts)))],
        compiler_params=params(56),
        cost_estimate=cost(2 * TOK * 4032 * 2688, 2 * 4032 * 2688 + 4 * TOK * 2688),
        name="near",
    )(*blocks, where, rows)


def far(rows, where, blocks, sums):
    m = len(blocks)
    parts = [(k, 0, REL[k]) for k in range(4)]

    def body(*refs):
        place, n_ref, s_ref, o_ref, w_ref, sems = refs[m:]
        slot = fetch_block(parts, place, refs[:m], w_ref, sems)
        acc = s_ref[...] + jnp.dot(n_ref[:, :1344], w_ref[slot], preferred_element_type=F32)
        last = acc[:, 256:]
        g = jnp.concatenate([acc[:, :128], last], axis=1)
        u = jnp.concatenate([acc[:, 128:256], pltpu.roll(last, 64, 1)], axis=1)
        o_ref[...] = (gelu(g) * u).T[:192].astype(BF)

    return pl.pallas_call(
        body,
        out_shape=jax.ShapeDtypeStruct((1344, TOK), BF),
        grid=(7,),
        in_specs=[HB] * m
        + [SM, pl.BlockSpec((TOK, GROUP), lambda j: (0, 3)), pl.BlockSpec((TOK, 384), lambda j: (0, j))],
        out_specs=pl.BlockSpec((192, TOK), lambda j: (j, 0)),
        scratch_shapes=[pltpu.VMEM((2, 1344, 384), BF), pltpu.SemaphoreType.DMA((2, len(parts)))],
        compiler_params=params(56),
        cost_estimate=cost(2 * TOK * 1344 * 2688, 2 * 1344 * 2688 + 4 * TOK * 2688),
        name="far",
    )(*blocks, where, rows, sums)


def turn(value, by):
    return lax.dynamic_slice_in_dim(jnp.concatenate([value, value], axis=0), by % 4, 4, 0)


def to_tokens(blocks, z, c):
    blocks = blocks.reshape(4, 2, *blocks.shape[1:])
    keep = jnp.where(c == 0, blocks[:, 0], blocks[:, 1])
    give = jnp.where(c == 0, blocks[:, 1], blocks[:, 0])
    take = shift(give, "c", 1)
    both = turn(jnp.stack([jnp.where(c == 0, keep, take), jnp.where(c == 0, take, keep)], axis=1), z)
    got = jnp.stack([both[0], shift(both[3], "z", 3), shift(both[2], "z", 2), shift(both[1], "z", 1)])
    return turn(got, 4 - z).reshape(8, *got.shape[2:])


def to_features(blocks, z, c):
    both = turn(blocks.reshape(4, 2, *blocks.shape[1:]), z)
    got = jnp.stack([both[0], shift(both[3], "z", 3), shift(both[2], "z", 2), shift(both[1], "z", 1)])
    got = turn(got, 4 - z)
    keep = jnp.where(c == 0, got[:, 0], got[:, 1])
    give = jnp.where(c == 0, got[:, 1], got[:, 0])
    take = shift(give, "c", 1)
    both = jnp.stack([jnp.where(c == 0, keep, take), jnp.where(c == 0, take, keep)], axis=1)
    return both.reshape(8, *got.shape[2:])


def per_device(queries, keys, values, doc_ids, out_weight, residual, post_gain, pre_gain, gate_weight, up_weight):
    y, x, z, c = (lax.axis_index(a) for a in ("y", "x", "z", "c"))
    where = jnp.stack([z, c, y, x]).astype(jnp.int32)

    kv0 = pair(keys, values)
    kv1 = behind(kv0)
    w = pack(gate_weight, up_weight)
    p = ring(w, -1, 0)
    kv1, w_late = lax.optimization_barrier((kv1, w))
    kv2 = behind(kv1)
    m = ring(w_late, 1, 0)
    b = ring(p, -1, 0)
    w_late, kv2 = lax.optimization_barrier((w_late, kv2))
    prev, following = [ring(w_late, 1, 1)], [ring(w_late, -1, 1)]

    gains = jnp.stack([post_gain, pre_gain])
    high = gains.astype(BF)
    low = (gains - high.astype(F32)).astype(BF)
    extra = jnp.stack([high[0], low[0], high[1], low[1]])
    extra = jnp.concatenate([extra, jnp.zeros((12, 672), BF)], axis=0)
    sent = jnp.concatenate([residual.reshape(8, PER, 672), jnp.broadcast_to(extra[None], (8, 16, 672))], axis=1)
    mine = to_tokens(sent, z, c)

    start = (4 * y + x) * TOK
    padded = jnp.concatenate([jnp.full((2 * TOK,), -1, jnp.int32), doc_ids])
    kid = lax.dynamic_slice_in_dim(padded, start, 3 * TOK, 0)[None, :]
    qid = lax.dynamic_slice_in_dim(doc_ids, start, TOK, 0)[:, None]

    queries, mine, p = lax.optimization_barrier((queries, mine, p))
    mix = attend(where, queries, kv2, kv1, kv0, qid, kid)
    other_weight = shift(out_weight, "c", 1)
    own, other = mix[0].reshape(256, 512), shift(mix[1].reshape(256, 512), "c", 1)
    other, m, following[0] = lax.optimization_barrier((other, m, following[0]))
    prev += [ring(v, 1, 1) for v in (m, p)]
    following += [ring(v, -1, 1) for v in (m, p)]
    p0, p1t, p1b, p2t, p2b, p3t, p3b = project(own, other, out_weight, other_weight)

    up_t = shift(p2t, "z", 1)
    dn_b = shift(p2b, "z", -1)
    a_b = shift(p1b, "z", 1)
    b_t = shift(p3t, "z", -1)
    up_t, dn_b, b, prev[0] = lax.optimization_barrier((up_t, dn_b, b, prev[0]))
    prev += [ring(b, 1, 1)]
    following += [ring(b, -1, 1)]
    add = lambda p, q: (p.astype(F32) + q.astype(F32)).astype(BF)
    a_t = shift(add(p1t, up_t), "z", 1)
    b_b = shift(add(p3b, dn_b), "z", -1)
    p0, prev[2], following[2] = lax.optimization_barrier((p0, prev[2], following[2]))
    new, nrm = norm(p0, a_t, a_b, b_t, b_b, mine)

    n_m, n_p = shift(nrm, "z", 1), shift(nrm, "z", -1)
    n_m, n_p, prev[1], following[1] = lax.optimization_barrier((n_m, n_p, prev[1], following[1]))
    pieces = [nrm, n_m, n_p, shift(n_m[:32], "z", 1), shift(n_p[32:], "z", -1)]
    places = [(0, None), (3, None), (1, None), (2, 0), (2, 1)]
    pieces += [shift(piece, "c", 1) for piece in pieces]
    tokens_at = [(dz, dc, part) for dc in range(2) for dz, part in places]
    pieces, prev[3], following[3] = lax.optimization_barrier((pieces, prev[3], following[3]))
    rows = order(pieces, tokens_at, where)

    last = [ring(prev[0], 1, 1), ring(prev[1], 1, 1), ring(following[2], -1, 1), ring(following[3], -1, 1)]
    new, rows = lax.optimization_barrier((new, rows))
    new_residual = to_features(new, z, c).reshape(TOK, 672)
    sums = near(rows, where, [w, m, p, b, *prev, *following])
    act = far(rows, where, last, sums)
    return new_residual, act.T


def solution(mesh):
    fine = Mesh(mesh.devices.reshape(4, 4, 4, 2), ("y", "x", "z", "c"))
    t, f = ("y", "x"), ("z", "c")
    in_specs = (P(t, f), P(t, f), P(t, f), P(), P(f, None), P(t, f), P(f), P(f), P(t, f), P(t, f))
    return jax.shard_map(per_device, mesh=fine, in_specs=in_specs, out_specs=(P(t, f), P(t, f)), check_vma=False)
```

time: 257 us -> 232 us (0.903)
  blocking collectives: 25.3 us -> 0 us
  local copies, waits for them, and re-layouts: 30.5 us -> 11.1 us
  waiting for transfers between devices: 78.8 us -> 97.3 us
  between operations: 15 us -> 1.42 us
  starting transfers between devices: 53.5 us -> 61.3 us
  Pallas kernels: 49 us -> 56.3 us
    ppermute x22 -> x25, waiting for transfers between devices: 26.6 us -> 55 us  [shift(): return lax.ppermute(value, axis, [(i, (i + by) % n) for i in range(n)])]
    ppermute x0 -> x15, waiting for transfers between devices: none -> 28.4 us  [ring(): return lax.ppermute(value, ('y', 'x', 'z', 'c'), pairs)]
    all_gather x2 -> x0, waiting for transfers between devices: 27.3 us -> none  [the longest x1 27.3 us: per_device(): w_first = lax.all_gather(w[:, :1920], ('y', 'x'), axis=0, tiled=True)]
    unnamed x1 -> x0, blocking collectives: 25.3 us -> none
    ppermute x0 -> x15, starting transfers between devices: none -> 16.2 us  [ring(): return lax.ppermute(value, ('y', 'x', 'z', 'c'), pairs)]
    all_to_all x2 -> x0, waiting for transfers between devices: 10.9 us -> none  [the longest x1 10.9 us: per_device(): new_residual = lax.all_to_all(new, ('z', 'c'), 1, 0, tiled=True)]
    ppermute x22 -> x25, starting transfers between devices: 29 us -> 38.8 us  [shift(): return lax.ppermute(value, axis, [(i, (i + by) % n) for i in range(n)])]
    unnamed x65 -> x60, local copies, waits for them, and re-layouts: 18.6 us -> 8.9 us
  transfers between devices with their start and end apart: 30 -> 42, of which waited for: 9 -> 19; matrix products, arithmetic and copies ran while one was open for 5% -> 4% of each run, Pallas kernels for 11% -> 19%
where the time goes in v3:
time: 232 us; the launch traced here: 231 us
  waiting for transfers between devices  97.3 us (42%)
  starting transfers between devices  61.3 us (26%)
  Pallas kernels  56.3 us (24%)
  local copies, waits for them, and re-layouts  11.1 us (5%)
  other arithmetic  4.06 us (2%)
    ppermute x25, waiting for transfers between devices, shift(): return lax.ppermute(value, axis, [(i, (i + by) % n) for i in range(n)])  55 us
    ppermute x25, starting transfers between devices, shift(): return lax.ppermute(value, axis, [(i, (i + by) % n) for i in range(n)])  38.8 us
    ppermute x15, waiting for transfers between devices, ring(): return lax.ppermute(value, ('y', 'x', 'z', 'c'), pairs)  28.4 us
    pallas_call x1, Pallas kernels, near(): pl.pallas_call(body, out_shape=jax.ShapeDtypeStruct((TOK, 2688), F32), gr...  23.6 us
    ppermute x15, starting transfers between devices, ring(): return lax.ppermute(value, ('y', 'x', 'z', 'c'), pairs)  16.2 us
    ppermute x2, waiting for transfers between devices, behind(): return lax.ppermute(value, ('y', 'x'), [(i, i + 1) for i in range(n - 1)])  13.9 us
    pallas_call x1, Pallas kernels, far(): pl.pallas_call(body, out_shape=jax.ShapeDtypeStruct((1344, TOK), BF), gri...  12.8 us
    unnamed x60, local copies, waits for them, and re-layouts  8.9 us
  transfers between devices with their start and end apart: 42, of which 19 were waited for; matrix products, arithmetic and copies ran while one was open for 4% of the time, Pallas kernels for 19%

profile of v3, /device:TPU:1, one launch (start us, length us, event | category | flops | bytes accessed | tf_op | source)
XLA Modules:
  0.0 231.4 jit_solution(6382583226932698907)
XLA Ops:
  0.6 1.5 collective-permute-start.10
  3.5 1.4 copy.19
  7.0 2.9 %collective-permute-start.4 = (bf16[336,2688]{1,0:T(8,128)(2,1)S(1)}, bf16[336,2688]{1,0:T(8,128)(2,1)}, u32[]{:S(2)}, u32[]{:S(2)}) collective-permute-start(bf16[336,2688]{1,0:T(8,128)(2,1)S(1)} %pack.1.refs_0_), channel_id=1, source_target_pairs={{0,24},{1,97},{2,26},{3,99},{4,28},{5,101},{6,30},{7,103},{8,0},{9... | collective-permute-start | bytes 5419016 | tf_op jit(solution)/shard_map/ppermute | solution.py:90
  9.9 3.1 %collective-permute-start.5 = (bf16[512,512]{1,0:T(8,128)(2,1)S(1)}, bf16[512,512]{1,0:T(8,128)(2,1)S(1)}, u32[]{:S(2)}, u32[]{:S(2)}) collective-permute-start(bf16[512,512]{1,0:T(8,128)(2,1)S(1)} %pair.1.kv0_ref), channel_id=1, source_target_pairs={{0,8},{8,16},{16,24},{24,32},{32,40},{40,48},{48,56},{56,64},{64,7... | collective-permute-start | bytes 1572872 | tf_op jit(solution)/shard_map/ppermute | solution.py:39
  13.6 1.8 select_bitcast_fusion
  16.0 3.8 %collective-permute-start.1 = (bf16[2,80,672]{2,1,0:T(8,128)(2,1)S(1)}, bf16[2,80,672]{2,1,0:T(8,128)(2,1)S(1)}, u32[]{:S(2)}, u32[]{:S(2)}) collective-permute-start(bf16[2,80,672]{2,1,0:T(8,128)(2,1)S(1)} %get-tuple-element.98), channel_id=1, source_target_pairs={{0,6},{2,0},{4,2},{6,4},{1,7},{3,1},{5,3},{7,5},{8,14},{10,8},{12,... | collective-permute-start | bytes 645128 | tf_op jit(solution)/shard_map/ppermute | solution.py:34
  19.9 3.4 %collective-permute-done.5.kv1_ref = bf16[512,512]{1,0:T(8,128)(2,1)S(1)} collective-permute-done((bf16[512,512]{1,0:T(8,128)(2,1)S(1)}, bf16[512,512]{1,0:T(8,128)(2,1)S(1)}, u32[]{:S(2)}, u32[]{:S(2)}) %collective-permute-start.5) | collective-permute-done | bytes 524320 | tf_op jit(solution)/shard_map/ppermute | solution.py:39
  23.4 1.6 collective-permute-start.3
  25.0 5.1 %collective-permute-done.1 = bf16[2,80,672]{2,1,0:T(8,128)(2,1)S(1)} collective-permute-done((bf16[2,80,672]{2,1,0:T(8,128)(2,1)S(1)}, bf16[2,80,672]{2,1,0:T(8,128)(2,1)S(1)}, u32[]{:S(2)}, u32[]{:S(2)}) %collective-permute-start.1) | collective-permute-done | bytes 215072 | tf_op jit(solution)/shard_map/ppermute | solution.py:34
  30.1 3.1 %collective-permute-start.6 = (bf16[512,512]{1,0:T(8,128)(2,1)S(1)}, bf16[512,512]{1,0:T(8,128)(2,1)S(1)}, u32[]{:S(2)}, u32[]{:S(2)}) collective-permute-start(bf16[512,512]{1,0:T(8,128)(2,1)S(1)} %collective-permute-done.5.kv1_ref), channel_id=1, source_target_pairs={{0,8},{8,16},{16,24},{24,32},{32,40},{40,48},{48,56},{56,64},{64,7... | collective-permute-start | bytes 1572872 | tf_op jit(solution)/shard_map/ppermute | solution.py:39
  34.3 10.5 %collective-permute-done.6.kv2_ref = bf16[512,512]{1,0:T(8,128)(2,1)S(1)} collective-permute-done((bf16[512,512]{1,0:T(8,128)(2,1)S(1)}, bf16[512,512]{1,0:T(8,128)(2,1)S(1)}, u32[]{:S(2)}, u32[]{:S(2)}) %collective-permute-start.6) | collective-permute-done | bytes 524320 | tf_op jit(solution)/shard_map/ppermute | solution.py:39
  44.8 1.3 collective-permute-start.9
  47.0 5.5 %attend.1 = bf16[2,4,64,512]{3,2,1,0:T(8,128)(2,1)S(1)} custom-call(s32[4]{0:T(128)S(1)} %pad_add_fusion.at_ref.refs_10_.refs_12_.refs_4_, bf16[512,512]{1,0:T(8,128)(2,1)S(1)} %copy-done.4, bf16[512,512]{1,0:T(8,128)(2,1)S(1)} %collective-permute-done.6.kv2_ref, bf16[512,512]{1,0:T(8,128)(2,1)S(1)} %collective-permute-done.5.kv1_ref, ...), custom_call_target="tpu_custom_call" | custom-call | bytes 1000 | tf_op jit(solution)/shard_map/attend/pallas_call | solution.py:123
  52.6 2.6 %collective-permute-start.7 = (bf16[256,512]{1,0:T(8,128)(2,1)S(1)}, bf16[256,512]{1,0:T(8,128)(2,1)S(1)}, u32[]{:S(2)}, u32[]{:S(2)}) collective-permute-start(bf16[256,512]{1,0:T(8,128)(2,1)S(1)} %bitcast.118), channel_id=1, source_target_pairs={{0,1},{1,0},{2,3},{3,2},{4,5},{5,4},{6,7},{7,6},{8,9},{9,8},{10,11... | collective-permute-start | bytes 786440 | tf_op jit(solution)/shard_map/ppermute | solution.py:34
  55.2 1.2 collective-permute-done.7.s
  56.3 2.9 %collective-permute-start.15 = (bf16[336,2688]{1,0:T(8,128)(2,1)}, bf16[336,2688]{1,0:T(8,128)(2,1)}, u32[]{:S(2)}, u32[]{:S(2)}) collective-permute-start(bf16[336,2688]{1,0:T(8,128)(2,1)} %collective-permute-done.4.refs_2_), channel_id=1, source_target_pairs={{0,24},{1,97},{2,26},{3,99},{4,28},{5,101},{6,30},{7,103},{8,0},{9... | collective-permute-start | bytes 5419016 | tf_op jit(solution)/shard_map/ppermute | solution.py:90
  59.3 19.3 %collective-permute-done.8.refs_1_ = bf16[336,2688]{1,0:T(8,128)(2,1)S(1)} collective-permute-done((bf16[336,2688]{1,0:T(8,128)(2,1)S(1)}, bf16[336,2688]{1,0:T(8,128)(2,1)S(1)}, u32[]{:S(2)}, u32[]{:S(2)}) %collective-permute-start.8) | collective-permute-done | bytes 1806368 | tf_op jit(solution)/shard_map/ppermute | solution.py:90
  78.6 2.7 %collective-permute-start.12 = (bf16[336,2688]{1,0:T(8,128)(2,1)}, bf16[336,2688]{1,0:T(8,128)(2,1)S(1)}, u32[]{:S(2)}, u32[]{:S(2)}) collective-permute-start(bf16[336,2688]{1,0:T(8,128)(2,1)} %collective-permute-done.4.refs_2_), channel_id=1, source_target_pairs={{0,96},{1,25},{2,98},{3,27},{4,100},{5,29},{6,102},{7,31},{8,104},... | collective-permute-start | bytes 5419016 | tf_op jit(solution)/shard_map/ppermute | solution.py:90
  81.3 7.3 %project.1 = (bf16[64,5376]{1,0:T(8,128)(2,1)S(1)}, bf16[32,5376]{1,0:T(8,128)(2,1)S(1)}, bf16[32,5376]{1,0:T(8,128)(2,1)S(1)}, bf16[32,5376]{1,0:T(8,128)(2,1)S...) custom-call(bf16[256,512]{1,0:T(8,128)(2,1)S(1)} %bitcast.112, ...), custom_call_target="tpu_custom_call" | custom-call | bytes 1000 | tf_op jit(solution)/shard_map/project/pallas_call | solution.py:147
  88.7 2.8 %collective-permute-start.14 = (bf16[32,5376]{1,0:T(8,128)(2,1)S(1)}, bf16[32,5376]{1,0:T(8,128)(2,1)S(1)}, u32[]{:S(2)}, u32[]{:S(2)}) collective-permute-start(bf16[32,5376]{1,0:T(8,128)(2,1)S(1)} %get-tuple-element.57), channel_id=1, source_target_pairs={{0,6},{2,0},{4,2},{6,4},{1,7},{3,1},{5,3},{7,5},{8,14},{10,8},{12,... | collective-permute-start | bytes 1032200 | tf_op jit(solution)/shard_map/ppermute | solution.py:34
  91.8 4.5 %collective-permute-done.13 = bf16[32,5376]{1,0:T(8,128)(2,1)S(1)} collective-permute-done((bf16[32,5376]{1,0:T(8,128)(2,1)S(1)}, bf16[32,5376]{1,0:T(8,128)(2,1)S(1)}, u32[]{:S(2)}, u32[]{:S(2)}) %collective-permute-start.13) | collective-permute-done | bytes 344096 | tf_op jit(solution)/shard_map/ppermute | solution.py:34
  96.3 1.2 collective-permute-start.24
  97.6 6.6 %collective-permute-done.11.refs_6_ = bf16[336,2688]{1,0:T(8,128)(2,1)S(1)} collective-permute-done((bf16[336,2688]{1,0:T(8,128)(2,1)}, bf16[336,2688]{1,0:T(8,128)(2,1)S(1)}, u32[]{:S(2)}, u32[]{:S(2)}) %collective-permute-start.11) | collective-permute-done | bytes 1806368 | tf_op jit(solution)/shard_map/ppermute | solution.py:90
  104.2 3.6 %collective-permute-start.19 = (bf16[32,5376]{1,0:T(8,128)(2,1)S(1)}, bf16[32,5376]{1,0:T(8,128)(2,1)S(1)}, u32[]{:S(2)}, u32[]{:S(2)}) collective-permute-start(bf16[32,5376]{1,0:T(8,128)(2,1)S(1)} %get-tuple-element.60), channel_id=1, source_target_pairs={{0,6},{2,0},{4,2},{6,4},{1,7},{3,1},{5,3},{7,5},{8,14},{10,8},{12,... | collective-permute-start | bytes 1032200 | tf_op jit(solution)/shard_map/ppermute | solution.py:34
  107.7 1.5 collective-permute-start.20
  109.4 3.5 %collective-permute-done.19.bt_ref = bf16[32,5376]{1,0:T(8,128)(2,1)S(1)} collective-permute-done((bf16[32,5376]{1,0:T(8,128)(2,1)S(1)}, bf16[32,5376]{1,0:T(8,128)(2,1)S(1)}, u32[]{:S(2)}, u32[]{:S(2)}) %collective-permute-start.19) | collective-permute-done | bytes 344096 | tf_op jit(solution)/shard_map/ppermute | solution.py:34
  112.9 7.4 %collective-permute-done.20.bb_ref = bf16[32,5376]{1,0:T(8,128)(2,1)S(1)} collective-permute-done((bf16[32,5376]{1,0:T(8,128)(2,1)S(1)}, bf16[32,5376]{1,0:T(8,128)(2,1)S(1)}, u32[]{:S(2)}, u32[]{:S(2)}) %collective-permute-start.20) | collective-permute-done | bytes 344096 | tf_op jit(solution)/shard_map/ppermute | solution.py:34
  121.5 2.2 collective-permute-done.23.refs_5_
  123.6 3.6 %collective-permute-start.22 = (bf16[64,5376]{1,0:T(8,128)(2,1)S(1)}, bf16[64,5376]{1,0:T(8,128)(2,1)S(1)}, u32[]{:S(2)}, u32[]{:S(2)}) collective-permute-start(bf16[64,5376]{1,0:T(8,128)(2,1)S(1)} %get-tuple-element.70.refs_0_), channel_id=1, source_target_pairs={{0,6},{2,0},{4,2},{6,4},{1,7},{3,1},{5,3},{7,5},{8,14},{10,8},{12,... | collective-permute-start | bytes 2064392 | tf_op jit(solution)/shard_map/ppermute | solution.py:34
  127.2 2.7 %collective-permute-start.27 = (bf16[64,5376]{1,0:T(8,128)(2,1)S(1)}, bf16[64,5376]{1,0:T(8,128)(2,1)S(1)}, u32[]{:S(2)}, u32[]{:S(2)}) collective-permute-start(bf16[64,5376]{1,0:T(8,128)(2,1)S(1)} %get-tuple-element.70.refs_0_), channel_id=1, source_target_pairs={{0,1},{1,0},{2,3},{3,2},{4,5},{5,4},{6,7},{7,6},{8,9},{9,8},{10,11... | collective-permute-start | bytes 2064392 | tf_op jit(solution)/shard_map/ppermute | solution.py:34
  129.9 6.3 %collective-permute-done.21.refs_1_ = bf16[64,5376]{1,0:T(8,128)(2,1)S(1)} collective-permute-done((bf16[64,5376]{1,0:T(8,128)(2,1)S(1)}, bf16[64,5376]{1,0:T(8,128)(2,1)S(1)}, u32[]{:S(2)}, u32[]{:S(2)}) %collective-permute-start.21) | collective-permute-done | bytes 688160 | tf_op jit(solution)/shard_map/ppermute | solution.py:34
  136.2 3.2 %collective-permute-done.22.refs_2_ = bf16[64,5376]{1,0:T(8,128)(2,1)S(1)} collective-permute-done((bf16[64,5376]{1,0:T(8,128)(2,1)S(1)}, bf16[64,5376]{1,0:T(8,128)(2,1)S(1)}, u32[]{:S(2)}, u32[]{:S(2)}) %collective-permute-start.22) | collective-permute-done | bytes 688160 | tf_op jit(solution)/shard_map/ppermute | solution.py:34
  139.6 3.6 %collective-permute-start.26 = (bf16[32,5376]{1,0:T(8,128)(2,1)S(1)}, bf16[32,5376]{1,0:T(8,128)(2,1)}, u32[]{:S(2)}, u32[]{:S(2)}) collective-permute-start(bf16[32,5376]{1,0:T(8,128)(2,1)S(1)} %slice.77), channel_id=1, source_target_pairs={{0,6},{2,0},{4,2},{6,4},{1,7},{3,1},{5,3},{7,5},{8,14},{10,8},{12,... | collective-permute-start | bytes 1032200 | tf_op jit(solution)/shard_map/ppermute | solution.py:34
  143.2 5.0 %collective-permute-done.25.refs_3_ = bf16[32,5376]{1,0:T(8,128)(2,1)S(1)} collective-permute-done((bf16[32,5376]{1,0:T(8,128)(2,1)S(1)}, bf16[32,5376]{1,0:T(8,128)(2,1)S(1)}, u32[]{:S(2)}, u32[]{:S(2)}) %collective-permute-start.25) | collective-permute-done | bytes 344096 | tf_op jit(solution)/shard_map/ppermute | solution.py:34
  148.2 3.9 %collective-permute-start.30 = (bf16[32,5376]{1,0:T(8,128)(2,1)S(1)}, bf16[32,5376]{1,0:T(8,128)(2,1)S(1)}, u32[]{:S(2)}, u32[]{:S(2)}) collective-permute-start(bf16[32,5376]{1,0:T(8,128)(2,1)S(1)} %collective-permute-done.25.refs_3_), channel_id=1, source_target_pairs={{0,1},{1,0},{2,3},{3,2},{4,5},{5,4},{6,7},{7,6},{8,9},{9,8},{10,11... | collective-permute-start | bytes 1032200 | tf_op jit(solution)/shard_map/ppermute | solution.py:34
  154.5 2.3 collective-permute-done.31.refs_9_
  160.6 5.5 %order.1.refs_13_.refs_5_ = bf16[512,5632]{1,0:T(8,128)(2,1)S(1)} custom-call(bf16[64,5376]{1,0:T(8,128)(2,1)S(1)} %get-tuple-element.70.refs_0_, bf16[64,5376]{1,0:T(8,128)(2,1)S(1)} %collective-permute-done.21.refs_1_, bf16[64,5376]{1,0:T(8,128)(2,1)S(1)} %collective-permute-done.22.refs_2_, bf16[32,5376]{1,0:T(8,128)(2,1)S(1)} %copy-done.6, ...), custom_call_target="tpu_custom_call" | custom-call | bytes 1000 | tf_op jit(solution)/shard_map/order/pallas_call | solution.py:241
  166.1 2.5 %copy-done = bf16[512,5632]{1,0:T(8,128)(2,1)} copy-done((bf16[512,5632]{1,0:T(8,128)(2,1)}, bf16[512,5632]{1,0:T(8,128)(2,1)S(1)}, u32[]{:S(2)}) %copy-start) | copy-done | bytes 5767192
  168.6 2.4 %collective-permute-start.41 = (bf16[336,2688]{1,0:T(8,128)(2,1)}, bf16[336,2688]{1,0:T(8,128)(2,1)}, u32[]{:S(2)}, u32[]{:S(2)}) collective-permute-start(bf16[336,2688]{1,0:T(8,128)(2,1)} %collective-permute-done.33.refs_11_), channel_id=1, source_target_pairs={{0,96},{1,25},{2,98},{3,27},{4,100},{5,29},{6,102},{7,31},{8,104},... | collective-permute-start | bytes 5419016 | tf_op jit(solution)/shard_map/ppermute | solution.py:90
  171.3 1.6 collective-permute-start.34
  172.9 4.7 %collective-permute-done.34 = bf16[2,64,672]{2,1,0:T(8,128)(2,1)S(1)} collective-permute-done((bf16[2,64,672]{2,1,0:T(8,128)(2,1)S(1)}, bf16[2,64,672]{2,1,0:T(8,128)(2,1)S(1)}, u32[]{:S(2)}, u32[]{:S(2)}) %collective-permute-start.34) | collective-permute-done | bytes 172064 | tf_op jit(solution)/shard_map/ppermute | solution.py:34
  177.6 1.1 collective-permute-start.35
  178.7 5.7 %collective-permute-done.35 = bf16[2,64,672]{2,1,0:T(8,128)(2,1)S(1)} collective-permute-done((bf16[2,64,672]{2,1,0:T(8,128)(2,1)S(1)}, bf16[2,64,672]{2,1,0:T(8,128)(2,1)S(1)}, u32[]{:S(2)}, u32[]{:S(2)}) %collective-permute-start.35) | collective-permute-done | bytes 172064 | tf_op jit(solution)/shard_map/ppermute | solution.py:34
  185.1 5.4 %collective-permute-done.36 = bf16[2,64,672]{2,1,0:T(8,128)(2,1)S(1)} collective-permute-done((bf16[2,64,672]{2,1,0:T(8,128)(2,1)S(1)}, bf16[2,64,672]{2,1,0:T(8,128)(2,1)S(1)}, u32[]{:S(2)}, u32[]{:S(2)}) %collective-permute-start.36) | collective-permute-done | bytes 172064 | tf_op jit(solution)/shard_map/ppermute | solution.py:34
  190.7 2.8 %collective-permute-start.37 = (bf16[4,64,672]{2,1,0:T(8,128)(2,1)S(1)}, bf16[4,64,672]{2,1,0:T(8,128)(2,1)S(1)}, u32[]{:S(2)}, u32[]{:S(2)}) collective-permute-start(bf16[4,64,672]{2,1,0:T(8,128)(2,1)S(1)} %select_bitcast_fusion.2), channel_id=1, source_target_pairs={{0,1},{1,0},{2,3},{3,2},{4,5},{5,4},{6,7},{7,6},{8,9},{9,8},{10,11... | collective-permute-start | bytes 1032200 | tf_op jit(solution)/shard_map/ppermute | solution.py:34
  193.5 23.6 %near.1.refs_6_ = f32[512,2688]{1,0:T(8,128)} custom-call(bf16[336,2688]{1,0:T(8,128)(2,1)} %copy-done.1, bf16[336,2688]{1,0:T(8,128)(2,1)} %copy-done.14, bf16[336,2688]{1,0:T(8,128)(2,1)} %collective-permute-done.4.refs_2_, bf16[336,2688]{1,0:T(8,128)(2,1)} %collective-permute-done.15.refs_3_, bf16[336,2688]{1,0:T(8,128)(2,1)} %copy-done.15, ...), custom_call_target="tpu_custom_call" | custom-call | flops 11098128384 | bytes 27181056 | tf_op jit(solution)/shard_map/near/pallas_call | solution.py:298
  217.3 1.1 copy.35
  218.5 12.8 %far.1 = bf16[1344,512]{1,0:T(8,128)(2,1)} custom-call(bf16[336,2688]{1,0:T(8,128)(2,1)} %collective-permute-done.38.refs_0_, bf16[336,2688]{1,0:T(8,128)(2,1)} %collective-permute-done.39.refs_1_, bf16[336,2688]{1,0:T(8,128)(2,1)} %collective-permute-done.40.refs_2_, bf16[336,2688]{1,0:T(8,128)(2,1)} %collective-permute-done.41.refs_3_, s32[4]{0:T(128)} %copy-done.11, ...), custom_call_target="tpu_custom_call" | custom-call | flops 3699376128 | bytes 12730368 | tf_op jit(solution)/shard_map/far/pallas_call | solution.py:324
  (135 shorter events, 16.0 us)
Async XLA Ops:
  0.6 80.6 %collective-permute-start.10 = (bf16[512,5376]{1,0:T(8,128)(2,1)}, bf16[512,5376]{1,0:T(8,128)(2,1)}, u32[]{:S(2)}, u32[]{:S(2)}) collective-permute-start(bf16[512,5376]{1,0:T(8,128)(2,1)} %w_ref.1), channel_id=1, source_target_pairs={{0,1},{1,0},{2,3},{3,2},{4,5},{5,4},{6,7},{7,6},{8,9},{9,8},{10,11... | collective-permute-start | bytes 16515080 | tf_op jit(solution)/shard_map/ppermute | solution.py:34
  6.1 7.4 %collective-permute-start = (bf16[4,80,672]{2,1,0:T(8,128)(2,1)}, bf16[4,80,672]{2,1,0:T(8,128)(2,1)}, u32[]{:S(2)}, u32[]{:S(2)}) collective-permute-start(bf16[4,80,672]{2,1,0:T(8,128)(2,1)} %fusion.4), channel_id=1, source_target_pairs={{0,1},{1,0},{2,3},{3,2},{4,5},{5,4},{6,7},{7,6},{8,9},{9,8},{10,11... | collective-permute-start | bytes 1290248 | tf_op jit(solution)/shard_map/ppermute | solution.py:34
  7.0 39.1 %copy-start.1 = (bf16[336,2688]{1,0:T(8,128)(2,1)}, bf16[336,2688]{1,0:T(8,128)(2,1)S(1)}, u32[]{:S(2)}) copy-start(bf16[336,2688]{1,0:T(8,128)(2,1)S(1)} %pack.1.refs_0_) | copy-start | bytes 5419012
  7.0 40.0 %collective-permute-start.4 = (bf16[336,2688]{1,0:T(8,128)(2,1)S(1)}, bf16[336,2688]{1,0:T(8,128)(2,1)}, u32[]{:S(2)}, u32[]{:S(2)}) collective-permute-start(bf16[336,2688]{1,0:T(8,128)(2,1)S(1)} %pack.1.refs_0_), channel_id=1, source_target_pairs={{0,24},{1,97},{2,26},{3,99},{4,28},{5,101},{6,30},{7,103},{8,0},{9... | collective-permute-start | bytes 5419016 | tf_op jit(solution)/shard_map/ppermute | solution.py:90
  9.9 13.4 %collective-permute-start.5 = (bf16[512,512]{1,0:T(8,128)(2,1)S(1)}, bf16[512,512]{1,0:T(8,128)(2,1)S(1)}, u32[]{:S(2)}, u32[]{:S(2)}) collective-permute-start(bf16[512,512]{1,0:T(8,128)(2,1)S(1)} %pair.1.kv0_ref), channel_id=1, source_target_pairs={{0,8},{8,16},{16,24},{24,32},{32,40},{40,48},{48,56},{56,64},{64,7... | collective-permute-start | bytes 1572872 | tf_op jit(solution)/shard_map/ppermute | solution.py:39
  13.5 145.0 %copy-start.11 = (s32[4]{0:T(128)}, s32[4]{0:T(128)S(1)}, u32[]{:S(2)}) copy-start(s32[4]{0:T(128)S(1)} %pad_add_fusion.at_ref.refs_10_.refs_12_.refs_4_) | copy-start | bytes 52
  13.6 67.7 %slice-start = ((s8[5505024]{0:T(1024)(128)(4,1)}), s8[4194304]{0:T(1024)(128)(4,1)S(1)}, s32[]{:S(2)}) async-start(s8[5505024]{0:T(1024)(128)(4,1)} %bitcast.109), calls=%async_computation | async-start | bytes 8388608
  16.0 14.1 %collective-permute-start.1 = (bf16[2,80,672]{2,1,0:T(8,128)(2,1)S(1)}, bf16[2,80,672]{2,1,0:T(8,128)(2,1)S(1)}, u32[]{:S(2)}, u32[]{:S(2)}) collective-permute-start(bf16[2,80,672]{2,1,0:T(8,128)(2,1)S(1)} %get-tuple-element.98), channel_id=1, source_target_pairs={{0,6},{2,0},{4,2},{6,4},{1,7},{3,1},{5,3},{7,5},{8,14},{10,8},{12,... | collective-permute-start | bytes 645128 | tf_op jit(solution)/shard_map/ppermute | solution.py:34
  19.8 13.4 %collective-permute-start.2 = (bf16[2,80,672]{2,1,0:T(8,128)(2,1)S(1)}, bf16[2,80,672]{2,1,0:T(8,128)(2,1)S(1)}, u32[]{:S(2)}, u32[]{:S(2)}) collective-permute-start(bf16[2,80,672]{2,1,0:T(8,128)(2,1)S(1)} %get-tuple-element.97), channel_id=1, source_target_pairs={{0,4},{2,6},{4,0},{6,2},{1,5},{3,7},{5,1},{7,3},{8,12},{10,14},{12... | collective-permute-start | bytes 645128 | tf_op jit(solution)/shard_map/ppermute | solution.py:34
  23.4 10.7 %collective-permute-start.3 = (bf16[2,80,672]{2,1,0:T(8,128)(2,1)S(1)}, bf16[2,80,672]{2,1,0:T(8,128)(2,1)S(1)}, u32[]{:S(2)}, u32[]{:S(2)}) collective-permute-start(bf16[2,80,672]{2,1,0:T(8,128)(2,1)S(1)} %get-tuple-element.96), channel_id=1, source_target_pairs={{0,2},{2,4},{4,6},{6,0},{1,3},{3,5},{5,7},{7,1},{8,10},{10,12},{12... | collective-permute-start | bytes 645128 | tf_op jit(solution)/shard_map/ppermute | solution.py:34
  30.1 14.7 %collective-permute-start.6 = (bf16[512,512]{1,0:T(8,128)(2,1)S(1)}, bf16[512,512]{1,0:T(8,128)(2,1)S(1)}, u32[]{:S(2)}, u32[]{:S(2)}) collective-permute-start(bf16[512,512]{1,0:T(8,128)(2,1)S(1)} %collective-permute-done.5.kv1_ref), channel_id=1, source_target_pairs={{0,8},{8,16},{16,24},{24,32},{32,40},{40,48},{48,56},{56,64},{64,7... | collective-permute-start | bytes 1572872 | tf_op jit(solution)/shard_map/ppermute | solution.py:39
  33.2 45.3 %collective-permute-start.8 = (bf16[336,2688]{1,0:T(8,128)(2,1)S(1)}, bf16[336,2688]{1,0:T(8,128)(2,1)S(1)}, u32[]{:S(2)}, u32[]{:S(2)}) collective-permute-start(bf16[336,2688]{1,0:T(8,128)(2,1)S(1)} %pack.1.refs_0_), channel_id=1, source_target_pairs={{0,8},{1,33},{2,10},{3,35},{4,12},{5,37},{6,14},{7,39},{8,16},{9,4... | collective-permute-start | bytes 5419016 | tf_op jit(solution)/shard_map/ppermute | solution.py:90
  34.1 47.2 %slice-start.1 = ((s8[5505024]{0:T(1024)(128)(4,1)}), s8[1310720]{0:T(1024)(128)(4,1)S(1)}, s32[]{:S(2)}) async-start(s8[5505024]{0:T(1024)(128)(4,1)} %bitcast.109), calls=%async_computation.1 | async-start | bytes 2621440
  44.8 33.8 %collective-permute-start.9 = (bf16[336,2688]{1,0:T(8,128)(2,1)S(1)}, bf16[336,2688]{1,0:T(8,128)(2,1)S(1)}, u32[]{:S(2)}, u32[]{:S(2)}) collective-permute-start(bf16[336,2688]{1,0:T(8,128)(2,1)S(1)} %pack.1.refs_0_), channel_id=1, source_target_pairs={{0,96},{1,25},{2,98},{3,27},{4,100},{5,29},{6,102},{7,31},{8,104},... | collective-permute-start | bytes 5419016 | tf_op jit(solution)/shard_map/ppermute | solution.py:90
  46.1 42.6 %collective-permute-start.16 = (bf16[336,2688]{1,0:T(8,128)(2,1)S(1)}, bf16[336,2688]{1,0:T(8,128)(2,1)S(1)}, u32[]{:S(2)}, u32[]{:S(2)}) collective-permute-start(bf16[336,2688]{1,0:T(8,128)(2,1)S(1)} %pack.1.refs_0_), channel_id=1, source_target_pairs={{0,32},{1,9},{2,34},{3,11},{4,36},{5,13},{6,38},{7,15},{8,40},{9,1... | collective-permute-start | bytes 5419016 | tf_op jit(solution)/shard_map/ppermute | solution.py:90
  52.6 3.7 %collective-permute-start.7 = (bf16[256,512]{1,0:T(8,128)(2,1)S(1)}, bf16[256,512]{1,0:T(8,128)(2,1)S(1)}, u32[]{:S(2)}, u32[]{:S(2)}) collective-permute-start(bf16[256,512]{1,0:T(8,128)(2,1)S(1)} %bitcast.118), channel_id=1, source_target_pairs={{0,1},{1,0},{2,3},{3,2},{4,5},{5,4},{6,7},{7,6},{8,9},{9,8},{10,11... | collective-permute-start | bytes 786440 | tf_op jit(solution)/shard_map/ppermute | solution.py:34
  56.3 35.4 %collective-permute-start.15 = (bf16[336,2688]{1,0:T(8,128)(2,1)}, bf16[336,2688]{1,0:T(8,128)(2,1)}, u32[]{:S(2)}, u32[]{:S(2)}) collective-permute-start(bf16[336,2688]{1,0:T(8,128)(2,1)} %collective-permute-done.4.refs_2_), channel_id=1, source_target_pairs={{0,24},{1,97},{2,26},{3,99},{4,28},{5,101},{6,30},{7,103},{8,0},{9... | collective-permute-start | bytes 5419016 | tf_op jit(solution)/shard_map/ppermute | solution.py:90
  78.6 25.6 %collective-permute-start.11 = (bf16[336,2688]{1,0:T(8,128)(2,1)}, bf16[336,2688]{1,0:T(8,128)(2,1)S(1)}, u32[]{:S(2)}, u32[]{:S(2)}) collective-permute-start(bf16[336,2688]{1,0:T(8,128)(2,1)} %collective-permute-done.4.refs_2_), channel_id=1, source_target_pairs={{0,32},{1,9},{2,34},{3,11},{4,36},{5,13},{6,38},{7,15},{8,40},{9,1... | collective-permute-start | bytes 5419016 | tf_op jit(solution)/shard_map/ppermute | solution.py:90
  78.6 29.1 %collective-permute-start.12 = (bf16[336,2688]{1,0:T(8,128)(2,1)}, bf16[336,2688]{1,0:T(8,128)(2,1)S(1)}, u32[]{:S(2)}, u32[]{:S(2)}) collective-permute-start(bf16[336,2688]{1,0:T(8,128)(2,1)} %collective-permute-done.4.refs_2_), channel_id=1, source_target_pairs={{0,96},{1,25},{2,98},{3,27},{4,100},{5,29},{6,102},{7,31},{8,104},... | collective-permute-start | bytes 5419016 | tf_op jit(solution)/shard_map/ppermute | solution.py:90
  88.6 7.7 %collective-permute-start.13 = (bf16[32,5376]{1,0:T(8,128)(2,1)S(1)}, bf16[32,5376]{1,0:T(8,128)(2,1)S(1)}, u32[]{:S(2)}, u32[]{:S(2)}) collective-permute-start(bf16[32,5376]{1,0:T(8,128)(2,1)S(1)} %get-tuple-element.56), channel_id=1, source_target_pairs={{0,2},{2,4},{4,6},{6,0},{1,3},{3,5},{5,7},{7,1},{8,10},{10,12},{12... | collective-permute-start | bytes 1032200 | tf_op jit(solution)/shard_map/ppermute | solution.py:34
  88.7 64.7 %copy-start.15 = (bf16[336,2688]{1,0:T(8,128)(2,1)}, bf16[336,2688]{1,0:T(8,128)(2,1)S(1)}, u32[]{:S(2)}) copy-start(bf16[336,2688]{1,0:T(8,128)(2,1)S(1)} %collective-permute-done.16.refs_4_) | copy-start | bytes 5419012
  88.7 8.9 %collective-permute-start.14 = (bf16[32,5376]{1,0:T(8,128)(2,1)S(1)}, bf16[32,5376]{1,0:T(8,128)(2,1)S(1)}, u32[]{:S(2)}, u32[]{:S(2)}) collective-permute-start(bf16[32,5376]{1,0:T(8,128)(2,1)S(1)} %get-tuple-element.57), channel_id=1, source_target_pairs={{0,6},{2,0},{4,2},{6,4},{1,7},{3,1},{5,3},{7,5},{8,14},{10,8},{12,... | collective-permute-start | bytes 1032200 | tf_op jit(solution)/shard_map/ppermute | solution.py:34
  91.8 31.8 %collective-permute-start.23 = (bf16[336,2688]{1,0:T(8,128)(2,1)S(1)}, bf16[336,2688]{1,0:T(8,128)(2,1)}, u32[]{:S(2)}, u32[]{:S(2)}) collective-permute-start(bf16[336,2688]{1,0:T(8,128)(2,1)S(1)} %collective-permute-done.8.refs_1_), channel_id=1, source_target_pairs={{0,32},{1,9},{2,34},{3,11},{4,36},{5,13},{6,38},{7,15},{8,40},{9,1... | collective-permute-start | bytes 5419016 | tf_op jit(solution)/shard_map/ppermute | solution.py:90
  96.3 30.9 %collective-permute-start.24 = (bf16[336,2688]{1,0:T(8,128)(2,1)S(1)}, bf16[336,2688]{1,0:T(8,128)(2,1)S(1)}, u32[]{:S(2)}, u32[]{:S(2)}) collective-permute-start(bf16[336,2688]{1,0:T(8,128)(2,1)S(1)} %collective-permute-done.8.refs_1_), channel_id=1, source_target_pairs={{0,96},{1,25},{2,98},{3,27},{4,100},{5,29},{6,102},{7,31},{8,104},... | collective-permute-start | bytes 5419016 | tf_op jit(solution)/shard_map/ppermute | solution.py:90
  97.5 11.8 %collective-permute-start.18 = (bf16[32,5376]{1,0:T(8,128)(2,1)S(1)}, bf16[32,5376]{1,0:T(8,128)(2,1)S(1)}, u32[]{:S(2)}, u32[]{:S(2)}) collective-permute-start(bf16[32,5376]{1,0:T(8,128)(2,1)S(1)} %get-tuple-element.59), channel_id=1, source_target_pairs={{0,2},{2,4},{4,6},{6,0},{1,3},{3,5},{5,7},{7,1},{8,10},{10,12},{12... | collective-permute-start | bytes 1032200 | tf_op jit(solution)/shard_map/ppermute | solution.py:34
  104.2 8.7 %collective-permute-start.19 = (bf16[32,5376]{1,0:T(8,128)(2,1)S(1)}, bf16[32,5376]{1,0:T(8,128)(2,1)S(1)}, u32[]{:S(2)}, u32[]{:S(2)}) collective-permute-start(bf16[32,5376]{1,0:T(8,128)(2,1)S(1)} %get-tuple-element.60), channel_id=1, source_target_pairs={{0,6},{2,0},{4,2},{6,4},{1,7},{3,1},{5,3},{7,5},{8,14},{10,8},{12,... | collective-permute-start | bytes 1032200 | tf_op jit(solution)/shard_map/ppermute | solution.py:34
  107.7 45.6 %copy-start.17 = (bf16[336,2688]{1,0:T(8,128)(2,1)}, bf16[336,2688]{1,0:T(8,128)(2,1)S(1)}, u32[]{:S(2)}) copy-start(bf16[336,2688]{1,0:T(8,128)(2,1)S(1)} %collective-permute-done.12.refs_10_) | copy-start | bytes 5419012
  107.7 12.6 %collective-permute-start.20 = (bf16[32,5376]{1,0:T(8,128)(2,1)S(1)}, bf16[32,5376]{1,0:T(8,128)(2,1)S(1)}, u32[]{:S(2)}, u32[]{:S(2)}) collective-permute-start(bf16[32,5376]{1,0:T(8,128)(2,1)S(1)} %add_convert_fusion), channel_id=1, source_target_pairs={{0,6},{2,0},{4,2},{6,4},{1,7},{3,1},{5,3},{7,5},{8,14},{10,8},{12,... | collective-permute-start | bytes 1032200 | tf_op jit(solution)/shard_map/ppermute | solution.py:34
  109.3 11.0 %collective-permute-start.17 = (bf16[32,5376]{1,0:T(8,128)(2,1)S(1)}, bf16[32,5376]{1,0:T(8,128)(2,1)S(1)}, u32[]{:S(2)}, u32[]{:S(2)}) collective-permute-start(bf16[32,5376]{1,0:T(8,128)(2,1)S(1)} %add_convert_fusion.1), channel_id=1, source_target_pairs={{0,2},{2,4},{4,6},{6,0},{1,3},{3,5},{5,7},{7,1},{8,10},{10,12},{12... | collective-permute-start | bytes 1032200 | tf_op jit(solution)/shard_map/ppermute | solution.py:34
  112.9 45.7 %collective-permute-start.32 = (bf16[336,2688]{1,0:T(8,128)(2,1)}, bf16[336,2688]{1,0:T(8,128)(2,1)}, u32[]{:S(2)}, u32[]{:S(2)}) collective-permute-start(bf16[336,2688]{1,0:T(8,128)(2,1)} %collective-permute-done.15.refs_3_), channel_id=1, source_target_pairs={{0,32},{1,9},{2,34},{3,11},{4,36},{5,13},{6,38},{7,15},{8,40},{9,1... | collective-permute-start | bytes 5419016 | tf_op jit(solution)/shard_map/ppermute | solution.py:90
  120.3 38.3 %collective-permute-start.33 = (bf16[336,2688]{1,0:T(8,128)(2,1)}, bf16[336,2688]{1,0:T(8,128)(2,1)}, u32[]{:S(2)}, u32[]{:S(2)}) collective-permute-start(bf16[336,2688]{1,0:T(8,128)(2,1)} %collective-permute-done.15.refs_3_), channel_id=1, source_target_pairs={{0,96},{1,25},{2,98},{3,27},{4,100},{5,29},{6,102},{7,31},{8,104},... | collective-permute-start | bytes 5419016 | tf_op jit(solution)/shard_map/ppermute | solution.py:90
  121.4 14.9 %collective-permute-start.21 = (bf16[64,5376]{1,0:T(8,128)(2,1)S(1)}, bf16[64,5376]{1,0:T(8,128)(2,1)S(1)}, u32[]{:S(2)}, u32[]{:S(2)}) collective-permute-start(bf16[64,5376]{1,0:T(8,128)(2,1)S(1)} %get-tuple-element.70.refs_0_), channel_id=1, source_target_pairs={{0,2},{2,4},{4,6},{6,0},{1,3},{3,5},{5,7},{7,1},{8,10},{10,12},{12... | collective-permute-start | bytes 2064392 | tf_op jit(solution)/shard_map/ppermute | solution.py:34
  123.6 15.8 %collective-permute-start.22 = (bf16[64,5376]{1,0:T(8,128)(2,1)S(1)}, bf16[64,5376]{1,0:T(8,128)(2,1)S(1)}, u32[]{:S(2)}, u32[]{:S(2)}) collective-permute-start(bf16[64,5376]{1,0:T(8,128)(2,1)S(1)} %get-tuple-element.70.refs_0_), channel_id=1, source_target_pairs={{0,6},{2,0},{4,2},{6,4},{1,7},{3,1},{5,3},{7,5},{8,14},{10,8},{12,... | collective-permute-start | bytes 2064392 | tf_op jit(solution)/shard_map/ppermute | solution.py:34
  127.2 25.6 %collective-permute-start.27 = (bf16[64,5376]{1,0:T(8,128)(2,1)S(1)}, bf16[64,5376]{1,0:T(8,128)(2,1)S(1)}, u32[]{:S(2)}, u32[]{:S(2)}) collective-permute-start(bf16[64,5376]{1,0:T(8,128)(2,1)S(1)} %get-tuple-element.70.refs_0_), channel_id=1, source_target_pairs={{0,1},{1,0},{2,3},{3,2},{4,5},{5,4},{6,7},{7,6},{8,9},{9,8},{10,11... | collective-permute-start | bytes 2064392 | tf_op jit(solution)/shard_map/ppermute | solution.py:34
  139.5 8.7 %collective-permute-start.25 = (bf16[32,5376]{1,0:T(8,128)(2,1)S(1)}, bf16[32,5376]{1,0:T(8,128)(2,1)S(1)}, u32[]{:S(2)}, u32[]{:S(2)}) collective-permute-start(bf16[32,5376]{1,0:T(8,128)(2,1)S(1)} %slice.76), channel_id=1, source_target_pairs={{0,2},{2,4},{4,6},{6,0},{1,3},{3,5},{5,7},{7,1},{8,10},{10,12},{12... | collective-permute-start | bytes 1032200 | tf_op jit(solution)/shard_map/ppermute | solution.py:34
  139.6 13.2 %collective-permute-start.26 = (bf16[32,5376]{1,0:T(8,128)(2,1)S(1)}, bf16[32,5376]{1,0:T(8,128)(2,1)}, u32[]{:S(2)}, u32[]{:S(2)}) collective-permute-start(bf16[32,5376]{1,0:T(8,128)(2,1)S(1)} %slice.77), channel_id=1, source_target_pairs={{0,6},{2,0},{4,2},{6,4},{1,7},{3,1},{5,3},{7,5},{8,14},{10,8},{12,... | collective-permute-start | bytes 1032200 | tf_op jit(solution)/shard_map/ppermute | solution.py:34
  148.2 5.2 %collective-permute-start.30 = (bf16[32,5376]{1,0:T(8,128)(2,1)S(1)}, bf16[32,5376]{1,0:T(8,128)(2,1)S(1)}, u32[]{:S(2)}, u32[]{:S(2)}) collective-permute-start(bf16[32,5376]{1,0:T(8,128)(2,1)S(1)} %collective-permute-done.25.refs_3_), channel_id=1, source_target_pairs={{0,1},{1,0},{2,3},{3,2},{4,5},{5,4},{6,7},{7,6},{8,9},{9,8},{10,11... | collective-permute-start | bytes 1032200 | tf_op jit(solution)/shard_map/ppermute | solution.py:34
  152.8 4.7 %collective-permute-start.28 = (bf16[64,5376]{1,0:T(8,128)(2,1)S(1)}, bf16[64,5376]{1,0:T(8,128)(2,1)}, u32[]{:S(2)}, u32[]{:S(2)}) collective-permute-start(bf16[64,5376]{1,0:T(8,128)(2,1)S(1)} %collective-permute-done.21.refs_1_), channel_id=1, source_target_pairs={{0,1},{1,0},{2,3},{3,2},{4,5},{5,4},{6,7},{7,6},{8,9},{9,8},{10,11... | collective-permute-start | bytes 2064392 | tf_op jit(solution)/shard_map/ppermute | solution.py:34
  152.8 5.4 %collective-permute-start.29 = (bf16[64,5376]{1,0:T(8,128)(2,1)S(1)}, bf16[64,5376]{1,0:T(8,128)(2,1)}, u32[]{:S(2)}, u32[]{:S(2)}) collective-permute-start(bf16[64,5376]{1,0:T(8,128)(2,1)S(1)} %collective-permute-done.22.refs_2_), channel_id=1, source_target_pairs={{0,1},{1,0},{2,3},{3,2},{4,5},{5,4},{6,7},{7,6},{8,9},{9,8},{10,11... | collective-permute-start | bytes 2064392 | tf_op jit(solution)/shard_map/ppermute | solution.py:34
  154.1 2.7 %collective-permute-start.31 = (bf16[32,5376]{1,0:T(8,128)(2,1)}, bf16[32,5376]{1,0:T(8,128)(2,1)}, u32[]{:S(2)}, u32[]{:S(2)}) collective-permute-start(bf16[32,5376]{1,0:T(8,128)(2,1)} %collective-permute-done.26.refs_4_), channel_id=1, source_target_pairs={{0,1},{1,0},{2,3},{3,2},{4,5},{5,4},{6,7},{7,6},{8,9},{9,8},{10,11... | collective-permute-start | bytes 1032200 | tf_op jit(solution)/shard_map/ppermute | solution.py:34
  156.8 61.6 %collective-permute-start.40 = (bf16[336,2688]{1,0:T(8,128)(2,1)}, bf16[336,2688]{1,0:T(8,128)(2,1)}, u32[]{:S(2)}, u32[]{:S(2)}) collective-permute-start(bf16[336,2688]{1,0:T(8,128)(2,1)} %copy-done.17), channel_id=1, source_target_pairs={{0,96},{1,25},{2,98},{3,27},{4,100},{5,29},{6,102},{7,31},{8,104},... | collective-permute-start | bytes 5419016 | tf_op jit(solution)/shard_map/ppermute | solution.py:90
  157.5 61.0 %collective-permute-start.38 = (bf16[336,2688]{1,0:T(8,128)(2,1)}, bf16[336,2688]{1,0:T(8,128)(2,1)}, u32[]{:S(2)}, u32[]{:S(2)}) collective-permute-start(bf16[336,2688]{1,0:T(8,128)(2,1)} %copy-done.15), channel_id=1, source_target_pairs={{0,32},{1,9},{2,34},{3,11},{4,36},{5,13},{6,38},{7,15},{8,40},{9,1... | collective-permute-start | bytes 5419016 | tf_op jit(solution)/shard_map/ppermute | solution.py:90
  158.3 60.2 %collective-permute-start.39 = (bf16[336,2688]{1,0:T(8,128)(2,1)}, bf16[336,2688]{1,0:T(8,128)(2,1)}, u32[]{:S(2)}, u32[]{:S(2)}) collective-permute-start(bf16[336,2688]{1,0:T(8,128)(2,1)} %collective-permute-done.23.refs_5_), channel_id=1, source_target_pairs={{0,32},{1,9},{2,34},{3,11},{4,36},{5,13},{6,38},{7,15},{8,40},{9,1... | collective-permute-start | bytes 5419016 | tf_op jit(solution)/shard_map/ppermute | solution.py:90
  168.6 49.9 %collective-permute-start.41 = (bf16[336,2688]{1,0:T(8,128)(2,1)}, bf16[336,2688]{1,0:T(8,128)(2,1)}, u32[]{:S(2)}, u32[]{:S(2)}) collective-permute-start(bf16[336,2688]{1,0:T(8,128)(2,1)} %collective-permute-done.33.refs_11_), channel_id=1, source_target_pairs={{0,96},{1,25},{2,98},{3,27},{4,100},{5,29},{6,102},{7,31},{8,104},... | collective-permute-start | bytes 5419016 | tf_op jit(solution)/shard_map/ppermute | solution.py:90
  171.3 6.3 %collective-permute-start.34 = (bf16[2,64,672]{2,1,0:T(8,128)(2,1)S(1)}, bf16[2,64,672]{2,1,0:T(8,128)(2,1)S(1)}, u32[]{:S(2)}, u32[]{:S(2)}) collective-permute-start(bf16[2,64,672]{2,1,0:T(8,128)(2,1)S(1)} %get-tuple-element.101), channel_id=1, source_target_pairs={{0,6},{2,0},{4,2},{6,4},{1,7},{3,1},{5,3},{7,5},{8,14},{10,8},{12,... | collective-permute-start | bytes 516104 | tf_op jit(solution)/shard_map/ppermute | solution.py:34
  177.6 6.8 %collective-permute-start.35 = (bf16[2,64,672]{2,1,0:T(8,128)(2,1)S(1)}, bf16[2,64,672]{2,1,0:T(8,128)(2,1)S(1)}, u32[]{:S(2)}, u32[]{:S(2)}) collective-permute-start(bf16[2,64,672]{2,1,0:T(8,128)(2,1)S(1)} %get-tuple-element.100), channel_id=1, source_target_pairs={{0,4},{2,6},{4,0},{6,2},{1,5},{3,7},{5,1},{7,3},{8,12},{10,14},{12... | collective-permute-start | bytes 516104 | tf_op jit(solution)/shard_map/ppermute | solution.py:34
  184.4 6.2 %collective-permute-start.36 = (bf16[2,64,672]{2,1,0:T(8,128)(2,1)S(1)}, bf16[2,64,672]{2,1,0:T(8,128)(2,1)S(1)}, u32[]{:S(2)}, u32[]{:S(2)}) collective-permute-start(bf16[2,64,672]{2,1,0:T(8,128)(2,1)S(1)} %get-tuple-element.99), channel_id=1, source_target_pairs={{0,2},{2,4},{4,6},{6,0},{1,3},{3,5},{5,7},{7,1},{8,10},{10,12},{12... | collective-permute-start | bytes 516104 | tf_op jit(solution)/shard_map/ppermute | solution.py:34
  190.7 26.4 %collective-permute-start.37 = (bf16[4,64,672]{2,1,0:T(8,128)(2,1)S(1)}, bf16[4,64,672]{2,1,0:T(8,128)(2,1)S(1)}, u32[]{:S(2)}, u32[]{:S(2)}) collective-permute-start(bf16[4,64,672]{2,1,0:T(8,128)(2,1)S(1)} %select_bitcast_fusion.2), channel_id=1, source_target_pairs={{0,1},{1,0},{2,3},{3,2},{4,5},{5,4},{6,7},{7,6},{8,9},{9,8},{10,11... | collective-permute-start | bytes 1032200 | tf_op jit(solution)/shard_map/ppermute | solution.py:34
  (16 other events, 105.3 us)

commit v4 on v3

--- a/solution.py
+++ b/solution.py
@@ -303,7 +303,7 @@
         out_specs=pl.BlockSpec((TOK, 384), lambda j: (0, j)),
         scratch_shapes=[pltpu.VMEM((2, 3 * 1344, 384), BF), pltpu.SemaphoreType.DMA((2, len(parts)))],
         compiler_params=params(56),
-        cost_estimate=cost(2 * TOK * 4032 * 2688, 2 * 4032 * 2688 + 4 * TOK * 2688),
+        cost_estimate=cost(0, 1000),
         name="near",
     )(*blocks, where, rows)
 
@@ -313,22 +313,48 @@
     parts = [(k, 0, REL[k]) for k in range(4)]
 
     def body(*refs):
-        place, n_ref, s_ref, o_ref, w_ref, sems = refs[m:]
-        slot = fetch_block(parts, place, refs[:m], w_ref, sems)
-        acc = s_ref[...] + jnp.dot(n_ref[:, :1344], w_ref[slot], preferred_element_type=F32)
+        place, n_ref, s_ref, o_ref, w_ref, acc_ref, sems = refs[m:]
+        j = pl.program_id(0)
+        slot = lax.rem(j, 2)
+
+        @pl.when(j == 0)
+        def _():
+            for copy in weight_copies(parts, place, refs[:m], 0, w_ref.at[0], sems.at[0]):
+                copy.start()
+
+        @pl.when(j + 1 < 7)
+        def _():
+            for copy in weight_copies(parts, place, refs[:m], j + 1, w_ref.at[1 - slot], sems.at[1 - slot]):
+                copy.start()
+
+        @pl.when(j < 7)
+        def _():
+            for copy in weight_copies(parts, place, refs[:m], j, w_ref.at[slot], sems.at[slot]):
+                copy.wait()
+
+        acc = acc_ref[1 - slot]
         last = acc[:, 256:]
         g = jnp.concatenate([acc[:, :128], last], axis=1)
         u = jnp.concatenate([acc[:, 128:256], pltpu.roll(last, 64, 1)], axis=1)
         o_ref[...] = (gelu(g) * u).T[:192].astype(BF)
+        acc_ref[slot] = s_ref[...] + jnp.dot(n_ref[:, :1344], w_ref[slot], preferred_element_type=F32)
 
     return pl.pallas_call(
         body,
         out_shape=jax.ShapeDtypeStruct((1344, TOK), BF),
-        grid=(7,),
+        grid=(8,),
         in_specs=[HB] * m
-        + [SM, pl.BlockSpec((TOK, GROUP), lambda j: (0, 3)), pl.BlockSpec((TOK, 384), lambda j: (0, j))],
-        out_specs=pl.BlockSpec((192, TOK), lambda j: (j, 0)),
-        scratch_shapes=[pltpu.VMEM((2, 1344, 384), BF), pltpu.SemaphoreType.DMA((2, len(parts)))],
+        + [
+            SM,
+            pl.BlockSpec((TOK, GROUP), lambda j: (0, 3)),
+            pl.BlockSpec((TOK, 384), lambda j: (0, jnp.minimum(j, 6))),
+        ],
+        out_specs=pl.BlockSpec((192, TOK), lambda j: (jnp.maximum(j - 1, 0), 0)),
+        scratch_shapes=[
+            pltpu.VMEM((2, 1344, 384), BF),
+            pltpu.VMEM((2, TOK, 384), F32),
+            pltpu.SemaphoreType.DMA((2, len(parts))),
+        ],
         compiler_params=params(56),
         cost_estimate=cost(2 * TOK * 1344 * 2688, 2 * 1344 * 2688 + 4 * TOK * 2688),
         name="far",
@@ -339,25 +365,18 @@
     return lax.dynamic_slice_in_dim(jnp.concatenate([value, value], axis=0), by % 4, 4, 0)
 
 
-def to_tokens(blocks, z, c):
+def swap(blocks, z, c):
     blocks = blocks.reshape(4, 2, *blocks.shape[1:])
     keep = jnp.where(c == 0, blocks[:, 0], blocks[:, 1])
     give = jnp.where(c == 0, blocks[:, 1], blocks[:, 0])
     take = shift(give, "c", 1)
     both = turn(jnp.stack([jnp.where(c == 0, keep, take), jnp.where(c == 0, take, keep)], axis=1), z)
-    got = jnp.stack([both[0], shift(both[3], "z", 3), shift(both[2], "z", 2), shift(both[1], "z", 1)])
+    return [both[0], shift(both[3], "z", 3), shift(both[2], "z", 2), shift(both[1], "z", 1)]
+
+
+def gather(got, z):
+    got = jnp.stack(got)
     return turn(got, 4 - z).reshape(8, *got.shape[2:])
-
-
-def to_features(blocks, z, c):
-    both = turn(blocks.reshape(4, 2, *blocks.shape[1:]), z)
-    got = jnp.stack([both[0], shift(both[3], "z", 3), shift(both[2], "z", 2), shift(both[1], "z", 1)])
-    got = turn(got, 4 - z)
-    keep = jnp.where(c == 0, got[:, 0], got[:, 1])
-    give = jnp.where(c == 0, got[:, 1], got[:, 0])
-    take = shift(give, "c", 1)
-    both = jnp.stack([jnp.where(c == 0, keep, take), jnp.where(c == 0, take, keep)], axis=1)
-    return both.reshape(8, *got.shape[2:])
 
 
 def per_device(queries, keys, values, doc_ids, out_weight, residual, post_gain, pre_gain, gate_weight, up_weight):
@@ -366,9 +385,10 @@
 
     kv0 = pair(keys, values)
     kv1 = behind(kv0)
+    gate_weight, kv0 = lax.optimization_barrier((gate_weight, kv0))
     w = pack(gate_weight, up_weight)
     p = ring(w, -1, 0)
-    kv1, w_late = lax.optimization_barrier((kv1, w))
+    kv1, w_late, residual, post_gain = lax.optimization_barrier((kv1, w, residual, post_gain))
     kv2 = behind(kv1)
     m = ring(w_late, 1, 0)
     b = ring(p, -1, 0)
@@ -381,7 +401,7 @@
     extra = jnp.stack([high[0], low[0], high[1], low[1]])
     extra = jnp.concatenate([extra, jnp.zeros((12, 672), BF)], axis=0)
     sent = jnp.concatenate([residual.reshape(8, PER, 672), jnp.broadcast_to(extra[None], (8, 16, 672))], axis=1)
-    mine = to_tokens(sent, z, c)
+    mine = gather(swap(sent, z, c), z)
 
     start = (4 * y + x) * TOK
     padded = jnp.concatenate([jnp.full((2 * TOK,), -1, jnp.int32), doc_ids])
@@ -392,38 +412,37 @@
     mix = attend(where, queries, kv2, kv1, kv0, qid, kid)
     other_weight = shift(out_weight, "c", 1)
     own, other = mix[0].reshape(256, 512), shift(mix[1].reshape(256, 512), "c", 1)
-    other, m, following[0] = lax.optimization_barrier((other, m, following[0]))
-    prev += [ring(v, 1, 1) for v in (m, p)]
-    following += [ring(v, -1, 1) for v in (m, p)]
     p0, p1t, p1b, p2t, p2b, p3t, p3b = project(own, other, out_weight, other_weight)
 
     up_t = shift(p2t, "z", 1)
     dn_b = shift(p2b, "z", -1)
     a_b = shift(p1b, "z", 1)
     b_t = shift(p3t, "z", -1)
-    up_t, dn_b, b, prev[0] = lax.optimization_barrier((up_t, dn_b, b, prev[0]))
-    prev += [ring(b, 1, 1)]
-    following += [ring(b, -1, 1)]
+    up_t, dn_b, m, following[0] = lax.optimization_barrier((up_t, dn_b, m, following[0]))
     add = lambda p, q: (p.astype(F32) + q.astype(F32)).astype(BF)
     a_t = shift(add(p1t, up_t), "z", 1)
     b_b = shift(add(p3b, dn_b), "z", -1)
-    p0, prev[2], following[2] = lax.optimization_barrier((p0, prev[2], following[2]))
+    p0, b, prev[0] = lax.optimization_barrier((p0, b, prev[0]))
+    prev += [ring(v, 1, 1) for v in (m, p, b)]
+    following += [ring(v, -1, 1) for v in (m, p, b)]
     new, nrm = norm(p0, a_t, a_b, b_t, b_b, mine)
 
     n_m, n_p = shift(nrm, "z", 1), shift(nrm, "z", -1)
-    n_m, n_p, prev[1], following[1] = lax.optimization_barrier((n_m, n_p, prev[1], following[1]))
+    n_m, n_p, prev[2], following[2] = lax.optimization_barrier((n_m, n_p, prev[2], following[2]))
     pieces = [nrm, n_m, n_p, shift(n_m[:32], "z", 1), shift(n_p[32:], "z", -1)]
     places = [(0, None), (3, None), (1, None), (2, 0), (2, 1)]
     pieces += [shift(piece, "c", 1) for piece in pieces]
     tokens_at = [(dz, dc, part) for dc in range(2) for dz, part in places]
-    pieces, prev[3], following[3] = lax.optimization_barrier((pieces, prev[3], following[3]))
+    pieces, prev[1], following[1] = lax.optimization_barrier((pieces, prev[1], following[1]))
     rows = order(pieces, tokens_at, where)
 
     last = [ring(prev[0], 1, 1), ring(prev[1], 1, 1), ring(following[2], -1, 1), ring(following[3], -1, 1)]
     new, rows = lax.optimization_barrier((new, rows))
-    new_residual = to_features(new, z, c).reshape(TOK, 672)
+    sent_back = swap(new, z, c)
     sums = near(rows, where, [w, m, p, b, *prev, *following])
     act = far(rows, where, last, sums)
+    sent_back, act = lax.optimization_barrier((sent_back, act))
+    new_residual = gather(sent_back, z).reshape(TOK, 672)
     return new_residual, act.T
 
 

time: 232 us -> 241 us (1.039)
  waiting for transfers between devices: 97.3 us -> 101 us
  local copies, waits for them, and re-layouts: 11.1 us -> 14.3 us
    ppermute x15, waiting for transfers between devices: 28.4 us -> 47 us  [ring(): return lax.ppermute(value, ('y', 'x', 'z', 'c'), pairs)]
    ppermute x25, waiting for transfers between devices: 55 us -> 40.8 us  [shift(): return lax.ppermute(value, axis, [(i, (i + by) % n) for i in range(n)])]
    ppermute x15, starting transfers between devices: 16.2 us -> 22.9 us  [ring(): return lax.ppermute(value, ('y', 'x', 'z', 'c'), pairs)]
    ppermute x25, starting transfers between devices: 38.8 us -> 33.9 us  [shift(): return lax.ppermute(value, axis, [(i, (i + by) % n) for i in range(n)])]
    unnamed x60 -> x57, local copies, waits for them, and re-layouts: 8.9 us -> 11.6 us
  transfers between devices with their start and end apart: 42 -> 42, of which waited for: 19 -> 14; matrix products, arithmetic and copies ran while one was open for 4% -> 3% of each run, Pallas kernels for 19% -> 24%
where the time goes in v4:
time: 241 us; the launch traced here: 240 us
  waiting for transfers between devices  101 us (42%)
  starting transfers between devices  61.4 us (25%)
  Pallas kernels  56.8 us (24%)
  local copies, waits for them, and re-layouts  14.3 us (6%)
  other arithmetic  5.22 us (2%)
    ppermute x15, waiting for transfers between devices, ring(): return lax.ppermute(value, ('y', 'x', 'z', 'c'), pairs)  47 us
    ppermute x25, waiting for transfers between devices, shift(): return lax.ppermute(value, axis, [(i, (i + by) % n) for i in range(n)])  40.8 us
    ppermute x25, starting transfers between devices, shift(): return lax.ppermute(value, axis, [(i, (i + by) % n) for i in range(n)])  33.9 us
    pallas_call x1, Pallas kernels, near(): pl.pallas_call(body, out_shape=jax.ShapeDtypeStruct((TOK, 2688), F32), gr...  23.8 us
    ppermute x15, starting transfers between devices, ring(): return lax.ppermute(value, ('y', 'x', 'z', 'c'), pairs)  22.9 us
    pallas_call x1, Pallas kernels, far(): pl.pallas_call(body, out_shape=jax.ShapeDtypeStruct((1344, TOK), BF), gri...  13.5 us
    ppermute x2, waiting for transfers between devices, behind(): return lax.ppermute(value, ('y', 'x'), [(i, i + 1) for i in range(n - 1)])  13.1 us
    unnamed x57, local copies, waits for them, and re-layouts  11.6 us
  transfers between devices with their start and end apart: 42, of which 14 were waited for; matrix products, arithmetic and copies ran while one was open for 3% of the time, Pallas kernels for 24%

profile of v4, /device:TPU:1, one launch (start us, length us, event | category | flops | bytes accessed | tf_op | source)
XLA Modules:
  0.0 239.9 jit_solution(1065326644965466497)
XLA Ops:
  0.6 1.5 collective-permute-start.8
  4.1 3.2 %collective-permute-start = (bf16[512,512]{1,0:T(8,128)(2,1)S(1)}, bf16[512,512]{1,0:T(8,128)(2,1)S(1)}, u32[]{:S(2)}, u32[]{:S(2)}) collective-permute-start(bf16[512,512]{1,0:T(8,128)(2,1)S(1)} %pair.1.kv0_ref), channel_id=1, source_target_pairs={{0,8},{8,16},{16,24},{24,32},{32,40},{40,48},{48,56},{56,64},{64,7... | collective-permute-start | bytes 1572872 | tf_op jit(solution)/shard_map/ppermute | solution.py:39
  8.1 1.2 copy-done.2
  9.3 1.2 copy-done.3
  10.9 7.8 %collective-permute-done.kv1_ref = bf16[512,512]{1,0:T(8,128)(2,1)S(1)} collective-permute-done((bf16[512,512]{1,0:T(8,128)(2,1)S(1)}, bf16[512,512]{1,0:T(8,128)(2,1)S(1)}, u32[]{:S(2)}, u32[]{:S(2)}) %collective-permute-start) | collective-permute-done | bytes 524320 | tf_op jit(solution)/shard_map/ppermute | solution.py:39
  18.7 1.2 copy.22
  20.1 2.0 fusion.6
  22.9 5.8 %collective-permute-start.5 = (bf16[336,2688]{1,0:T(8,128)(2,1)S(1)}, bf16[336,2688]{1,0:T(8,128)(2,1)}, u32[]{:S(2)}, u32[]{:S(2)}) collective-permute-start(bf16[336,2688]{1,0:T(8,128)(2,1)S(1)} %pack.1.refs_0_), channel_id=1, source_target_pairs={{0,24},{1,97},{2,26},{3,99},{4,28},{5,101},{6,30},{7,103},{8,0},{9... | collective-permute-start | bytes 5419016 | tf_op jit(solution)/shard_map/ppermute | solution.py:90
  29.2 1.3 collective-permute-start.6
  30.6 1.8 select_bitcast_fusion
  33.0 3.8 %collective-permute-start.2 = (bf16[2,80,672]{2,1,0:T(8,128)(2,1)S(1)}, bf16[2,80,672]{2,1,0:T(8,128)(2,1)S(1)}, u32[]{:S(2)}, u32[]{:S(2)}) collective-permute-start(bf16[2,80,672]{2,1,0:T(8,128)(2,1)S(1)} %get-tuple-element.110), channel_id=1, source_target_pairs={{0,6},{2,0},{4,2},{6,4},{1,7},{3,1},{5,3},{7,5},{8,14},{10,8},{12,... | collective-permute-start | bytes 645128 | tf_op jit(solution)/shard_map/ppermute | solution.py:34
  36.9 5.4 %collective-permute-done.6.kv2_ref = bf16[512,512]{1,0:T(8,128)(2,1)S(1)} collective-permute-done((bf16[512,512]{1,0:T(8,128)(2,1)S(1)}, bf16[512,512]{1,0:T(8,128)(2,1)S(1)}, u32[]{:S(2)}, u32[]{:S(2)}) %collective-permute-start.6) | collective-permute-done | bytes 524320 | tf_op jit(solution)/shard_map/ppermute | solution.py:39
  42.2 3.6 %collective-permute-start.3 = (bf16[2,80,672]{2,1,0:T(8,128)(2,1)S(1)}, bf16[2,80,672]{2,1,0:T(8,128)(2,1)S(1)}, u32[]{:S(2)}, u32[]{:S(2)}) collective-permute-start(bf16[2,80,672]{2,1,0:T(8,128)(2,1)S(1)} %get-tuple-element.109), channel_id=1, source_target_pairs={{0,4},{2,6},{4,0},{6,2},{1,5},{3,7},{5,1},{7,3},{8,12},{10,14},{12... | collective-permute-start | bytes 645128 | tf_op jit(solution)/shard_map/ppermute | solution.py:34
  46.6 4.6 %collective-permute-done.3 = bf16[2,80,672]{2,1,0:T(8,128)(2,1)S(1)} collective-permute-done((bf16[2,80,672]{2,1,0:T(8,128)(2,1)S(1)}, bf16[2,80,672]{2,1,0:T(8,128)(2,1)S(1)}, u32[]{:S(2)}, u32[]{:S(2)}) %collective-permute-start.3) | collective-permute-done | bytes 215072 | tf_op jit(solution)/shard_map/ppermute | solution.py:34
  51.2 4.2 %collective-permute-start.14 = (bf16[336,2688]{1,0:T(8,128)(2,1)S(1)}, bf16[336,2688]{1,0:T(8,128)(2,1)S(1)}, u32[]{:S(2)}, u32[]{:S(2)}) collective-permute-start(bf16[336,2688]{1,0:T(8,128)(2,1)S(1)} %pack.1.refs_0_), channel_id=1, source_target_pairs={{0,96},{1,25},{2,98},{3,27},{4,100},{5,29},{6,102},{7,31},{8,104},... | collective-permute-start | bytes 5419016 | tf_op jit(solution)/shard_map/ppermute | solution.py:90
  56.6 5.6 %attend.1 = bf16[2,4,64,512]{3,2,1,0:T(8,128)(2,1)S(1)} custom-call(s32[4]{0:T(128)S(1)} %pad_add_fusion.at_ref.refs_10_.refs_12_.refs_4_, bf16[512,512]{1,0:T(8,128)(2,1)S(1)} %copy-done.4, bf16[512,512]{1,0:T(8,128)(2,1)S(1)} %collective-permute-done.6.kv2_ref, bf16[512,512]{1,0:T(8,128)(2,1)S(1)} %collective-permute-done.kv1_ref, ...), custom_call_target="tpu_custom_call" | custom-call | bytes 1000 | tf_op jit(solution)/shard_map/attend/pallas_call | solution.py:123
  62.2 3.8 %collective-permute-start.7 = (bf16[256,512]{1,0:T(8,128)(2,1)S(1)}, bf16[256,512]{1,0:T(8,128)(2,1)S(1)}, u32[]{:S(2)}, u32[]{:S(2)}) collective-permute-start(bf16[256,512]{1,0:T(8,128)(2,1)S(1)} %bitcast.134), channel_id=1, source_target_pairs={{0,1},{1,0},{2,3},{3,2},{4,5},{5,4},{6,7},{7,6},{8,9},{9,8},{10,11... | collective-permute-start | bytes 786440 | tf_op jit(solution)/shard_map/ppermute | solution.py:34
  66.0 1.2 collective-permute-done.7.s
  67.2 7.3 %project.1 = (bf16[64,5376]{1,0:T(8,128)(2,1)S(1)}, bf16[32,5376]{1,0:T(8,128)(2,1)S(1)}, bf16[32,5376]{1,0:T(8,128)(2,1)S(1)}, bf16[32,5376]{1,0:T(8,128)(2,1)S...) custom-call(bf16[256,512]{1,0:T(8,128)(2,1)S(1)} %bitcast.129, ...), custom_call_target="tpu_custom_call" | custom-call | bytes 1000 | tf_op jit(solution)/shard_map/project/pallas_call | solution.py:147
  74.8 2.7 %collective-permute-start.12 = (bf16[32,5376]{1,0:T(8,128)(2,1)S(1)}, bf16[32,5376]{1,0:T(8,128)(2,1)S(1)}, u32[]{:S(2)}, u32[]{:S(2)}) collective-permute-start(bf16[32,5376]{1,0:T(8,128)(2,1)S(1)} %get-tuple-element.65), channel_id=1, source_target_pairs={{0,6},{2,0},{4,2},{6,4},{1,7},{3,1},{5,3},{7,5},{8,14},{10,8},{12,... | collective-permute-start | bytes 1032200 | tf_op jit(solution)/shard_map/ppermute | solution.py:34
  77.4 2.7 %collective-permute-start.22 = (bf16[336,2688]{1,0:T(8,128)(2,1)}, bf16[336,2688]{1,0:T(8,128)(2,1)}, u32[]{:S(2)}, u32[]{:S(2)}) collective-permute-start(bf16[336,2688]{1,0:T(8,128)(2,1)} %collective-permute-done.5.refs_2_), channel_id=1, source_target_pairs={{0,96},{1,25},{2,98},{3,27},{4,100},{5,29},{6,102},{7,31},{8,104},... | collective-permute-start | bytes 5419016 | tf_op jit(solution)/shard_map/ppermute | solution.py:90
  80.1 5.1 %collective-permute-done.11 = bf16[32,5376]{1,0:T(8,128)(2,1)S(1)} collective-permute-done((bf16[32,5376]{1,0:T(8,128)(2,1)S(1)}, bf16[32,5376]{1,0:T(8,128)(2,1)S(1)}, u32[]{:S(2)}, u32[]{:S(2)}) %collective-permute-start.11) | collective-permute-done | bytes 344096 | tf_op jit(solution)/shard_map/ppermute | solution.py:34
  85.2 3.8 %collective-permute-start.9 = (bf16[336,2688]{1,0:T(8,128)(2,1)}, bf16[336,2688]{1,0:T(8,128)(2,1)S(1)}, u32[]{:S(2)}, u32[]{:S(2)}) collective-permute-start(bf16[336,2688]{1,0:T(8,128)(2,1)} %collective-permute-done.5.refs_2_), channel_id=1, source_target_pairs={{0,24},{1,97},{2,26},{3,99},{4,28},{5,101},{6,30},{7,103},{8,0},{9... | collective-permute-start | bytes 5419016 | tf_op jit(solution)/shard_map/ppermute | solution.py:90
  89.4 2.4 %collective-permute-start.17 = (bf16[32,5376]{1,0:T(8,128)(2,1)S(1)}, bf16[32,5376]{1,0:T(8,128)(2,1)S(1)}, u32[]{:S(2)}, u32[]{:S(2)}) collective-permute-start(bf16[32,5376]{1,0:T(8,128)(2,1)S(1)} %get-tuple-element.68), channel_id=1, source_target_pairs={{0,6},{2,0},{4,2},{6,4},{1,7},{3,1},{5,3},{7,5},{8,14},{10,8},{12,... | collective-permute-start | bytes 1032200 | tf_op jit(solution)/shard_map/ppermute | solution.py:34
  91.9 31.0 %collective-permute-done.9.refs_3_ = bf16[336,2688]{1,0:T(8,128)(2,1)S(1)} collective-permute-done((bf16[336,2688]{1,0:T(8,128)(2,1)}, bf16[336,2688]{1,0:T(8,128)(2,1)S(1)}, u32[]{:S(2)}, u32[]{:S(2)}) %collective-permute-start.9) | collective-permute-done | bytes 1806368 | tf_op jit(solution)/shard_map/ppermute | solution.py:90
  122.9 1.9 collective-permute-start.18
  124.9 5.8 %collective-permute-done.18.bb_ref = bf16[32,5376]{1,0:T(8,128)(2,1)S(1)} collective-permute-done((bf16[32,5376]{1,0:T(8,128)(2,1)S(1)}, bf16[32,5376]{1,0:T(8,128)(2,1)S(1)}, u32[]{:S(2)}, u32[]{:S(2)}) %collective-permute-start.18) | collective-permute-done | bytes 344096 | tf_op jit(solution)/shard_map/ppermute | solution.py:34
  130.7 2.1 collective-permute-done.15.at_ref
  133.9 2.7 %collective-permute-start.20 = (bf16[64,5376]{1,0:T(8,128)(2,1)S(1)}, bf16[64,5376]{1,0:T(8,128)(2,1)S(1)}, u32[]{:S(2)}, u32[]{:S(2)}) collective-permute-start(bf16[64,5376]{1,0:T(8,128)(2,1)S(1)} %get-tuple-element.78.refs_0_), channel_id=1, source_target_pairs={{0,6},{2,0},{4,2},{6,4},{1,7},{3,1},{5,3},{7,5},{8,14},{10,8},{12,... | collective-permute-start | bytes 2064392 | tf_op jit(solution)/shard_map/ppermute | solution.py:34
  137.7 13.0 %collective-permute-done.19.refs_1_ = bf16[64,5376]{1,0:T(8,128)(2,1)S(1)} collective-permute-done((bf16[64,5376]{1,0:T(8,128)(2,1)S(1)}, bf16[64,5376]{1,0:T(8,128)(2,1)S(1)}, u32[]{:S(2)}, u32[]{:S(2)}) %collective-permute-start.19) | collective-permute-done | bytes 688160 | tf_op jit(solution)/shard_map/ppermute | solution.py:34
  150.9 3.0 %collective-permute-start.24 = (bf16[32,5376]{1,0:T(8,128)(2,1)S(1)}, bf16[32,5376]{1,0:T(8,128)(2,1)S(1)}, u32[]{:S(2)}, u32[]{:S(2)}) collective-permute-start(bf16[32,5376]{1,0:T(8,128)(2,1)S(1)} %slice.77), channel_id=1, source_target_pairs={{0,6},{2,0},{4,2},{6,4},{1,7},{3,1},{5,3},{7,5},{8,14},{10,8},{12,... | collective-permute-start | bytes 1032200 | tf_op jit(solution)/shard_map/ppermute | solution.py:34
  153.9 7.4 %collective-permute-done.23.refs_3_ = bf16[32,5376]{1,0:T(8,128)(2,1)S(1)} collective-permute-done((bf16[32,5376]{1,0:T(8,128)(2,1)S(1)}, bf16[32,5376]{1,0:T(8,128)(2,1)S(1)}, u32[]{:S(2)}, u32[]{:S(2)}) %collective-permute-start.23) | collective-permute-done | bytes 344096 | tf_op jit(solution)/shard_map/ppermute | solution.py:34
  161.3 1.5 collective-permute-start.28
  162.8 2.0 collective-permute-start.41
  165.4 1.6 collective-permute-done.26.refs_6_
  167.0 1.2 collective-permute-start.36
  168.2 1.5 collective-permute-start.38
  169.9 2.9 %collective-permute-done.31.refs_9_ = bf16[336,2688]{1,0:T(8,128)(2,1)S(1)} collective-permute-done((bf16[336,2688]{1,0:T(8,128)(2,1)S(1)}, bf16[336,2688]{1,0:T(8,128)(2,1)S(1)}, u32[]{:S(2)}, u32[]{:S(2)}) %collective-permute-start.31) | collective-permute-done | bytes 1806368 | tf_op jit(solution)/shard_map/ppermute | solution.py:90
  172.8 1.2 copy-done.14
  174.3 5.1 %order.1.refs_13_.refs_5_ = bf16[512,5632]{1,0:T(8,128)(2,1)S(1)} custom-call(bf16[64,5376]{1,0:T(8,128)(2,1)S(1)} %get-tuple-element.78.refs_0_, bf16[64,5376]{1,0:T(8,128)(2,1)S(1)} %collective-permute-done.19.refs_1_, bf16[64,5376]{1,0:T(8,128)(2,1)S(1)} %collective-permute-done.20.refs_2_, bf16[32,5376]{1,0:T(8,128)(2,1)S(1)} %collective-permute-done.23.refs_3_, ...), custom_call_target="tpu_custom_call" | custom-call | bytes 1000 | tf_op jit(solution)/shard_map/order/pallas_call | solution.py:241
  179.4 2.5 %copy-done = bf16[512,5632]{1,0:T(8,128)(2,1)} copy-done((bf16[512,5632]{1,0:T(8,128)(2,1)}, bf16[512,5632]{1,0:T(8,128)(2,1)S(1)}, u32[]{:S(2)}) %copy-start) | copy-done | bytes 5767192
  181.9 4.3 %collective-permute-done.41.refs_7_ = bf16[336,2688]{1,0:T(8,128)(2,1)S(1)} collective-permute-done((bf16[336,2688]{1,0:T(8,128)(2,1)S(1)}, bf16[336,2688]{1,0:T(8,128)(2,1)S(1)}, u32[]{:S(2)}, u32[]{:S(2)}) %collective-permute-start.41) | collective-permute-done | bytes 1806368 | tf_op jit(solution)/shard_map/ppermute | solution.py:90
  186.2 1.2 copy-done.15
  187.4 1.3 collective-permute-start.32
  188.7 23.8 %near.1.refs_6_ = f32[512,2688]{1,0:T(8,128)} custom-call(bf16[336,2688]{1,0:T(8,128)(2,1)} %copy-done.1, bf16[336,2688]{1,0:T(8,128)(2,1)} %copy-done.11, bf16[336,2688]{1,0:T(8,128)(2,1)} %collective-permute-done.5.refs_2_, bf16[336,2688]{1,0:T(8,128)(2,1)} %copy-done.13, bf16[336,2688]{1,0:T(8,128)(2,1)} %collective-permute-done.10.refs_4_, ...), custom_call_target="tpu_custom_call" | custom-call | bytes 1000 | tf_op jit(solution)/shard_map/near/pallas_call | solution.py:298
  213.0 2.4 %collective-permute-start.33 = (bf16[2,64,672]{2,1,0:T(8,128)(2,1)S(1)}, bf16[2,64,672]{2,1,0:T(8,128)(2,1)S(1)}, u32[]{:S(2)}, u32[]{:S(2)}) collective-permute-start(bf16[2,64,672]{2,1,0:T(8,128)(2,1)S(1)} %get-tuple-element.113), channel_id=1, source_target_pairs={{0,6},{2,0},{4,2},{6,4},{1,7},{3,1},{5,3},{7,5},{8,14},{10,8},{12,... | collective-permute-start | bytes 516104 | tf_op jit(solution)/shard_map/ppermute | solution.py:34
  216.2 8.8 %collective-permute-done.37.refs_1_ = bf16[336,2688]{1,0:T(8,128)(2,1)} collective-permute-done((bf16[336,2688]{1,0:T(8,128)(2,1)}, bf16[336,2688]{1,0:T(8,128)(2,1)}, u32[]{:S(2)}, u32[]{:S(2)}) %collective-permute-start.37) | collective-permute-done | bytes 1806368 | tf_op jit(solution)/shard_map/ppermute | solution.py:90
  225.0 13.5 %far.1 = bf16[1344,512]{1,0:T(8,128)(2,1)} custom-call(bf16[336,2688]{1,0:T(8,128)(2,1)} %copy-done.8, bf16[336,2688]{1,0:T(8,128)(2,1)} %collective-permute-done.37.refs_1_, bf16[336,2688]{1,0:T(8,128)(2,1)} %copy-done.9, bf16[336,2688]{1,0:T(8,128)(2,1)} %copy-done.10, s32[4]{0:T(128)} %copy-done.7, bf16[512,5632]{1,0:T(8,128)(2,1)} %copy-done, ...), custom_call_target="tpu_custom_call" | custom-call | flops 3699376128 | bytes 12730368 | tf_op jit(solution)/shard_map/far/pallas_call | solution.py:342
  (133 shorter events, 14.1 us)
Async XLA Ops:
  0.6 66.6 %collective-permute-start.8 = (bf16[512,5376]{1,0:T(8,128)(2,1)}, bf16[512,5376]{1,0:T(8,128)(2,1)}, u32[]{:S(2)}, u32[]{:S(2)}) collective-permute-start(bf16[512,5376]{1,0:T(8,128)(2,1)} %w_ref.1), channel_id=1, source_target_pairs={{0,1},{1,0},{2,3},{3,2},{4,5},{5,4},{6,7},{7,6},{8,9},{9,8},{10,11... | collective-permute-start | bytes 16515080 | tf_op jit(solution)/shard_map/ppermute | solution.py:34
  4.1 14.5 %collective-permute-start = (bf16[512,512]{1,0:T(8,128)(2,1)S(1)}, bf16[512,512]{1,0:T(8,128)(2,1)S(1)}, u32[]{:S(2)}, u32[]{:S(2)}) collective-permute-start(bf16[512,512]{1,0:T(8,128)(2,1)S(1)} %pair.1.kv0_ref), channel_id=1, source_target_pairs={{0,8},{8,16},{16,24},{24,32},{32,40},{40,48},{48,56},{56,64},{64,7... | collective-permute-start | bytes 1572872 | tf_op jit(solution)/shard_map/ppermute | solution.py:39
  10.8 55.2 %copy-start.1 = (bf16[336,2688]{1,0:T(8,128)(2,1)}, bf16[336,2688]{1,0:T(8,128)(2,1)S(1)}, u32[]{:S(2)}) copy-start(bf16[336,2688]{1,0:T(8,128)(2,1)S(1)} %pack.1.refs_0_) | copy-start | bytes 5419012
  22.1 8.4 %collective-permute-start.1 = (bf16[4,80,672]{2,1,0:T(8,128)(2,1)}, bf16[4,80,672]{2,1,0:T(8,128)(2,1)}, u32[]{:S(2)}, u32[]{:S(2)}) collective-permute-start(bf16[4,80,672]{2,1,0:T(8,128)(2,1)} %fusion.6), channel_id=1, source_target_pairs={{0,1},{1,0},{2,3},{3,2},{4,5},{5,4},{6,7},{7,6},{8,9},{9,8},{10,11... | collective-permute-start | bytes 1290248 | tf_op jit(solution)/shard_map/ppermute | solution.py:34
  22.9 32.7 %collective-permute-start.5 = (bf16[336,2688]{1,0:T(8,128)(2,1)S(1)}, bf16[336,2688]{1,0:T(8,128)(2,1)}, u32[]{:S(2)}, u32[]{:S(2)}) collective-permute-start(bf16[336,2688]{1,0:T(8,128)(2,1)S(1)} %pack.1.refs_0_), channel_id=1, source_target_pairs={{0,24},{1,97},{2,26},{3,99},{4,28},{5,101},{6,30},{7,103},{8,0},{9... | collective-permute-start | bytes 5419016 | tf_op jit(solution)/shard_map/ppermute | solution.py:90
  29.2 145.1 %copy-start.7 = (s32[4]{0:T(128)}, s32[4]{0:T(128)S(1)}, u32[]{:S(2)}) copy-start(s32[4]{0:T(128)S(1)} %pad_add_fusion.at_ref.refs_10_.refs_12_.refs_4_) | copy-start | bytes 52
  29.2 13.1 %collective-permute-start.6 = (bf16[512,512]{1,0:T(8,128)(2,1)S(1)}, bf16[512,512]{1,0:T(8,128)(2,1)S(1)}, u32[]{:S(2)}, u32[]{:S(2)}) collective-permute-start(bf16[512,512]{1,0:T(8,128)(2,1)S(1)} %collective-permute-done.kv1_ref), channel_id=1, source_target_pairs={{0,8},{8,16},{16,24},{24,32},{32,40},{40,48},{48,56},{56,64},{64,7... | collective-permute-start | bytes 1572872 | tf_op jit(solution)/shard_map/ppermute | solution.py:39
  30.5 46.9 %collective-permute-start.13 = (bf16[336,2688]{1,0:T(8,128)(2,1)S(1)}, bf16[336,2688]{1,0:T(8,128)(2,1)S(1)}, u32[]{:S(2)}, u32[]{:S(2)}) collective-permute-start(bf16[336,2688]{1,0:T(8,128)(2,1)S(1)} %pack.1.refs_0_), channel_id=1, source_target_pairs={{0,8},{1,33},{2,10},{3,35},{4,12},{5,37},{6,14},{7,39},{8,16},{9,4... | collective-permute-start | bytes 5419016 | tf_op jit(solution)/shard_map/ppermute | solution.py:90
  30.6 36.6 %slice-start = ((s8[5505024]{0:T(1024)(128)(4,1)}), s8[4194304]{0:T(1024)(128)(4,1)S(1)}, s32[]{:S(2)}) async-start(s8[5505024]{0:T(1024)(128)(4,1)} %bitcast.124), calls=%async_computation | async-start | bytes 8388608
  33.0 12.8 %collective-permute-start.2 = (bf16[2,80,672]{2,1,0:T(8,128)(2,1)S(1)}, bf16[2,80,672]{2,1,0:T(8,128)(2,1)S(1)}, u32[]{:S(2)}, u32[]{:S(2)}) collective-permute-start(bf16[2,80,672]{2,1,0:T(8,128)(2,1)S(1)} %get-tuple-element.110), channel_id=1, source_target_pairs={{0,6},{2,0},{4,2},{6,4},{1,7},{3,1},{5,3},{7,5},{8,14},{10,8},{12,... | collective-permute-start | bytes 645128 | tf_op jit(solution)/shard_map/ppermute | solution.py:34
  42.2 9.0 %collective-permute-start.3 = (bf16[2,80,672]{2,1,0:T(8,128)(2,1)S(1)}, bf16[2,80,672]{2,1,0:T(8,128)(2,1)S(1)}, u32[]{:S(2)}, u32[]{:S(2)}) collective-permute-start(bf16[2,80,672]{2,1,0:T(8,128)(2,1)S(1)} %get-tuple-element.109), channel_id=1, source_target_pairs={{0,4},{2,6},{4,0},{6,2},{1,5},{3,7},{5,1},{7,3},{8,12},{10,14},{12... | collective-permute-start | bytes 645128 | tf_op jit(solution)/shard_map/ppermute | solution.py:34
  45.8 9.5 %collective-permute-start.4 = (bf16[2,80,672]{2,1,0:T(8,128)(2,1)S(1)}, bf16[2,80,672]{2,1,0:T(8,128)(2,1)S(1)}, u32[]{:S(2)}, u32[]{:S(2)}) collective-permute-start(bf16[2,80,672]{2,1,0:T(8,128)(2,1)S(1)} %get-tuple-element.108), channel_id=1, source_target_pairs={{0,2},{2,4},{4,6},{6,0},{1,3},{3,5},{5,7},{7,1},{8,10},{10,12},{12... | collective-permute-start | bytes 645128 | tf_op jit(solution)/shard_map/ppermute | solution.py:34
  51.2 26.2 %collective-permute-start.14 = (bf16[336,2688]{1,0:T(8,128)(2,1)S(1)}, bf16[336,2688]{1,0:T(8,128)(2,1)S(1)}, u32[]{:S(2)}, u32[]{:S(2)}) collective-permute-start(bf16[336,2688]{1,0:T(8,128)(2,1)S(1)} %pack.1.refs_0_), channel_id=1, source_target_pairs={{0,96},{1,25},{2,98},{3,27},{4,100},{5,29},{6,102},{7,31},{8,104},... | collective-permute-start | bytes 5419016 | tf_op jit(solution)/shard_map/ppermute | solution.py:90
  62.2 4.9 %collective-permute-start.7 = (bf16[256,512]{1,0:T(8,128)(2,1)S(1)}, bf16[256,512]{1,0:T(8,128)(2,1)S(1)}, u32[]{:S(2)}, u32[]{:S(2)}) collective-permute-start(bf16[256,512]{1,0:T(8,128)(2,1)S(1)} %bitcast.134), channel_id=1, source_target_pairs={{0,1},{1,0},{2,3},{3,2},{4,5},{5,4},{6,7},{7,6},{8,9},{9,8},{10,11... | collective-permute-start | bytes 786440 | tf_op jit(solution)/shard_map/ppermute | solution.py:34
  66.0 23.4 %collective-permute-start.10 = (bf16[336,2688]{1,0:T(8,128)(2,1)S(1)}, bf16[336,2688]{1,0:T(8,128)(2,1)}, u32[]{:S(2)}, u32[]{:S(2)}) collective-permute-start(bf16[336,2688]{1,0:T(8,128)(2,1)S(1)} %pack.1.refs_0_), channel_id=1, source_target_pairs={{0,32},{1,9},{2,34},{3,11},{4,36},{5,13},{6,38},{7,15},{8,40},{9,1... | collective-permute-start | bytes 5419016 | tf_op jit(solution)/shard_map/ppermute | solution.py:90
  74.5 10.7 %collective-permute-start.11 = (bf16[32,5376]{1,0:T(8,128)(2,1)S(1)}, bf16[32,5376]{1,0:T(8,128)(2,1)S(1)}, u32[]{:S(2)}, u32[]{:S(2)}) collective-permute-start(bf16[32,5376]{1,0:T(8,128)(2,1)S(1)} %get-tuple-element.64), channel_id=1, source_target_pairs={{0,2},{2,4},{4,6},{6,0},{1,3},{3,5},{5,7},{7,1},{8,10},{10,12},{12... | collective-permute-start | bytes 1032200 | tf_op jit(solution)/shard_map/ppermute | solution.py:34
  74.8 14.2 %collective-permute-start.12 = (bf16[32,5376]{1,0:T(8,128)(2,1)S(1)}, bf16[32,5376]{1,0:T(8,128)(2,1)S(1)}, u32[]{:S(2)}, u32[]{:S(2)}) collective-permute-start(bf16[32,5376]{1,0:T(8,128)(2,1)S(1)} %get-tuple-element.65), channel_id=1, source_target_pairs={{0,6},{2,0},{4,2},{6,4},{1,7},{3,1},{5,3},{7,5},{8,14},{10,8},{12,... | collective-permute-start | bytes 1032200 | tf_op jit(solution)/shard_map/ppermute | solution.py:34
  77.4 73.3 %copy-start.11 = (bf16[336,2688]{1,0:T(8,128)(2,1)}, bf16[336,2688]{1,0:T(8,128)(2,1)S(1)}, u32[]{:S(2)}) copy-start(bf16[336,2688]{1,0:T(8,128)(2,1)S(1)} %collective-permute-done.13.refs_1_) | copy-start | bytes 5419012
  77.4 59.2 %collective-permute-start.21 = (bf16[336,2688]{1,0:T(8,128)(2,1)}, bf16[336,2688]{1,0:T(8,128)(2,1)}, u32[]{:S(2)}, u32[]{:S(2)}) collective-permute-start(bf16[336,2688]{1,0:T(8,128)(2,1)} %collective-permute-done.5.refs_2_), channel_id=1, source_target_pairs={{0,32},{1,9},{2,34},{3,11},{4,36},{5,13},{6,38},{7,15},{8,40},{9,1... | collective-permute-start | bytes 5419016 | tf_op jit(solution)/shard_map/ppermute | solution.py:90
  77.4 56.4 %copy-start.12 = (bf16[336,2688]{1,0:T(8,128)(2,1)}, bf16[336,2688]{1,0:T(8,128)(2,1)S(1)}, u32[]{:S(2)}) copy-start(bf16[336,2688]{1,0:T(8,128)(2,1)S(1)} %collective-permute-done.14.refs_8_) | copy-start | bytes 5419012
  77.4 59.2 %collective-permute-start.22 = (bf16[336,2688]{1,0:T(8,128)(2,1)}, bf16[336,2688]{1,0:T(8,128)(2,1)}, u32[]{:S(2)}, u32[]{:S(2)}) collective-permute-start(bf16[336,2688]{1,0:T(8,128)(2,1)} %collective-permute-done.5.refs_2_), channel_id=1, source_target_pairs={{0,96},{1,25},{2,98},{3,27},{4,100},{5,29},{6,102},{7,31},{8,104},... | collective-permute-start | bytes 5419016 | tf_op jit(solution)/shard_map/ppermute | solution.py:90
  85.2 37.7 %collective-permute-start.9 = (bf16[336,2688]{1,0:T(8,128)(2,1)}, bf16[336,2688]{1,0:T(8,128)(2,1)S(1)}, u32[]{:S(2)}, u32[]{:S(2)}) collective-permute-start(bf16[336,2688]{1,0:T(8,128)(2,1)} %collective-permute-done.5.refs_2_), channel_id=1, source_target_pairs={{0,24},{1,97},{2,26},{3,99},{4,28},{5,101},{6,30},{7,103},{8,0},{9... | collective-permute-start | bytes 5419016 | tf_op jit(solution)/shard_map/ppermute | solution.py:90
  89.0 35.8 %collective-permute-start.16 = (bf16[32,5376]{1,0:T(8,128)(2,1)S(1)}, bf16[32,5376]{1,0:T(8,128)(2,1)S(1)}, u32[]{:S(2)}, u32[]{:S(2)}) collective-permute-start(bf16[32,5376]{1,0:T(8,128)(2,1)S(1)} %get-tuple-element.67), channel_id=1, source_target_pairs={{0,2},{2,4},{4,6},{6,0},{1,3},{3,5},{5,7},{7,1},{8,10},{10,12},{12... | collective-permute-start | bytes 1032200 | tf_op jit(solution)/shard_map/ppermute | solution.py:34
  89.4 35.4 %collective-permute-start.17 = (bf16[32,5376]{1,0:T(8,128)(2,1)S(1)}, bf16[32,5376]{1,0:T(8,128)(2,1)S(1)}, u32[]{:S(2)}, u32[]{:S(2)}) collective-permute-start(bf16[32,5376]{1,0:T(8,128)(2,1)S(1)} %get-tuple-element.68), channel_id=1, source_target_pairs={{0,6},{2,0},{4,2},{6,4},{1,7},{3,1},{5,3},{7,5},{8,14},{10,8},{12,... | collective-permute-start | bytes 1032200 | tf_op jit(solution)/shard_map/ppermute | solution.py:34
  122.9 39.9 %copy-start.13 = (bf16[336,2688]{1,0:T(8,128)(2,1)}, bf16[336,2688]{1,0:T(8,128)(2,1)S(1)}, u32[]{:S(2)}) copy-start(bf16[336,2688]{1,0:T(8,128)(2,1)S(1)} %collective-permute-done.9.refs_3_) | copy-start | bytes 5419012
  122.9 7.8 %collective-permute-start.18 = (bf16[32,5376]{1,0:T(8,128)(2,1)S(1)}, bf16[32,5376]{1,0:T(8,128)(2,1)S(1)}, u32[]{:S(2)}, u32[]{:S(2)}) collective-permute-start(bf16[32,5376]{1,0:T(8,128)(2,1)S(1)} %add_convert_fusion), channel_id=1, source_target_pairs={{0,6},{2,0},{4,2},{6,4},{1,7},{3,1},{5,3},{7,5},{8,14},{10,8},{12,... | collective-permute-start | bytes 1032200 | tf_op jit(solution)/shard_map/ppermute | solution.py:34
  124.8 8.0 %collective-permute-start.15 = (bf16[32,5376]{1,0:T(8,128)(2,1)S(1)}, bf16[32,5376]{1,0:T(8,128)(2,1)S(1)}, u32[]{:S(2)}, u32[]{:S(2)}) collective-permute-start(bf16[32,5376]{1,0:T(8,128)(2,1)S(1)} %add_convert_fusion.1), channel_id=1, source_target_pairs={{0,2},{2,4},{4,6},{6,0},{1,3},{3,5},{5,7},{7,1},{8,10},{10,12},{12... | collective-permute-start | bytes 1032200 | tf_op jit(solution)/shard_map/ppermute | solution.py:34
  124.8 38.0 %collective-permute-start.39 = (bf16[336,2688]{1,0:T(8,128)(2,1)S(1)}, bf16[336,2688]{1,0:T(8,128)(2,1)}, u32[]{:S(2)}, u32[]{:S(2)}) collective-permute-start(bf16[336,2688]{1,0:T(8,128)(2,1)S(1)} %collective-permute-done.9.refs_3_), channel_id=1, source_target_pairs={{0,96},{1,25},{2,98},{3,27},{4,100},{5,29},{6,102},{7,31},{8,104},... | collective-permute-start | bytes 5419016 | tf_op jit(solution)/shard_map/ppermute | solution.py:90
  133.9 16.9 %collective-permute-start.19 = (bf16[64,5376]{1,0:T(8,128)(2,1)S(1)}, bf16[64,5376]{1,0:T(8,128)(2,1)S(1)}, u32[]{:S(2)}, u32[]{:S(2)}) collective-permute-start(bf16[64,5376]{1,0:T(8,128)(2,1)S(1)} %get-tuple-element.78.refs_0_), channel_id=1, source_target_pairs={{0,2},{2,4},{4,6},{6,0},{1,3},{3,5},{5,7},{7,1},{8,10},{10,12},{12... | collective-permute-start | bytes 2064392 | tf_op jit(solution)/shard_map/ppermute | solution.py:34
  133.9 16.8 %collective-permute-start.20 = (bf16[64,5376]{1,0:T(8,128)(2,1)S(1)}, bf16[64,5376]{1,0:T(8,128)(2,1)S(1)}, u32[]{:S(2)}, u32[]{:S(2)}) collective-permute-start(bf16[64,5376]{1,0:T(8,128)(2,1)S(1)} %get-tuple-element.78.refs_0_), channel_id=1, source_target_pairs={{0,6},{2,0},{4,2},{6,4},{1,7},{3,1},{5,3},{7,5},{8,14},{10,8},{12,... | collective-permute-start | bytes 2064392 | tf_op jit(solution)/shard_map/ppermute | solution.py:34
  136.6 14.3 %collective-permute-start.25 = (bf16[64,5376]{1,0:T(8,128)(2,1)S(1)}, bf16[64,5376]{1,0:T(8,128)(2,1)S(1)}, u32[]{:S(2)}, u32[]{:S(2)}) collective-permute-start(bf16[64,5376]{1,0:T(8,128)(2,1)S(1)} %get-tuple-element.78.refs_0_), channel_id=1, source_target_pairs={{0,1},{1,0},{2,3},{3,2},{4,5},{5,4},{6,7},{7,6},{8,9},{9,8},{10,11... | collective-permute-start | bytes 2064392 | tf_op jit(solution)/shard_map/ppermute | solution.py:34
  136.6 33.1 %collective-permute-start.30 = (bf16[336,2688]{1,0:T(8,128)(2,1)S(1)}, bf16[336,2688]{1,0:T(8,128)(2,1)}, u32[]{:S(2)}, u32[]{:S(2)}) collective-permute-start(bf16[336,2688]{1,0:T(8,128)(2,1)S(1)} %collective-permute-done.13.refs_1_), channel_id=1, source_target_pairs={{0,32},{1,9},{2,34},{3,11},{4,36},{5,13},{6,38},{7,15},{8,40},{9,1... | collective-permute-start | bytes 5419016 | tf_op jit(solution)/shard_map/ppermute | solution.py:90
  150.7 22.1 %collective-permute-start.31 = (bf16[336,2688]{1,0:T(8,128)(2,1)S(1)}, bf16[336,2688]{1,0:T(8,128)(2,1)S(1)}, u32[]{:S(2)}, u32[]{:S(2)}) collective-permute-start(bf16[336,2688]{1,0:T(8,128)(2,1)S(1)} %collective-permute-done.13.refs_1_), channel_id=1, source_target_pairs={{0,96},{1,25},{2,98},{3,27},{4,100},{5,29},{6,102},{7,31},{8,104},... | collective-permute-start | bytes 5419016 | tf_op jit(solution)/shard_map/ppermute | solution.py:90
  150.8 10.5 %collective-permute-start.23 = (bf16[32,5376]{1,0:T(8,128)(2,1)S(1)}, bf16[32,5376]{1,0:T(8,128)(2,1)S(1)}, u32[]{:S(2)}, u32[]{:S(2)}) collective-permute-start(bf16[32,5376]{1,0:T(8,128)(2,1)S(1)} %slice.76), channel_id=1, source_target_pairs={{0,2},{2,4},{4,6},{6,0},{1,3},{3,5},{5,7},{7,1},{8,10},{10,12},{12... | collective-permute-start | bytes 1032200 | tf_op jit(solution)/shard_map/ppermute | solution.py:34
  150.9 11.9 %collective-permute-start.24 = (bf16[32,5376]{1,0:T(8,128)(2,1)S(1)}, bf16[32,5376]{1,0:T(8,128)(2,1)S(1)}, u32[]{:S(2)}, u32[]{:S(2)}) collective-permute-start(bf16[32,5376]{1,0:T(8,128)(2,1)S(1)} %slice.77), channel_id=1, source_target_pairs={{0,6},{2,0},{4,2},{6,4},{1,7},{3,1},{5,3},{7,5},{8,14},{10,8},{12,... | collective-permute-start | bytes 1032200 | tf_op jit(solution)/shard_map/ppermute | solution.py:34
  161.3 3.5 %collective-permute-start.28 = (bf16[32,5376]{1,0:T(8,128)(2,1)S(1)}, bf16[32,5376]{1,0:T(8,128)(2,1)S(1)}, u32[]{:S(2)}, u32[]{:S(2)}) collective-permute-start(bf16[32,5376]{1,0:T(8,128)(2,1)S(1)} %collective-permute-done.23.refs_3_), channel_id=1, source_target_pairs={{0,1},{1,0},{2,3},{3,2},{4,5},{5,4},{6,7},{7,6},{8,9},{9,8},{10,11... | collective-permute-start | bytes 1032200 | tf_op jit(solution)/shard_map/ppermute | solution.py:34
  162.8 2.3 collective-permute-start.29
  162.8 23.3 %collective-permute-start.41 = (bf16[336,2688]{1,0:T(8,128)(2,1)S(1)}, bf16[336,2688]{1,0:T(8,128)(2,1)S(1)}, u32[]{:S(2)}, u32[]{:S(2)}) collective-permute-start(bf16[336,2688]{1,0:T(8,128)(2,1)S(1)} %collective-permute-done.9.refs_3_), channel_id=1, source_target_pairs={{0,32},{1,9},{2,34},{3,11},{4,36},{5,13},{6,38},{7,15},{8,40},{9,1... | collective-permute-start | bytes 5419016 | tf_op jit(solution)/shard_map/ppermute | solution.py:90
  164.8 2.1 collective-permute-start.26
  165.1 3.0 %collective-permute-start.27 = (bf16[64,5376]{1,0:T(8,128)(2,1)S(1)}, bf16[64,5376]{1,0:T(8,128)(2,1)S(1)}, u32[]{:S(2)}, u32[]{:S(2)}) collective-permute-start(bf16[64,5376]{1,0:T(8,128)(2,1)S(1)} %collective-permute-done.20.refs_2_), channel_id=1, source_target_pairs={{0,1},{1,0},{2,3},{3,2},{4,5},{5,4},{6,7},{7,6},{8,9},{9,8},{10,11... | collective-permute-start | bytes 2064392 | tf_op jit(solution)/shard_map/ppermute | solution.py:34
  167.0 48.5 %collective-permute-start.36 = (bf16[336,2688]{1,0:T(8,128)(2,1)}, bf16[336,2688]{1,0:T(8,128)(2,1)S(1)}, u32[]{:S(2)}, u32[]{:S(2)}) collective-permute-start(bf16[336,2688]{1,0:T(8,128)(2,1)} %collective-permute-done.10.refs_4_), channel_id=1, source_target_pairs={{0,32},{1,9},{2,34},{3,11},{4,36},{5,13},{6,38},{7,15},{8,40},{9,1... | collective-permute-start | bytes 5419016 | tf_op jit(solution)/shard_map/ppermute | solution.py:90
  168.2 47.3 %collective-permute-start.38 = (bf16[336,2688]{1,0:T(8,128)(2,1)}, bf16[336,2688]{1,0:T(8,128)(2,1)S(1)}, u32[]{:S(2)}, u32[]{:S(2)}) collective-permute-start(bf16[336,2688]{1,0:T(8,128)(2,1)} %collective-permute-done.22.refs_10_), channel_id=1, source_target_pairs={{0,96},{1,25},{2,98},{3,27},{4,100},{5,29},{6,102},{7,31},{8,104},... | collective-permute-start | bytes 5419016 | tf_op jit(solution)/shard_map/ppermute | solution.py:90
  169.7 46.5 %collective-permute-start.40 = (bf16[336,2688]{1,0:T(8,128)(2,1)}, bf16[336,2688]{1,0:T(8,128)(2,1)S(1)}, u32[]{:S(2)}, u32[]{:S(2)}) collective-permute-start(bf16[336,2688]{1,0:T(8,128)(2,1)} %collective-permute-done.39.refs_11_), channel_id=1, source_target_pairs={{0,96},{1,25},{2,98},{3,27},{4,100},{5,29},{6,102},{7,31},{8,104},... | collective-permute-start | bytes 5419016 | tf_op jit(solution)/shard_map/ppermute | solution.py:90
  174.1 50.9 %collective-permute-start.37 = (bf16[336,2688]{1,0:T(8,128)(2,1)}, bf16[336,2688]{1,0:T(8,128)(2,1)}, u32[]{:S(2)}, u32[]{:S(2)}) collective-permute-start(bf16[336,2688]{1,0:T(8,128)(2,1)} %collective-permute-done.30.refs_5_), channel_id=1, source_target_pairs={{0,32},{1,9},{2,34},{3,11},{4,36},{5,13},{6,38},{7,15},{8,40},{9,1... | collective-permute-start | bytes 5419016 | tf_op jit(solution)/shard_map/ppermute | solution.py:90
  187.4 25.1 %collective-permute-start.32 = (bf16[4,64,672]{2,1,0:T(8,128)(2,1)S(1)}, bf16[4,64,672]{2,1,0:T(8,128)(2,1)S(1)}, u32[]{:S(2)}, u32[]{:S(2)}) collective-permute-start(bf16[4,64,672]{2,1,0:T(8,128)(2,1)S(1)} %select_bitcast_fusion.2), channel_id=1, source_target_pairs={{0,1},{1,0},{2,3},{3,2},{4,5},{5,4},{6,7},{7,6},{8,9},{9,8},{10,11... | collective-permute-start | bytes 1032200 | tf_op jit(solution)/shard_map/ppermute | solution.py:34
  213.0 25.5 %collective-permute-start.33 = (bf16[2,64,672]{2,1,0:T(8,128)(2,1)S(1)}, bf16[2,64,672]{2,1,0:T(8,128)(2,1)S(1)}, u32[]{:S(2)}, u32[]{:S(2)}) collective-permute-start(bf16[2,64,672]{2,1,0:T(8,128)(2,1)S(1)} %get-tuple-element.113), channel_id=1, source_target_pairs={{0,6},{2,0},{4,2},{6,4},{1,7},{3,1},{5,3},{7,5},{8,14},{10,8},{12,... | collective-permute-start | bytes 516104 | tf_op jit(solution)/shard_map/ppermute | solution.py:34
  215.5 23.1 %collective-permute-start.34 = (bf16[2,64,672]{2,1,0:T(8,128)(2,1)S(1)}, bf16[2,64,672]{2,1,0:T(8,128)(2,1)S(1)}, u32[]{:S(2)}, u32[]{:S(2)}) collective-permute-start(bf16[2,64,672]{2,1,0:T(8,128)(2,1)S(1)} %get-tuple-element.112), channel_id=1, source_target_pairs={{0,4},{2,6},{4,0},{6,2},{1,5},{3,7},{5,1},{7,3},{8,12},{10,14},{12... | collective-permute-start | bytes 516104 | tf_op jit(solution)/shard_map/ppermute | solution.py:34
  215.5 23.1 %collective-permute-start.35 = (bf16[2,64,672]{2,1,0:T(8,128)(2,1)S(1)}, bf16[2,64,672]{2,1,0:T(8,128)(2,1)S(1)}, u32[]{:S(2)}, u32[]{:S(2)}) collective-permute-start(bf16[2,64,672]{2,1,0:T(8,128)(2,1)S(1)} %get-tuple-element.111), channel_id=1, source_target_pairs={{0,2},{2,4},{4,6},{6,0},{1,3},{3,5},{5,7},{7,1},{8,10},{10,12},{12... | collective-permute-start | bytes 516104 | tf_op jit(solution)/shard_map/ppermute | solution.py:34
  (15 other events, 75.4 us)

commit v5 on v4

--- a/solution.py
+++ b/solution.py
@@ -250,45 +250,45 @@
     )(*pieces, where)
 
 
-def weight_copies(parts, where, arrays, block, w_ref, sems):
+def weight_copies(parts, where, arrays, block, w_ref, sems, width=384):
     c, y, x = where[1], where[2], where[3]
     first = jnp.where(c == 0, x, y)
-    cols = pl.ds(pl.multiple_of(384 * block, 128), 384)
+    cols = pl.ds(pl.multiple_of(width * block, 128), width)
     copies = []
-    for i, (array, slot, rel) in enumerate(parts):
+    for i, (array, lo, slot, rel) in enumerate(parts):
         row = pl.multiple_of(1344 * slot + 336 * ((first + rel) % 4), 16)
         copies.append(
-            pltpu.make_async_copy(arrays[array].at[:, cols], w_ref.at[pl.ds(row, 336)], sems.at[i])
+            pltpu.make_async_copy(arrays[array].at[pl.ds(lo, 336), cols], w_ref.at[pl.ds(row, 336)], sems.at[i])
         )
     return copies
 
 
-def fetch_block(parts, place, arrays, w_ref, sems):
+def fetch_block(parts, place, arrays, w_ref, sems, width):
     j = pl.program_id(0)
     slot = lax.rem(j, 2)
 
     @pl.when(j == 0)
     def _():
-        for copy in weight_copies(parts, place, arrays, 0, w_ref.at[0], sems.at[0]):
+        for copy in weight_copies(parts, place, arrays, 0, w_ref.at[0], sems.at[0], width):
             copy.start()
 
-    @pl.when(j + 1 < 7)
+    @pl.when(j + 1 < 2688 // width)
     def _():
-        for copy in weight_copies(parts, place, arrays, j + 1, w_ref.at[1 - slot], sems.at[1 - slot]):
+        for copy in weight_copies(parts, place, arrays, j + 1, w_ref.at[1 - slot], sems.at[1 - slot], width):
             copy.start()
 
-    for copy in weight_copies(parts, place, arrays, j, w_ref.at[slot], sems.at[slot]):
+    for copy in weight_copies(parts, place, arrays, j, w_ref.at[slot], sems.at[slot], width):
         copy.wait()
     return slot
 
 
 def near(rows, where, blocks):
     m = len(blocks)
-    parts = [(4 * g + k, g, REL[k]) for g in range(3) for k in range(4)]
+    parts = [(g, 336 * k, g, REL[k]) for g in range(3) for k in range(4)]
 
     def body(*refs):
         place, n_ref, o_ref, w_ref, sems = refs[m:]
-        slot = fetch_block(parts, place, refs[:m], w_ref, sems)
+        slot = fetch_block(parts, place, refs[:m], w_ref, sems, 896)
         acc = jnp.dot(n_ref[:, :1344], w_ref[slot, :1344], preferred_element_type=F32)
         for g in (1, 2):
             lhs = n_ref[:, GROUP * g:GROUP * g + 1344]
@@ -298,10 +298,10 @@
     return pl.pallas_call(
         body,
         out_shape=jax.ShapeDtypeStruct((TOK, 2688), F32),
-        grid=(7,),
+        grid=(3,),
         in_specs=[HB] * m + [SM, pl.BlockSpec((TOK, 3 * GROUP), lambda j: (0, 0))],
-        out_specs=pl.BlockSpec((TOK, 384), lambda j: (0, j)),
-        scratch_shapes=[pltpu.VMEM((2, 3 * 1344, 384), BF), pltpu.SemaphoreType.DMA((2, len(parts)))],
+        out_specs=pl.BlockSpec((TOK, 896), lambda j: (0, j)),
+        scratch_shapes=[pltpu.VMEM((2, 3 * 1344, 896), BF), pltpu.SemaphoreType.DMA((2, len(parts)))],
         compiler_params=params(56),
         cost_estimate=cost(0, 1000),
         name="near",
@@ -310,7 +310,7 @@
 
 def far(rows, where, blocks, sums):
     m = len(blocks)
-    parts = [(k, 0, REL[k]) for k in range(4)]
+    parts = [(k // 2, 336 * (k % 2), 0, REL[k]) for k in range(4)]
 
     def body(*refs):
         place, n_ref, s_ref, o_ref, w_ref, acc_ref, sems = refs[m:]
@@ -388,12 +388,13 @@
     gate_weight, kv0 = lax.optimization_barrier((gate_weight, kv0))
     w = pack(gate_weight, up_weight)
     p = ring(w, -1, 0)
-    kv1, w_late, residual, post_gain = lax.optimization_barrier((kv1, w, residual, post_gain))
     kv2 = behind(kv1)
+    kv2, w_late = lax.optimization_barrier((kv2, w))
     m = ring(w_late, 1, 0)
     b = ring(p, -1, 0)
-    w_late, kv2 = lax.optimization_barrier((w_late, kv2))
-    prev, following = [ring(w_late, 1, 1)], [ring(w_late, -1, 1)]
+    kv2, residual, post_gain = lax.optimization_barrier((kv2, residual, post_gain))
+    group = jnp.concatenate([w, m, p, b], axis=0)
+    prev, following = ring(group, 1, 1), ring(group, -1, 1)
 
     gains = jnp.stack([post_gain, pre_gain])
     high = gains.astype(BF)
@@ -408,38 +409,33 @@
     kid = lax.dynamic_slice_in_dim(padded, start, 3 * TOK, 0)[None, :]
     qid = lax.dynamic_slice_in_dim(doc_ids, start, TOK, 0)[:, None]
 
-    queries, mine, p = lax.optimization_barrier((queries, mine, p))
     mix = attend(where, queries, kv2, kv1, kv0, qid, kid)
     other_weight = shift(out_weight, "c", 1)
     own, other = mix[0].reshape(256, 512), shift(mix[1].reshape(256, 512), "c", 1)
+    other, mine = lax.optimization_barrier((other, mine))
     p0, p1t, p1b, p2t, p2b, p3t, p3b = project(own, other, out_weight, other_weight)
 
     up_t = shift(p2t, "z", 1)
     dn_b = shift(p2b, "z", -1)
     a_b = shift(p1b, "z", 1)
     b_t = shift(p3t, "z", -1)
-    up_t, dn_b, m, following[0] = lax.optimization_barrier((up_t, dn_b, m, following[0]))
     add = lambda p, q: (p.astype(F32) + q.astype(F32)).astype(BF)
     a_t = shift(add(p1t, up_t), "z", 1)
     b_b = shift(add(p3b, dn_b), "z", -1)
-    p0, b, prev[0] = lax.optimization_barrier((p0, b, prev[0]))
-    prev += [ring(v, 1, 1) for v in (m, p, b)]
-    following += [ring(v, -1, 1) for v in (m, p, b)]
     new, nrm = norm(p0, a_t, a_b, b_t, b_b, mine)
 
     n_m, n_p = shift(nrm, "z", 1), shift(nrm, "z", -1)
-    n_m, n_p, prev[2], following[2] = lax.optimization_barrier((n_m, n_p, prev[2], following[2]))
     pieces = [nrm, n_m, n_p, shift(n_m[:32], "z", 1), shift(n_p[32:], "z", -1)]
     places = [(0, None), (3, None), (1, None), (2, 0), (2, 1)]
     pieces += [shift(piece, "c", 1) for piece in pieces]
     tokens_at = [(dz, dc, part) for dc in range(2) for dz, part in places]
-    pieces, prev[1], following[1] = lax.optimization_barrier((pieces, prev[1], following[1]))
     rows = order(pieces, tokens_at, where)
 
-    last = [ring(prev[0], 1, 1), ring(prev[1], 1, 1), ring(following[2], -1, 1), ring(following[3], -1, 1)]
+    prev, following, rows = lax.optimization_barrier((prev, following, rows))
+    last = [ring(prev[:672], 1, 1), ring(following[672:], -1, 1)]
     new, rows = lax.optimization_barrier((new, rows))
     sent_back = swap(new, z, c)
-    sums = near(rows, where, [w, m, p, b, *prev, *following])
+    sums = near(rows, where, [group, prev, following])
     act = far(rows, where, last, sums)
     sent_back, act = lax.optimization_barrier((sent_back, act))
     new_residual = gather(sent_back, z).reshape(TOK, 672)

time: 241 us -> 248 us (1.029)
  waiting for transfers between devices: 101 us -> 72.8 us
  starting transfers between devices: 61.4 us -> 78.9 us
  local copies, waits for them, and re-layouts: 14.3 us -> 27.1 us
  other arithmetic: 5.22 us -> 12.6 us
    ppermute x15 -> x7, waiting for transfers between devices: 47 us -> 15.1 us  [ring(): return lax.ppermute(value, ('y', 'x', 'z', 'c'), pairs)]
    ppermute x25, starting transfers between devices: 33.9 us -> 58.7 us  [shift(): return lax.ppermute(value, axis, [(i, (i + by) % n) for i in range(n)])]
    ppermute x15 -> x7, starting transfers between devices: 22.9 us -> 12.8 us  [ring(): return lax.ppermute(value, ('y', 'x', 'z', 'c'), pairs)]
    ppermute x2, waiting for transfers between devices: 13.1 us -> 21.5 us  [behind(): return lax.ppermute(value, ('y', 'x'), [(i, i + 1) for i in range(n - 1)])]
    slice x0 -> x2, local copies, waits for them, and re-layouts: none -> 8 us  [per_device(): last = [ring(prev[:672], 1, 1), ring(following[672:], -1, 1)]]
    concatenate x0 -> x1, other arithmetic: none -> 6.18 us  [per_device(): group = jnp.concatenate([w, m, p, b], axis=0)]
    ppermute x25, waiting for transfers between devices: 40.8 us -> 36.1 us  [shift(): return lax.ppermute(value, axis, [(i, (i + by) % n) for i in range(n)])]
    ppermute x2, starting transfers between devices: 4.54 us -> 7.37 us  [behind(): return lax.ppermute(value, ('y', 'x'), [(i, i + 1) for i in range(n - 1)])]
  transfers between devices with their start and end apart: 42 -> 34, of which waited for: 14 -> 12; matrix products, arithmetic and copies ran while one was open for 3% -> 7% of each run, Pallas kernels for 24% -> 22%
where the time goes in v5:
time: 248 us; the launch traced here: 247 us
  starting transfers between devices  78.9 us (32%)
  waiting for transfers between devices  72.8 us (29%)
  Pallas kernels  54.6 us (22%)
  local copies, waits for them, and re-layouts  27.1 us (11%)
  other arithmetic  12.6 us (5%)
    ppermute x25, starting transfers between devices, shift(): return lax.ppermute(value, axis, [(i, (i + by) % n) for i in range(n)])  58.7 us
    ppermute x25, waiting for transfers between devices, shift(): return lax.ppermute(value, axis, [(i, (i + by) % n) for i in range(n)])  36.1 us
    pallas_call x1, Pallas kernels, near(): pl.pallas_call(body, out_shape=jax.ShapeDtypeStruct((TOK, 2688), F32), gr...  21.8 us
    ppermute x2, waiting for transfers between devices, behind(): return lax.ppermute(value, ('y', 'x'), [(i, i + 1) for i in range(n - 1)])  21.5 us
    ppermute x7, waiting for transfers between devices, ring(): return lax.ppermute(value, ('y', 'x', 'z', 'c'), pairs)  15.1 us
    unnamed x53, local copies, waits for them, and re-layouts  14.2 us
    pallas_call x1, Pallas kernels, far(): pl.pallas_call(body, out_shape=jax.ShapeDtypeStruct((1344, TOK), BF), gri...  13.4 us
    ppermute x7, starting transfers between devices, ring(): return lax.ppermute(value, ('y', 'x', 'z', 'c'), pairs)  12.8 us
  transfers between devices with their start and end apart: 34, of which 12 were waited for; matrix products, arithmetic and copies ran while one was open for 7% of the time, Pallas kernels for 22%

profile of v5, /device:TPU:1, one launch (start us, length us, event | category | flops | bytes accessed | tf_op | source)
XLA Modules:
  0.0 247.1 jit_solution(7292002906420899926)
XLA Ops:
  2.6 1.2 copy-done.1
  3.8 1.2 copy-done.2
  5.4 3.6 %collective-permute-start.15 = (bf16[336,2688]{1,0:T(8,128)(2,1)S(1)}, bf16[336,2688]{1,0:T(8,128)(2,1)}, u32[]{:S(2)}, u32[]{:S(2)}) collective-permute-start(bf16[336,2688]{1,0:T(8,128)(2,1)S(1)} %pack.1), channel_id=1, source_target_pairs={{0,24},{1,97},{2,26},{3,99},{4,28},{5,101},{6,30},{7,103},{8,0},{9... | collective-permute-start | bytes 5419016 | tf_op jit(solution)/shard_map/ppermute | solution.py:90
  9.1 3.1 %collective-permute-start = (bf16[512,512]{1,0:T(8,128)(2,1)S(1)}, bf16[512,512]{1,0:T(8,128)(2,1)S(1)}, u32[]{:S(2)}, u32[]{:S(2)}) collective-permute-start(bf16[512,512]{1,0:T(8,128)(2,1)S(1)} %pair.1.kv0_ref), channel_id=1, source_target_pairs={{0,8},{8,16},{16,24},{24,32},{32,40},{40,48},{48,56},{56,64},{64,7... | collective-permute-start | bytes 1572872 | tf_op jit(solution)/shard_map/ppermute | solution.py:39
  12.2 10.7 %collective-permute-done.kv1_ref = bf16[512,512]{1,0:T(8,128)(2,1)S(1)} collective-permute-done((bf16[512,512]{1,0:T(8,128)(2,1)S(1)}, bf16[512,512]{1,0:T(8,128)(2,1)S(1)}, u32[]{:S(2)}, u32[]{:S(2)}) %collective-permute-start) | collective-permute-done | bytes 524320 | tf_op jit(solution)/shard_map/ppermute | solution.py:39
  22.9 4.2 %collective-permute-start.1 = (bf16[512,512]{1,0:T(8,128)(2,1)S(1)}, bf16[512,512]{1,0:T(8,128)(2,1)S(1)}, u32[]{:S(2)}, u32[]{:S(2)}) collective-permute-start(bf16[512,512]{1,0:T(8,128)(2,1)S(1)} %collective-permute-done.kv1_ref), channel_id=1, source_target_pairs={{0,8},{8,16},{16,24},{24,32},{32,40},{40,48},{48,56},{56,64},{64,7... | collective-permute-start | bytes 1572872 | tf_op jit(solution)/shard_map/ppermute | solution.py:39
  28.0 10.7 %collective-permute-done.1.kv2_ref = bf16[512,512]{1,0:T(8,128)(2,1)S(1)} collective-permute-done((bf16[512,512]{1,0:T(8,128)(2,1)S(1)}, bf16[512,512]{1,0:T(8,128)(2,1)S(1)}, u32[]{:S(2)}, u32[]{:S(2)}) %collective-permute-start.1) | collective-permute-done | bytes 524320 | tf_op jit(solution)/shard_map/ppermute | solution.py:39
  40.1 2.1 collective-permute-start.16
  43.6 1.2 copy.23
  45.1 2.0 fusion.6
  47.1 1.8 collective-permute-start.3
  52.0 5.5 %attend.1 = bf16[2,4,64,512]{3,2,1,0:T(8,128)(2,1)S(1)} custom-call(s32[4]{0:T(128)S(1)} %pad_add_fusion.at_ref.refs_10_.refs_3_.refs_2_, bf16[512,512]{1,0:T(8,128)(2,1)S(1)} %copy-done.3, bf16[512,512]{1,0:T(8,128)(2,1)S(1)} %copy-done.7, bf16[512,512]{1,0:T(8,128)(2,1)S(1)} %copy-done.5, bf16[512,512]{1,0:T(8,128)(2,1)S(1)} %pair.1.kv0_ref, ...), custom_call_target="tpu_custom_call" | custom-call | bytes 1000 | tf_op jit(solution)/shard_map/attend/pallas_call | solution.py:123
  57.7 1.3 select_bitcast_fusion
  59.5 3.3 %collective-permute-done.14 = bf16[336,2688]{1,0:T(8,128)(2,1)} collective-permute-done((bf16[336,2688]{1,0:T(8,128)(2,1)S(1)}, bf16[336,2688]{1,0:T(8,128)(2,1)}, u32[]{:S(2)}, u32[]{:S(2)}) %collective-permute-start.14) | collective-permute-done | bytes 1806368 | tf_op jit(solution)/shard_map/ppermute | solution.py:90
  62.9 6.2 %pad_maximum_fusion.refs_0_ = bf16[1344,2688]{1,0:T(8,128)(2,1)} fusion(bf16[336,2688]{1,0:T(8,128)(2,1)} %collective-permute-done.16, bf16[336,2688]{1,0:T(8,128)(2,1)} %collective-permute-done.15, bf16[336,2688]{1,0:T(8,128)(2,1)} %collective-permute-done.14, bf16[336,2688]{1,0:T(8,128)(2,1)S(1)} %pack.1), kind=kLoop, calls=%fused_computation | loop fusion | flops 28901376 | bytes 14450688 | tf_op jit(solution)/shard_map/concatenate | solution.py:396
  69.1 3.8 %collective-permute-start.18 = (bf16[1344,2688]{1,0:T(8,128)(2,1)}, bf16[1344,2688]{1,0:T(8,128)(2,1)S(1)}, u32[]{:S(2)}, u32[]{:S(2)}) collective-permute-start(bf16[1344,2688]{1,0:T(8,128)(2,1)} %pad_maximum_fusion.refs_0_), channel_id=1, source_target_pairs={{0,96},{1,25},{2,98},{3,27},{4,100},{5,29},{6,102},{7,31},{8,104},... | collective-permute-start | bytes 21676040 | tf_op jit(solution)/shard_map/ppermute | solution.py:90
  72.9 3.8 %collective-permute-start.4 = (bf16[2,80,672]{2,1,0:T(8,128)(2,1)S(1)}, bf16[2,80,672]{2,1,0:T(8,128)(2,1)S(1)}, u32[]{:S(2)}, u32[]{:S(2)}) collective-permute-start(bf16[2,80,672]{2,1,0:T(8,128)(2,1)S(1)} %get-tuple-element.66), channel_id=1, source_target_pairs={{0,6},{2,0},{4,2},{6,4},{1,7},{3,1},{5,3},{7,5},{8,14},{10,8},{12,... | collective-permute-start | bytes 645128 | tf_op jit(solution)/shard_map/ppermute | solution.py:34
  76.8 3.6 %collective-permute-done.4 = bf16[2,80,672]{2,1,0:T(8,128)(2,1)S(1)} collective-permute-done((bf16[2,80,672]{2,1,0:T(8,128)(2,1)S(1)}, bf16[2,80,672]{2,1,0:T(8,128)(2,1)S(1)}, u32[]{:S(2)}, u32[]{:S(2)}) %collective-permute-start.4) | collective-permute-done | bytes 215072 | tf_op jit(solution)/shard_map/ppermute | solution.py:34
  80.4 2.1 collective-permute-start.5
  82.6 4.4 %collective-permute-done.5 = bf16[2,80,672]{2,1,0:T(8,128)(2,1)S(1)} collective-permute-done((bf16[2,80,672]{2,1,0:T(8,128)(2,1)S(1)}, bf16[2,80,672]{2,1,0:T(8,128)(2,1)S(1)}, u32[]{:S(2)}, u32[]{:S(2)}) %collective-permute-start.5) | collective-permute-done | bytes 215072 | tf_op jit(solution)/shard_map/ppermute | solution.py:34
  86.9 1.5 collective-permute-start.6
  88.5 6.0 %collective-permute-done.6 = bf16[2,80,672]{2,1,0:T(8,128)(2,1)S(1)} collective-permute-done((bf16[2,80,672]{2,1,0:T(8,128)(2,1)S(1)}, bf16[2,80,672]{2,1,0:T(8,128)(2,1)S(1)}, u32[]{:S(2)}, u32[]{:S(2)}) %collective-permute-start.6) | collective-permute-done | bytes 215072 | tf_op jit(solution)/shard_map/ppermute | solution.py:34
  94.7 7.3 %project.1 = (bf16[64,5376]{1,0:T(8,128)(2,1)S(1)}, bf16[32,5376]{1,0:T(8,128)(2,1)S(1)}, bf16[32,5376]{1,0:T(8,128)(2,1)S(1)}, bf16[32,5376]{1,0:T(8,128)(2,1)S...) custom-call(bf16[256,512]{1,0:T(8,128)(2,1)S(1)} %bitcast.129, ...), custom_call_target="tpu_custom_call" | custom-call | bytes 1000 | tf_op jit(solution)/shard_map/project/pallas_call | solution.py:147
  102.3 2.5 %collective-permute-start.11 = (bf16[32,5376]{1,0:T(8,128)(2,1)S(1)}, bf16[32,5376]{1,0:T(8,128)(2,1)S(1)}, u32[]{:S(2)}, u32[]{:S(2)}) collective-permute-start(bf16[32,5376]{1,0:T(8,128)(2,1)S(1)} %get-tuple-element.41), channel_id=1, source_target_pairs={{0,6},{2,0},{4,2},{6,4},{1,7},{3,1},{5,3},{7,5},{8,14},{10,8},{12,... | collective-permute-start | bytes 1032200 | tf_op jit(solution)/shard_map/ppermute | solution.py:34
  104.8 5.0 %collective-permute-done.8 = bf16[32,5376]{1,0:T(8,128)(2,1)S(1)} collective-permute-done((bf16[32,5376]{1,0:T(8,128)(2,1)S(1)}, bf16[32,5376]{1,0:T(8,128)(2,1)S(1)}, u32[]{:S(2)}, u32[]{:S(2)}) %collective-permute-start.8) | collective-permute-done | bytes 344096 | tf_op jit(solution)/shard_map/ppermute | solution.py:34
  110.1 8.1 %collective-permute-done.12 = bf16[32,5376]{1,0:T(8,128)(2,1)S(1)} collective-permute-done((bf16[32,5376]{1,0:T(8,128)(2,1)S(1)}, bf16[32,5376]{1,0:T(8,128)(2,1)S(1)}, u32[]{:S(2)}, u32[]{:S(2)}) %collective-permute-start.12) | collective-permute-done | bytes 344096 | tf_op jit(solution)/shard_map/ppermute | solution.py:34
  118.3 2.9 %collective-permute-start.13 = (bf16[32,5376]{1,0:T(8,128)(2,1)S(1)}, bf16[32,5376]{1,0:T(8,128)(2,1)S(1)}, u32[]{:S(2)}, u32[]{:S(2)}) collective-permute-start(bf16[32,5376]{1,0:T(8,128)(2,1)S(1)} %add_convert_fusion), channel_id=1, source_target_pairs={{0,6},{2,0},{4,2},{6,4},{1,7},{3,1},{5,3},{7,5},{8,14},{10,8},{12,... | collective-permute-start | bytes 1032200 | tf_op jit(solution)/shard_map/ppermute | solution.py:34
  121.2 4.8 %collective-permute-done.9.at_ref = bf16[32,5376]{1,0:T(8,128)(2,1)S(1)} collective-permute-done((bf16[32,5376]{1,0:T(8,128)(2,1)S(1)}, bf16[32,5376]{1,0:T(8,128)(2,1)S(1)}, u32[]{:S(2)}, u32[]{:S(2)}) %collective-permute-start.9) | collective-permute-done | bytes 344096 | tf_op jit(solution)/shard_map/ppermute | solution.py:34
  126.0 2.0 collective-permute-done.13.bb_ref
  129.2 1.5 collective-permute-start.20
  130.7 14.0 %collective-permute-start.23 = (bf16[64,5376]{1,0:T(8,128)(2,1)S(1)}, bf16[64,5376]{1,0:T(8,128)(2,1)S(1)}, u32[]{:S(2)}, u32[]{:S(2)}) collective-permute-start(bf16[64,5376]{1,0:T(8,128)(2,1)S(1)} %get-tuple-element.47.refs_0_), channel_id=1, source_target_pairs={{0,1},{1,0},{2,3},{3,2},{4,5},{5,4},{6,7},{7,6},{8,9},{9,8},{10,11... | collective-permute-start | bytes 2064392 | tf_op jit(solution)/shard_map/ppermute | solution.py:34
  144.7 3.0 %collective-permute-start.22 = (bf16[32,5376]{1,0:T(8,128)(2,1)S(1)}, bf16[32,5376]{1,0:T(8,128)(2,1)S(1)}, u32[]{:S(2)}, u32[]{:S(2)}) collective-permute-start(bf16[32,5376]{1,0:T(8,128)(2,1)S(1)} %slice.105), channel_id=1, source_target_pairs={{0,6},{2,0},{4,2},{6,4},{1,7},{3,1},{5,3},{7,5},{8,14},{10,8},{12,... | collective-permute-start | bytes 1032200 | tf_op jit(solution)/shard_map/ppermute | solution.py:34
  147.8 13.0 %collective-permute-start.25 = (bf16[64,5376]{1,0:T(8,128)(2,1)S(1)}, bf16[64,5376]{1,0:T(8,128)(2,1)S(1)}, u32[]{:S(2)}, u32[]{:S(2)}) collective-permute-start(bf16[64,5376]{1,0:T(8,128)(2,1)S(1)} %collective-permute-done.20.refs_2_), channel_id=1, source_target_pairs={{0,1},{1,0},{2,3},{3,2},{4,5},{5,4},{6,7},{7,6},{8,9},{9,8},{10,11... | collective-permute-start | bytes 2064392 | tf_op jit(solution)/shard_map/ppermute | solution.py:34
  160.8 4.6 %collective-permute-start.27 = (bf16[32,5376]{1,0:T(8,128)(2,1)S(1)}, bf16[32,5376]{1,0:T(8,128)(2,1)S(1)}, u32[]{:S(2)}, u32[]{:S(2)}) collective-permute-start(bf16[32,5376]{1,0:T(8,128)(2,1)S(1)} %collective-permute-done.22.refs_4_), channel_id=1, source_target_pairs={{0,1},{1,0},{2,3},{3,2},{4,5},{5,4},{6,7},{7,6},{8,9},{9,8},{10,11... | collective-permute-start | bytes 1032200 | tf_op jit(solution)/shard_map/ppermute | solution.py:34
  165.4 3.8 %collective-permute-start.24 = (bf16[64,5376]{1,0:T(8,128)(2,1)S(1)}, bf16[64,5376]{1,0:T(8,128)(2,1)S(1)}, u32[]{:S(2)}, u32[]{:S(2)}) collective-permute-start(bf16[64,5376]{1,0:T(8,128)(2,1)S(1)} %collective-permute-done.19.refs_1_), channel_id=1, source_target_pairs={{0,1},{1,0},{2,3},{3,2},{4,5},{5,4},{6,7},{7,6},{8,9},{9,8},{10,11... | collective-permute-start | bytes 2064392 | tf_op jit(solution)/shard_map/ppermute | solution.py:34
  169.2 2.3 collective-permute-done.26.refs_8_
  171.4 5.1 %order.1.refs_4_.refs_3_ = bf16[512,5632]{1,0:T(8,128)(2,1)S(1)} custom-call(bf16[64,5376]{1,0:T(8,128)(2,1)S(1)} %get-tuple-element.47.refs_0_, bf16[64,5376]{1,0:T(8,128)(2,1)S(1)} %collective-permute-done.19.refs_1_, bf16[64,5376]{1,0:T(8,128)(2,1)S(1)} %collective-permute-done.20.refs_2_, bf16[32,5376]{1,0:T(8,128)(2,1)S(1)} %collective-permute-done.21.refs_3_, ...), custom_call_target="tpu_custom_call" | custom-call | bytes 1000 | tf_op jit(solution)/shard_map/order/pallas_call | solution.py:241
  176.5 2.3 slice.91
  178.8 1.3 copy-done
  180.1 5.7 %slice.90 = bf16[672,2688]{1,0:T(8,128)(2,1)} slice(bf16[1344,2688]{1,0:T(8,128)(2,1)} %collective-permute-done.17.refs_1_), slice={[0:672], [0:2688]} | slice | bytes 7225344 | tf_op jit(solution)/shard_map/slice | solution.py:435
  185.9 2.7 %collective-permute-start.33 = (bf16[672,2688]{1,0:T(8,128)(2,1)}, bf16[672,2688]{1,0:T(8,128)(2,1)S(1)}, u32[]{:S(2)}, u32[]{:S(2)}) collective-permute-start(bf16[672,2688]{1,0:T(8,128)(2,1)} %slice.91), channel_id=1, source_target_pairs={{0,96},{1,25},{2,98},{3,27},{4,100},{5,29},{6,102},{7,31},{8,104},... | collective-permute-start | bytes 10838024 | tf_op jit(solution)/shard_map/ppermute | solution.py:90
  190.1 21.8 %near.1.refs_4_ = f32[512,2688]{1,0:T(8,128)} custom-call(bf16[1344,2688]{1,0:T(8,128)(2,1)} %pad_maximum_fusion.refs_0_, bf16[1344,2688]{1,0:T(8,128)(2,1)} %collective-permute-done.17.refs_1_, bf16[1344,2688]{1,0:T(8,128)(2,1)} %copy-done.11, s32[4]{0:T(128)} %copy-done.10, bf16[512,5632]{1,0:T(8,128)(2,1)} %copy-done), custom_call_target="tpu_custom_call" | custom-call | bytes 1000 | tf_op jit(solution)/shard_map/near/pallas_call | solution.py:298
  214.2 1.5 collective-permute-start.30
  215.7 1.2 collective-permute-start.29
  216.9 11.8 %collective-permute-done.32.refs_0_ = bf16[672,2688]{1,0:T(8,128)(2,1)S(1)} collective-permute-done((bf16[672,2688]{1,0:T(8,128)(2,1)}, bf16[672,2688]{1,0:T(8,128)(2,1)S(1)}, u32[]{:S(2)}, u32[]{:S(2)}) %collective-permute-start.32) | collective-permute-done | bytes 3612704 | tf_op jit(solution)/shard_map/ppermute | solution.py:90
  228.7 1.8 copy-done.13
  230.5 1.8 copy-done.14
  232.2 13.4 %far.1 = bf16[1344,512]{1,0:T(8,128)(2,1)} custom-call(bf16[672,2688]{1,0:T(8,128)(2,1)} %copy-done.13, bf16[672,2688]{1,0:T(8,128)(2,1)} %copy-done.14, s32[4]{0:T(128)} %copy-done.10, bf16[512,5632]{1,0:T(8,128)(2,1)} %copy-done, f32[512,2688]{1,0:T(8,128)} %near.1.refs_4_), custom_call_target="tpu_custom_call" | custom-call | flops 3699376128 | bytes 12730368 | tf_op jit(solution)/shard_map/far/pallas_call | solution.py:342
  (116 shorter events, 17.4 us)
Async XLA Ops:
  2.6 1.2 copy-start.1
  3.8 1.2 copy-start.2
  5.0 37.2 %copy-start.16 = (f32[672]{0:T(1024)S(1)}, f32[672]{0:T(1024)}, u32[]{:S(2)}) copy-start(f32[672]{0:T(1024)} %param.17) | copy-start | bytes 8068
  5.0 38.6 %copy-start.15 = (bf16[512,672]{0,1:T(8,128)(2,1)S(1)}, bf16[512,672]{0,1:T(8,128)(2,1)}, u32[]{:S(2)}) copy-start(bf16[512,672]{0,1:T(8,128)(2,1)} %param.15) | copy-start | bytes 2064388
  5.4 44.5 %copy-start.3 = (bf16[512,512]{1,0:T(8,128)(2,1)S(1)}, bf16[512,512]{1,0:T(8,128)(2,1)}, u32[]{:S(2)}) copy-start(bf16[512,512]{1,0:T(8,128)(2,1)} %q_ref.1) | copy-start | bytes 1572868
  5.4 34.6 %collective-permute-start.15 = (bf16[336,2688]{1,0:T(8,128)(2,1)S(1)}, bf16[336,2688]{1,0:T(8,128)(2,1)}, u32[]{:S(2)}, u32[]{:S(2)}) collective-permute-start(bf16[336,2688]{1,0:T(8,128)(2,1)S(1)} %pack.1), channel_id=1, source_target_pairs={{0,24},{1,97},{2,26},{3,99},{4,28},{5,101},{6,30},{7,103},{8,0},{9... | collective-permute-start | bytes 5419016 | tf_op jit(solution)/shard_map/ppermute | solution.py:90
  9.1 13.9 %collective-permute-start = (bf16[512,512]{1,0:T(8,128)(2,1)S(1)}, bf16[512,512]{1,0:T(8,128)(2,1)S(1)}, u32[]{:S(2)}, u32[]{:S(2)}) collective-permute-start(bf16[512,512]{1,0:T(8,128)(2,1)S(1)} %pair.1.kv0_ref), channel_id=1, source_target_pairs={{0,8},{8,16},{16,24},{24,32},{32,40},{40,48},{48,56},{56,64},{64,7... | collective-permute-start | bytes 1572872 | tf_op jit(solution)/shard_map/ppermute | solution.py:39
  22.9 15.7 %collective-permute-start.1 = (bf16[512,512]{1,0:T(8,128)(2,1)S(1)}, bf16[512,512]{1,0:T(8,128)(2,1)S(1)}, u32[]{:S(2)}, u32[]{:S(2)}) collective-permute-start(bf16[512,512]{1,0:T(8,128)(2,1)S(1)} %collective-permute-done.kv1_ref), channel_id=1, source_target_pairs={{0,8},{8,16},{16,24},{24,32},{32,40},{40,48},{48,56},{56,64},{64,7... | collective-permute-start | bytes 1572872 | tf_op jit(solution)/shard_map/ppermute | solution.py:39
  28.0 66.7 %collective-permute-start.7 = (bf16[512,5376]{1,0:T(8,128)(2,1)}, bf16[512,5376]{1,0:T(8,128)(2,1)}, u32[]{:S(2)}, u32[]{:S(2)}) collective-permute-start(bf16[512,5376]{1,0:T(8,128)(2,1)} %w_ref.1), channel_id=1, source_target_pairs={{0,1},{1,0},{2,3},{3,2},{4,5},{5,4},{6,7},{7,6},{8,9},{9,8},{10,11... | collective-permute-start | bytes 16515080 | tf_op jit(solution)/shard_map/ppermute | solution.py:34
  39.5 23.4 %collective-permute-start.14 = (bf16[336,2688]{1,0:T(8,128)(2,1)S(1)}, bf16[336,2688]{1,0:T(8,128)(2,1)}, u32[]{:S(2)}, u32[]{:S(2)}) collective-permute-start(bf16[336,2688]{1,0:T(8,128)(2,1)S(1)} %pack.1), channel_id=1, source_target_pairs={{0,8},{1,33},{2,10},{3,35},{4,12},{5,37},{6,14},{7,39},{8,16},{9,4... | collective-permute-start | bytes 5419016 | tf_op jit(solution)/shard_map/ppermute | solution.py:90
  40.1 22.8 %collective-permute-start.16 = (bf16[336,2688]{1,0:T(8,128)(2,1)}, bf16[336,2688]{1,0:T(8,128)(2,1)}, u32[]{:S(2)}, u32[]{:S(2)}) collective-permute-start(bf16[336,2688]{1,0:T(8,128)(2,1)} %collective-permute-done.15), channel_id=1, source_target_pairs={{0,24},{1,97},{2,26},{3,99},{4,28},{5,101},{6,30},{7,103},{8,0},{9... | collective-permute-start | bytes 5419016 | tf_op jit(solution)/shard_map/ppermute | solution.py:90
  47.1 10.6 %collective-permute-start.3 = (bf16[4,80,672]{2,1,0:T(8,128)(2,1)}, bf16[4,80,672]{2,1,0:T(8,128)(2,1)}, u32[]{:S(2)}, u32[]{:S(2)}) collective-permute-start(bf16[4,80,672]{2,1,0:T(8,128)(2,1)} %fusion.6), channel_id=1, source_target_pairs={{0,1},{1,0},{2,3},{3,2},{4,5},{5,4},{6,7},{7,6},{8,9},{9,8},{10,11... | collective-permute-start | bytes 1290248 | tf_op jit(solution)/shard_map/ppermute | solution.py:34
  49.9 1.0 copy-start.5
  52.0 119.4 %copy-start.10 = (s32[4]{0:T(128)}, s32[4]{0:T(128)S(1)}, u32[]{:S(2)}) copy-start(s32[4]{0:T(128)S(1)} %pad_add_fusion.at_ref.refs_10_.refs_3_.refs_2_) | copy-start | bytes 52
  52.0 5.7 %copy-start.12 = (bf16[512,672]{1,0:T(8,128)(2,1)S(1)}, bf16[512,672]{1,0:T(8,128)(2,1)}, u32[]{:S(2)}) copy-start(bf16[512,672]{1,0:T(8,128)(2,1)} %copy.23) | copy-start | bytes 2064388
  57.6 37.1 %collective-permute-start.2 = (bf16[256,512]{1,0:T(8,128)(2,1)S(1)}, bf16[256,512]{1,0:T(8,128)(2,1)S(1)}, u32[]{:S(2)}, u32[]{:S(2)}) collective-permute-start(bf16[256,512]{1,0:T(8,128)(2,1)S(1)} %bitcast.134), channel_id=1, source_target_pairs={{0,1},{1,0},{2,3},{3,2},{4,5},{5,4},{6,7},{7,6},{8,9},{9,8},{10,11... | collective-permute-start | bytes 786440 | tf_op jit(solution)/shard_map/ppermute | solution.py:34
  59.0 35.7 %slice-start = ((s8[5505024]{0:T(1024)(128)(4,1)}), s8[4194304]{0:T(1024)(128)(4,1)S(1)}, s32[]{:S(2)}) async-start(s8[5505024]{0:T(1024)(128)(4,1)} %bitcast.124), calls=%async_computation | async-start | bytes 8388608
  59.5 35.1 %slice-start.1 = ((s8[5505024]{0:T(1024)(128)(4,1)}), s8[1310720]{0:T(1024)(128)(4,1)S(1)}, s32[]{:S(2)}) async-start(s8[5505024]{0:T(1024)(128)(4,1)} %bitcast.124), calls=%async_computation.1 | async-start | bytes 2621440
  69.1 107.4 %collective-permute-start.18 = (bf16[1344,2688]{1,0:T(8,128)(2,1)}, bf16[1344,2688]{1,0:T(8,128)(2,1)S(1)}, u32[]{:S(2)}, u32[]{:S(2)}) collective-permute-start(bf16[1344,2688]{1,0:T(8,128)(2,1)} %pad_maximum_fusion.refs_0_), channel_id=1, source_target_pairs={{0,96},{1,25},{2,98},{3,27},{4,100},{5,29},{6,102},{7,31},{8,104},... | collective-permute-start | bytes 21676040 | tf_op jit(solution)/shard_map/ppermute | solution.py:90
  72.9 103.6 %collective-permute-start.17 = (bf16[1344,2688]{1,0:T(8,128)(2,1)}, bf16[1344,2688]{1,0:T(8,128)(2,1)}, u32[]{:S(2)}, u32[]{:S(2)}) collective-permute-start(bf16[1344,2688]{1,0:T(8,128)(2,1)} %pad_maximum_fusion.refs_0_), channel_id=1, source_target_pairs={{0,32},{1,9},{2,34},{3,11},{4,36},{5,13},{6,38},{7,15},{8,40},{9,1... | collective-permute-start | bytes 21676040 | tf_op jit(solution)/shard_map/ppermute | solution.py:90
  72.9 7.5 %collective-permute-start.4 = (bf16[2,80,672]{2,1,0:T(8,128)(2,1)S(1)}, bf16[2,80,672]{2,1,0:T(8,128)(2,1)S(1)}, u32[]{:S(2)}, u32[]{:S(2)}) collective-permute-start(bf16[2,80,672]{2,1,0:T(8,128)(2,1)S(1)} %get-tuple-element.66), channel_id=1, source_target_pairs={{0,6},{2,0},{4,2},{6,4},{1,7},{3,1},{5,3},{7,5},{8,14},{10,8},{12,... | collective-permute-start | bytes 645128 | tf_op jit(solution)/shard_map/ppermute | solution.py:34
  80.4 6.6 %collective-permute-start.5 = (bf16[2,80,672]{2,1,0:T(8,128)(2,1)S(1)}, bf16[2,80,672]{2,1,0:T(8,128)(2,1)S(1)}, u32[]{:S(2)}, u32[]{:S(2)}) collective-permute-start(bf16[2,80,672]{2,1,0:T(8,128)(2,1)S(1)} %get-tuple-element.65), channel_id=1, source_target_pairs={{0,4},{2,6},{4,0},{6,2},{1,5},{3,7},{5,1},{7,3},{8,12},{10,14},{12... | collective-permute-start | bytes 645128 | tf_op jit(solution)/shard_map/ppermute | solution.py:34
  86.9 7.5 %collective-permute-start.6 = (bf16[2,80,672]{2,1,0:T(8,128)(2,1)S(1)}, bf16[2,80,672]{2,1,0:T(8,128)(2,1)S(1)}, u32[]{:S(2)}, u32[]{:S(2)}) collective-permute-start(bf16[2,80,672]{2,1,0:T(8,128)(2,1)S(1)} %get-tuple-element.64), channel_id=1, source_target_pairs={{0,2},{2,4},{4,6},{6,0},{1,3},{3,5},{5,7},{7,1},{8,10},{10,12},{12... | collective-permute-start | bytes 645128 | tf_op jit(solution)/shard_map/ppermute | solution.py:34
  102.0 7.8 %collective-permute-start.8 = (bf16[32,5376]{1,0:T(8,128)(2,1)S(1)}, bf16[32,5376]{1,0:T(8,128)(2,1)S(1)}, u32[]{:S(2)}, u32[]{:S(2)}) collective-permute-start(bf16[32,5376]{1,0:T(8,128)(2,1)S(1)} %get-tuple-element.39), channel_id=1, source_target_pairs={{0,2},{2,4},{4,6},{6,0},{1,3},{3,5},{5,7},{7,1},{8,10},{10,12},{12... | collective-permute-start | bytes 1032200 | tf_op jit(solution)/shard_map/ppermute | solution.py:34
  102.1 16.2 %collective-permute-start.10 = (bf16[32,5376]{1,0:T(8,128)(2,1)S(1)}, bf16[32,5376]{1,0:T(8,128)(2,1)S(1)}, u32[]{:S(2)}, u32[]{:S(2)}) collective-permute-start(bf16[32,5376]{1,0:T(8,128)(2,1)S(1)} %get-tuple-element.40), channel_id=1, source_target_pairs={{0,2},{2,4},{4,6},{6,0},{1,3},{3,5},{5,7},{7,1},{8,10},{10,12},{12... | collective-permute-start | bytes 1032200 | tf_op jit(solution)/shard_map/ppermute | solution.py:34
  102.3 18.9 %collective-permute-start.11 = (bf16[32,5376]{1,0:T(8,128)(2,1)S(1)}, bf16[32,5376]{1,0:T(8,128)(2,1)S(1)}, u32[]{:S(2)}, u32[]{:S(2)}) collective-permute-start(bf16[32,5376]{1,0:T(8,128)(2,1)S(1)} %get-tuple-element.41), channel_id=1, source_target_pairs={{0,6},{2,0},{4,2},{6,4},{1,7},{3,1},{5,3},{7,5},{8,14},{10,8},{12,... | collective-permute-start | bytes 1032200 | tf_op jit(solution)/shard_map/ppermute | solution.py:34
  109.8 8.4 %collective-permute-start.12 = (bf16[32,5376]{1,0:T(8,128)(2,1)S(1)}, bf16[32,5376]{1,0:T(8,128)(2,1)S(1)}, u32[]{:S(2)}, u32[]{:S(2)}) collective-permute-start(bf16[32,5376]{1,0:T(8,128)(2,1)S(1)} %get-tuple-element.43), channel_id=1, source_target_pairs={{0,6},{2,0},{4,2},{6,4},{1,7},{3,1},{5,3},{7,5},{8,14},{10,8},{12,... | collective-permute-start | bytes 1032200 | tf_op jit(solution)/shard_map/ppermute | solution.py:34
  118.2 7.9 %collective-permute-start.9 = (bf16[32,5376]{1,0:T(8,128)(2,1)S(1)}, bf16[32,5376]{1,0:T(8,128)(2,1)S(1)}, u32[]{:S(2)}, u32[]{:S(2)}) collective-permute-start(bf16[32,5376]{1,0:T(8,128)(2,1)S(1)} %add_convert_fusion.1), channel_id=1, source_target_pairs={{0,2},{2,4},{4,6},{6,0},{1,3},{3,5},{5,7},{7,1},{8,10},{10,12},{12... | collective-permute-start | bytes 1032200 | tf_op jit(solution)/shard_map/ppermute | solution.py:34
  118.3 9.8 %collective-permute-start.13 = (bf16[32,5376]{1,0:T(8,128)(2,1)S(1)}, bf16[32,5376]{1,0:T(8,128)(2,1)S(1)}, u32[]{:S(2)}, u32[]{:S(2)}) collective-permute-start(bf16[32,5376]{1,0:T(8,128)(2,1)S(1)} %add_convert_fusion), channel_id=1, source_target_pairs={{0,6},{2,0},{4,2},{6,4},{1,7},{3,1},{5,3},{7,5},{8,14},{10,8},{12,... | collective-permute-start | bytes 1032200 | tf_op jit(solution)/shard_map/ppermute | solution.py:34
  129.2 15.5 %collective-permute-start.20 = (bf16[64,5376]{1,0:T(8,128)(2,1)S(1)}, bf16[64,5376]{1,0:T(8,128)(2,1)S(1)}, u32[]{:S(2)}, u32[]{:S(2)}) collective-permute-start(bf16[64,5376]{1,0:T(8,128)(2,1)S(1)} %get-tuple-element.47.refs_0_), channel_id=1, source_target_pairs={{0,6},{2,0},{4,2},{6,4},{1,7},{3,1},{5,3},{7,5},{8,14},{10,8},{12,... | collective-permute-start | bytes 2064392 | tf_op jit(solution)/shard_map/ppermute | solution.py:34
  130.7 17.0 %collective-permute-start.19 = (bf16[64,5376]{1,0:T(8,128)(2,1)S(1)}, bf16[64,5376]{1,0:T(8,128)(2,1)S(1)}, u32[]{:S(2)}, u32[]{:S(2)}) collective-permute-start(bf16[64,5376]{1,0:T(8,128)(2,1)S(1)} %get-tuple-element.47.refs_0_), channel_id=1, source_target_pairs={{0,2},{2,4},{4,6},{6,0},{1,3},{3,5},{5,7},{7,1},{8,10},{10,12},{12... | collective-permute-start | bytes 2064392 | tf_op jit(solution)/shard_map/ppermute | solution.py:34
  130.7 17.1 %collective-permute-start.23 = (bf16[64,5376]{1,0:T(8,128)(2,1)S(1)}, bf16[64,5376]{1,0:T(8,128)(2,1)S(1)}, u32[]{:S(2)}, u32[]{:S(2)}) collective-permute-start(bf16[64,5376]{1,0:T(8,128)(2,1)S(1)} %get-tuple-element.47.refs_0_), channel_id=1, source_target_pairs={{0,1},{1,0},{2,3},{3,2},{4,5},{5,4},{6,7},{7,6},{8,9},{9,8},{10,11... | collective-permute-start | bytes 2064392 | tf_op jit(solution)/shard_map/ppermute | solution.py:34
  144.7 16.1 %collective-permute-start.22 = (bf16[32,5376]{1,0:T(8,128)(2,1)S(1)}, bf16[32,5376]{1,0:T(8,128)(2,1)S(1)}, u32[]{:S(2)}, u32[]{:S(2)}) collective-permute-start(bf16[32,5376]{1,0:T(8,128)(2,1)S(1)} %slice.105), channel_id=1, source_target_pairs={{0,6},{2,0},{4,2},{6,4},{1,7},{3,1},{5,3},{7,5},{8,14},{10,8},{12,... | collective-permute-start | bytes 1032200 | tf_op jit(solution)/shard_map/ppermute | solution.py:34
  147.8 17.6 %collective-permute-start.21 = (bf16[32,5376]{1,0:T(8,128)(2,1)S(1)}, bf16[32,5376]{1,0:T(8,128)(2,1)S(1)}, u32[]{:S(2)}, u32[]{:S(2)}) collective-permute-start(bf16[32,5376]{1,0:T(8,128)(2,1)S(1)} %slice.104), channel_id=1, source_target_pairs={{0,2},{2,4},{4,6},{6,0},{1,3},{3,5},{5,7},{7,1},{8,10},{10,12},{12... | collective-permute-start | bytes 1032200 | tf_op jit(solution)/shard_map/ppermute | solution.py:34
  147.8 21.3 %collective-permute-start.25 = (bf16[64,5376]{1,0:T(8,128)(2,1)S(1)}, bf16[64,5376]{1,0:T(8,128)(2,1)S(1)}, u32[]{:S(2)}, u32[]{:S(2)}) collective-permute-start(bf16[64,5376]{1,0:T(8,128)(2,1)S(1)} %collective-permute-done.20.refs_2_), channel_id=1, source_target_pairs={{0,1},{1,0},{2,3},{3,2},{4,5},{5,4},{6,7},{7,6},{8,9},{9,8},{10,11... | collective-permute-start | bytes 2064392 | tf_op jit(solution)/shard_map/ppermute | solution.py:34
  160.8 8.4 %collective-permute-start.27 = (bf16[32,5376]{1,0:T(8,128)(2,1)S(1)}, bf16[32,5376]{1,0:T(8,128)(2,1)S(1)}, u32[]{:S(2)}, u32[]{:S(2)}) collective-permute-start(bf16[32,5376]{1,0:T(8,128)(2,1)S(1)} %collective-permute-done.22.refs_4_), channel_id=1, source_target_pairs={{0,1},{1,0},{2,3},{3,2},{4,5},{5,4},{6,7},{7,6},{8,9},{9,8},{10,11... | collective-permute-start | bytes 1032200 | tf_op jit(solution)/shard_map/ppermute | solution.py:34
  165.4 6.1 %collective-permute-start.24 = (bf16[64,5376]{1,0:T(8,128)(2,1)S(1)}, bf16[64,5376]{1,0:T(8,128)(2,1)S(1)}, u32[]{:S(2)}, u32[]{:S(2)}) collective-permute-start(bf16[64,5376]{1,0:T(8,128)(2,1)S(1)} %collective-permute-done.19.refs_1_), channel_id=1, source_target_pairs={{0,1},{1,0},{2,3},{3,2},{4,5},{5,4},{6,7},{7,6},{8,9},{9,8},{10,11... | collective-permute-start | bytes 2064392 | tf_op jit(solution)/shard_map/ppermute | solution.py:34
  169.2 2.3 collective-permute-start.26
  176.5 3.6 %copy-start = (bf16[512,5632]{1,0:T(8,128)(2,1)}, bf16[512,5632]{1,0:T(8,128)(2,1)S(1)}, u32[]{:S(2)}) copy-start(bf16[512,5632]{1,0:T(8,128)(2,1)S(1)} %order.1.refs_4_.refs_3_) | copy-start | bytes 17301508
  176.5 9.4 %copy-start.11 = (bf16[1344,2688]{1,0:T(8,128)(2,1)}, bf16[1344,2688]{1,0:T(8,128)(2,1)S(1)}, u32[]{:S(2)}) copy-start(bf16[1344,2688]{1,0:T(8,128)(2,1)S(1)} %collective-permute-done.18.refs_2_) | copy-start | bytes 21676036
  185.9 42.8 %collective-permute-start.32 = (bf16[672,2688]{1,0:T(8,128)(2,1)}, bf16[672,2688]{1,0:T(8,128)(2,1)S(1)}, u32[]{:S(2)}, u32[]{:S(2)}) collective-permute-start(bf16[672,2688]{1,0:T(8,128)(2,1)} %slice.90), channel_id=1, source_target_pairs={{0,32},{1,9},{2,34},{3,11},{4,36},{5,13},{6,38},{7,15},{8,40},{9,1... | collective-permute-start | bytes 10838024 | tf_op jit(solution)/shard_map/ppermute | solution.py:90
  185.9 42.8 %collective-permute-start.33 = (bf16[672,2688]{1,0:T(8,128)(2,1)}, bf16[672,2688]{1,0:T(8,128)(2,1)S(1)}, u32[]{:S(2)}, u32[]{:S(2)}) collective-permute-start(bf16[672,2688]{1,0:T(8,128)(2,1)} %slice.91), channel_id=1, source_target_pairs={{0,96},{1,25},{2,98},{3,27},{4,100},{5,29},{6,102},{7,31},{8,104},... | collective-permute-start | bytes 10838024 | tf_op jit(solution)/shard_map/ppermute | solution.py:90
  189.3 22.5 %collective-permute-start.28 = (bf16[4,64,672]{2,1,0:T(8,128)(2,1)}, bf16[4,64,672]{2,1,0:T(8,128)(2,1)}, u32[]{:S(2)}, u32[]{:S(2)}) collective-permute-start(bf16[4,64,672]{2,1,0:T(8,128)(2,1)} %select_bitcast_fusion.2), channel_id=1, source_target_pairs={{0,1},{1,0},{2,3},{3,2},{4,5},{5,4},{6,7},{7,6},{8,9},{9,8},{10,11... | collective-permute-start | bytes 1032200 | tf_op jit(solution)/shard_map/ppermute | solution.py:34
  214.2 31.5 %collective-permute-start.31 = (bf16[2,64,672]{2,1,0:T(8,128)(2,1)}, bf16[2,64,672]{2,1,0:T(8,128)(2,1)S(1)}, u32[]{:S(2)}, u32[]{:S(2)}) collective-permute-start(bf16[2,64,672]{2,1,0:T(8,128)(2,1)} %get-tuple-element.67), channel_id=1, source_target_pairs={{0,2},{2,4},{4,6},{6,0},{1,3},{3,5},{5,7},{7,1},{8,10},{10,12},{12... | collective-permute-start | bytes 516104 | tf_op jit(solution)/shard_map/ppermute | solution.py:34
  214.2 31.5 %collective-permute-start.30 = (bf16[2,64,672]{2,1,0:T(8,128)(2,1)}, bf16[2,64,672]{2,1,0:T(8,128)(2,1)S(1)}, u32[]{:S(2)}, u32[]{:S(2)}) collective-permute-start(bf16[2,64,672]{2,1,0:T(8,128)(2,1)} %get-tuple-element.68), channel_id=1, source_target_pairs={{0,4},{2,6},{4,0},{6,2},{1,5},{3,7},{5,1},{7,3},{8,12},{10,14},{12... | collective-permute-start | bytes 516104 | tf_op jit(solution)/shard_map/ppermute | solution.py:34
  215.7 30.0 %collective-permute-start.29 = (bf16[2,64,672]{2,1,0:T(8,128)(2,1)S(1)}, bf16[2,64,672]{2,1,0:T(8,128)(2,1)S(1)}, u32[]{:S(2)}, u32[]{:S(2)}) collective-permute-start(bf16[2,64,672]{2,1,0:T(8,128)(2,1)S(1)} %get-tuple-element.69), channel_id=1, source_target_pairs={{0,6},{2,0},{4,2},{6,4},{1,7},{3,1},{5,3},{7,5},{8,14},{10,8},{12,... | collective-permute-start | bytes 516104 | tf_op jit(solution)/shard_map/ppermute | solution.py:34
  228.7 1.8 copy-start.13
  230.5 1.8 copy-start.14
  (5 other events, 4.5 us)

commit v6 on v5

--- a/solution.py
+++ b/solution.py
@@ -255,10 +255,10 @@
     first = jnp.where(c == 0, x, y)
     cols = pl.ds(pl.multiple_of(width * block, 128), width)
     copies = []
-    for i, (array, lo, slot, rel) in enumerate(parts):
+    for i, (array, slot, rel) in enumerate(parts):
         row = pl.multiple_of(1344 * slot + 336 * ((first + rel) % 4), 16)
         copies.append(
-            pltpu.make_async_copy(arrays[array].at[pl.ds(lo, 336), cols], w_ref.at[pl.ds(row, 336)], sems.at[i])
+            pltpu.make_async_copy(arrays[array].at[:, cols], w_ref.at[pl.ds(row, 336)], sems.at[i])
         )
     return copies
 
@@ -284,7 +284,7 @@
 
 def near(rows, where, blocks):
     m = len(blocks)
-    parts = [(g, 336 * k, g, REL[k]) for g in range(3) for k in range(4)]
+    parts = [(4 * g + k, g, REL[k]) for g in range(3) for k in range(4)]
 
     def body(*refs):
         place, n_ref, o_ref, w_ref, sems = refs[m:]
@@ -310,7 +310,7 @@
 
 def far(rows, where, blocks, sums):
     m = len(blocks)
-    parts = [(k // 2, 336 * (k % 2), 0, REL[k]) for k in range(4)]
+    parts = [(k, 0, REL[k]) for k in range(4)]
 
     def body(*refs):
         place, n_ref, s_ref, o_ref, w_ref, acc_ref, sems = refs[m:]
@@ -388,13 +388,13 @@
     gate_weight, kv0 = lax.optimization_barrier((gate_weight, kv0))
     w = pack(gate_weight, up_weight)
     p = ring(w, -1, 0)
+    kv1, w = lax.optimization_barrier((kv1, w))
     kv2 = behind(kv1)
-    kv2, w_late = lax.optimization_barrier((kv2, w))
+    kv2, w_late, p = lax.optimization_barrier((kv2, w, p))
     m = ring(w_late, 1, 0)
     b = ring(p, -1, 0)
     kv2, residual, post_gain = lax.optimization_barrier((kv2, residual, post_gain))
-    group = jnp.concatenate([w, m, p, b], axis=0)
-    prev, following = ring(group, 1, 1), ring(group, -1, 1)
+    prev, following = [ring(w_late, 1, 1)], [ring(w, -1, 1)]
 
     gains = jnp.stack([post_gain, pre_gain])
     high = gains.astype(BF)
@@ -409,33 +409,39 @@
     kid = lax.dynamic_slice_in_dim(padded, start, 3 * TOK, 0)[None, :]
     qid = lax.dynamic_slice_in_dim(doc_ids, start, TOK, 0)[:, None]
 
+    queries, p, following[0] = lax.optimization_barrier((queries, p, following[0]))
     mix = attend(where, queries, kv2, kv1, kv0, qid, kid)
     other_weight = shift(out_weight, "c", 1)
     own, other = mix[0].reshape(256, 512), shift(mix[1].reshape(256, 512), "c", 1)
-    other, mine = lax.optimization_barrier((other, mine))
+    other, m = lax.optimization_barrier((other, m))
     p0, p1t, p1b, p2t, p2b, p3t, p3b = project(own, other, out_weight, other_weight)
 
     up_t = shift(p2t, "z", 1)
     dn_b = shift(p2b, "z", -1)
     a_b = shift(p1b, "z", 1)
     b_t = shift(p3t, "z", -1)
+    up_t, dn_b, mine, m, b, prev, following = lax.optimization_barrier((up_t, dn_b, mine, m, b, prev, following))
+    prev += [ring(v, 1, 1) for v in (m, p, b)]
+    following += [ring(v, -1, 1) for v in (m, p, b)]
     add = lambda p, q: (p.astype(F32) + q.astype(F32)).astype(BF)
     a_t = shift(add(p1t, up_t), "z", 1)
     b_b = shift(add(p3b, dn_b), "z", -1)
+    p0, prev[2], following[2] = lax.optimization_barrier((p0, prev[2], following[2]))
     new, nrm = norm(p0, a_t, a_b, b_t, b_b, mine)
 
     n_m, n_p = shift(nrm, "z", 1), shift(nrm, "z", -1)
+    n_m, n_p, prev[1], following[1] = lax.optimization_barrier((n_m, n_p, prev[1], following[1]))
     pieces = [nrm, n_m, n_p, shift(n_m[:32], "z", 1), shift(n_p[32:], "z", -1)]
     places = [(0, None), (3, None), (1, None), (2, 0), (2, 1)]
     pieces += [shift(piece, "c", 1) for piece in pieces]
     tokens_at = [(dz, dc, part) for dc in range(2) for dz, part in places]
+    pieces, prev[3], following[3] = lax.optimization_barrier((pieces, prev[3], following[3]))
     rows = order(pieces, tokens_at, where)
 
-    prev, following, rows = lax.optimization_barrier((prev, following, rows))
-    last = [ring(prev[:672], 1, 1), ring(following[672:], -1, 1)]
+    last = [ring(prev[0], 1, 1), ring(prev[1], 1, 1), ring(following[2], -1, 1), ring(following[3], -1, 1)]
     new, rows = lax.optimization_barrier((new, rows))
     sent_back = swap(new, z, c)
-    sums = near(rows, where, [group, prev, following])
+    sums = near(rows, where, [w, m, p, b, *prev, *following])
     act = far(rows, where, last, sums)
     sent_back, act = lax.optimization_barrier((sent_back, act))
     new_residual = gather(sent_back, z).reshape(TOK, 672)

time: 248 us -> 234 us (0.944)
  local copies, waits for them, and re-layouts: 27.1 us -> 15.8 us
  waiting for transfers between devices: 72.8 us -> 81.1 us
  other arithmetic: 12.6 us -> 5.1 us
  starting transfers between devices: 78.9 us -> 74.2 us
    ppermute x7 -> x15, waiting for transfers between devices: 15.1 us -> 32.2 us  [ring(): return lax.ppermute(value, ('y', 'x', 'z', 'c'), pairs)]
    ppermute x25, starting transfers between devices: 58.7 us -> 43.8 us  [shift(): return lax.ppermute(value, axis, [(i, (i + by) % n) for i in range(n)])]
    ppermute x7 -> x15, starting transfers between devices: 12.8 us -> 22.2 us  [ring(): return lax.ppermute(value, ('y', 'x', 'z', 'c'), pairs)]
    slice x2 -> x0, local copies, waits for them, and re-layouts: 8 us -> none  [per_device(): last = [ring(prev[:672], 1, 1), ring(following[672:], -1, 1)]]
    concatenate x1 -> x0, other arithmetic: 6.18 us -> none  [per_device(): group = jnp.concatenate([w, m, p, b], axis=0)]
    ppermute x25, waiting for transfers between devices: 36.1 us -> 31.2 us  [shift(): return lax.ppermute(value, axis, [(i, (i + by) % n) for i in range(n)])]
    ppermute x2, waiting for transfers between devices: 21.5 us -> 17.7 us  [behind(): return lax.ppermute(value, ('y', 'x'), [(i, i + 1) for i in range(n - 1)])]
    unnamed x53 -> x57, local copies, waits for them, and re-layouts: 14.2 us -> 13.8 us
  transfers between devices with their start and end apart: 34 -> 42, of which waited for: 12 -> 13; matrix products, arithmetic and copies ran while one was open for 7% -> 3% of each run, Pallas kernels for 22% -> 24%
where the time goes in v6:
time: 234 us; the launch traced here: 233 us
  waiting for transfers between devices  81.1 us (35%)
  starting transfers between devices  74.2 us (32%)
  Pallas kernels  55.4 us (24%)
  local copies, waits for them, and re-layouts  15.8 us (7%)
  other arithmetic  5.1 us (2%)
    ppermute x25, starting transfers between devices, shift(): return lax.ppermute(value, axis, [(i, (i + by) % n) for i in range(n)])  43.8 us
    ppermute x15, waiting for transfers between devices, ring(): return lax.ppermute(value, ('y', 'x', 'z', 'c'), pairs)  32.2 us
    ppermute x25, waiting for transfers between devices, shift(): return lax.ppermute(value, axis, [(i, (i + by) % n) for i in range(n)])  31.2 us
    ppermute x15, starting transfers between devices, ring(): return lax.ppermute(value, ('y', 'x', 'z', 'c'), pairs)  22.2 us
    pallas_call x1, Pallas kernels, near(): pl.pallas_call(body, out_shape=jax.ShapeDtypeStruct((TOK, 2688), F32), gr...  22 us
    ppermute x2, waiting for transfers between devices, behind(): return lax.ppermute(value, ('y', 'x'), [(i, i + 1) for i in range(n - 1)])  17.7 us
    unnamed x57, local copies, waits for them, and re-layouts  13.8 us
    pallas_call x1, Pallas kernels, far(): pl.pallas_call(body, out_shape=jax.ShapeDtypeStruct((1344, TOK), BF), gri...  13.5 us
  transfers between devices with their start and end apart: 42, of which 13 were waited for; matrix products, arithmetic and copies ran while one was open for 3% of the time, Pallas kernels for 24%

profile of v6, /device:TPU:1, one launch (start us, length us, event | category | flops | bytes accessed | tf_op | source)
XLA Modules:
  0.0 232.9 jit_solution(7174308020360164914)
XLA Ops:
  0.6 1.5 collective-permute-start.6
  4.1 1.2 copy-done.3
  5.3 1.2 copy-done.4
  6.9 2.9 %collective-permute-start.2 = (bf16[336,2688]{1,0:T(8,128)(2,1)S(1)}, bf16[336,2688]{1,0:T(8,128)(2,1)}, u32[]{:S(2)}, u32[]{:S(2)}) collective-permute-start(bf16[336,2688]{1,0:T(8,128)(2,1)S(1)} %pack.1.refs_0_), channel_id=1, source_target_pairs={{0,24},{1,97},{2,26},{3,99},{4,28},{5,101},{6,30},{7,103},{8,0},{9... | collective-permute-start | bytes 5419016 | tf_op jit(solution)/shard_map/ppermute | solution.py:90
  9.8 3.1 %collective-permute-start = (bf16[512,512]{1,0:T(8,128)(2,1)S(1)}, bf16[512,512]{1,0:T(8,128)(2,1)S(1)}, u32[]{:S(2)}, u32[]{:S(2)}) collective-permute-start(bf16[512,512]{1,0:T(8,128)(2,1)S(1)} %pair.1.kv0_ref), channel_id=1, source_target_pairs={{0,8},{8,16},{16,24},{24,32},{32,40},{40,48},{48,56},{56,64},{64,7... | collective-permute-start | bytes 1572872 | tf_op jit(solution)/shard_map/ppermute | solution.py:39
  13.0 10.1 %collective-permute-done.kv1_ref = bf16[512,512]{1,0:T(8,128)(2,1)S(1)} collective-permute-done((bf16[512,512]{1,0:T(8,128)(2,1)S(1)}, bf16[512,512]{1,0:T(8,128)(2,1)S(1)}, u32[]{:S(2)}, u32[]{:S(2)}) %collective-permute-start) | collective-permute-done | bytes 524320 | tf_op jit(solution)/shard_map/ppermute | solution.py:39
  23.0 5.0 %collective-permute-start.1 = (bf16[512,512]{1,0:T(8,128)(2,1)S(1)}, bf16[512,512]{1,0:T(8,128)(2,1)}, u32[]{:S(2)}, u32[]{:S(2)}) collective-permute-start(bf16[512,512]{1,0:T(8,128)(2,1)S(1)} %collective-permute-done.kv1_ref), channel_id=1, source_target_pairs={{0,8},{8,16},{16,24},{24,32},{32,40},{40,48},{48,56},{56,64},{64,7... | collective-permute-start | bytes 1572872 | tf_op jit(solution)/shard_map/ppermute | solution.py:39
  28.1 2.4 %collective-permute-start.3 = (bf16[336,2688]{1,0:T(8,128)(2,1)S(1)}, bf16[336,2688]{1,0:T(8,128)(2,1)}, u32[]{:S(2)}, u32[]{:S(2)}) collective-permute-start(bf16[336,2688]{1,0:T(8,128)(2,1)S(1)} %pack.1.refs_0_), channel_id=1, source_target_pairs={{0,96},{1,25},{2,98},{3,27},{4,100},{5,29},{6,102},{7,31},{8,104},... | collective-permute-start | bytes 5419016 | tf_op jit(solution)/shard_map/ppermute | solution.py:90
  30.5 7.6 %collective-permute-done.1.kv2_ref = bf16[512,512]{1,0:T(8,128)(2,1)} collective-permute-done((bf16[512,512]{1,0:T(8,128)(2,1)S(1)}, bf16[512,512]{1,0:T(8,128)(2,1)}, u32[]{:S(2)}, u32[]{:S(2)}) %collective-permute-start.1) | collective-permute-done | bytes 524320 | tf_op jit(solution)/shard_map/ppermute | solution.py:39
  38.1 1.2 copy.23
  39.5 2.0 fusion.6
  42.0 6.5 %collective-permute-start.5 = (bf16[336,2688]{1,0:T(8,128)(2,1)S(1)}, bf16[336,2688]{1,0:T(8,128)(2,1)S(1)}, u32[]{:S(2)}, u32[]{:S(2)}) collective-permute-start(bf16[336,2688]{1,0:T(8,128)(2,1)S(1)} %pack.1.refs_0_), channel_id=1, source_target_pairs={{0,8},{1,33},{2,10},{3,35},{4,12},{5,37},{6,14},{7,39},{8,16},{9,4... | collective-permute-start | bytes 5419016 | tf_op jit(solution)/shard_map/ppermute | solution.py:90
  49.1 1.7 select_bitcast_fusion
  51.5 3.8 %collective-permute-start.12 = (bf16[2,80,672]{2,1,0:T(8,128)(2,1)S(1)}, bf16[2,80,672]{2,1,0:T(8,128)(2,1)S(1)}, u32[]{:S(2)}, u32[]{:S(2)}) collective-permute-start(bf16[2,80,672]{2,1,0:T(8,128)(2,1)S(1)} %get-tuple-element.124), channel_id=1, source_target_pairs={{0,6},{2,0},{4,2},{6,4},{1,7},{3,1},{5,3},{7,5},{8,14},{10,8},{12,... | collective-permute-start | bytes 645128 | tf_op jit(solution)/shard_map/ppermute | solution.py:34
  55.4 6.1 %attend.1 = bf16[2,4,64,512]{3,2,1,0:T(8,128)(2,1)S(1)} custom-call(s32[4]{0:T(128)S(1)} %pad_add_fusion.at_ref.refs_10_.refs_12_.refs_4_, bf16[512,512]{1,0:T(8,128)(2,1)S(1)} %copy-done.5, bf16[512,512]{1,0:T(8,128)(2,1)} %collective-permute-done.1.kv2_ref, bf16[512,512]{1,0:T(8,128)(2,1)S(1)} %collective-permute-done.kv1_ref, ...), custom_call_target="tpu_custom_call" | custom-call | bytes 1000 | tf_op jit(solution)/shard_map/attend/pallas_call | solution.py:123
  61.7 6.4 %collective-permute-done.13 = bf16[2,80,672]{2,1,0:T(8,128)(2,1)S(1)} collective-permute-done((bf16[2,80,672]{2,1,0:T(8,128)(2,1)S(1)}, bf16[2,80,672]{2,1,0:T(8,128)(2,1)S(1)}, u32[]{:S(2)}, u32[]{:S(2)}) %collective-permute-start.13) | collective-permute-done | bytes 215072 | tf_op jit(solution)/shard_map/ppermute | solution.py:34
  68.2 7.1 %collective-permute-done.14 = bf16[2,80,672]{2,1,0:T(8,128)(2,1)S(1)} collective-permute-done((bf16[2,80,672]{2,1,0:T(8,128)(2,1)S(1)}, bf16[2,80,672]{2,1,0:T(8,128)(2,1)S(1)}, u32[]{:S(2)}, u32[]{:S(2)}) %collective-permute-start.14) | collective-permute-done | bytes 215072 | tf_op jit(solution)/shard_map/ppermute | solution.py:34
  75.2 5.5 %collective-permute-start.4 = (bf16[256,512]{1,0:T(8,128)(2,1)S(1)}, bf16[256,512]{1,0:T(8,128)(2,1)S(1)}, u32[]{:S(2)}, u32[]{:S(2)}) collective-permute-start(bf16[256,512]{1,0:T(8,128)(2,1)S(1)} %bitcast.132), channel_id=1, source_target_pairs={{0,1},{1,0},{2,3},{3,2},{4,5},{5,4},{6,7},{7,6},{8,9},{9,8},{10,11... | collective-permute-start | bytes 786440 | tf_op jit(solution)/shard_map/ppermute | solution.py:34
  82.1 5.3 %collective-permute-done.5.refs_1_ = bf16[336,2688]{1,0:T(8,128)(2,1)S(1)} collective-permute-done((bf16[336,2688]{1,0:T(8,128)(2,1)S(1)}, bf16[336,2688]{1,0:T(8,128)(2,1)S(1)}, u32[]{:S(2)}, u32[]{:S(2)}) %collective-permute-start.5) | collective-permute-done | bytes 1806368 | tf_op jit(solution)/shard_map/ppermute | solution.py:90
  87.4 3.2 %copy-done.2 = bf16[512,5376]{1,0:T(8,128)(2,1)S(1)} copy-done((bf16[512,5376]{1,0:T(8,128)(2,1)S(1)}, bf16[512,5376]{1,0:T(8,128)(2,1)}, u32[]{:S(2)}) %copy-start.2) | copy-done | bytes 5505048
  90.6 7.3 %project.1 = (bf16[64,5376]{1,0:T(8,128)(2,1)S(1)}, bf16[32,5376]{1,0:T(8,128)(2,1)S(1)}, bf16[32,5376]{1,0:T(8,128)(2,1)S(1)}, bf16[32,5376]{1,0:T(8,128)(2,1)S...) custom-call(bf16[256,512]{1,0:T(8,128)(2,1)S(1)} %bitcast.127, ...), custom_call_target="tpu_custom_call" | custom-call | bytes 1000 | tf_op jit(solution)/shard_map/project/pallas_call | solution.py:147
  97.9 3.8 %collective-permute-start.10 = (bf16[32,5376]{1,0:T(8,128)(2,1)S(1)}, bf16[32,5376]{1,0:T(8,128)(2,1)S(1)}, u32[]{:S(2)}, u32[]{:S(2)}) collective-permute-start(bf16[32,5376]{1,0:T(8,128)(2,1)S(1)} %get-tuple-element.74), channel_id=1, source_target_pairs={{0,6},{2,0},{4,2},{6,4},{1,7},{3,1},{5,3},{7,5},{8,14},{10,8},{12,... | collective-permute-start | bytes 1032200 | tf_op jit(solution)/shard_map/ppermute | solution.py:34
  101.8 1.2 collective-permute-start.8
  103.0 3.4 %collective-permute-done.10 = bf16[32,5376]{1,0:T(8,128)(2,1)S(1)} collective-permute-done((bf16[32,5376]{1,0:T(8,128)(2,1)S(1)}, bf16[32,5376]{1,0:T(8,128)(2,1)S(1)}, u32[]{:S(2)}, u32[]{:S(2)}) %collective-permute-start.10) | collective-permute-done | bytes 344096 | tf_op jit(solution)/shard_map/ppermute | solution.py:34
  106.5 3.4 %collective-permute-start.19 = (bf16[32,5376]{1,0:T(8,128)(2,1)S(1)}, bf16[32,5376]{1,0:T(8,128)(2,1)S(1)}, u32[]{:S(2)}, u32[]{:S(2)}) collective-permute-start(bf16[32,5376]{1,0:T(8,128)(2,1)S(1)} %get-tuple-element.81), channel_id=1, source_target_pairs={{0,6},{2,0},{4,2},{6,4},{1,7},{3,1},{5,3},{7,5},{8,14},{10,8},{12,... | collective-permute-start | bytes 1032200 | tf_op jit(solution)/shard_map/ppermute | solution.py:34
  110.2 1.5 collective-permute-start.17
  111.7 12.6 %collective-permute-done.8.refs_10_ = bf16[336,2688]{1,0:T(8,128)(2,1)} collective-permute-done((bf16[336,2688]{1,0:T(8,128)(2,1)}, bf16[336,2688]{1,0:T(8,128)(2,1)}, u32[]{:S(2)}, u32[]{:S(2)}) %collective-permute-start.8) | collective-permute-done | bytes 1806368 | tf_op jit(solution)/shard_map/ppermute | solution.py:90
  124.3 2.7 %collective-permute-start.24 = (bf16[336,2688]{1,0:T(8,128)(2,1)S(1)}, bf16[336,2688]{1,0:T(8,128)(2,1)S(1)}, u32[]{:S(2)}, u32[]{:S(2)}) collective-permute-start(bf16[336,2688]{1,0:T(8,128)(2,1)S(1)} %collective-permute-done.5.refs_1_), channel_id=1, source_target_pairs={{0,96},{1,25},{2,98},{3,27},{4,100},{5,29},{6,102},{7,31},{8,104},... | collective-permute-start | bytes 5419016 | tf_op jit(solution)/shard_map/ppermute | solution.py:90
  127.0 1.1 norm.1
  128.2 2.7 %collective-permute-start.22 = (bf16[64,5376]{1,0:T(8,128)(2,1)S(1)}, bf16[64,5376]{1,0:T(8,128)(2,1)S(1)}, u32[]{:S(2)}, u32[]{:S(2)}) collective-permute-start(bf16[64,5376]{1,0:T(8,128)(2,1)S(1)} %get-tuple-element.91.refs_0_), channel_id=1, source_target_pairs={{0,6},{2,0},{4,2},{6,4},{1,7},{3,1},{5,3},{7,5},{8,14},{10,8},{12,... | collective-permute-start | bytes 2064392 | tf_op jit(solution)/shard_map/ppermute | solution.py:34
  131.0 11.0 %collective-permute-done.21.refs_1_ = bf16[64,5376]{1,0:T(8,128)(2,1)S(1)} collective-permute-done((bf16[64,5376]{1,0:T(8,128)(2,1)S(1)}, bf16[64,5376]{1,0:T(8,128)(2,1)S(1)}, u32[]{:S(2)}, u32[]{:S(2)}) %collective-permute-start.21) | collective-permute-done | bytes 688160 | tf_op jit(solution)/shard_map/ppermute | solution.py:34
  142.0 2.8 %collective-permute-start.33 = (bf16[336,2688]{1,0:T(8,128)(2,1)S(1)}, bf16[336,2688]{1,0:T(8,128)(2,1)}, u32[]{:S(2)}, u32[]{:S(2)}) collective-permute-start(bf16[336,2688]{1,0:T(8,128)(2,1)S(1)} %collective-permute-done.15.refs_3_), channel_id=1, source_target_pairs={{0,96},{1,25},{2,98},{3,27},{4,100},{5,29},{6,102},{7,31},{8,104},... | collective-permute-start | bytes 5419016 | tf_op jit(solution)/shard_map/ppermute | solution.py:90
  144.8 4.1 %collective-permute-start.27 = (bf16[64,5376]{1,0:T(8,128)(2,1)S(1)}, bf16[64,5376]{1,0:T(8,128)(2,1)S(1)}, u32[]{:S(2)}, u32[]{:S(2)}) collective-permute-start(bf16[64,5376]{1,0:T(8,128)(2,1)S(1)} %get-tuple-element.91.refs_0_), channel_id=1, source_target_pairs={{0,1},{1,0},{2,3},{3,2},{4,5},{5,4},{6,7},{7,6},{8,9},{9,8},{10,11... | collective-permute-start | bytes 2064392 | tf_op jit(solution)/shard_map/ppermute | solution.py:34
  148.9 1.2 copy-done.15
  150.3 2.7 %collective-permute-start.26 = (bf16[32,5376]{1,0:T(8,128)(2,1)S(1)}, bf16[32,5376]{1,0:T(8,128)(2,1)S(1)}, u32[]{:S(2)}, u32[]{:S(2)}) collective-permute-start(bf16[32,5376]{1,0:T(8,128)(2,1)S(1)} %slice.77), channel_id=1, source_target_pairs={{0,6},{2,0},{4,2},{6,4},{1,7},{3,1},{5,3},{7,5},{8,14},{10,8},{12,... | collective-permute-start | bytes 1032200 | tf_op jit(solution)/shard_map/ppermute | solution.py:34
  153.0 4.7 %collective-permute-start.28 = (bf16[64,5376]{1,0:T(8,128)(2,1)S(1)}, bf16[64,5376]{1,0:T(8,128)(2,1)S(1)}, u32[]{:S(2)}, u32[]{:S(2)}) collective-permute-start(bf16[64,5376]{1,0:T(8,128)(2,1)S(1)} %collective-permute-done.21.refs_1_), channel_id=1, source_target_pairs={{0,1},{1,0},{2,3},{3,2},{4,5},{5,4},{6,7},{7,6},{8,9},{9,8},{10,11... | collective-permute-start | bytes 2064392 | tf_op jit(solution)/shard_map/ppermute | solution.py:34
  157.7 9.2 %collective-permute-done.32.refs_7_ = bf16[336,2688]{1,0:T(8,128)(2,1)S(1)} collective-permute-done((bf16[336,2688]{1,0:T(8,128)(2,1)S(1)}, bf16[336,2688]{1,0:T(8,128)(2,1)S(1)}, u32[]{:S(2)}, u32[]{:S(2)}) %collective-permute-start.32) | collective-permute-done | bytes 1806368 | tf_op jit(solution)/shard_map/ppermute | solution.py:90
  166.9 4.7 %collective-permute-start.29 = (bf16[64,5376]{1,0:T(8,128)(2,1)S(1)}, bf16[64,5376]{1,0:T(8,128)(2,1)S(1)}, u32[]{:S(2)}, u32[]{:S(2)}) collective-permute-start(bf16[64,5376]{1,0:T(8,128)(2,1)S(1)} %collective-permute-done.22.refs_2_), channel_id=1, source_target_pairs={{0,1},{1,0},{2,3},{3,2},{4,5},{5,4},{6,7},{7,6},{8,9},{9,8},{10,11... | collective-permute-start | bytes 2064392 | tf_op jit(solution)/shard_map/ppermute | solution.py:34
  172.1 1.7 collective-permute-done.30.refs_8_
  174.4 2.7 %collective-permute-start.41 = (bf16[336,2688]{1,0:T(8,128)(2,1)}, bf16[336,2688]{1,0:T(8,128)(2,1)}, u32[]{:S(2)}, u32[]{:S(2)}) collective-permute-start(bf16[336,2688]{1,0:T(8,128)(2,1)} %collective-permute-done.33.refs_11_), channel_id=1, source_target_pairs={{0,96},{1,25},{2,98},{3,27},{4,100},{5,29},{6,102},{7,31},{8,104},... | collective-permute-start | bytes 5419016 | tf_op jit(solution)/shard_map/ppermute | solution.py:90
  177.1 5.1 %order.1.refs_13_.refs_5_ = bf16[512,5632]{1,0:T(8,128)(2,1)S(1)} custom-call(bf16[64,5376]{1,0:T(8,128)(2,1)S(1)} %get-tuple-element.91.refs_0_, bf16[64,5376]{1,0:T(8,128)(2,1)S(1)} %collective-permute-done.21.refs_1_, bf16[64,5376]{1,0:T(8,128)(2,1)S(1)} %collective-permute-done.22.refs_2_, bf16[32,5376]{1,0:T(8,128)(2,1)S(1)} %collective-permute-done.25.refs_3_, ...), custom_call_target="tpu_custom_call" | custom-call | bytes 1000 | tf_op jit(solution)/shard_map/order/pallas_call | solution.py:241
  182.2 2.5 %copy-done = bf16[512,5632]{1,0:T(8,128)(2,1)} copy-done((bf16[512,5632]{1,0:T(8,128)(2,1)}, bf16[512,5632]{1,0:T(8,128)(2,1)S(1)}, u32[]{:S(2)}) %copy-start) | copy-done | bytes 5767192
  185.3 22.0 %near.1.refs_6_ = f32[512,2688]{1,0:T(8,128)} custom-call(bf16[336,2688]{1,0:T(8,128)(2,1)} %copy-done.1, bf16[336,2688]{1,0:T(8,128)(2,1)} %copy-done.12, bf16[336,2688]{1,0:T(8,128)(2,1)} %collective-permute-done.2.refs_2_, bf16[336,2688]{1,0:T(8,128)(2,1)} %copy-done.13, bf16[336,2688]{1,0:T(8,128)(2,1)} %collective-permute-done.16.refs_4_, ...), custom_call_target="tpu_custom_call" | custom-call | bytes 1000 | tf_op jit(solution)/shard_map/near/pallas_call | solution.py:298
  207.9 3.0 %collective-permute-start.35 = (bf16[2,64,672]{2,1,0:T(8,128)(2,1)S(1)}, bf16[2,64,672]{2,1,0:T(8,128)(2,1)S(1)}, u32[]{:S(2)}, u32[]{:S(2)}) collective-permute-start(bf16[2,64,672]{2,1,0:T(8,128)(2,1)S(1)} %get-tuple-element.127), channel_id=1, source_target_pairs={{0,6},{2,0},{4,2},{6,4},{1,7},{3,1},{5,3},{7,5},{8,14},{10,8},{12,... | collective-permute-start | bytes 516104 | tf_op jit(solution)/shard_map/ppermute | solution.py:34
  211.6 5.1 %collective-permute-done.39.refs_1_ = bf16[336,2688]{1,0:T(8,128)(2,1)S(1)} collective-permute-done((bf16[336,2688]{1,0:T(8,128)(2,1)}, bf16[336,2688]{1,0:T(8,128)(2,1)S(1)}, u32[]{:S(2)}, u32[]{:S(2)}) %collective-permute-start.39) | collective-permute-done | bytes 1806368 | tf_op jit(solution)/shard_map/ppermute | solution.py:90
  216.7 1.3 copy-done.11
  218.0 13.5 %far.1 = bf16[1344,512]{1,0:T(8,128)(2,1)} custom-call(bf16[336,2688]{1,0:T(8,128)(2,1)} %copy-done.10, bf16[336,2688]{1,0:T(8,128)(2,1)} %copy-done.11, bf16[336,2688]{1,0:T(8,128)(2,1)} %copy-done.9, bf16[336,2688]{1,0:T(8,128)(2,1)} %collective-permute-done.41.refs_3_, s32[4]{0:T(128)} %copy-done.8, bf16[512,5632]{1,0:T(8,128)(2,1)} %copy-done, ...), custom_call_target="tpu_custom_call" | custom-call | flops 3699376128 | bytes 12730368 | tf_op jit(solution)/shard_map/far/pallas_call | solution.py:342
  231.8 1.1 copy.34
  (132 shorter events, 9.8 us)
Async XLA Ops:
  0.6 86.8 %collective-permute-start.6 = (bf16[512,5376]{1,0:T(8,128)(2,1)}, bf16[512,5376]{1,0:T(8,128)(2,1)}, u32[]{:S(2)}, u32[]{:S(2)}) collective-permute-start(bf16[512,5376]{1,0:T(8,128)(2,1)} %w_ref.1), channel_id=1, source_target_pairs={{0,1},{1,0},{2,3},{3,2},{4,5},{5,4},{6,7},{7,6},{8,9},{9,8},{10,11... | collective-permute-start | bytes 16515080 | tf_op jit(solution)/shard_map/ppermute | solution.py:34
  6.5 31.6 %copy-start.20 = (f32[672]{0:T(1024)S(1)}, f32[672]{0:T(1024)}, u32[]{:S(2)}) copy-start(f32[672]{0:T(1024)} %param.16) | copy-start | bytes 8068
  6.5 31.6 %copy-start.17 = (bf16[512,672]{0,1:T(8,128)(2,1)S(1)}, bf16[512,672]{0,1:T(8,128)(2,1)}, u32[]{:S(2)}) copy-start(bf16[512,672]{0,1:T(8,128)(2,1)} %param.15) | copy-start | bytes 2064388
  6.9 41.5 %copy-start.1 = (bf16[336,2688]{1,0:T(8,128)(2,1)}, bf16[336,2688]{1,0:T(8,128)(2,1)S(1)}, u32[]{:S(2)}) copy-start(bf16[336,2688]{1,0:T(8,128)(2,1)S(1)} %pack.1.refs_0_) | copy-start | bytes 5419012
  6.9 31.1 %collective-permute-start.2 = (bf16[336,2688]{1,0:T(8,128)(2,1)S(1)}, bf16[336,2688]{1,0:T(8,128)(2,1)}, u32[]{:S(2)}, u32[]{:S(2)}) collective-permute-start(bf16[336,2688]{1,0:T(8,128)(2,1)S(1)} %pack.1.refs_0_), channel_id=1, source_target_pairs={{0,24},{1,97},{2,26},{3,99},{4,28},{5,101},{6,30},{7,103},{8,0},{9... | collective-permute-start | bytes 5419016 | tf_op jit(solution)/shard_map/ppermute | solution.py:90
  9.8 13.2 %collective-permute-start = (bf16[512,512]{1,0:T(8,128)(2,1)S(1)}, bf16[512,512]{1,0:T(8,128)(2,1)S(1)}, u32[]{:S(2)}, u32[]{:S(2)}) collective-permute-start(bf16[512,512]{1,0:T(8,128)(2,1)S(1)} %pair.1.kv0_ref), channel_id=1, source_target_pairs={{0,8},{8,16},{16,24},{24,32},{32,40},{40,48},{48,56},{56,64},{64,7... | collective-permute-start | bytes 1572872 | tf_op jit(solution)/shard_map/ppermute | solution.py:39
  23.0 15.0 %collective-permute-start.1 = (bf16[512,512]{1,0:T(8,128)(2,1)S(1)}, bf16[512,512]{1,0:T(8,128)(2,1)}, u32[]{:S(2)}, u32[]{:S(2)}) collective-permute-start(bf16[512,512]{1,0:T(8,128)(2,1)S(1)} %collective-permute-done.kv1_ref), channel_id=1, source_target_pairs={{0,8},{8,16},{16,24},{24,32},{32,40},{40,48},{48,56},{56,64},{64,7... | collective-permute-start | bytes 1572872 | tf_op jit(solution)/shard_map/ppermute | solution.py:39
  28.1 23.5 %collective-permute-start.3 = (bf16[336,2688]{1,0:T(8,128)(2,1)S(1)}, bf16[336,2688]{1,0:T(8,128)(2,1)}, u32[]{:S(2)}, u32[]{:S(2)}) collective-permute-start(bf16[336,2688]{1,0:T(8,128)(2,1)S(1)} %pack.1.refs_0_), channel_id=1, source_target_pairs={{0,96},{1,25},{2,98},{3,27},{4,100},{5,29},{6,102},{7,31},{8,104},... | collective-permute-start | bytes 5419016 | tf_op jit(solution)/shard_map/ppermute | solution.py:90
  41.5 6.9 %collective-permute-start.11 = (bf16[4,80,672]{2,1,0:T(8,128)(2,1)}, bf16[4,80,672]{2,1,0:T(8,128)(2,1)}, u32[]{:S(2)}, u32[]{:S(2)}) collective-permute-start(bf16[4,80,672]{2,1,0:T(8,128)(2,1)} %fusion.6), channel_id=1, source_target_pairs={{0,1},{1,0},{2,3},{3,2},{4,5},{5,4},{6,7},{7,6},{8,9},{9,8},{10,11... | collective-permute-start | bytes 1290248 | tf_op jit(solution)/shard_map/ppermute | solution.py:34
  42.0 135.1 %copy-start.8 = (s32[4]{0:T(128)}, s32[4]{0:T(128)S(1)}, u32[]{:S(2)}) copy-start(s32[4]{0:T(128)S(1)} %pad_add_fusion.at_ref.refs_10_.refs_12_.refs_4_) | copy-start | bytes 52
  42.0 45.4 %collective-permute-start.5 = (bf16[336,2688]{1,0:T(8,128)(2,1)S(1)}, bf16[336,2688]{1,0:T(8,128)(2,1)S(1)}, u32[]{:S(2)}, u32[]{:S(2)}) collective-permute-start(bf16[336,2688]{1,0:T(8,128)(2,1)S(1)} %pack.1.refs_0_), channel_id=1, source_target_pairs={{0,8},{1,33},{2,10},{3,35},{4,12},{5,37},{6,14},{7,39},{8,16},{9,4... | collective-permute-start | bytes 5419016 | tf_op jit(solution)/shard_map/ppermute | solution.py:90
  48.4 54.6 %collective-permute-start.16 = (bf16[336,2688]{1,0:T(8,128)(2,1)S(1)}, bf16[336,2688]{1,0:T(8,128)(2,1)}, u32[]{:S(2)}, u32[]{:S(2)}) collective-permute-start(bf16[336,2688]{1,0:T(8,128)(2,1)S(1)} %pack.1.refs_0_), channel_id=1, source_target_pairs={{0,32},{1,9},{2,34},{3,11},{4,36},{5,13},{6,38},{7,15},{8,40},{9,1... | collective-permute-start | bytes 5419016 | tf_op jit(solution)/shard_map/ppermute | solution.py:90
  48.5 53.3 %collective-permute-start.15 = (bf16[336,2688]{1,0:T(8,128)(2,1)}, bf16[336,2688]{1,0:T(8,128)(2,1)S(1)}, u32[]{:S(2)}, u32[]{:S(2)}) collective-permute-start(bf16[336,2688]{1,0:T(8,128)(2,1)} %collective-permute-done.2.refs_2_), channel_id=1, source_target_pairs={{0,24},{1,97},{2,26},{3,99},{4,28},{5,101},{6,30},{7,103},{8,0},{9... | collective-permute-start | bytes 5419016 | tf_op jit(solution)/shard_map/ppermute | solution.py:90
  51.5 10.0 %collective-permute-start.12 = (bf16[2,80,672]{2,1,0:T(8,128)(2,1)S(1)}, bf16[2,80,672]{2,1,0:T(8,128)(2,1)S(1)}, u32[]{:S(2)}, u32[]{:S(2)}) collective-permute-start(bf16[2,80,672]{2,1,0:T(8,128)(2,1)S(1)} %get-tuple-element.124), channel_id=1, source_target_pairs={{0,6},{2,0},{4,2},{6,4},{1,7},{3,1},{5,3},{7,5},{8,14},{10,8},{12,... | collective-permute-start | bytes 645128 | tf_op jit(solution)/shard_map/ppermute | solution.py:34
  61.5 6.6 %collective-permute-start.13 = (bf16[2,80,672]{2,1,0:T(8,128)(2,1)S(1)}, bf16[2,80,672]{2,1,0:T(8,128)(2,1)S(1)}, u32[]{:S(2)}, u32[]{:S(2)}) collective-permute-start(bf16[2,80,672]{2,1,0:T(8,128)(2,1)S(1)} %get-tuple-element.123), channel_id=1, source_target_pairs={{0,4},{2,6},{4,0},{6,2},{1,5},{3,7},{5,1},{7,3},{8,12},{10,14},{12... | collective-permute-start | bytes 645128 | tf_op jit(solution)/shard_map/ppermute | solution.py:34
  68.1 7.1 %collective-permute-start.14 = (bf16[2,80,672]{2,1,0:T(8,128)(2,1)S(1)}, bf16[2,80,672]{2,1,0:T(8,128)(2,1)S(1)}, u32[]{:S(2)}, u32[]{:S(2)}) collective-permute-start(bf16[2,80,672]{2,1,0:T(8,128)(2,1)S(1)} %get-tuple-element.122), channel_id=1, source_target_pairs={{0,2},{2,4},{4,6},{6,0},{1,3},{3,5},{5,7},{7,1},{8,10},{10,12},{12... | collective-permute-start | bytes 645128 | tf_op jit(solution)/shard_map/ppermute | solution.py:34
  75.2 6.6 %collective-permute-start.4 = (bf16[256,512]{1,0:T(8,128)(2,1)S(1)}, bf16[256,512]{1,0:T(8,128)(2,1)S(1)}, u32[]{:S(2)}, u32[]{:S(2)}) collective-permute-start(bf16[256,512]{1,0:T(8,128)(2,1)S(1)} %bitcast.132), channel_id=1, source_target_pairs={{0,1},{1,0},{2,3},{3,2},{4,5},{5,4},{6,7},{7,6},{8,9},{9,8},{10,11... | collective-permute-start | bytes 786440 | tf_op jit(solution)/shard_map/ppermute | solution.py:34
  81.9 28.3 %collective-permute-start.7 = (bf16[336,2688]{1,0:T(8,128)(2,1)}, bf16[336,2688]{1,0:T(8,128)(2,1)S(1)}, u32[]{:S(2)}, u32[]{:S(2)}) collective-permute-start(bf16[336,2688]{1,0:T(8,128)(2,1)} %collective-permute-done.2.refs_2_), channel_id=1, source_target_pairs={{0,32},{1,9},{2,34},{3,11},{4,36},{5,13},{6,38},{7,15},{8,40},{9,1... | collective-permute-start | bytes 5419016 | tf_op jit(solution)/shard_map/ppermute | solution.py:90
  87.4 36.9 %copy-start.12 = (bf16[336,2688]{1,0:T(8,128)(2,1)}, bf16[336,2688]{1,0:T(8,128)(2,1)S(1)}, u32[]{:S(2)}) copy-start(bf16[336,2688]{1,0:T(8,128)(2,1)S(1)} %collective-permute-done.5.refs_1_) | copy-start | bytes 5419012
  97.9 8.6 %collective-permute-start.10 = (bf16[32,5376]{1,0:T(8,128)(2,1)S(1)}, bf16[32,5376]{1,0:T(8,128)(2,1)S(1)}, u32[]{:S(2)}, u32[]{:S(2)}) collective-permute-start(bf16[32,5376]{1,0:T(8,128)(2,1)S(1)} %get-tuple-element.74), channel_id=1, source_target_pairs={{0,6},{2,0},{4,2},{6,4},{1,7},{3,1},{5,3},{7,5},{8,14},{10,8},{12,... | collective-permute-start | bytes 1032200 | tf_op jit(solution)/shard_map/ppermute | solution.py:34
  101.7 8.2 %collective-permute-start.9 = (bf16[32,5376]{1,0:T(8,128)(2,1)S(1)}, bf16[32,5376]{1,0:T(8,128)(2,1)S(1)}, u32[]{:S(2)}, u32[]{:S(2)}) collective-permute-start(bf16[32,5376]{1,0:T(8,128)(2,1)S(1)} %get-tuple-element.73), channel_id=1, source_target_pairs={{0,2},{2,4},{4,6},{6,0},{1,3},{3,5},{5,7},{7,1},{8,10},{10,12},{12... | collective-permute-start | bytes 1032200 | tf_op jit(solution)/shard_map/ppermute | solution.py:34
  101.8 40.2 %copy-start.13 = (bf16[336,2688]{1,0:T(8,128)(2,1)}, bf16[336,2688]{1,0:T(8,128)(2,1)S(1)}, u32[]{:S(2)}) copy-start(bf16[336,2688]{1,0:T(8,128)(2,1)S(1)} %collective-permute-done.15.refs_3_) | copy-start | bytes 5419012
  101.8 22.4 %collective-permute-start.8 = (bf16[336,2688]{1,0:T(8,128)(2,1)}, bf16[336,2688]{1,0:T(8,128)(2,1)}, u32[]{:S(2)}, u32[]{:S(2)}) collective-permute-start(bf16[336,2688]{1,0:T(8,128)(2,1)} %collective-permute-done.2.refs_2_), channel_id=1, source_target_pairs={{0,96},{1,25},{2,98},{3,27},{4,100},{5,29},{6,102},{7,31},{8,104},... | collective-permute-start | bytes 5419016 | tf_op jit(solution)/shard_map/ppermute | solution.py:90
  103.0 21.2 %collective-permute-start.18 = (bf16[32,5376]{1,0:T(8,128)(2,1)S(1)}, bf16[32,5376]{1,0:T(8,128)(2,1)S(1)}, u32[]{:S(2)}, u32[]{:S(2)}) collective-permute-start(bf16[32,5376]{1,0:T(8,128)(2,1)S(1)} %get-tuple-element.80), channel_id=1, source_target_pairs={{0,2},{2,4},{4,6},{6,0},{1,3},{3,5},{5,7},{7,1},{8,10},{10,12},{12... | collective-permute-start | bytes 1032200 | tf_op jit(solution)/shard_map/ppermute | solution.py:34
  106.5 20.5 %collective-permute-start.19 = (bf16[32,5376]{1,0:T(8,128)(2,1)S(1)}, bf16[32,5376]{1,0:T(8,128)(2,1)S(1)}, u32[]{:S(2)}, u32[]{:S(2)}) collective-permute-start(bf16[32,5376]{1,0:T(8,128)(2,1)S(1)} %get-tuple-element.81), channel_id=1, source_target_pairs={{0,6},{2,0},{4,2},{6,4},{1,7},{3,1},{5,3},{7,5},{8,14},{10,8},{12,... | collective-permute-start | bytes 1032200 | tf_op jit(solution)/shard_map/ppermute | solution.py:34
  110.0 17.0 %collective-permute-start.20 = (bf16[32,5376]{1,0:T(8,128)(2,1)S(1)}, bf16[32,5376]{1,0:T(8,128)(2,1)S(1)}, u32[]{:S(2)}, u32[]{:S(2)}) collective-permute-start(bf16[32,5376]{1,0:T(8,128)(2,1)S(1)} %add_convert_fusion), channel_id=1, source_target_pairs={{0,6},{2,0},{4,2},{6,4},{1,7},{3,1},{5,3},{7,5},{8,14},{10,8},{12,... | collective-permute-start | bytes 1032200 | tf_op jit(solution)/shard_map/ppermute | solution.py:34
  110.2 16.8 %collective-permute-start.17 = (bf16[32,5376]{1,0:T(8,128)(2,1)S(1)}, bf16[32,5376]{1,0:T(8,128)(2,1)S(1)}, u32[]{:S(2)}, u32[]{:S(2)}) collective-permute-start(bf16[32,5376]{1,0:T(8,128)(2,1)S(1)} %add_convert_fusion.1), channel_id=1, source_target_pairs={{0,2},{2,4},{4,6},{6,0},{1,3},{3,5},{5,7},{7,1},{8,10},{10,12},{12... | collective-permute-start | bytes 1032200 | tf_op jit(solution)/shard_map/ppermute | solution.py:34
  124.3 24.6 %collective-permute-start.23 = (bf16[336,2688]{1,0:T(8,128)(2,1)S(1)}, bf16[336,2688]{1,0:T(8,128)(2,1)}, u32[]{:S(2)}, u32[]{:S(2)}) collective-permute-start(bf16[336,2688]{1,0:T(8,128)(2,1)S(1)} %collective-permute-done.5.refs_1_), channel_id=1, source_target_pairs={{0,32},{1,9},{2,34},{3,11},{4,36},{5,13},{6,38},{7,15},{8,40},{9,1... | collective-permute-start | bytes 5419016 | tf_op jit(solution)/shard_map/ppermute | solution.py:90
  124.3 24.6 %collective-permute-start.24 = (bf16[336,2688]{1,0:T(8,128)(2,1)S(1)}, bf16[336,2688]{1,0:T(8,128)(2,1)S(1)}, u32[]{:S(2)}, u32[]{:S(2)}) collective-permute-start(bf16[336,2688]{1,0:T(8,128)(2,1)S(1)} %collective-permute-done.5.refs_1_), channel_id=1, source_target_pairs={{0,96},{1,25},{2,98},{3,27},{4,100},{5,29},{6,102},{7,31},{8,104},... | collective-permute-start | bytes 5419016 | tf_op jit(solution)/shard_map/ppermute | solution.py:90
  128.1 13.9 %collective-permute-start.21 = (bf16[64,5376]{1,0:T(8,128)(2,1)S(1)}, bf16[64,5376]{1,0:T(8,128)(2,1)S(1)}, u32[]{:S(2)}, u32[]{:S(2)}) collective-permute-start(bf16[64,5376]{1,0:T(8,128)(2,1)S(1)} %get-tuple-element.91.refs_0_), channel_id=1, source_target_pairs={{0,2},{2,4},{4,6},{6,0},{1,3},{3,5},{5,7},{7,1},{8,10},{10,12},{12... | collective-permute-start | bytes 2064392 | tf_op jit(solution)/shard_map/ppermute | solution.py:34
  128.2 38.7 %collective-permute-start.32 = (bf16[336,2688]{1,0:T(8,128)(2,1)S(1)}, bf16[336,2688]{1,0:T(8,128)(2,1)S(1)}, u32[]{:S(2)}, u32[]{:S(2)}) collective-permute-start(bf16[336,2688]{1,0:T(8,128)(2,1)S(1)} %collective-permute-done.15.refs_3_), channel_id=1, source_target_pairs={{0,32},{1,9},{2,34},{3,11},{4,36},{5,13},{6,38},{7,15},{8,40},{9,1... | collective-permute-start | bytes 5419016 | tf_op jit(solution)/shard_map/ppermute | solution.py:90
  128.2 16.6 %collective-permute-start.22 = (bf16[64,5376]{1,0:T(8,128)(2,1)S(1)}, bf16[64,5376]{1,0:T(8,128)(2,1)S(1)}, u32[]{:S(2)}, u32[]{:S(2)}) collective-permute-start(bf16[64,5376]{1,0:T(8,128)(2,1)S(1)} %get-tuple-element.91.refs_0_), channel_id=1, source_target_pairs={{0,6},{2,0},{4,2},{6,4},{1,7},{3,1},{5,3},{7,5},{8,14},{10,8},{12,... | collective-permute-start | bytes 2064392 | tf_op jit(solution)/shard_map/ppermute | solution.py:34
  142.0 30.1 %collective-permute-start.33 = (bf16[336,2688]{1,0:T(8,128)(2,1)S(1)}, bf16[336,2688]{1,0:T(8,128)(2,1)}, u32[]{:S(2)}, u32[]{:S(2)}) collective-permute-start(bf16[336,2688]{1,0:T(8,128)(2,1)S(1)} %collective-permute-done.15.refs_3_), channel_id=1, source_target_pairs={{0,96},{1,25},{2,98},{3,27},{4,100},{5,29},{6,102},{7,31},{8,104},... | collective-permute-start | bytes 5419016 | tf_op jit(solution)/shard_map/ppermute | solution.py:90
  144.8 8.2 %collective-permute-start.27 = (bf16[64,5376]{1,0:T(8,128)(2,1)S(1)}, bf16[64,5376]{1,0:T(8,128)(2,1)S(1)}, u32[]{:S(2)}, u32[]{:S(2)}) collective-permute-start(bf16[64,5376]{1,0:T(8,128)(2,1)S(1)} %get-tuple-element.91.refs_0_), channel_id=1, source_target_pairs={{0,1},{1,0},{2,3},{3,2},{4,5},{5,4},{6,7},{7,6},{8,9},{9,8},{10,11... | collective-permute-start | bytes 2064392 | tf_op jit(solution)/shard_map/ppermute | solution.py:34
  150.1 21.4 %collective-permute-start.25 = (bf16[32,5376]{1,0:T(8,128)(2,1)S(1)}, bf16[32,5376]{1,0:T(8,128)(2,1)S(1)}, u32[]{:S(2)}, u32[]{:S(2)}) collective-permute-start(bf16[32,5376]{1,0:T(8,128)(2,1)S(1)} %slice.76), channel_id=1, source_target_pairs={{0,2},{2,4},{4,6},{6,0},{1,3},{3,5},{5,7},{7,1},{8,10},{10,12},{12... | collective-permute-start | bytes 1032200 | tf_op jit(solution)/shard_map/ppermute | solution.py:34
  150.3 21.4 %collective-permute-start.26 = (bf16[32,5376]{1,0:T(8,128)(2,1)S(1)}, bf16[32,5376]{1,0:T(8,128)(2,1)S(1)}, u32[]{:S(2)}, u32[]{:S(2)}) collective-permute-start(bf16[32,5376]{1,0:T(8,128)(2,1)S(1)} %slice.77), channel_id=1, source_target_pairs={{0,6},{2,0},{4,2},{6,4},{1,7},{3,1},{5,3},{7,5},{8,14},{10,8},{12,... | collective-permute-start | bytes 1032200 | tf_op jit(solution)/shard_map/ppermute | solution.py:34
  153.0 21.4 %collective-permute-start.28 = (bf16[64,5376]{1,0:T(8,128)(2,1)S(1)}, bf16[64,5376]{1,0:T(8,128)(2,1)S(1)}, u32[]{:S(2)}, u32[]{:S(2)}) collective-permute-start(bf16[64,5376]{1,0:T(8,128)(2,1)S(1)} %collective-permute-done.21.refs_1_), channel_id=1, source_target_pairs={{0,1},{1,0},{2,3},{3,2},{4,5},{5,4},{6,7},{7,6},{8,9},{9,8},{10,11... | collective-permute-start | bytes 2064392 | tf_op jit(solution)/shard_map/ppermute | solution.py:34
  166.9 7.5 %collective-permute-start.29 = (bf16[64,5376]{1,0:T(8,128)(2,1)S(1)}, bf16[64,5376]{1,0:T(8,128)(2,1)S(1)}, u32[]{:S(2)}, u32[]{:S(2)}) collective-permute-start(bf16[64,5376]{1,0:T(8,128)(2,1)S(1)} %collective-permute-done.22.refs_2_), channel_id=1, source_target_pairs={{0,1},{1,0},{2,3},{3,2},{4,5},{5,4},{6,7},{7,6},{8,9},{9,8},{10,11... | collective-permute-start | bytes 2064392 | tf_op jit(solution)/shard_map/ppermute | solution.py:34
  171.6 2.3 collective-permute-start.30
  171.7 2.7 %collective-permute-start.31 = (bf16[32,5376]{1,0:T(8,128)(2,1)S(1)}, bf16[32,5376]{1,0:T(8,128)(2,1)S(1)}, u32[]{:S(2)}, u32[]{:S(2)}) collective-permute-start(bf16[32,5376]{1,0:T(8,128)(2,1)S(1)} %collective-permute-done.26.refs_4_), channel_id=1, source_target_pairs={{0,1},{1,0},{2,3},{3,2},{4,5},{5,4},{6,7},{7,6},{8,9},{9,8},{10,11... | collective-permute-start | bytes 1032200 | tf_op jit(solution)/shard_map/ppermute | solution.py:34
  172.1 38.8 %collective-permute-start.40 = (bf16[336,2688]{1,0:T(8,128)(2,1)}, bf16[336,2688]{1,0:T(8,128)(2,1)S(1)}, u32[]{:S(2)}, u32[]{:S(2)}) collective-permute-start(bf16[336,2688]{1,0:T(8,128)(2,1)} %collective-permute-done.8.refs_10_), channel_id=1, source_target_pairs={{0,96},{1,25},{2,98},{3,27},{4,100},{5,29},{6,102},{7,31},{8,104},... | collective-permute-start | bytes 5419016 | tf_op jit(solution)/shard_map/ppermute | solution.py:90
  173.9 37.0 %collective-permute-start.38 = (bf16[336,2688]{1,0:T(8,128)(2,1)}, bf16[336,2688]{1,0:T(8,128)(2,1)S(1)}, u32[]{:S(2)}, u32[]{:S(2)}) collective-permute-start(bf16[336,2688]{1,0:T(8,128)(2,1)} %collective-permute-done.16.refs_4_), channel_id=1, source_target_pairs={{0,32},{1,9},{2,34},{3,11},{4,36},{5,13},{6,38},{7,15},{8,40},{9,1... | collective-permute-start | bytes 5419016 | tf_op jit(solution)/shard_map/ppermute | solution.py:90
  174.3 42.3 %collective-permute-start.39 = (bf16[336,2688]{1,0:T(8,128)(2,1)}, bf16[336,2688]{1,0:T(8,128)(2,1)S(1)}, u32[]{:S(2)}, u32[]{:S(2)}) collective-permute-start(bf16[336,2688]{1,0:T(8,128)(2,1)} %collective-permute-done.23.refs_5_), channel_id=1, source_target_pairs={{0,32},{1,9},{2,34},{3,11},{4,36},{5,13},{6,38},{7,15},{8,40},{9,1... | collective-permute-start | bytes 5419016 | tf_op jit(solution)/shard_map/ppermute | solution.py:90
  174.4 42.3 %collective-permute-start.41 = (bf16[336,2688]{1,0:T(8,128)(2,1)}, bf16[336,2688]{1,0:T(8,128)(2,1)}, u32[]{:S(2)}, u32[]{:S(2)}) collective-permute-start(bf16[336,2688]{1,0:T(8,128)(2,1)} %collective-permute-done.33.refs_11_), channel_id=1, source_target_pairs={{0,96},{1,25},{2,98},{3,27},{4,100},{5,29},{6,102},{7,31},{8,104},... | collective-permute-start | bytes 5419016 | tf_op jit(solution)/shard_map/ppermute | solution.py:90
  184.7 22.6 %collective-permute-start.34 = (bf16[4,64,672]{2,1,0:T(8,128)(2,1)S(1)}, bf16[4,64,672]{2,1,0:T(8,128)(2,1)S(1)}, u32[]{:S(2)}, u32[]{:S(2)}) collective-permute-start(bf16[4,64,672]{2,1,0:T(8,128)(2,1)S(1)} %select_bitcast_fusion.2), channel_id=1, source_target_pairs={{0,1},{1,0},{2,3},{3,2},{4,5},{5,4},{6,7},{7,6},{8,9},{9,8},{10,11... | collective-permute-start | bytes 1032200 | tf_op jit(solution)/shard_map/ppermute | solution.py:34
  207.9 23.6 %collective-permute-start.35 = (bf16[2,64,672]{2,1,0:T(8,128)(2,1)S(1)}, bf16[2,64,672]{2,1,0:T(8,128)(2,1)S(1)}, u32[]{:S(2)}, u32[]{:S(2)}) collective-permute-start(bf16[2,64,672]{2,1,0:T(8,128)(2,1)S(1)} %get-tuple-element.127), channel_id=1, source_target_pairs={{0,6},{2,0},{4,2},{6,4},{1,7},{3,1},{5,3},{7,5},{8,14},{10,8},{12,... | collective-permute-start | bytes 516104 | tf_op jit(solution)/shard_map/ppermute | solution.py:34
  210.9 20.6 %collective-permute-start.36 = (bf16[2,64,672]{2,1,0:T(8,128)(2,1)S(1)}, bf16[2,64,672]{2,1,0:T(8,128)(2,1)S(1)}, u32[]{:S(2)}, u32[]{:S(2)}) collective-permute-start(bf16[2,64,672]{2,1,0:T(8,128)(2,1)S(1)} %get-tuple-element.126), channel_id=1, source_target_pairs={{0,4},{2,6},{4,0},{6,2},{1,5},{3,7},{5,1},{7,3},{8,12},{10,14},{12... | collective-permute-start | bytes 516104 | tf_op jit(solution)/shard_map/ppermute | solution.py:34
  210.9 20.6 %collective-permute-start.37 = (bf16[2,64,672]{2,1,0:T(8,128)(2,1)S(1)}, bf16[2,64,672]{2,1,0:T(8,128)(2,1)S(1)}, u32[]{:S(2)}, u32[]{:S(2)}) collective-permute-start(bf16[2,64,672]{2,1,0:T(8,128)(2,1)S(1)} %get-tuple-element.125), channel_id=1, source_target_pairs={{0,2},{2,4},{4,6},{6,0},{1,3},{3,5},{5,7},{7,1},{8,10},{10,12},{12... | collective-permute-start | bytes 516104 | tf_op jit(solution)/shard_map/ppermute | solution.py:34
  (15 other events, 77.8 us)

commit v7 on v6

--- a/solution.py
+++ b/solution.py
@@ -393,7 +393,6 @@
     kv2, w_late, p = lax.optimization_barrier((kv2, w, p))
     m = ring(w_late, 1, 0)
     b = ring(p, -1, 0)
-    kv2, residual, post_gain = lax.optimization_barrier((kv2, residual, post_gain))
     prev, following = [ring(w_late, 1, 1)], [ring(w, -1, 1)]
 
     gains = jnp.stack([post_gain, pre_gain])
@@ -409,7 +408,7 @@
     kid = lax.dynamic_slice_in_dim(padded, start, 3 * TOK, 0)[None, :]
     qid = lax.dynamic_slice_in_dim(doc_ids, start, TOK, 0)[:, None]
 
-    queries, p, following[0] = lax.optimization_barrier((queries, p, following[0]))
+    queries, mine, p, following[0] = lax.optimization_barrier((queries, mine, p, following[0]))
     mix = attend(where, queries, kv2, kv1, kv0, qid, kid)
     other_weight = shift(out_weight, "c", 1)
     own, other = mix[0].reshape(256, 512), shift(mix[1].reshape(256, 512), "c", 1)
@@ -420,7 +419,7 @@
     dn_b = shift(p2b, "z", -1)
     a_b = shift(p1b, "z", 1)
     b_t = shift(p3t, "z", -1)
-    up_t, dn_b, mine, m, b, prev, following = lax.optimization_barrier((up_t, dn_b, mine, m, b, prev, following))
+    up_t, dn_b, m, b, prev, following = lax.optimization_barrier((up_t, dn_b, m, b, prev, following))
     prev += [ring(v, 1, 1) for v in (m, p, b)]
     following += [ring(v, -1, 1) for v in (m, p, b)]
     add = lambda p, q: (p.astype(F32) + q.astype(F32)).astype(BF)

time: 234 us -> 235 us (level)
  starting transfers between devices: 74.2 us -> 78.1 us
  local copies, waits for them, and re-layouts: 15.8 us -> 12.8 us
    ppermute x2, waiting for transfers between devices: 17.7 us -> 3.99 us  [behind(): return lax.ppermute(value, ('y', 'x'), [(i, i + 1) for i in range(n - 1)])]
    ppermute x15, waiting for transfers between devices: 32.2 us -> 40.8 us  [ring(): return lax.ppermute(value, ('y', 'x', 'z', 'c'), pairs)]
    ppermute x25, starting transfers between devices: 43.8 us -> 52.3 us  [shift(): return lax.ppermute(value, axis, [(i, (i + by) % n) for i in range(n)])]
    ppermute x25, waiting for transfers between devices: 31.2 us -> 36.3 us  [shift(): return lax.ppermute(value, axis, [(i, (i + by) % n) for i in range(n)])]
    ppermute x15, starting transfers between devices: 22.2 us -> 18.4 us  [ring(): return lax.ppermute(value, ('y', 'x', 'z', 'c'), pairs)]
    unnamed x57 -> x62, local copies, waits for them, and re-layouts: 13.8 us -> 11.9 us
  transfers between devices with their start and end apart: 42 -> 42, of which waited for: 13 -> 14; matrix products, arithmetic and copies ran while one was open for 3% -> 3% of each run, Pallas kernels for 24% -> 24%
where the time goes in v7:
time: 235 us; the launch traced here: 233 us
  waiting for transfers between devices  81.1 us (35%)
  starting transfers between devices  78.1 us (33%)
  Pallas kernels  55.6 us (24%)
  local copies, waits for them, and re-layouts  12.8 us (5%)
  other arithmetic  4.1 us (2%)
    ppermute x25, starting transfers between devices, shift(): return lax.ppermute(value, axis, [(i, (i + by) % n) for i in range(n)])  52.3 us
    ppermute x15, waiting for transfers between devices, ring(): return lax.ppermute(value, ('y', 'x', 'z', 'c'), pairs)  40.8 us
    ppermute x25, waiting for transfers between devices, shift(): return lax.ppermute(value, axis, [(i, (i + by) % n) for i in range(n)])  36.3 us
    pallas_call x1, Pallas kernels, near(): pl.pallas_call(body, out_shape=jax.ShapeDtypeStruct((TOK, 2688), F32), gr...  22.1 us
    ppermute x15, starting transfers between devices, ring(): return lax.ppermute(value, ('y', 'x', 'z', 'c'), pairs)  18.4 us
    pallas_call x1, Pallas kernels, far(): pl.pallas_call(body, out_shape=jax.ShapeDtypeStruct((1344, TOK), BF), gri...  13.5 us
    unnamed x62, local copies, waits for them, and re-layouts  11.9 us
    pallas_call x1, Pallas kernels, project(): pl.pallas_call(project_kernel, out_shape=[jax.ShapeDtypeStruct((64, D), B...  7.84 us
  transfers between devices with their start and end apart: 42, of which 14 were waited for; matrix products, arithmetic and copies ran while one was open for 3% of the time, Pallas kernels for 24%

profile of v7, /device:TPU:1, one launch (start us, length us, event | category | flops | bytes accessed | tf_op | source)
XLA Modules:
  0.0 233.0 jit_solution(9980816655560022396)
XLA Ops:
  0.6 1.5 collective-permute-start.10
  3.1 0.9 copy-done.6
  4.1 1.2 copy-done.2
  5.3 1.2 copy-done.3
  6.9 2.9 %collective-permute-start.6 = (bf16[336,2688]{1,0:T(8,128)(2,1)S(1)}, bf16[336,2688]{1,0:T(8,128)(2,1)}, u32[]{:S(2)}, u32[]{:S(2)}) collective-permute-start(bf16[336,2688]{1,0:T(8,128)(2,1)S(1)} %pack.1.refs_0_), channel_id=1, source_target_pairs={{0,24},{1,97},{2,26},{3,99},{4,28},{5,101},{6,30},{7,103},{8,0},{9... | collective-permute-start | bytes 5419016 | tf_op jit(solution)/shard_map/ppermute | solution.py:90
  9.8 1.4 copy.22
  12.5 3.1 %collective-permute-start.4 = (bf16[512,512]{1,0:T(8,128)(2,1)S(1)}, bf16[512,512]{1,0:T(8,128)(2,1)S(1)}, u32[]{:S(2)}, u32[]{:S(2)}) collective-permute-start(bf16[512,512]{1,0:T(8,128)(2,1)S(1)} %pair.1.kv0_ref), channel_id=1, source_target_pairs={{0,8},{8,16},{16,24},{24,32},{32,40},{40,48},{48,56},{56,64},{64,7... | collective-permute-start | bytes 1572872 | tf_op jit(solution)/shard_map/ppermute | solution.py:39
  16.1 1.8 select_bitcast_fusion
  18.5 3.8 %collective-permute-start.1 = (bf16[2,80,672]{2,1,0:T(8,128)(2,1)S(1)}, bf16[2,80,672]{2,1,0:T(8,128)(2,1)S(1)}, u32[]{:S(2)}, u32[]{:S(2)}) collective-permute-start(bf16[2,80,672]{2,1,0:T(8,128)(2,1)S(1)} %get-tuple-element.118), channel_id=1, source_target_pairs={{0,6},{2,0},{4,2},{6,4},{1,7},{3,1},{5,3},{7,5},{8,14},{10,8},{12,... | collective-permute-start | bytes 645128 | tf_op jit(solution)/shard_map/ppermute | solution.py:34
  22.3 4.0 %collective-permute-done.4.kv1_ref = bf16[512,512]{1,0:T(8,128)(2,1)S(1)} collective-permute-done((bf16[512,512]{1,0:T(8,128)(2,1)S(1)}, bf16[512,512]{1,0:T(8,128)(2,1)S(1)}, u32[]{:S(2)}, u32[]{:S(2)}) %collective-permute-start.4) | collective-permute-done | bytes 524320 | tf_op jit(solution)/shard_map/ppermute | solution.py:39
  26.3 4.2 %collective-permute-start.5 = (bf16[512,512]{1,0:T(8,128)(2,1)S(1)}, bf16[512,512]{1,0:T(8,128)(2,1)S(1)}, u32[]{:S(2)}, u32[]{:S(2)}) collective-permute-start(bf16[512,512]{1,0:T(8,128)(2,1)S(1)} %collective-permute-done.4.kv1_ref), channel_id=1, source_target_pairs={{0,8},{8,16},{16,24},{24,32},{32,40},{40,48},{48,56},{56,64},{64,7... | collective-permute-start | bytes 1572872 | tf_op jit(solution)/shard_map/ppermute | solution.py:39
  30.6 5.1 %collective-permute-start.7 = (bf16[336,2688]{1,0:T(8,128)(2,1)S(1)}, bf16[336,2688]{1,0:T(8,128)(2,1)S(1)}, u32[]{:S(2)}, u32[]{:S(2)}) collective-permute-start(bf16[336,2688]{1,0:T(8,128)(2,1)S(1)} %pack.1.refs_0_), channel_id=1, source_target_pairs={{0,96},{1,25},{2,98},{3,27},{4,100},{5,29},{6,102},{7,31},{8,104},... | collective-permute-start | bytes 5419016 | tf_op jit(solution)/shard_map/ppermute | solution.py:90
  35.7 3.7 %collective-permute-start.2 = (bf16[2,80,672]{2,1,0:T(8,128)(2,1)S(1)}, bf16[2,80,672]{2,1,0:T(8,128)(2,1)S(1)}, u32[]{:S(2)}, u32[]{:S(2)}) collective-permute-start(bf16[2,80,672]{2,1,0:T(8,128)(2,1)S(1)} %get-tuple-element.117), channel_id=1, source_target_pairs={{0,4},{2,6},{4,0},{6,2},{1,5},{3,7},{5,1},{7,3},{8,12},{10,14},{12... | collective-permute-start | bytes 645128 | tf_op jit(solution)/shard_map/ppermute | solution.py:34
  39.4 6.2 %collective-permute-done.2 = bf16[2,80,672]{2,1,0:T(8,128)(2,1)S(1)} collective-permute-done((bf16[2,80,672]{2,1,0:T(8,128)(2,1)S(1)}, bf16[2,80,672]{2,1,0:T(8,128)(2,1)S(1)}, u32[]{:S(2)}, u32[]{:S(2)}) %collective-permute-start.2) | collective-permute-done | bytes 215072 | tf_op jit(solution)/shard_map/ppermute | solution.py:34
  46.4 1.6 collective-permute-start.9
  48.0 5.9 %collective-permute-done.3 = bf16[2,80,672]{2,1,0:T(8,128)(2,1)S(1)} collective-permute-done((bf16[2,80,672]{2,1,0:T(8,128)(2,1)S(1)}, bf16[2,80,672]{2,1,0:T(8,128)(2,1)S(1)}, u32[]{:S(2)}, u32[]{:S(2)}) %collective-permute-start.3) | collective-permute-done | bytes 215072 | tf_op jit(solution)/shard_map/ppermute | solution.py:34
  55.6 1.2 copy-done.12
  56.8 5.6 %attend.1 = bf16[2,4,64,512]{3,2,1,0:T(8,128)(2,1)S(1)} custom-call(s32[4]{0:T(128)S(1)} %pad_add_fusion.at_ref.refs_10_.refs_12_.refs_4_, bf16[512,512]{1,0:T(8,128)(2,1)S(1)} %copy-done.4, bf16[512,512]{1,0:T(8,128)(2,1)S(1)} %collective-permute-done.5.kv2_ref, bf16[512,512]{1,0:T(8,128)(2,1)S(1)} %collective-permute-done.4.kv1_ref, ...), custom_call_target="tpu_custom_call" | custom-call | bytes 1000 | tf_op jit(solution)/shard_map/attend/pallas_call | solution.py:123
  62.4 1.5 collective-permute-start.8
  64.0 1.2 collective-permute-done.8.s
  65.1 15.1 %collective-permute-done.9.refs_1_ = bf16[336,2688]{1,0:T(8,128)(2,1)S(1)} collective-permute-done((bf16[336,2688]{1,0:T(8,128)(2,1)S(1)}, bf16[336,2688]{1,0:T(8,128)(2,1)S(1)}, u32[]{:S(2)}, u32[]{:S(2)}) %collective-permute-start.9) | collective-permute-done | bytes 1806368 | tf_op jit(solution)/shard_map/ppermute | solution.py:90
  80.2 7.8 %project.1 = (bf16[64,5376]{1,0:T(8,128)(2,1)S(1)}, bf16[32,5376]{1,0:T(8,128)(2,1)S(1)}, bf16[32,5376]{1,0:T(8,128)(2,1)S(1)}, bf16[32,5376]{1,0:T(8,128)(2,1)S...) custom-call(bf16[256,512]{1,0:T(8,128)(2,1)S(1)} %bitcast.129, ...), custom_call_target="tpu_custom_call" | custom-call | bytes 1000 | tf_op jit(solution)/shard_map/project/pallas_call | solution.py:147
  88.1 4.0 %collective-permute-start.13 = (bf16[32,5376]{1,0:T(8,128)(2,1)S(1)}, bf16[32,5376]{1,0:T(8,128)(2,1)S(1)}, u32[]{:S(2)}, u32[]{:S(2)}) collective-permute-start(bf16[32,5376]{1,0:T(8,128)(2,1)S(1)} %get-tuple-element.69), channel_id=1, source_target_pairs={{0,2},{2,4},{4,6},{6,0},{1,3},{3,5},{5,7},{7,1},{8,10},{10,12},{12... | collective-permute-start | bytes 1032200 | tf_op jit(solution)/shard_map/ppermute | solution.py:34
  92.1 2.2 collective-permute-start.14
  94.3 2.7 %collective-permute-start.12 = (bf16[336,2688]{1,0:T(8,128)(2,1)}, bf16[336,2688]{1,0:T(8,128)(2,1)}, u32[]{:S(2)}, u32[]{:S(2)}) collective-permute-start(bf16[336,2688]{1,0:T(8,128)(2,1)} %collective-permute-done.6.refs_2_), channel_id=1, source_target_pairs={{0,96},{1,25},{2,98},{3,27},{4,100},{5,29},{6,102},{7,31},{8,104},... | collective-permute-start | bytes 5419016 | tf_op jit(solution)/shard_map/ppermute | solution.py:90
  97.0 3.6 %collective-permute-done.13 = bf16[32,5376]{1,0:T(8,128)(2,1)S(1)} collective-permute-done((bf16[32,5376]{1,0:T(8,128)(2,1)S(1)}, bf16[32,5376]{1,0:T(8,128)(2,1)S(1)}, u32[]{:S(2)}, u32[]{:S(2)}) %collective-permute-start.13) | collective-permute-done | bytes 344096 | tf_op jit(solution)/shard_map/ppermute | solution.py:34
  100.7 1.1 collective-permute-start.20
  101.9 15.9 %collective-permute-done.11.refs_6_ = bf16[336,2688]{1,0:T(8,128)(2,1)S(1)} collective-permute-done((bf16[336,2688]{1,0:T(8,128)(2,1)}, bf16[336,2688]{1,0:T(8,128)(2,1)S(1)}, u32[]{:S(2)}, u32[]{:S(2)}) %collective-permute-start.11) | collective-permute-done | bytes 1806368 | tf_op jit(solution)/shard_map/ppermute | solution.py:90
  117.9 2.6 %collective-permute-start.24 = (bf16[336,2688]{1,0:T(8,128)(2,1)S(1)}, bf16[336,2688]{1,0:T(8,128)(2,1)S(1)}, u32[]{:S(2)}, u32[]{:S(2)}) collective-permute-start(bf16[336,2688]{1,0:T(8,128)(2,1)S(1)} %collective-permute-done.9.refs_1_), channel_id=1, source_target_pairs={{0,96},{1,25},{2,98},{3,27},{4,100},{5,29},{6,102},{7,31},{8,104},... | collective-permute-start | bytes 5419016 | tf_op jit(solution)/shard_map/ppermute | solution.py:90
  120.5 4.8 %collective-permute-done.17.at_ref = bf16[32,5376]{1,0:T(8,128)(2,1)S(1)} collective-permute-done((bf16[32,5376]{1,0:T(8,128)(2,1)S(1)}, bf16[32,5376]{1,0:T(8,128)(2,1)S(1)}, u32[]{:S(2)}, u32[]{:S(2)}) %collective-permute-start.17) | collective-permute-done | bytes 344096 | tf_op jit(solution)/shard_map/ppermute | solution.py:34
  125.4 1.1 norm.1
  126.7 2.6 %collective-permute-start.22 = (bf16[64,5376]{1,0:T(8,128)(2,1)S(1)}, bf16[64,5376]{1,0:T(8,128)(2,1)S(1)}, u32[]{:S(2)}, u32[]{:S(2)}) collective-permute-start(bf16[64,5376]{1,0:T(8,128)(2,1)S(1)} %get-tuple-element.85.refs_0_), channel_id=1, source_target_pairs={{0,6},{2,0},{4,2},{6,4},{1,7},{3,1},{5,3},{7,5},{8,14},{10,8},{12,... | collective-permute-start | bytes 2064392 | tf_op jit(solution)/shard_map/ppermute | solution.py:34
  129.2 12.3 %collective-permute-done.21.refs_1_ = bf16[64,5376]{1,0:T(8,128)(2,1)S(1)} collective-permute-done((bf16[64,5376]{1,0:T(8,128)(2,1)S(1)}, bf16[64,5376]{1,0:T(8,128)(2,1)S(1)}, u32[]{:S(2)}, u32[]{:S(2)}) %collective-permute-start.21) | collective-permute-done | bytes 688160 | tf_op jit(solution)/shard_map/ppermute | solution.py:34
  141.6 11.6 %collective-permute-start.27 = (bf16[64,5376]{1,0:T(8,128)(2,1)S(1)}, bf16[64,5376]{1,0:T(8,128)(2,1)S(1)}, u32[]{:S(2)}, u32[]{:S(2)}) collective-permute-start(bf16[64,5376]{1,0:T(8,128)(2,1)S(1)} %get-tuple-element.85.refs_0_), channel_id=1, source_target_pairs={{0,1},{1,0},{2,3},{3,2},{4,5},{5,4},{6,7},{7,6},{8,9},{9,8},{10,11... | collective-permute-start | bytes 2064392 | tf_op jit(solution)/shard_map/ppermute | solution.py:34
  153.4 3.5 %collective-permute-start.26 = (bf16[32,5376]{1,0:T(8,128)(2,1)S(1)}, bf16[32,5376]{1,0:T(8,128)(2,1)S(1)}, u32[]{:S(2)}, u32[]{:S(2)}) collective-permute-start(bf16[32,5376]{1,0:T(8,128)(2,1)S(1)} %slice.77), channel_id=1, source_target_pairs={{0,6},{2,0},{4,2},{6,4},{1,7},{3,1},{5,3},{7,5},{8,14},{10,8},{12,... | collective-permute-start | bytes 1032200 | tf_op jit(solution)/shard_map/ppermute | solution.py:34
  157.1 3.3 %collective-permute-done.32.refs_7_ = bf16[336,2688]{1,0:T(8,128)(2,1)S(1)} collective-permute-done((bf16[336,2688]{1,0:T(8,128)(2,1)S(1)}, bf16[336,2688]{1,0:T(8,128)(2,1)S(1)}, u32[]{:S(2)}, u32[]{:S(2)}) %collective-permute-start.32) | collective-permute-done | bytes 1806368 | tf_op jit(solution)/shard_map/ppermute | solution.py:90
  160.5 11.3 %collective-permute-start.29 = (bf16[64,5376]{1,0:T(8,128)(2,1)S(1)}, bf16[64,5376]{1,0:T(8,128)(2,1)S(1)}, u32[]{:S(2)}, u32[]{:S(2)}) collective-permute-start(bf16[64,5376]{1,0:T(8,128)(2,1)S(1)} %collective-permute-done.22.refs_2_), channel_id=1, source_target_pairs={{0,1},{1,0},{2,3},{3,2},{4,5},{5,4},{6,7},{7,6},{8,9},{9,8},{10,11... | collective-permute-start | bytes 2064392 | tf_op jit(solution)/shard_map/ppermute | solution.py:34
  172.3 1.7 collective-permute-done.30.refs_8_
  174.6 2.7 %collective-permute-start.41 = (bf16[336,2688]{1,0:T(8,128)(2,1)}, bf16[336,2688]{1,0:T(8,128)(2,1)}, u32[]{:S(2)}, u32[]{:S(2)}) collective-permute-start(bf16[336,2688]{1,0:T(8,128)(2,1)} %collective-permute-done.33.refs_11_), channel_id=1, source_target_pairs={{0,96},{1,25},{2,98},{3,27},{4,100},{5,29},{6,102},{7,31},{8,104},... | collective-permute-start | bytes 5419016 | tf_op jit(solution)/shard_map/ppermute | solution.py:90
  177.3 5.1 %order.1.refs_13_.refs_5_ = bf16[512,5632]{1,0:T(8,128)(2,1)S(1)} custom-call(bf16[64,5376]{1,0:T(8,128)(2,1)S(1)} %get-tuple-element.85.refs_0_, bf16[64,5376]{1,0:T(8,128)(2,1)S(1)} %collective-permute-done.21.refs_1_, bf16[64,5376]{1,0:T(8,128)(2,1)S(1)} %collective-permute-done.22.refs_2_, bf16[32,5376]{1,0:T(8,128)(2,1)S(1)} %collective-permute-done.25.refs_3_, ...), custom_call_target="tpu_custom_call" | custom-call | bytes 1000 | tf_op jit(solution)/shard_map/order/pallas_call | solution.py:241
  182.4 2.5 %copy-done = bf16[512,5632]{1,0:T(8,128)(2,1)} copy-done((bf16[512,5632]{1,0:T(8,128)(2,1)}, bf16[512,5632]{1,0:T(8,128)(2,1)S(1)}, u32[]{:S(2)}) %copy-start) | copy-done | bytes 5767192
  184.9 2.1 collective-permute-start.34
  187.0 22.1 %near.1.refs_6_ = f32[512,2688]{1,0:T(8,128)} custom-call(bf16[336,2688]{1,0:T(8,128)(2,1)} %copy-done.1, bf16[336,2688]{1,0:T(8,128)(2,1)} %copy-done.13, bf16[336,2688]{1,0:T(8,128)(2,1)} %collective-permute-done.6.refs_2_, bf16[336,2688]{1,0:T(8,128)(2,1)} %copy-done.14, bf16[336,2688]{1,0:T(8,128)(2,1)} %collective-permute-done.16.refs_4_, ...), custom_call_target="tpu_custom_call" | custom-call | bytes 1000 | tf_op jit(solution)/shard_map/near/pallas_call | solution.py:298
  210.0 1.3 collective-permute-start.37
  211.3 5.6 %collective-permute-done.39.refs_1_ = bf16[336,2688]{1,0:T(8,128)(2,1)S(1)} collective-permute-done((bf16[336,2688]{1,0:T(8,128)(2,1)}, bf16[336,2688]{1,0:T(8,128)(2,1)S(1)}, u32[]{:S(2)}, u32[]{:S(2)}) %collective-permute-start.39) | collective-permute-done | bytes 1806368 | tf_op jit(solution)/shard_map/ppermute | solution.py:90
  216.9 1.2 copy-done.11
  218.1 13.5 %far.1 = bf16[1344,512]{1,0:T(8,128)(2,1)} custom-call(bf16[336,2688]{1,0:T(8,128)(2,1)} %copy-done.10, bf16[336,2688]{1,0:T(8,128)(2,1)} %copy-done.11, bf16[336,2688]{1,0:T(8,128)(2,1)} %copy-done.9, bf16[336,2688]{1,0:T(8,128)(2,1)} %collective-permute-done.41.refs_3_, s32[4]{0:T(128)} %copy-done.7, bf16[512,5632]{1,0:T(8,128)(2,1)} %copy-done, ...), custom_call_target="tpu_custom_call" | custom-call | flops 3699376128 | bytes 12730368 | tf_op jit(solution)/shard_map/far/pallas_call | solution.py:342
  231.9 1.1 copy.34
  (137 shorter events, 9.2 us)
Async XLA Ops:
  0.6 79.6 %collective-permute-start.10 = (bf16[512,5376]{1,0:T(8,128)(2,1)}, bf16[512,5376]{1,0:T(8,128)(2,1)}, u32[]{:S(2)}, u32[]{:S(2)}) collective-permute-start(bf16[512,5376]{1,0:T(8,128)(2,1)} %w_ref.1), channel_id=1, source_target_pairs={{0,1},{1,0},{2,3},{3,2},{4,5},{5,4},{6,7},{7,6},{8,9},{9,8},{10,11... | collective-permute-start | bytes 16515080 | tf_op jit(solution)/shard_map/ppermute | solution.py:34
  6.9 47.0 %copy-start.1 = (bf16[336,2688]{1,0:T(8,128)(2,1)}, bf16[336,2688]{1,0:T(8,128)(2,1)S(1)}, u32[]{:S(2)}) copy-start(bf16[336,2688]{1,0:T(8,128)(2,1)S(1)} %pack.1.refs_0_) | copy-start | bytes 5419012
  6.9 39.5 %collective-permute-start.6 = (bf16[336,2688]{1,0:T(8,128)(2,1)S(1)}, bf16[336,2688]{1,0:T(8,128)(2,1)}, u32[]{:S(2)}, u32[]{:S(2)}) collective-permute-start(bf16[336,2688]{1,0:T(8,128)(2,1)S(1)} %pack.1.refs_0_), channel_id=1, source_target_pairs={{0,24},{1,97},{2,26},{3,99},{4,28},{5,101},{6,30},{7,103},{8,0},{9... | collective-permute-start | bytes 5419016 | tf_op jit(solution)/shard_map/ppermute | solution.py:90
  12.4 3.6 %collective-permute-start = (bf16[4,80,672]{2,1,0:T(8,128)(2,1)}, bf16[4,80,672]{2,1,0:T(8,128)(2,1)}, u32[]{:S(2)}, u32[]{:S(2)}) collective-permute-start(bf16[4,80,672]{2,1,0:T(8,128)(2,1)} %fusion.6), channel_id=1, source_target_pairs={{0,1},{1,0},{2,3},{3,2},{4,5},{5,4},{6,7},{7,6},{8,9},{9,8},{10,11... | collective-permute-start | bytes 1290248 | tf_op jit(solution)/shard_map/ppermute | solution.py:34
  12.5 13.8 %collective-permute-start.4 = (bf16[512,512]{1,0:T(8,128)(2,1)S(1)}, bf16[512,512]{1,0:T(8,128)(2,1)S(1)}, u32[]{:S(2)}, u32[]{:S(2)}) collective-permute-start(bf16[512,512]{1,0:T(8,128)(2,1)S(1)} %pair.1.kv0_ref), channel_id=1, source_target_pairs={{0,8},{8,16},{16,24},{24,32},{32,40},{40,48},{48,56},{56,64},{64,7... | collective-permute-start | bytes 1572872 | tf_op jit(solution)/shard_map/ppermute | solution.py:39
  16.0 161.3 %copy-start.7 = (s32[4]{0:T(128)}, s32[4]{0:T(128)S(1)}, u32[]{:S(2)}) copy-start(s32[4]{0:T(128)S(1)} %pad_add_fusion.at_ref.refs_10_.refs_12_.refs_4_) | copy-start | bytes 52
  16.1 64.2 %slice-start = ((s8[5505024]{0:T(1024)(128)(4,1)}), s8[4194304]{0:T(1024)(128)(4,1)S(1)}, s32[]{:S(2)}) async-start(s8[5505024]{0:T(1024)(128)(4,1)} %bitcast.124), calls=%async_computation | async-start | bytes 8388608
  18.5 17.2 %collective-permute-start.1 = (bf16[2,80,672]{2,1,0:T(8,128)(2,1)S(1)}, bf16[2,80,672]{2,1,0:T(8,128)(2,1)S(1)}, u32[]{:S(2)}, u32[]{:S(2)}) collective-permute-start(bf16[2,80,672]{2,1,0:T(8,128)(2,1)S(1)} %get-tuple-element.118), channel_id=1, source_target_pairs={{0,6},{2,0},{4,2},{6,4},{1,7},{3,1},{5,3},{7,5},{8,14},{10,8},{12,... | collective-permute-start | bytes 645128 | tf_op jit(solution)/shard_map/ppermute | solution.py:34
  26.3 20.1 %collective-permute-start.5 = (bf16[512,512]{1,0:T(8,128)(2,1)S(1)}, bf16[512,512]{1,0:T(8,128)(2,1)S(1)}, u32[]{:S(2)}, u32[]{:S(2)}) collective-permute-start(bf16[512,512]{1,0:T(8,128)(2,1)S(1)} %collective-permute-done.4.kv1_ref), channel_id=1, source_target_pairs={{0,8},{8,16},{16,24},{24,32},{32,40},{40,48},{48,56},{56,64},{64,7... | collective-permute-start | bytes 1572872 | tf_op jit(solution)/shard_map/ppermute | solution.py:39
  30.6 25.0 %collective-permute-start.7 = (bf16[336,2688]{1,0:T(8,128)(2,1)S(1)}, bf16[336,2688]{1,0:T(8,128)(2,1)S(1)}, u32[]{:S(2)}, u32[]{:S(2)}) collective-permute-start(bf16[336,2688]{1,0:T(8,128)(2,1)S(1)} %pack.1.refs_0_), channel_id=1, source_target_pairs={{0,96},{1,25},{2,98},{3,27},{4,100},{5,29},{6,102},{7,31},{8,104},... | collective-permute-start | bytes 5419016 | tf_op jit(solution)/shard_map/ppermute | solution.py:90
  35.7 9.9 %collective-permute-start.2 = (bf16[2,80,672]{2,1,0:T(8,128)(2,1)S(1)}, bf16[2,80,672]{2,1,0:T(8,128)(2,1)S(1)}, u32[]{:S(2)}, u32[]{:S(2)}) collective-permute-start(bf16[2,80,672]{2,1,0:T(8,128)(2,1)S(1)} %get-tuple-element.117), channel_id=1, source_target_pairs={{0,4},{2,6},{4,0},{6,2},{1,5},{3,7},{5,1},{7,3},{8,12},{10,14},{12... | collective-permute-start | bytes 645128 | tf_op jit(solution)/shard_map/ppermute | solution.py:34
  45.6 8.2 %collective-permute-start.3 = (bf16[2,80,672]{2,1,0:T(8,128)(2,1)S(1)}, bf16[2,80,672]{2,1,0:T(8,128)(2,1)S(1)}, u32[]{:S(2)}, u32[]{:S(2)}) collective-permute-start(bf16[2,80,672]{2,1,0:T(8,128)(2,1)S(1)} %get-tuple-element.116), channel_id=1, source_target_pairs={{0,2},{2,4},{4,6},{6,0},{1,3},{3,5},{5,7},{7,1},{8,10},{10,12},{12... | collective-permute-start | bytes 645128 | tf_op jit(solution)/shard_map/ppermute | solution.py:34
  46.4 33.8 %collective-permute-start.9 = (bf16[336,2688]{1,0:T(8,128)(2,1)S(1)}, bf16[336,2688]{1,0:T(8,128)(2,1)S(1)}, u32[]{:S(2)}, u32[]{:S(2)}) collective-permute-start(bf16[336,2688]{1,0:T(8,128)(2,1)S(1)} %pack.1.refs_0_), channel_id=1, source_target_pairs={{0,8},{1,33},{2,10},{3,35},{4,12},{5,37},{6,14},{7,39},{8,16},{9,4... | collective-permute-start | bytes 5419016 | tf_op jit(solution)/shard_map/ppermute | solution.py:90
  53.9 26.3 %slice-start.1 = ((s8[5505024]{0:T(1024)(128)(4,1)}), s8[1310720]{0:T(1024)(128)(4,1)S(1)}, s32[]{:S(2)}) async-start(s8[5505024]{0:T(1024)(128)(4,1)} %bitcast.124), calls=%async_computation.1 | async-start | bytes 2621440
  53.9 43.1 %collective-permute-start.16 = (bf16[336,2688]{1,0:T(8,128)(2,1)S(1)}, bf16[336,2688]{1,0:T(8,128)(2,1)}, u32[]{:S(2)}, u32[]{:S(2)}) collective-permute-start(bf16[336,2688]{1,0:T(8,128)(2,1)S(1)} %pack.1.refs_0_), channel_id=1, source_target_pairs={{0,32},{1,9},{2,34},{3,11},{4,36},{5,13},{6,38},{7,15},{8,40},{9,1... | collective-permute-start | bytes 5419016 | tf_op jit(solution)/shard_map/ppermute | solution.py:90
  54.0 40.3 %collective-permute-start.15 = (bf16[336,2688]{1,0:T(8,128)(2,1)}, bf16[336,2688]{1,0:T(8,128)(2,1)S(1)}, u32[]{:S(2)}, u32[]{:S(2)}) collective-permute-start(bf16[336,2688]{1,0:T(8,128)(2,1)} %collective-permute-done.6.refs_2_), channel_id=1, source_target_pairs={{0,24},{1,97},{2,26},{3,99},{4,28},{5,101},{6,30},{7,103},{8,0},{9... | collective-permute-start | bytes 5419016 | tf_op jit(solution)/shard_map/ppermute | solution.py:90
  62.4 2.7 %collective-permute-start.8 = (bf16[256,512]{1,0:T(8,128)(2,1)S(1)}, bf16[256,512]{1,0:T(8,128)(2,1)S(1)}, u32[]{:S(2)}, u32[]{:S(2)}) collective-permute-start(bf16[256,512]{1,0:T(8,128)(2,1)S(1)} %bitcast.134), channel_id=1, source_target_pairs={{0,1},{1,0},{2,3},{3,2},{4,5},{5,4},{6,7},{7,6},{8,9},{9,8},{10,11... | collective-permute-start | bytes 786440 | tf_op jit(solution)/shard_map/ppermute | solution.py:34
  80.2 37.7 %copy-start.13 = (bf16[336,2688]{1,0:T(8,128)(2,1)}, bf16[336,2688]{1,0:T(8,128)(2,1)S(1)}, u32[]{:S(2)}) copy-start(bf16[336,2688]{1,0:T(8,128)(2,1)S(1)} %collective-permute-done.9.refs_1_) | copy-start | bytes 5419012
  88.1 12.5 %collective-permute-start.13 = (bf16[32,5376]{1,0:T(8,128)(2,1)S(1)}, bf16[32,5376]{1,0:T(8,128)(2,1)S(1)}, u32[]{:S(2)}, u32[]{:S(2)}) collective-permute-start(bf16[32,5376]{1,0:T(8,128)(2,1)S(1)} %get-tuple-element.69), channel_id=1, source_target_pairs={{0,2},{2,4},{4,6},{6,0},{1,3},{3,5},{5,7},{7,1},{8,10},{10,12},{12... | collective-permute-start | bytes 1032200 | tf_op jit(solution)/shard_map/ppermute | solution.py:34
  92.1 8.5 %collective-permute-start.14 = (bf16[32,5376]{1,0:T(8,128)(2,1)S(1)}, bf16[32,5376]{1,0:T(8,128)(2,1)S(1)}, u32[]{:S(2)}, u32[]{:S(2)}) collective-permute-start(bf16[32,5376]{1,0:T(8,128)(2,1)S(1)} %get-tuple-element.70), channel_id=1, source_target_pairs={{0,6},{2,0},{4,2},{6,4},{1,7},{3,1},{5,3},{7,5},{8,14},{10,8},{12,... | collective-permute-start | bytes 1032200 | tf_op jit(solution)/shard_map/ppermute | solution.py:34
  94.3 23.5 %collective-permute-start.11 = (bf16[336,2688]{1,0:T(8,128)(2,1)}, bf16[336,2688]{1,0:T(8,128)(2,1)S(1)}, u32[]{:S(2)}, u32[]{:S(2)}) collective-permute-start(bf16[336,2688]{1,0:T(8,128)(2,1)} %collective-permute-done.6.refs_2_), channel_id=1, source_target_pairs={{0,32},{1,9},{2,34},{3,11},{4,36},{5,13},{6,38},{7,15},{8,40},{9,1... | collective-permute-start | bytes 5419016 | tf_op jit(solution)/shard_map/ppermute | solution.py:90
  94.3 47.3 %copy-start.14 = (bf16[336,2688]{1,0:T(8,128)(2,1)}, bf16[336,2688]{1,0:T(8,128)(2,1)S(1)}, u32[]{:S(2)}) copy-start(bf16[336,2688]{1,0:T(8,128)(2,1)S(1)} %collective-permute-done.15.refs_3_) | copy-start | bytes 5419012
  94.3 23.5 %collective-permute-start.12 = (bf16[336,2688]{1,0:T(8,128)(2,1)}, bf16[336,2688]{1,0:T(8,128)(2,1)}, u32[]{:S(2)}, u32[]{:S(2)}) collective-permute-start(bf16[336,2688]{1,0:T(8,128)(2,1)} %collective-permute-done.6.refs_2_), channel_id=1, source_target_pairs={{0,96},{1,25},{2,98},{3,27},{4,100},{5,29},{6,102},{7,31},{8,104},... | collective-permute-start | bytes 5419016 | tf_op jit(solution)/shard_map/ppermute | solution.py:90
  97.0 20.9 %collective-permute-start.18 = (bf16[32,5376]{1,0:T(8,128)(2,1)S(1)}, bf16[32,5376]{1,0:T(8,128)(2,1)S(1)}, u32[]{:S(2)}, u32[]{:S(2)}) collective-permute-start(bf16[32,5376]{1,0:T(8,128)(2,1)S(1)} %get-tuple-element.74), channel_id=1, source_target_pairs={{0,2},{2,4},{4,6},{6,0},{1,3},{3,5},{5,7},{7,1},{8,10},{10,12},{12... | collective-permute-start | bytes 1032200 | tf_op jit(solution)/shard_map/ppermute | solution.py:34
  100.6 20.0 %collective-permute-start.19 = (bf16[32,5376]{1,0:T(8,128)(2,1)S(1)}, bf16[32,5376]{1,0:T(8,128)(2,1)S(1)}, u32[]{:S(2)}, u32[]{:S(2)}) collective-permute-start(bf16[32,5376]{1,0:T(8,128)(2,1)S(1)} %get-tuple-element.75), channel_id=1, source_target_pairs={{0,6},{2,0},{4,2},{6,4},{1,7},{3,1},{5,3},{7,5},{8,14},{10,8},{12,... | collective-permute-start | bytes 1032200 | tf_op jit(solution)/shard_map/ppermute | solution.py:34
  100.7 19.9 %collective-permute-start.20 = (bf16[32,5376]{1,0:T(8,128)(2,1)S(1)}, bf16[32,5376]{1,0:T(8,128)(2,1)S(1)}, u32[]{:S(2)}, u32[]{:S(2)}) collective-permute-start(bf16[32,5376]{1,0:T(8,128)(2,1)S(1)} %add_convert_fusion), channel_id=1, source_target_pairs={{0,6},{2,0},{4,2},{6,4},{1,7},{3,1},{5,3},{7,5},{8,14},{10,8},{12,... | collective-permute-start | bytes 1032200 | tf_op jit(solution)/shard_map/ppermute | solution.py:34
  117.8 7.6 %collective-permute-start.17 = (bf16[32,5376]{1,0:T(8,128)(2,1)S(1)}, bf16[32,5376]{1,0:T(8,128)(2,1)S(1)}, u32[]{:S(2)}, u32[]{:S(2)}) collective-permute-start(bf16[32,5376]{1,0:T(8,128)(2,1)S(1)} %add_convert_fusion.1), channel_id=1, source_target_pairs={{0,2},{2,4},{4,6},{6,0},{1,3},{3,5},{5,7},{7,1},{8,10},{10,12},{12... | collective-permute-start | bytes 1032200 | tf_op jit(solution)/shard_map/ppermute | solution.py:34
  117.8 35.4 %collective-permute-start.23 = (bf16[336,2688]{1,0:T(8,128)(2,1)S(1)}, bf16[336,2688]{1,0:T(8,128)(2,1)}, u32[]{:S(2)}, u32[]{:S(2)}) collective-permute-start(bf16[336,2688]{1,0:T(8,128)(2,1)S(1)} %collective-permute-done.9.refs_1_), channel_id=1, source_target_pairs={{0,32},{1,9},{2,34},{3,11},{4,36},{5,13},{6,38},{7,15},{8,40},{9,1... | collective-permute-start | bytes 5419016 | tf_op jit(solution)/shard_map/ppermute | solution.py:90
  117.9 35.3 %collective-permute-start.24 = (bf16[336,2688]{1,0:T(8,128)(2,1)S(1)}, bf16[336,2688]{1,0:T(8,128)(2,1)S(1)}, u32[]{:S(2)}, u32[]{:S(2)}) collective-permute-start(bf16[336,2688]{1,0:T(8,128)(2,1)S(1)} %collective-permute-done.9.refs_1_), channel_id=1, source_target_pairs={{0,96},{1,25},{2,98},{3,27},{4,100},{5,29},{6,102},{7,31},{8,104},... | collective-permute-start | bytes 5419016 | tf_op jit(solution)/shard_map/ppermute | solution.py:90
  126.5 15.1 %collective-permute-start.21 = (bf16[64,5376]{1,0:T(8,128)(2,1)S(1)}, bf16[64,5376]{1,0:T(8,128)(2,1)S(1)}, u32[]{:S(2)}, u32[]{:S(2)}) collective-permute-start(bf16[64,5376]{1,0:T(8,128)(2,1)S(1)} %get-tuple-element.85.refs_0_), channel_id=1, source_target_pairs={{0,2},{2,4},{4,6},{6,0},{1,3},{3,5},{5,7},{7,1},{8,10},{10,12},{12... | collective-permute-start | bytes 2064392 | tf_op jit(solution)/shard_map/ppermute | solution.py:34
  126.6 33.9 %collective-permute-start.32 = (bf16[336,2688]{1,0:T(8,128)(2,1)S(1)}, bf16[336,2688]{1,0:T(8,128)(2,1)S(1)}, u32[]{:S(2)}, u32[]{:S(2)}) collective-permute-start(bf16[336,2688]{1,0:T(8,128)(2,1)S(1)} %collective-permute-done.15.refs_3_), channel_id=1, source_target_pairs={{0,32},{1,9},{2,34},{3,11},{4,36},{5,13},{6,38},{7,15},{8,40},{9,1... | collective-permute-start | bytes 5419016 | tf_op jit(solution)/shard_map/ppermute | solution.py:90
  126.7 14.9 %collective-permute-start.22 = (bf16[64,5376]{1,0:T(8,128)(2,1)S(1)}, bf16[64,5376]{1,0:T(8,128)(2,1)S(1)}, u32[]{:S(2)}, u32[]{:S(2)}) collective-permute-start(bf16[64,5376]{1,0:T(8,128)(2,1)S(1)} %get-tuple-element.85.refs_0_), channel_id=1, source_target_pairs={{0,6},{2,0},{4,2},{6,4},{1,7},{3,1},{5,3},{7,5},{8,14},{10,8},{12,... | collective-permute-start | bytes 2064392 | tf_op jit(solution)/shard_map/ppermute | solution.py:34
  141.6 30.7 %collective-permute-start.33 = (bf16[336,2688]{1,0:T(8,128)(2,1)S(1)}, bf16[336,2688]{1,0:T(8,128)(2,1)}, u32[]{:S(2)}, u32[]{:S(2)}) collective-permute-start(bf16[336,2688]{1,0:T(8,128)(2,1)S(1)} %collective-permute-done.15.refs_3_), channel_id=1, source_target_pairs={{0,96},{1,25},{2,98},{3,27},{4,100},{5,29},{6,102},{7,31},{8,104},... | collective-permute-start | bytes 5419016 | tf_op jit(solution)/shard_map/ppermute | solution.py:90
  141.6 15.3 %collective-permute-start.27 = (bf16[64,5376]{1,0:T(8,128)(2,1)S(1)}, bf16[64,5376]{1,0:T(8,128)(2,1)S(1)}, u32[]{:S(2)}, u32[]{:S(2)}) collective-permute-start(bf16[64,5376]{1,0:T(8,128)(2,1)S(1)} %get-tuple-element.85.refs_0_), channel_id=1, source_target_pairs={{0,1},{1,0},{2,3},{3,2},{4,5},{5,4},{6,7},{7,6},{8,9},{9,8},{10,11... | collective-permute-start | bytes 2064392 | tf_op jit(solution)/shard_map/ppermute | solution.py:34
  153.3 18.5 %collective-permute-start.25 = (bf16[32,5376]{1,0:T(8,128)(2,1)S(1)}, bf16[32,5376]{1,0:T(8,128)(2,1)S(1)}, u32[]{:S(2)}, u32[]{:S(2)}) collective-permute-start(bf16[32,5376]{1,0:T(8,128)(2,1)S(1)} %slice.76), channel_id=1, source_target_pairs={{0,2},{2,4},{4,6},{6,0},{1,3},{3,5},{5,7},{7,1},{8,10},{10,12},{12... | collective-permute-start | bytes 1032200 | tf_op jit(solution)/shard_map/ppermute | solution.py:34
  153.4 18.5 %collective-permute-start.26 = (bf16[32,5376]{1,0:T(8,128)(2,1)S(1)}, bf16[32,5376]{1,0:T(8,128)(2,1)S(1)}, u32[]{:S(2)}, u32[]{:S(2)}) collective-permute-start(bf16[32,5376]{1,0:T(8,128)(2,1)S(1)} %slice.77), channel_id=1, source_target_pairs={{0,6},{2,0},{4,2},{6,4},{1,7},{3,1},{5,3},{7,5},{8,14},{10,8},{12,... | collective-permute-start | bytes 1032200 | tf_op jit(solution)/shard_map/ppermute | solution.py:34
  156.8 17.7 %collective-permute-start.28 = (bf16[64,5376]{1,0:T(8,128)(2,1)S(1)}, bf16[64,5376]{1,0:T(8,128)(2,1)S(1)}, u32[]{:S(2)}, u32[]{:S(2)}) collective-permute-start(bf16[64,5376]{1,0:T(8,128)(2,1)S(1)} %collective-permute-done.21.refs_1_), channel_id=1, source_target_pairs={{0,1},{1,0},{2,3},{3,2},{4,5},{5,4},{6,7},{7,6},{8,9},{9,8},{10,11... | collective-permute-start | bytes 2064392 | tf_op jit(solution)/shard_map/ppermute | solution.py:34
  160.5 14.1 %collective-permute-start.29 = (bf16[64,5376]{1,0:T(8,128)(2,1)S(1)}, bf16[64,5376]{1,0:T(8,128)(2,1)S(1)}, u32[]{:S(2)}, u32[]{:S(2)}) collective-permute-start(bf16[64,5376]{1,0:T(8,128)(2,1)S(1)} %collective-permute-done.22.refs_2_), channel_id=1, source_target_pairs={{0,1},{1,0},{2,3},{3,2},{4,5},{5,4},{6,7},{7,6},{8,9},{9,8},{10,11... | collective-permute-start | bytes 2064392 | tf_op jit(solution)/shard_map/ppermute | solution.py:34
  171.8 2.3 collective-permute-start.30
  171.9 2.7 %collective-permute-start.31 = (bf16[32,5376]{1,0:T(8,128)(2,1)S(1)}, bf16[32,5376]{1,0:T(8,128)(2,1)S(1)}, u32[]{:S(2)}, u32[]{:S(2)}) collective-permute-start(bf16[32,5376]{1,0:T(8,128)(2,1)S(1)} %collective-permute-done.26.refs_4_), channel_id=1, source_target_pairs={{0,1},{1,0},{2,3},{3,2},{4,5},{5,4},{6,7},{7,6},{8,9},{9,8},{10,11... | collective-permute-start | bytes 1032200 | tf_op jit(solution)/shard_map/ppermute | solution.py:34
  172.3 37.6 %collective-permute-start.40 = (bf16[336,2688]{1,0:T(8,128)(2,1)}, bf16[336,2688]{1,0:T(8,128)(2,1)S(1)}, u32[]{:S(2)}, u32[]{:S(2)}) collective-permute-start(bf16[336,2688]{1,0:T(8,128)(2,1)} %collective-permute-done.12.refs_10_), channel_id=1, source_target_pairs={{0,96},{1,25},{2,98},{3,27},{4,100},{5,29},{6,102},{7,31},{8,104},... | collective-permute-start | bytes 5419016 | tf_op jit(solution)/shard_map/ppermute | solution.py:90
  174.1 36.0 %collective-permute-start.38 = (bf16[336,2688]{1,0:T(8,128)(2,1)}, bf16[336,2688]{1,0:T(8,128)(2,1)S(1)}, u32[]{:S(2)}, u32[]{:S(2)}) collective-permute-start(bf16[336,2688]{1,0:T(8,128)(2,1)} %collective-permute-done.16.refs_4_), channel_id=1, source_target_pairs={{0,32},{1,9},{2,34},{3,11},{4,36},{5,13},{6,38},{7,15},{8,40},{9,1... | collective-permute-start | bytes 5419016 | tf_op jit(solution)/shard_map/ppermute | solution.py:90
  174.5 42.3 %collective-permute-start.39 = (bf16[336,2688]{1,0:T(8,128)(2,1)}, bf16[336,2688]{1,0:T(8,128)(2,1)S(1)}, u32[]{:S(2)}, u32[]{:S(2)}) collective-permute-start(bf16[336,2688]{1,0:T(8,128)(2,1)} %collective-permute-done.23.refs_5_), channel_id=1, source_target_pairs={{0,32},{1,9},{2,34},{3,11},{4,36},{5,13},{6,38},{7,15},{8,40},{9,1... | collective-permute-start | bytes 5419016 | tf_op jit(solution)/shard_map/ppermute | solution.py:90
  174.6 42.3 %collective-permute-start.41 = (bf16[336,2688]{1,0:T(8,128)(2,1)}, bf16[336,2688]{1,0:T(8,128)(2,1)}, u32[]{:S(2)}, u32[]{:S(2)}) collective-permute-start(bf16[336,2688]{1,0:T(8,128)(2,1)} %collective-permute-done.33.refs_11_), channel_id=1, source_target_pairs={{0,96},{1,25},{2,98},{3,27},{4,100},{5,29},{6,102},{7,31},{8,104},... | collective-permute-start | bytes 5419016 | tf_op jit(solution)/shard_map/ppermute | solution.py:90
  184.9 24.2 %collective-permute-start.34 = (bf16[4,64,672]{2,1,0:T(8,128)(2,1)S(1)}, bf16[4,64,672]{2,1,0:T(8,128)(2,1)S(1)}, u32[]{:S(2)}, u32[]{:S(2)}) collective-permute-start(bf16[4,64,672]{2,1,0:T(8,128)(2,1)S(1)} %select_bitcast_fusion.2), channel_id=1, source_target_pairs={{0,1},{1,0},{2,3},{3,2},{4,5},{5,4},{6,7},{7,6},{8,9},{9,8},{10,11... | collective-permute-start | bytes 1032200 | tf_op jit(solution)/shard_map/ppermute | solution.py:34
  209.7 21.9 %collective-permute-start.35 = (bf16[2,64,672]{2,1,0:T(8,128)(2,1)S(1)}, bf16[2,64,672]{2,1,0:T(8,128)(2,1)S(1)}, u32[]{:S(2)}, u32[]{:S(2)}) collective-permute-start(bf16[2,64,672]{2,1,0:T(8,128)(2,1)S(1)} %get-tuple-element.121), channel_id=1, source_target_pairs={{0,6},{2,0},{4,2},{6,4},{1,7},{3,1},{5,3},{7,5},{8,14},{10,8},{12,... | collective-permute-start | bytes 516104 | tf_op jit(solution)/shard_map/ppermute | solution.py:34
  209.9 21.7 %collective-permute-start.36 = (bf16[2,64,672]{2,1,0:T(8,128)(2,1)S(1)}, bf16[2,64,672]{2,1,0:T(8,128)(2,1)S(1)}, u32[]{:S(2)}, u32[]{:S(2)}) collective-permute-start(bf16[2,64,672]{2,1,0:T(8,128)(2,1)S(1)} %get-tuple-element.120), channel_id=1, source_target_pairs={{0,4},{2,6},{4,0},{6,2},{1,5},{3,7},{5,1},{7,3},{8,12},{10,14},{12... | collective-permute-start | bytes 516104 | tf_op jit(solution)/shard_map/ppermute | solution.py:34
  210.0 21.6 %collective-permute-start.37 = (bf16[2,64,672]{2,1,0:T(8,128)(2,1)S(1)}, bf16[2,64,672]{2,1,0:T(8,128)(2,1)S(1)}, u32[]{:S(2)}, u32[]{:S(2)}) collective-permute-start(bf16[2,64,672]{2,1,0:T(8,128)(2,1)S(1)} %get-tuple-element.119), channel_id=1, source_target_pairs={{0,2},{2,4},{4,6},{6,0},{1,3},{3,5},{5,7},{7,1},{8,10},{10,12},{12... | collective-permute-start | bytes 516104 | tf_op jit(solution)/shard_map/ppermute | solution.py:34
  (17 other events, 86.0 us)

commit v8 on v5

--- a/solution.py
+++ b/solution.py
@@ -59,11 +59,10 @@
 
 def pack_kernel(g_ref, u_ref, o_ref):
     g, u = g_ref[...], u_ref[...]
-    for j in range(7):
-        lo = 192 * j
-        o_ref[:, 384 * j:384 * j + 384] = jnp.concatenate(
-            [g[:, lo:lo + 128], u[:, lo:lo + 128], g[:, lo + 128:lo + 192], u[:, lo + 128:lo + 192]], axis=1
-        )
+    for j in range(10):
+        o_ref[:, 256 * j:256 * j + 128] = g[:, 128 * j:128 * j + 128]
+        o_ref[:, 256 * j + 128:256 * j + 256] = u[:, 128 * j:128 * j + 128]
+    o_ref[:, 2560:] = jnp.concatenate([g[:, 1280:], u[:, 1280:]], axis=1)
 
 
 def pack(gate, up):
@@ -76,18 +75,6 @@
         cost_estimate=cost(0, 1000),
         name="pack",
     )(gate, up)
-
-
-def ring(value, by, phase):
-    pairs = []
-    for y in range(4):
-        for x in range(4):
-            for z in range(4):
-                for c in range(2):
-                    along_x = (c == 0) == (phase == 0)
-                    yy, xx = (y, (x + by) % 4) if along_x else ((y + by) % 4, x)
-                    pairs.append((((y * 4 + x) * 4 + z) * 2 + c, ((yy * 4 + xx) * 4 + z) * 2 + c))
-    return lax.ppermute(value, ("y", "x", "z", "c"), pairs)
 
 
 def attend_kernel(at_ref, q_ref, kv2_ref, kv1_ref, kv0_ref, qid_ref, kid_ref, o_ref):
@@ -202,163 +189,42 @@
 REL = (0, 3, 1, 2)
 
 
-REL = (0, 3, 1, 2)
-GROUP = 1408
-
-
-def order(pieces, tokens_at, where):
+def gated(pieces, tokens_at, where, w):
     n = len(pieces)
 
     def body(*refs):
-        place, o_ref, n_ref, sems = refs[n:]
-        copies = token_copies(place, refs[:n], tokens_at, n_ref, sems)
-        for copy in copies:
-            copy.start()
-        for copy in copies:
-            copy.wait()
-        c, y, x = place[1], place[2], place[3]
-
-        def put(i, me, value, rows):
-            rel = (i - me + 4) % 4
-            slot = jnp.where(rel == 0, 0, jnp.where(rel == 3, 1, rel + 1))
-            o_ref[rows, pl.ds(pl.multiple_of(GROUP * slot, 128), 1344)] = value
-
-        @pl.loop(0, 8)
-        def _(r):
-            rows = pl.ds(pl.multiple_of(64 * r, 64), 64)
-
-            @pl.when(c == 0)
-            def _():
-                for i in range(4):
-                    put(i, y, n_ref[rows, 1344 * i:1344 * i + 1344], rows)
-
-            @pl.when(c == 1)
-            def _():
-                for i in range(4):
-                    cols = [1344 * k + 336 * i for k in range(4)]
-                    put(i, x, jnp.concatenate([n_ref[rows, lo:lo + 336] for lo in cols], axis=1), rows)
-
-    return pl.pallas_call(
-        body,
-        out_shape=jax.ShapeDtypeStruct((TOK, 4 * GROUP), BF),
-        in_specs=[HB] * n + [SM],
-        out_specs=VM,
-        scratch_shapes=[pltpu.VMEM((TOK, D), BF), pltpu.SemaphoreType.DMA((n,))],
-        compiler_params=params(40),
-        cost_estimate=cost(0, 1000),
-        name="order",
-    )(*pieces, where)
-
-
-def weight_copies(parts, where, arrays, block, w_ref, sems, width=384):
-    c, y, x = where[1], where[2], where[3]
-    first = jnp.where(c == 0, x, y)
-    cols = pl.ds(pl.multiple_of(width * block, 128), width)
-    copies = []
-    for i, (array, lo, slot, rel) in enumerate(parts):
-        row = pl.multiple_of(1344 * slot + 336 * ((first + rel) % 4), 16)
-        copies.append(
-            pltpu.make_async_copy(arrays[array].at[pl.ds(lo, 336), cols], w_ref.at[pl.ds(row, 336)], sems.at[i])
-        )
-    return copies
-
-
-def fetch_block(parts, place, arrays, w_ref, sems, width):
-    j = pl.program_id(0)
-    slot = lax.rem(j, 2)
-
-    @pl.when(j == 0)
-    def _():
-        for copy in weight_copies(parts, place, arrays, 0, w_ref.at[0], sems.at[0], width):
-            copy.start()
-
-    @pl.when(j + 1 < 2688 // width)
-    def _():
-        for copy in weight_copies(parts, place, arrays, j + 1, w_ref.at[1 - slot], sems.at[1 - slot], width):
-            copy.start()
-
-    for copy in weight_copies(parts, place, arrays, j, w_ref.at[slot], sems.at[slot], width):
-        copy.wait()
-    return slot
-
-
-def near(rows, where, blocks):
-    m = len(blocks)
-    parts = [(g, 336 * k, g, REL[k]) for g in range(3) for k in range(4)]
-
-    def body(*refs):
-        place, n_ref, o_ref, w_ref, sems = refs[m:]
-        slot = fetch_block(parts, place, refs[:m], w_ref, sems, 896)
-        acc = jnp.dot(n_ref[:, :1344], w_ref[slot, :1344], preferred_element_type=F32)
-        for g in (1, 2):
-            lhs = n_ref[:, GROUP * g:GROUP * g + 1344]
-            acc += jnp.dot(lhs, w_ref[slot, 1344 * g:1344 * g + 1344], preferred_element_type=F32)
-        o_ref[...] = acc
-
-    return pl.pallas_call(
-        body,
-        out_shape=jax.ShapeDtypeStruct((TOK, 2688), F32),
-        grid=(3,),
-        in_specs=[HB] * m + [SM, pl.BlockSpec((TOK, 3 * GROUP), lambda j: (0, 0))],
-        out_specs=pl.BlockSpec((TOK, 896), lambda j: (0, j)),
-        scratch_shapes=[pltpu.VMEM((2, 3 * 1344, 896), BF), pltpu.SemaphoreType.DMA((2, len(parts)))],
-        compiler_params=params(56),
-        cost_estimate=cost(0, 1000),
-        name="near",
-    )(*blocks, where, rows)
-
-
-def far(rows, where, blocks, sums):
-    m = len(blocks)
-    parts = [(k // 2, 336 * (k % 2), 0, REL[k]) for k in range(4)]
-
-    def body(*refs):
-        place, n_ref, s_ref, o_ref, w_ref, acc_ref, sems = refs[m:]
+        place, w_ref, o_ref, n_ref, sems = refs[n:]
         j = pl.program_id(0)
-        slot = lax.rem(j, 2)
 
         @pl.when(j == 0)
         def _():
-            for copy in weight_copies(parts, place, refs[:m], 0, w_ref.at[0], sems.at[0]):
+            copies = token_copies(place, refs[:n], tokens_at, n_ref, sems)
+            for copy in copies:
                 copy.start()
-
-        @pl.when(j + 1 < 7)
+            for copy in copies:
+                copy.wait()
+
+        @pl.when(j < 10)
         def _():
-            for copy in weight_copies(parts, place, refs[:m], j + 1, w_ref.at[1 - slot], sems.at[1 - slot]):
-                copy.start()
-
-        @pl.when(j < 7)
+            acc = jnp.dot(n_ref[...], w_ref[...], preferred_element_type=F32)
+            o_ref[...] = (gelu(acc[:, :128]) * acc[:, 128:]).T.astype(BF)
+
+        @pl.when(j == 10)
         def _():
-            for copy in weight_copies(parts, place, refs[:m], j, w_ref.at[slot], sems.at[slot]):
-                copy.wait()
-
-        acc = acc_ref[1 - slot]
-        last = acc[:, 256:]
-        g = jnp.concatenate([acc[:, :128], last], axis=1)
-        u = jnp.concatenate([acc[:, 128:256], pltpu.roll(last, 64, 1)], axis=1)
-        o_ref[...] = (gelu(g) * u).T[:192].astype(BF)
-        acc_ref[slot] = s_ref[...] + jnp.dot(n_ref[:, :1344], w_ref[slot], preferred_element_type=F32)
+            acc = jnp.dot(n_ref[...], w_ref[:, :128], preferred_element_type=F32)
+            o_ref[...] = (gelu(acc) * pltpu.roll(acc, 64, 1)).T.astype(BF)
 
     return pl.pallas_call(
         body,
         out_shape=jax.ShapeDtypeStruct((1344, TOK), BF),
-        grid=(8,),
-        in_specs=[HB] * m
-        + [
-            SM,
-            pl.BlockSpec((TOK, GROUP), lambda j: (0, 3)),
-            pl.BlockSpec((TOK, 384), lambda j: (0, jnp.minimum(j, 6))),
-        ],
-        out_specs=pl.BlockSpec((192, TOK), lambda j: (jnp.maximum(j - 1, 0), 0)),
-        scratch_shapes=[
-            pltpu.VMEM((2, 1344, 384), BF),
-            pltpu.VMEM((2, TOK, 384), F32),
-            pltpu.SemaphoreType.DMA((2, len(parts))),
-        ],
+        grid=(11,),
+        in_specs=[HB] * n + [SM, pl.BlockSpec((D, 256), lambda j: (0, j))],
+        out_specs=pl.BlockSpec((128, TOK), lambda j: (j, 0)),
+        scratch_shapes=[pltpu.VMEM((TOK, D), BF), pltpu.SemaphoreType.DMA((n,))],
         compiler_params=params(56),
-        cost_estimate=cost(2 * TOK * 1344 * 2688, 2 * 1344 * 2688 + 4 * TOK * 2688),
-        name="far",
-    )(*blocks, where, rows, sums)
+        cost_estimate=cost(2 * TOK * D * 2688, 2 * D * 2688 + 2 * TOK * D),
+        name="gated",
+    )(*pieces, where, w)
 
 
 def turn(value, by):
@@ -383,18 +249,11 @@
     y, x, z, c = (lax.axis_index(a) for a in ("y", "x", "z", "c"))
     where = jnp.stack([z, c, y, x]).astype(jnp.int32)
 
+    w = pack(gate_weight, up_weight)
+    w_all = lax.all_gather(w, ("y", "x"), axis=0, tiled=True)
     kv0 = pair(keys, values)
     kv1 = behind(kv0)
-    gate_weight, kv0 = lax.optimization_barrier((gate_weight, kv0))
-    w = pack(gate_weight, up_weight)
-    p = ring(w, -1, 0)
     kv2 = behind(kv1)
-    kv2, w_late = lax.optimization_barrier((kv2, w))
-    m = ring(w_late, 1, 0)
-    b = ring(p, -1, 0)
-    kv2, residual, post_gain = lax.optimization_barrier((kv2, residual, post_gain))
-    group = jnp.concatenate([w, m, p, b], axis=0)
-    prev, following = ring(group, 1, 1), ring(group, -1, 1)
 
     gains = jnp.stack([post_gain, pre_gain])
     high = gains.astype(BF)
@@ -409,10 +268,10 @@
     kid = lax.dynamic_slice_in_dim(padded, start, 3 * TOK, 0)[None, :]
     qid = lax.dynamic_slice_in_dim(doc_ids, start, TOK, 0)[:, None]
 
+    queries, mine = lax.optimization_barrier((queries, mine))
     mix = attend(where, queries, kv2, kv1, kv0, qid, kid)
     other_weight = shift(out_weight, "c", 1)
     own, other = mix[0].reshape(256, 512), shift(mix[1].reshape(256, 512), "c", 1)
-    other, mine = lax.optimization_barrier((other, mine))
     p0, p1t, p1b, p2t, p2b, p3t, p3b = project(own, other, out_weight, other_weight)
 
     up_t = shift(p2t, "z", 1)
@@ -429,17 +288,10 @@
     places = [(0, None), (3, None), (1, None), (2, 0), (2, 1)]
     pieces += [shift(piece, "c", 1) for piece in pieces]
     tokens_at = [(dz, dc, part) for dc in range(2) for dz, part in places]
-    rows = order(pieces, tokens_at, where)
-
-    prev, following, rows = lax.optimization_barrier((prev, following, rows))
-    last = [ring(prev[:672], 1, 1), ring(following[672:], -1, 1)]
-    new, rows = lax.optimization_barrier((new, rows))
-    sent_back = swap(new, z, c)
-    sums = near(rows, where, [group, prev, following])
-    act = far(rows, where, last, sums)
-    sent_back, act = lax.optimization_barrier((sent_back, act))
-    new_residual = gather(sent_back, z).reshape(TOK, 672)
-    return new_residual, act.T
+    new, pieces = lax.optimization_barrier((new, pieces))
+    new_residual = gather(swap(new, z, c), z).reshape(TOK, 672)
+    new_residual, pieces = lax.optimization_barrier((new_residual, pieces))
+    return new_residual, gated(pieces, tokens_at, where, w_all).T
 
 
 def solution(mesh):

time: 248 us -> 232 us (0.935)
  waiting for transfers between devices: 72.8 us -> 123 us
  starting transfers between devices: 78.9 us -> 47.6 us
  local copies, waits for them, and re-layouts: 27.1 us -> 4.95 us
  Pallas kernels: 54.6 us -> 39.9 us
  between operations: 1.18 us -> 14.6 us
  other arithmetic: 12.6 us -> 1.7 us
    all_gather x0 -> x1, waiting for transfers between devices: none -> 45.8 us  [per_device(): w_all = lax.all_gather(w, ('y', 'x'), axis=0, tiled=True)]
    ppermute x25, waiting for transfers between devices: 36.1 us -> 62.4 us  [shift(): return lax.ppermute(value, axis, [(i, (i + by) % n) for i in range(n)])]
    ppermute x25, starting transfers between devices: 58.7 us -> 40.1 us  [shift(): return lax.ppermute(value, axis, [(i, (i + by) % n) for i in range(n)])]
    pallas_call x3 -> x1, Pallas kernels: 40.3 us -> 24.6 us  [gated(): pl.pallas_call(body, out_shape=jax.ShapeDtypeStruct((1344, TOK), BF), gri...]
    ppermute x7 -> x0, waiting for transfers between devices: 15.1 us -> none  [ring(): return lax.ppermute(value, ('y', 'x', 'z', 'c'), pairs)]
    ppermute x7 -> x0, starting transfers between devices: 12.8 us -> none  [ring(): return lax.ppermute(value, ('y', 'x', 'z', 'c'), pairs)]
    unnamed x53 -> x59, local copies, waits for them, and re-layouts: 14.2 us -> 4.05 us
    slice x2 -> x0, local copies, waits for them, and re-layouts: 8 us -> none  [per_device(): last = [ring(prev[:672], 1, 1), ring(following[672:], -1, 1)]]
  transfers between devices with their start and end apart: 34 -> 28, of which waited for: 12 -> 18; matrix products, arithmetic and copies ran while one was open for 7% -> 2% of each run, Pallas kernels for 22% -> 6%
where the time goes in v8:
time: 232 us
  waiting for transfers between devices  123 us (53%)
  starting transfers between devices  47.6 us (21%)
  Pallas kernels  39.9 us (17%)
  between operations  14.6 us (6%)
  local copies, waits for them, and re-layouts  4.95 us (2%)
    ppermute x25, waiting for transfers between devices, shift(): return lax.ppermute(value, axis, [(i, (i + by) % n) for i in range(n)])  62.4 us
    all_gather x1, waiting for transfers between devices, per_device(): w_all = lax.all_gather(w, ('y', 'x'), axis=0, tiled=True)  45.8 us
    ppermute x25, starting transfers between devices, shift(): return lax.ppermute(value, axis, [(i, (i + by) % n) for i in range(n)])  40.1 us
    pallas_call x1, Pallas kernels, gated(): pl.pallas_call(body, out_shape=jax.ShapeDtypeStruct((1344, TOK), BF), gri...  24.6 us
    ppermute x2, waiting for transfers between devices, behind(): return lax.ppermute(value, ('y', 'x'), [(i, i + 1) for i in range(n - 1)])  14.6 us
    ppermute x2, starting transfers between devices, behind(): return lax.ppermute(value, ('y', 'x'), [(i, i + 1) for i in range(n - 1)])  7.46 us
    pallas_call x1, Pallas kernels, project(): pl.pallas_call(project_kernel, out_shape=[jax.ShapeDtypeStruct((64, D), B...  7.28 us
    pallas_call x1, Pallas kernels, attend(): pl.pallas_call(attend_kernel, out_shape=jax.ShapeDtypeStruct((2, 4, PER,...  5.39 us
  transfers between devices with their start and end apart: 28, of which 18 were waited for; matrix products, arithmetic and copies ran while one was open for 2% of the time, Pallas kernels for 6%

profile of v8, /device:TPU:1, one launch (start us, length us, event | category | flops | bytes accessed | tf_op | source)
XLA Modules:
  0.0 231.6 jit_solution(419238029976624792)
XLA Ops:
  7.2 1.2 copy-done
  8.4 1.2 copy-done.1
  9.6 1.5 pack.1
  11.1 1.5 collective-permute-start.7
  13.6 3.2 %collective-permute-start.4 = (bf16[512,512]{1,0:T(8,128)(2,1)S(1)}, bf16[512,512]{1,0:T(8,128)(2,1)S(1)}, u32[]{:S(2)}, u32[]{:S(2)}) collective-permute-start(bf16[512,512]{1,0:T(8,128)(2,1)S(1)} %pair.1.kv0_ref), channel_id=1, source_target_pairs={{0,8},{8,16},{16,24},{24,32},{32,40},{40,48},{48,56},{56,64},{64,7... | collective-permute-start | bytes 1572872 | tf_op jit(solution)/shard_map/ppermute | solution.py:39
  17.3 4.7 %collective-permute-done = bf16[4,80,672]{2,1,0:T(8,128)(2,1)S(1)} collective-permute-done((bf16[4,80,672]{2,1,0:T(8,128)(2,1)S(1)}, bf16[4,80,672]{2,1,0:T(8,128)(2,1)S(1)}, u32[]{:S(2)}, u32[]{:S(2)}) %collective-permute-start) | collective-permute-done | bytes 430112 | tf_op jit(solution)/shard_map/ppermute | solution.py:34
  22.2 0.5 fusion.1
  22.8 3.9 %collective-permute-start.1 = (bf16[2,80,672]{2,1,0:T(8,128)(2,1)S(1)}, bf16[2,80,672]{2,1,0:T(8,128)(2,1)S(1)}, u32[]{:S(2)}, u32[]{:S(2)}) collective-permute-start(bf16[2,80,672]{2,1,0:T(8,128)(2,1)S(1)} %get-tuple-element.76), channel_id=1, source_target_pairs={{0,6},{2,0},{4,2},{6,4},{1,7},{3,1},{5,3},{7,5},{8,14},{10,8},{12,... | collective-permute-start | bytes 645128 | tf_op jit(solution)/shard_map/ppermute | solution.py:34
  26.8 0.7 collective-permute-start.3
  27.5 1.1 collective-permute-done.4.kv1_ref
  28.6 4.2 %collective-permute-start.5 = (bf16[512,512]{1,0:T(8,128)(2,1)S(1)}, bf16[512,512]{1,0:T(8,128)(2,1)S(1)}, u32[]{:S(2)}, u32[]{:S(2)}) collective-permute-start(bf16[512,512]{1,0:T(8,128)(2,1)S(1)} %collective-permute-done.4.kv1_ref), channel_id=1, source_target_pairs={{0,8},{8,16},{16,24},{24,32},{32,40},{40,48},{48,56},{56,64},{64,7... | collective-permute-start | bytes 1572872 | tf_op jit(solution)/shard_map/ppermute | solution.py:39
  32.8 4.1 %collective-permute-done.1 = bf16[2,80,672]{2,1,0:T(8,128)(2,1)S(1)} collective-permute-done((bf16[2,80,672]{2,1,0:T(8,128)(2,1)S(1)}, bf16[2,80,672]{2,1,0:T(8,128)(2,1)S(1)}, u32[]{:S(2)}, u32[]{:S(2)}) %collective-permute-start.1) | collective-permute-done | bytes 215072 | tf_op jit(solution)/shard_map/ppermute | solution.py:34
  37.0 3.9 %collective-permute-done.3 = bf16[2,80,672]{2,1,0:T(8,128)(2,1)S(1)} collective-permute-done((bf16[2,80,672]{2,1,0:T(8,128)(2,1)S(1)}, bf16[2,80,672]{2,1,0:T(8,128)(2,1)S(1)}, u32[]{:S(2)}, u32[]{:S(2)}) %collective-permute-start.3) | collective-permute-done | bytes 215072 | tf_op jit(solution)/shard_map/ppermute | solution.py:34
  41.1 13.4 %collective-permute-done.5.kv2_ref = bf16[512,512]{1,0:T(8,128)(2,1)S(1)} collective-permute-done((bf16[512,512]{1,0:T(8,128)(2,1)S(1)}, bf16[512,512]{1,0:T(8,128)(2,1)S(1)}, u32[]{:S(2)}, u32[]{:S(2)}) %collective-permute-start.5) | collective-permute-done | bytes 524320 | tf_op jit(solution)/shard_map/ppermute | solution.py:39
  54.6 5.4 %attend.1 = bf16[2,4,64,512]{3,2,1,0:T(8,128)(2,1)S(1)} custom-call(s32[4]{0:T(128)S(1)} %pad_add_fusion.at_ref.refs_10_, bf16[512,512]{1,0:T(8,128)(2,1)S(1)} %copy-done.2, bf16[512,512]{1,0:T(8,128)(2,1)S(1)} %collective-permute-done.5.kv2_ref, bf16[512,512]{1,0:T(8,128)(2,1)S(1)} %collective-permute-done.4.kv1_ref, bf16[512,512]{1,0:T(8,128)(2,1)S(1)} %pair.1.kv0_ref, ...), custom_call_target="tpu_custom_call" | custom-call | bytes 1000 | tf_op jit(solution)/shard_map/attend/pallas_call | solution.py:110
  60.0 4.0 %collective-permute-start.6 = (bf16[256,512]{1,0:T(8,128)(2,1)S(1)}, bf16[256,512]{1,0:T(8,128)(2,1)S(1)}, u32[]{:S(2)}, u32[]{:S(2)}) collective-permute-start(bf16[256,512]{1,0:T(8,128)(2,1)S(1)} %bitcast.128), channel_id=1, source_target_pairs={{0,1},{1,0},{2,3},{3,2},{4,5},{5,4},{6,7},{7,6},{8,9},{9,8},{10,11... | collective-permute-start | bytes 786440 | tf_op jit(solution)/shard_map/ppermute | solution.py:34
  64.0 1.2 collective-permute-done.6.s
  65.2 7.3 %project.1 = (bf16[64,5376]{1,0:T(8,128)(2,1)S(1)}, bf16[32,5376]{1,0:T(8,128)(2,1)S(1)}, bf16[32,5376]{1,0:T(8,128)(2,1)S(1)}, bf16[32,5376]{1,0:T(8,128)(2,1)S...) custom-call(bf16[256,512]{1,0:T(8,128)(2,1)S(1)} %bitcast.124, ...), custom_call_target="tpu_custom_call" | custom-call | bytes 1000 | tf_op jit(solution)/shard_map/project/pallas_call | solution.py:134
  72.4 1.8 collective-permute-start.8
  74.3 2.0 collective-permute-start.10
  76.3 1.0 collective-permute-start.11
  77.3 1.4 collective-permute-start.12
  78.7 6.7 %collective-permute-done.8 = bf16[32,5376]{1,0:T(8,128)(2,1)S(1)} collective-permute-done((bf16[32,5376]{1,0:T(8,128)(2,1)S(1)}, bf16[32,5376]{1,0:T(8,128)(2,1)S(1)}, u32[]{:S(2)}, u32[]{:S(2)}) %collective-permute-start.8) | collective-permute-done | bytes 344096 | tf_op jit(solution)/shard_map/ppermute | solution.py:34
  85.7 7.2 %collective-permute-done.12 = bf16[32,5376]{1,0:T(8,128)(2,1)S(1)} collective-permute-done((bf16[32,5376]{1,0:T(8,128)(2,1)S(1)}, bf16[32,5376]{1,0:T(8,128)(2,1)S(1)}, u32[]{:S(2)}, u32[]{:S(2)}) %collective-permute-start.12) | collective-permute-done | bytes 344096 | tf_op jit(solution)/shard_map/ppermute | solution.py:34
  93.0 2.1 collective-permute-start.13
  95.2 5.0 %collective-permute-done.9.at_ref = bf16[32,5376]{1,0:T(8,128)(2,1)S(1)} collective-permute-done((bf16[32,5376]{1,0:T(8,128)(2,1)S(1)}, bf16[32,5376]{1,0:T(8,128)(2,1)S(1)}, u32[]{:S(2)}, u32[]{:S(2)}) %collective-permute-start.9) | collective-permute-done | bytes 344096 | tf_op jit(solution)/shard_map/ppermute | solution.py:34
  100.1 1.1 collective-permute-done.13.bb_ref
  101.3 1.1 norm.1
  102.3 1.0 collective-permute-start.14
  103.3 2.6 %collective-permute-start.15 = (bf16[64,5376]{1,0:T(8,128)(2,1)S(1)}, bf16[64,5376]{1,0:T(8,128)(2,1)S(1)}, u32[]{:S(2)}, u32[]{:S(2)}) collective-permute-start(bf16[64,5376]{1,0:T(8,128)(2,1)S(1)} %get-tuple-element.58.refs_0_), channel_id=1, source_target_pairs={{0,6},{2,0},{4,2},{6,4},{1,7},{3,1},{5,3},{7,5},{8,14},{10,8},{12,... | collective-permute-start | bytes 2064392 | tf_op jit(solution)/shard_map/ppermute | solution.py:34
  105.9 2.5 %collective-permute-start.18 = (bf16[64,5376]{1,0:T(8,128)(2,1)S(1)}, bf16[64,5376]{1,0:T(8,128)(2,1)S(1)}, u32[]{:S(2)}, u32[]{:S(2)}) collective-permute-start(bf16[64,5376]{1,0:T(8,128)(2,1)S(1)} %get-tuple-element.58.refs_0_), channel_id=1, source_target_pairs={{0,1},{1,0},{2,3},{3,2},{4,5},{5,4},{6,7},{7,6},{8,9},{9,8},{10,11... | collective-permute-start | bytes 2064392 | tf_op jit(solution)/shard_map/ppermute | solution.py:34
  108.3 11.1 %collective-permute-done.14.refs_1_ = bf16[64,5376]{1,0:T(8,128)(2,1)S(1)} collective-permute-done((bf16[64,5376]{1,0:T(8,128)(2,1)S(1)}, bf16[64,5376]{1,0:T(8,128)(2,1)S(1)}, u32[]{:S(2)}, u32[]{:S(2)}) %collective-permute-start.14) | collective-permute-done | bytes 688160 | tf_op jit(solution)/shard_map/ppermute | solution.py:34
  119.6 2.8 %collective-permute-start.19 = (bf16[64,5376]{1,0:T(8,128)(2,1)S(1)}, bf16[64,5376]{1,0:T(8,128)(2,1)S(1)}, u32[]{:S(2)}, u32[]{:S(2)}) collective-permute-start(bf16[64,5376]{1,0:T(8,128)(2,1)S(1)} %collective-permute-done.14.refs_1_), channel_id=1, source_target_pairs={{0,1},{1,0},{2,3},{3,2},{4,5},{5,4},{6,7},{7,6},{8,9},{9,8},{10,11... | collective-permute-start | bytes 2064392 | tf_op jit(solution)/shard_map/ppermute | solution.py:34
  122.5 2.9 %collective-permute-start.17 = (bf16[32,5376]{1,0:T(8,128)(2,1)S(1)}, bf16[32,5376]{1,0:T(8,128)(2,1)S(1)}, u32[]{:S(2)}, u32[]{:S(2)}) collective-permute-start(bf16[32,5376]{1,0:T(8,128)(2,1)S(1)} %slice.97), channel_id=1, source_target_pairs={{0,6},{2,0},{4,2},{6,4},{1,7},{3,1},{5,3},{7,5},{8,14},{10,8},{12,... | collective-permute-start | bytes 1032200 | tf_op jit(solution)/shard_map/ppermute | solution.py:34
  125.4 2.3 collective-permute-done.16.refs_3_
  127.7 3.5 %collective-permute-start.21 = (bf16[32,5376]{1,0:T(8,128)(2,1)S(1)}, bf16[32,5376]{1,0:T(8,128)(2,1)S(1)}, u32[]{:S(2)}, u32[]{:S(2)}) collective-permute-start(bf16[32,5376]{1,0:T(8,128)(2,1)S(1)} %collective-permute-done.16.refs_3_), channel_id=1, source_target_pairs={{0,1},{1,0},{2,3},{3,2},{4,5},{5,4},{6,7},{7,6},{8,9},{9,8},{10,11... | collective-permute-start | bytes 1032200 | tf_op jit(solution)/shard_map/ppermute | solution.py:34
  131.3 1.2 collective-permute-done.17.refs_4_
  132.5 1.3 collective-permute-start.22
  133.8 1.2 collective-permute-done.22.refs_9_
  135.1 0.5 collective-permute-start.23
  135.5 1.3 collective-permute-done.23
  137.5 3.5 %collective-permute-start.24 = (bf16[2,64,672]{2,1,0:T(8,128)(2,1)S(1)}, bf16[2,64,672]{2,1,0:T(8,128)(2,1)S(1)}, u32[]{:S(2)}, u32[]{:S(2)}) collective-permute-start(bf16[2,64,672]{2,1,0:T(8,128)(2,1)S(1)} %get-tuple-element.80), channel_id=1, source_target_pairs={{0,6},{2,0},{4,2},{6,4},{1,7},{3,1},{5,3},{7,5},{8,14},{10,8},{12,... | collective-permute-start | bytes 516104 | tf_op jit(solution)/shard_map/ppermute | solution.py:34
  141.0 0.7 collective-permute-start.26
  141.6 7.3 %collective-permute-done.24 = bf16[2,64,672]{2,1,0:T(8,128)(2,1)S(1)} collective-permute-done((bf16[2,64,672]{2,1,0:T(8,128)(2,1)S(1)}, bf16[2,64,672]{2,1,0:T(8,128)(2,1)S(1)}, u32[]{:S(2)}, u32[]{:S(2)}) %collective-permute-start.24) | collective-permute-done | bytes 172064 | tf_op jit(solution)/shard_map/ppermute | solution.py:34
  149.0 4.0 %collective-permute-done.26 = bf16[2,64,672]{2,1,0:T(8,128)(2,1)S(1)} collective-permute-done((bf16[2,64,672]{2,1,0:T(8,128)(2,1)S(1)}, bf16[2,64,672]{2,1,0:T(8,128)(2,1)S(1)}, u32[]{:S(2)}, u32[]{:S(2)}) %collective-permute-start.26) | collective-permute-done | bytes 172064 | tf_op jit(solution)/shard_map/ppermute | solution.py:34
  153.2 1.1 copy.34
  154.3 45.8 %all-gather.2.cloned.1.call-done.refs_11_ = bf16[5376,2688]{1,0:T(8,128)(2,1)} async-done(((bf16[336,2688]{1,0:T(8,128)(2,1)}), bf16[5376,2688]{1,0:T(8,128)(2,1)}) %all-gather.2.cloned.1.call-update) | async-done | bytes 28901392 | tf_op jit(solution)/shard_map/all_gather | solution.py:253
  200.1 24.6 %gated.1 = bf16[1344,512]{1,0:T(8,128)(2,1)} custom-call(bf16[64,5376]{1,0:T(8,128)(2,1)} %copy-done.6, bf16[64,5376]{1,0:T(8,128)(2,1)} %copy-done.8, bf16[64,5376]{1,0:T(8,128)(2,1)} %copy-done.9, bf16[32,5376]{1,0:T(8,128)(2,1)} %copy-done.16, bf16[32,5376]{1,0:T(8,128)(2,1)} %copy-done.17, bf16[64,5376]{1,0:T(8,128)(2,1)} %copy-done.13, ...), custom_call_target="tpu_custom_call" | custom-call | flops 14797504512 | bytes 34406400 | tf_op jit(solution)/shard_map/gated/pallas_call | solution.py:217
  (105 shorter events, 3.4 us)
Async XLA Ops:
  7.2 192.9 %all-gather.2.cloned.1.call-start = ((), (), s32[]{:S(2)}) async-start(), calls=%async_computation | async-start | bytes 30707712 | tf_op jit(solution)/shard_map/all_gather | solution.py:253
  9.6 3.0 %copy-start.11 = (f32[672]{0:T(1024)S(1)}, f32[672]{0:T(1024)}, u32[]{:S(2)}) copy-start(f32[672]{0:T(1024)} %param.17) | copy-start | bytes 8068
  9.6 3.0 %copy-start.12 = (f32[672]{0:T(1024)S(1)}, f32[672]{0:T(1024)}, u32[]{:S(2)}) copy-start(f32[672]{0:T(1024)} %param.16) | copy-start | bytes 8068
  9.6 3.0 %copy-start.7 = (bf16[512,672]{0,1:T(8,128)(2,1)S(1)}, bf16[512,672]{0,1:T(8,128)(2,1)}, u32[]{:S(2)}) copy-start(bf16[512,672]{0,1:T(8,128)(2,1)} %param.15) | copy-start | bytes 2064388
  11.1 2.4 %copy-start.3 = (bf16[512,256]{1,0:T(8,128)(2,1)S(1)}, bf16[512,256]{1,0:T(8,128)(2,1)}, u32[]{:S(2)}) copy-start(bf16[512,256]{1,0:T(8,128)(2,1)} %k_ref.1) | copy-start | bytes 786436
  11.1 2.4 %copy-start.4 = (bf16[512,256]{1,0:T(8,128)(2,1)S(1)}, bf16[512,256]{1,0:T(8,128)(2,1)}, u32[]{:S(2)}) copy-start(bf16[512,256]{1,0:T(8,128)(2,1)} %v_ref.1) | copy-start | bytes 786436
  11.1 54.0 %collective-permute-start.7 = (bf16[512,5376]{1,0:T(8,128)(2,1)}, bf16[512,5376]{1,0:T(8,128)(2,1)}, u32[]{:S(2)}, u32[]{:S(2)}) collective-permute-start(bf16[512,5376]{1,0:T(8,128)(2,1)} %w_ref.1), channel_id=1, source_target_pairs={{0,1},{1,0},{2,3},{3,2},{4,5},{5,4},{6,7},{7,6},{8,9},{9,8},{10,11... | collective-permute-start | bytes 16515080 | tf_op jit(solution)/shard_map/ppermute | solution.py:34
  12.7 4.2 %copy-start.10 = (s32[8192]{0:T(1024)S(1)}, s32[8192]{0:T(1024)}, u32[]{:S(2)}) copy-start(s32[8192]{0:T(1024)} %param.13) | copy-start | bytes 98308
  13.4 8.6 %collective-permute-start = (bf16[4,80,672]{2,1,0:T(8,128)(2,1)S(1)}, bf16[4,80,672]{2,1,0:T(8,128)(2,1)S(1)}, u32[]{:S(2)}, u32[]{:S(2)}) collective-permute-start(bf16[4,80,672]{2,1,0:T(8,128)(2,1)S(1)} %fusion.6), channel_id=1, source_target_pairs={{0,1},{1,0},{2,3},{3,2},{4,5},{5,4},{6,7},{7,6},{8,9},{9,8},{10,11... | collective-permute-start | bytes 1290248 | tf_op jit(solution)/shard_map/ppermute | solution.py:34
  13.6 15.0 %collective-permute-start.4 = (bf16[512,512]{1,0:T(8,128)(2,1)S(1)}, bf16[512,512]{1,0:T(8,128)(2,1)S(1)}, u32[]{:S(2)}, u32[]{:S(2)}) collective-permute-start(bf16[512,512]{1,0:T(8,128)(2,1)S(1)} %pair.1.kv0_ref), channel_id=1, source_target_pairs={{0,8},{8,16},{16,24},{24,32},{32,40},{40,48},{48,56},{56,64},{64,7... | collective-permute-start | bytes 1572872 | tf_op jit(solution)/shard_map/ppermute | solution.py:39
  17.3 37.3 %copy-start.5 = (s32[4]{0:T(128)}, s32[4]{0:T(128)S(1)}, u32[]{:S(2)}) copy-start(s32[4]{0:T(128)S(1)} %pad_add_fusion.at_ref.refs_10_) | copy-start | bytes 52
  22.0 43.2 %slice-start = ((s8[5505024]{0:T(1024)(128)(4,1)}), s8[4194304]{0:T(1024)(128)(4,1)S(1)}, s32[]{:S(2)}) async-start(s8[5505024]{0:T(1024)(128)(4,1)} %bitcast.119), calls=%async_computation.1 | async-start | bytes 8388608
  22.8 14.1 %collective-permute-start.1 = (bf16[2,80,672]{2,1,0:T(8,128)(2,1)S(1)}, bf16[2,80,672]{2,1,0:T(8,128)(2,1)S(1)}, u32[]{:S(2)}, u32[]{:S(2)}) collective-permute-start(bf16[2,80,672]{2,1,0:T(8,128)(2,1)S(1)} %get-tuple-element.76), channel_id=1, source_target_pairs={{0,6},{2,0},{4,2},{6,4},{1,7},{3,1},{5,3},{7,5},{8,14},{10,8},{12,... | collective-permute-start | bytes 645128 | tf_op jit(solution)/shard_map/ppermute | solution.py:34
  26.8 10.3 %collective-permute-start.2 = (bf16[2,80,672]{2,1,0:T(8,128)(2,1)S(1)}, bf16[2,80,672]{2,1,0:T(8,128)(2,1)S(1)}, u32[]{:S(2)}, u32[]{:S(2)}) collective-permute-start(bf16[2,80,672]{2,1,0:T(8,128)(2,1)S(1)} %get-tuple-element.75), channel_id=1, source_target_pairs={{0,4},{2,6},{4,0},{6,2},{1,5},{3,7},{5,1},{7,3},{8,12},{10,14},{12... | collective-permute-start | bytes 645128 | tf_op jit(solution)/shard_map/ppermute | solution.py:34
  26.8 14.2 %collective-permute-start.3 = (bf16[2,80,672]{2,1,0:T(8,128)(2,1)S(1)}, bf16[2,80,672]{2,1,0:T(8,128)(2,1)S(1)}, u32[]{:S(2)}, u32[]{:S(2)}) collective-permute-start(bf16[2,80,672]{2,1,0:T(8,128)(2,1)S(1)} %get-tuple-element.74), channel_id=1, source_target_pairs={{0,2},{2,4},{4,6},{6,0},{1,3},{3,5},{5,7},{7,1},{8,10},{10,12},{12... | collective-permute-start | bytes 645128 | tf_op jit(solution)/shard_map/ppermute | solution.py:34
  28.6 26.0 %collective-permute-start.5 = (bf16[512,512]{1,0:T(8,128)(2,1)S(1)}, bf16[512,512]{1,0:T(8,128)(2,1)S(1)}, u32[]{:S(2)}, u32[]{:S(2)}) collective-permute-start(bf16[512,512]{1,0:T(8,128)(2,1)S(1)} %collective-permute-done.4.kv1_ref), channel_id=1, source_target_pairs={{0,8},{8,16},{16,24},{24,32},{32,40},{40,48},{48,56},{56,64},{64,7... | collective-permute-start | bytes 1572872 | tf_op jit(solution)/shard_map/ppermute | solution.py:39
  40.9 13.6 %copy-start.2 = (bf16[512,512]{1,0:T(8,128)(2,1)S(1)}, bf16[512,512]{1,0:T(8,128)(2,1)}, u32[]{:S(2)}) copy-start(bf16[512,512]{1,0:T(8,128)(2,1)} %q_ref) | copy-start | bytes 1572868
  40.9 24.2 %slice-start.1 = ((s8[5505024]{0:T(1024)(128)(4,1)}), s8[1310720]{0:T(1024)(128)(4,1)S(1)}, s32[]{:S(2)}) async-start(s8[5505024]{0:T(1024)(128)(4,1)} %bitcast.119), calls=%async_computation.2 | async-start | bytes 2621440
  60.0 5.1 %collective-permute-start.6 = (bf16[256,512]{1,0:T(8,128)(2,1)S(1)}, bf16[256,512]{1,0:T(8,128)(2,1)S(1)}, u32[]{:S(2)}, u32[]{:S(2)}) collective-permute-start(bf16[256,512]{1,0:T(8,128)(2,1)S(1)} %bitcast.128), channel_id=1, source_target_pairs={{0,1},{1,0},{2,3},{3,2},{4,5},{5,4},{6,7},{7,6},{8,9},{9,8},{10,11... | collective-permute-start | bytes 786440 | tf_op jit(solution)/shard_map/ppermute | solution.py:34
  72.4 12.9 %collective-permute-start.8 = (bf16[32,5376]{1,0:T(8,128)(2,1)S(1)}, bf16[32,5376]{1,0:T(8,128)(2,1)S(1)}, u32[]{:S(2)}, u32[]{:S(2)}) collective-permute-start(bf16[32,5376]{1,0:T(8,128)(2,1)S(1)} %get-tuple-element.38), channel_id=1, source_target_pairs={{0,2},{2,4},{4,6},{6,0},{1,3},{3,5},{5,7},{7,1},{8,10},{10,12},{12... | collective-permute-start | bytes 1032200 | tf_op jit(solution)/shard_map/ppermute | solution.py:34
  74.3 20.9 %collective-permute-start.10 = (bf16[32,5376]{1,0:T(8,128)(2,1)S(1)}, bf16[32,5376]{1,0:T(8,128)(2,1)S(1)}, u32[]{:S(2)}, u32[]{:S(2)}) collective-permute-start(bf16[32,5376]{1,0:T(8,128)(2,1)S(1)} %get-tuple-element.39), channel_id=1, source_target_pairs={{0,2},{2,4},{4,6},{6,0},{1,3},{3,5},{5,7},{7,1},{8,10},{10,12},{12... | collective-permute-start | bytes 1032200 | tf_op jit(solution)/shard_map/ppermute | solution.py:34
  76.3 18.9 %collective-permute-start.11 = (bf16[32,5376]{1,0:T(8,128)(2,1)S(1)}, bf16[32,5376]{1,0:T(8,128)(2,1)S(1)}, u32[]{:S(2)}, u32[]{:S(2)}) collective-permute-start(bf16[32,5376]{1,0:T(8,128)(2,1)S(1)} %get-tuple-element.40), channel_id=1, source_target_pairs={{0,6},{2,0},{4,2},{6,4},{1,7},{3,1},{5,3},{7,5},{8,14},{10,8},{12,... | collective-permute-start | bytes 1032200 | tf_op jit(solution)/shard_map/ppermute | solution.py:34
  77.3 15.6 %collective-permute-start.12 = (bf16[32,5376]{1,0:T(8,128)(2,1)S(1)}, bf16[32,5376]{1,0:T(8,128)(2,1)S(1)}, u32[]{:S(2)}, u32[]{:S(2)}) collective-permute-start(bf16[32,5376]{1,0:T(8,128)(2,1)S(1)} %get-tuple-element.42), channel_id=1, source_target_pairs={{0,6},{2,0},{4,2},{6,4},{1,7},{3,1},{5,3},{7,5},{8,14},{10,8},{12,... | collective-permute-start | bytes 1032200 | tf_op jit(solution)/shard_map/ppermute | solution.py:34
  85.4 14.7 %collective-permute-start.9 = (bf16[32,5376]{1,0:T(8,128)(2,1)S(1)}, bf16[32,5376]{1,0:T(8,128)(2,1)S(1)}, u32[]{:S(2)}, u32[]{:S(2)}) collective-permute-start(bf16[32,5376]{1,0:T(8,128)(2,1)S(1)} %add_convert_fusion.1), channel_id=1, source_target_pairs={{0,2},{2,4},{4,6},{6,0},{1,3},{3,5},{5,7},{7,1},{8,10},{10,12},{12... | collective-permute-start | bytes 1032200 | tf_op jit(solution)/shard_map/ppermute | solution.py:34
  93.0 8.3 %collective-permute-start.13 = (bf16[32,5376]{1,0:T(8,128)(2,1)S(1)}, bf16[32,5376]{1,0:T(8,128)(2,1)S(1)}, u32[]{:S(2)}, u32[]{:S(2)}) collective-permute-start(bf16[32,5376]{1,0:T(8,128)(2,1)S(1)} %add_convert_fusion), channel_id=1, source_target_pairs={{0,6},{2,0},{4,2},{6,4},{1,7},{3,1},{5,3},{7,5},{8,14},{10,8},{12,... | collective-permute-start | bytes 1032200 | tf_op jit(solution)/shard_map/ppermute | solution.py:34
  102.3 34.6 %copy-start.6 = (bf16[64,5376]{1,0:T(8,128)(2,1)}, bf16[64,5376]{1,0:T(8,128)(2,1)S(1)}, u32[]{:S(2)}) copy-start(bf16[64,5376]{1,0:T(8,128)(2,1)S(1)} %get-tuple-element.58.refs_0_) | copy-start | bytes 2064388
  102.3 17.1 %collective-permute-start.14 = (bf16[64,5376]{1,0:T(8,128)(2,1)S(1)}, bf16[64,5376]{1,0:T(8,128)(2,1)S(1)}, u32[]{:S(2)}, u32[]{:S(2)}) collective-permute-start(bf16[64,5376]{1,0:T(8,128)(2,1)S(1)} %get-tuple-element.58.refs_0_), channel_id=1, source_target_pairs={{0,2},{2,4},{4,6},{6,0},{1,3},{3,5},{5,7},{7,1},{8,10},{10,12},{12... | collective-permute-start | bytes 2064392 | tf_op jit(solution)/shard_map/ppermute | solution.py:34
  103.3 19.1 %collective-permute-start.15 = (bf16[64,5376]{1,0:T(8,128)(2,1)S(1)}, bf16[64,5376]{1,0:T(8,128)(2,1)S(1)}, u32[]{:S(2)}, u32[]{:S(2)}) collective-permute-start(bf16[64,5376]{1,0:T(8,128)(2,1)S(1)} %get-tuple-element.58.refs_0_), channel_id=1, source_target_pairs={{0,6},{2,0},{4,2},{6,4},{1,7},{3,1},{5,3},{7,5},{8,14},{10,8},{12,... | collective-permute-start | bytes 2064392 | tf_op jit(solution)/shard_map/ppermute | solution.py:34
  105.9 27.8 %collective-permute-start.18 = (bf16[64,5376]{1,0:T(8,128)(2,1)S(1)}, bf16[64,5376]{1,0:T(8,128)(2,1)S(1)}, u32[]{:S(2)}, u32[]{:S(2)}) collective-permute-start(bf16[64,5376]{1,0:T(8,128)(2,1)S(1)} %get-tuple-element.58.refs_0_), channel_id=1, source_target_pairs={{0,1},{1,0},{2,3},{3,2},{4,5},{5,4},{6,7},{7,6},{8,9},{9,8},{10,11... | collective-permute-start | bytes 2064392 | tf_op jit(solution)/shard_map/ppermute | solution.py:34
  119.5 17.5 %copy-start.8 = (bf16[64,5376]{1,0:T(8,128)(2,1)}, bf16[64,5376]{1,0:T(8,128)(2,1)S(1)}, u32[]{:S(2)}) copy-start(bf16[64,5376]{1,0:T(8,128)(2,1)S(1)} %collective-permute-done.14.refs_1_) | copy-start | bytes 2064388
  119.5 8.2 %collective-permute-start.16 = (bf16[32,5376]{1,0:T(8,128)(2,1)S(1)}, bf16[32,5376]{1,0:T(8,128)(2,1)S(1)}, u32[]{:S(2)}, u32[]{:S(2)}) collective-permute-start(bf16[32,5376]{1,0:T(8,128)(2,1)S(1)} %slice.96), channel_id=1, source_target_pairs={{0,2},{2,4},{4,6},{6,0},{1,3},{3,5},{5,7},{7,1},{8,10},{10,12},{12... | collective-permute-start | bytes 1032200 | tf_op jit(solution)/shard_map/ppermute | solution.py:34
  119.6 14.1 %collective-permute-start.19 = (bf16[64,5376]{1,0:T(8,128)(2,1)S(1)}, bf16[64,5376]{1,0:T(8,128)(2,1)S(1)}, u32[]{:S(2)}, u32[]{:S(2)}) collective-permute-start(bf16[64,5376]{1,0:T(8,128)(2,1)S(1)} %collective-permute-done.14.refs_1_), channel_id=1, source_target_pairs={{0,1},{1,0},{2,3},{3,2},{4,5},{5,4},{6,7},{7,6},{8,9},{9,8},{10,11... | collective-permute-start | bytes 2064392 | tf_op jit(solution)/shard_map/ppermute | solution.py:34
  122.4 15.0 %copy-start.9 = (bf16[64,5376]{1,0:T(8,128)(2,1)}, bf16[64,5376]{1,0:T(8,128)(2,1)S(1)}, u32[]{:S(2)}) copy-start(bf16[64,5376]{1,0:T(8,128)(2,1)S(1)} %collective-permute-done.15.refs_2_) | copy-start | bytes 2064388
  122.4 11.3 %collective-permute-start.20 = (bf16[64,5376]{1,0:T(8,128)(2,1)S(1)}, bf16[64,5376]{1,0:T(8,128)(2,1)S(1)}, u32[]{:S(2)}, u32[]{:S(2)}) collective-permute-start(bf16[64,5376]{1,0:T(8,128)(2,1)S(1)} %collective-permute-done.15.refs_2_), channel_id=1, source_target_pairs={{0,1},{1,0},{2,3},{3,2},{4,5},{5,4},{6,7},{7,6},{8,9},{9,8},{10,11... | collective-permute-start | bytes 2064392 | tf_op jit(solution)/shard_map/ppermute | solution.py:34
  122.5 9.9 %collective-permute-start.17 = (bf16[32,5376]{1,0:T(8,128)(2,1)S(1)}, bf16[32,5376]{1,0:T(8,128)(2,1)S(1)}, u32[]{:S(2)}, u32[]{:S(2)}) collective-permute-start(bf16[32,5376]{1,0:T(8,128)(2,1)S(1)} %slice.97), channel_id=1, source_target_pairs={{0,6},{2,0},{4,2},{6,4},{1,7},{3,1},{5,3},{7,5},{8,14},{10,8},{12,... | collective-permute-start | bytes 1032200 | tf_op jit(solution)/shard_map/ppermute | solution.py:34
  127.7 7.3 %copy-start.16 = (bf16[32,5376]{1,0:T(8,128)(2,1)}, bf16[32,5376]{1,0:T(8,128)(2,1)S(1)}, u32[]{:S(2)}) copy-start(bf16[32,5376]{1,0:T(8,128)(2,1)S(1)} %collective-permute-done.16.refs_3_) | copy-start | bytes 1032196
  127.7 6.0 %collective-permute-start.21 = (bf16[32,5376]{1,0:T(8,128)(2,1)S(1)}, bf16[32,5376]{1,0:T(8,128)(2,1)S(1)}, u32[]{:S(2)}, u32[]{:S(2)}) collective-permute-start(bf16[32,5376]{1,0:T(8,128)(2,1)S(1)} %collective-permute-done.16.refs_3_), channel_id=1, source_target_pairs={{0,1},{1,0},{2,3},{3,2},{4,5},{5,4},{6,7},{7,6},{8,9},{9,8},{10,11... | collective-permute-start | bytes 1032200 | tf_op jit(solution)/shard_map/ppermute | solution.py:34
  132.5 2.6 %copy-start.17 = (bf16[32,5376]{1,0:T(8,128)(2,1)}, bf16[32,5376]{1,0:T(8,128)(2,1)S(1)}, u32[]{:S(2)}) copy-start(bf16[32,5376]{1,0:T(8,128)(2,1)S(1)} %collective-permute-done.17.refs_4_) | copy-start | bytes 1032196
  132.5 2.5 %collective-permute-start.22 = (bf16[32,5376]{1,0:T(8,128)(2,1)S(1)}, bf16[32,5376]{1,0:T(8,128)(2,1)S(1)}, u32[]{:S(2)}, u32[]{:S(2)}) collective-permute-start(bf16[32,5376]{1,0:T(8,128)(2,1)S(1)} %collective-permute-done.17.refs_4_), channel_id=1, source_target_pairs={{0,1},{1,0},{2,3},{3,2},{4,5},{5,4},{6,7},{7,6},{8,9},{9,8},{10,11... | collective-permute-start | bytes 1032200 | tf_op jit(solution)/shard_map/ppermute | solution.py:34
  133.7 3.7 %copy-start.13 = (bf16[64,5376]{1,0:T(8,128)(2,1)}, bf16[64,5376]{1,0:T(8,128)(2,1)S(1)}, u32[]{:S(2)}) copy-start(bf16[64,5376]{1,0:T(8,128)(2,1)S(1)} %collective-permute-done.18.refs_5_) | copy-start | bytes 2064388
  133.7 3.7 %copy-start.14 = (bf16[64,5376]{1,0:T(8,128)(2,1)}, bf16[64,5376]{1,0:T(8,128)(2,1)S(1)}, u32[]{:S(2)}) copy-start(bf16[64,5376]{1,0:T(8,128)(2,1)S(1)} %collective-permute-done.19.refs_6_) | copy-start | bytes 2064388
  133.8 1.8 copy-start.15
  133.8 3.2 %copy-start.18 = (bf16[32,5376]{1,0:T(8,128)(2,1)}, bf16[32,5376]{1,0:T(8,128)(2,1)S(1)}, u32[]{:S(2)}) copy-start(bf16[32,5376]{1,0:T(8,128)(2,1)S(1)} %collective-permute-done.21.refs_8_) | copy-start | bytes 1032196
  135.0 2.0 copy-start.19
  135.1 1.8 collective-permute-start.23
  137.5 11.5 %collective-permute-start.24 = (bf16[2,64,672]{2,1,0:T(8,128)(2,1)S(1)}, bf16[2,64,672]{2,1,0:T(8,128)(2,1)S(1)}, u32[]{:S(2)}, u32[]{:S(2)}) collective-permute-start(bf16[2,64,672]{2,1,0:T(8,128)(2,1)S(1)} %get-tuple-element.80), channel_id=1, source_target_pairs={{0,6},{2,0},{4,2},{6,4},{1,7},{3,1},{5,3},{7,5},{8,14},{10,8},{12,... | collective-permute-start | bytes 516104 | tf_op jit(solution)/shard_map/ppermute | solution.py:34
  140.9 8.0 %collective-permute-start.25 = (bf16[2,64,672]{2,1,0:T(8,128)(2,1)S(1)}, bf16[2,64,672]{2,1,0:T(8,128)(2,1)S(1)}, u32[]{:S(2)}, u32[]{:S(2)}) collective-permute-start(bf16[2,64,672]{2,1,0:T(8,128)(2,1)S(1)} %get-tuple-element.79), channel_id=1, source_target_pairs={{0,4},{2,6},{4,0},{6,2},{1,5},{3,7},{5,1},{7,3},{8,12},{10,14},{12... | collective-permute-start | bytes 516104 | tf_op jit(solution)/shard_map/ppermute | solution.py:34
  141.0 12.1 %collective-permute-start.26 = (bf16[2,64,672]{2,1,0:T(8,128)(2,1)S(1)}, bf16[2,64,672]{2,1,0:T(8,128)(2,1)S(1)}, u32[]{:S(2)}, u32[]{:S(2)}) collective-permute-start(bf16[2,64,672]{2,1,0:T(8,128)(2,1)S(1)} %get-tuple-element.77), channel_id=1, source_target_pairs={{0,2},{2,4},{4,6},{6,0},{1,3},{3,5},{5,7},{7,1},{8,10},{10,12},{12... | collective-permute-start | bytes 516104 | tf_op jit(solution)/shard_map/ppermute | solution.py:34
  (2 other events, 2.4 us)
Sparse Core Ops, SparseCore 0:
  11.2 188.8 all-gather.1

commit v9 on v7

--- a/solution.py
+++ b/solution.py
@@ -412,7 +412,6 @@
     mix = attend(where, queries, kv2, kv1, kv0, qid, kid)
     other_weight = shift(out_weight, "c", 1)
     own, other = mix[0].reshape(256, 512), shift(mix[1].reshape(256, 512), "c", 1)
-    other, m = lax.optimization_barrier((other, m))
     p0, p1t, p1b, p2t, p2b, p3t, p3b = project(own, other, out_weight, other_weight)
 
     up_t = shift(p2t, "z", 1)
@@ -434,10 +433,11 @@
     places = [(0, None), (3, None), (1, None), (2, 0), (2, 1)]
     pieces += [shift(piece, "c", 1) for piece in pieces]
     tokens_at = [(dz, dc, part) for dc in range(2) for dz, part in places]
-    pieces, prev[3], following[3] = lax.optimization_barrier((pieces, prev[3], following[3]))
+    early = [ring(prev[0], 1, 1), ring(following[2], -1, 1)]
     rows = order(pieces, tokens_at, where)
-
-    last = [ring(prev[0], 1, 1), ring(prev[1], 1, 1), ring(following[2], -1, 1), ring(following[3], -1, 1)]
+    rows, prev[3], following[3], early = lax.optimization_barrier((rows, prev[3], following[3], early))
+
+    last = [early[0], ring(prev[1], 1, 1), early[1], ring(following[3], -1, 1)]
     new, rows = lax.optimization_barrier((new, rows))
     sent_back = swap(new, z, c)
     sums = near(rows, where, [w, m, p, b, *prev, *following])

time: 235 us -> 245 us (1.043)
  waiting for transfers between devices: 81.1 us -> 88.2 us
    ppermute x15, waiting for transfers between devices: 40.8 us -> 54.4 us  [ring(): return lax.ppermute(value, ('y', 'x', 'z', 'c'), pairs)]
    ppermute x2, waiting for transfers between devices: 3.99 us -> 0.01 us  [behind(): return lax.ppermute(value, ('y', 'x'), [(i, i + 1) for i in range(n - 1)])]
    ppermute x15, starting transfers between devices: 18.4 us -> 21.3 us  [ring(): return lax.ppermute(value, ('y', 'x', 'z', 'c'), pairs)]
    unnamed x62 -> x64, local copies, waits for them, and re-layouts: 11.9 us -> 11.5 us
  transfers between devices with their start and end apart: 42 -> 42, of which waited for: 14 -> 18; matrix products, arithmetic and copies ran while one was open for 3% -> 4% of each run, Pallas kernels for 24% -> 23%
where the time goes in v9:
time: 245 us; the launch traced here: 244 us
  waiting for transfers between devices  88.2 us (36%)
  starting transfers between devices  80 us (33%)
  Pallas kernels  55.2 us (23%)
  local copies, waits for them, and re-layouts  13.7 us (6%)
  other arithmetic  5.8 us (2%)
    ppermute x15, waiting for transfers between devices, ring(): return lax.ppermute(value, ('y', 'x', 'z', 'c'), pairs)  54.4 us
    ppermute x25, starting transfers between devices, shift(): return lax.ppermute(value, axis, [(i, (i + by) % n) for i in range(n)])  53 us
    ppermute x25, waiting for transfers between devices, shift(): return lax.ppermute(value, axis, [(i, (i + by) % n) for i in range(n)])  33.8 us
    pallas_call x1, Pallas kernels, near(): pl.pallas_call(body, out_shape=jax.ShapeDtypeStruct((TOK, 2688), F32), gr...  21.8 us
    ppermute x15, starting transfers between devices, ring(): return lax.ppermute(value, ('y', 'x', 'z', 'c'), pairs)  21.3 us
    pallas_call x1, Pallas kernels, far(): pl.pallas_call(body, out_shape=jax.ShapeDtypeStruct((1344, TOK), BF), gri...  13.4 us
    unnamed x64, local copies, waits for them, and re-layouts  11.5 us
    pallas_call x1, Pallas kernels, project(): pl.pallas_call(project_kernel, out_shape=[jax.ShapeDtypeStruct((64, D), B...  7.28 us
  transfers between devices with their start and end apart: 42, of which 18 were waited for; matrix products, arithmetic and copies ran while one was open for 4% of the time, Pallas kernels for 23%

profile of v9, /device:TPU:1, one launch (start us, length us, event | category | flops | bytes accessed | tf_op | source)
XLA Modules:
  0.0 244.1 jit_solution(649582240221985982)
XLA Ops:
  0.7 1.5 collective-permute-start.9
  3.5 1.4 copy.22
  6.3 4.0 %collective-permute-start.4 = (bf16[512,512]{1,0:T(8,128)(2,1)S(1)}, bf16[512,512]{1,0:T(8,128)(2,1)}, u32[]{:S(2)}, u32[]{:S(2)}) collective-permute-start(bf16[512,512]{1,0:T(8,128)(2,1)S(1)} %pair.1.kv0_ref), channel_id=1, source_target_pairs={{0,8},{8,16},{16,24},{24,32},{32,40},{40,48},{48,56},{56,64},{64,7... | collective-permute-start | bytes 1572872 | tf_op jit(solution)/shard_map/ppermute | solution.py:39
  11.9 2.0 collective-permute-start.6
  14.3 1.8 select_bitcast_fusion
  16.8 3.8 %collective-permute-start.1 = (bf16[2,80,672]{2,1,0:T(8,128)(2,1)S(1)}, bf16[2,80,672]{2,1,0:T(8,128)(2,1)S(1)}, u32[]{:S(2)}, u32[]{:S(2)}) collective-permute-start(bf16[2,80,672]{2,1,0:T(8,128)(2,1)S(1)} %get-tuple-element.100), channel_id=1, source_target_pairs={{0,6},{2,0},{4,2},{6,4},{1,7},{3,1},{5,3},{7,5},{8,14},{10,8},{12,... | collective-permute-start | bytes 645128 | tf_op jit(solution)/shard_map/ppermute | solution.py:34
  20.6 3.3 %collective-permute-start.7 = (bf16[336,2688]{1,0:T(8,128)(2,1)S(1)}, bf16[336,2688]{1,0:T(8,128)(2,1)S(1)}, u32[]{:S(2)}, u32[]{:S(2)}) collective-permute-start(bf16[336,2688]{1,0:T(8,128)(2,1)S(1)} %pack.1.refs_0_), channel_id=1, source_target_pairs={{0,96},{1,25},{2,98},{3,27},{4,100},{5,29},{6,102},{7,31},{8,104},... | collective-permute-start | bytes 5419016 | tf_op jit(solution)/shard_map/ppermute | solution.py:90
  23.9 3.7 %collective-permute-start.2 = (bf16[2,80,672]{2,1,0:T(8,128)(2,1)S(1)}, bf16[2,80,672]{2,1,0:T(8,128)(2,1)S(1)}, u32[]{:S(2)}, u32[]{:S(2)}) collective-permute-start(bf16[2,80,672]{2,1,0:T(8,128)(2,1)S(1)} %get-tuple-element.99), channel_id=1, source_target_pairs={{0,4},{2,6},{4,0},{6,2},{1,5},{3,7},{5,1},{7,3},{8,12},{10,14},{12... | collective-permute-start | bytes 645128 | tf_op jit(solution)/shard_map/ppermute | solution.py:34
  27.6 1.7 collective-permute-start.5
  29.3 1.9 collective-permute-done.2
  32.2 5.7 %collective-permute-done.3 = bf16[2,80,672]{2,1,0:T(8,128)(2,1)S(1)} collective-permute-done((bf16[2,80,672]{2,1,0:T(8,128)(2,1)S(1)}, bf16[2,80,672]{2,1,0:T(8,128)(2,1)S(1)}, u32[]{:S(2)}, u32[]{:S(2)}) %collective-permute-start.3) | collective-permute-done | bytes 215072 | tf_op jit(solution)/shard_map/ppermute | solution.py:34
  38.0 2.6 %collective-permute-done.6.refs_2_ = bf16[336,2688]{1,0:T(8,128)(2,1)} collective-permute-done((bf16[336,2688]{1,0:T(8,128)(2,1)S(1)}, bf16[336,2688]{1,0:T(8,128)(2,1)}, u32[]{:S(2)}, u32[]{:S(2)}) %collective-permute-start.6) | collective-permute-done | bytes 1806368 | tf_op jit(solution)/shard_map/ppermute | solution.py:90
  40.6 4.7 %collective-permute-start.14 = (bf16[336,2688]{1,0:T(8,128)(2,1)S(1)}, bf16[336,2688]{1,0:T(8,128)(2,1)S(1)}, u32[]{:S(2)}, u32[]{:S(2)}) collective-permute-start(bf16[336,2688]{1,0:T(8,128)(2,1)S(1)} %pack.1.refs_0_), channel_id=1, source_target_pairs={{0,8},{1,33},{2,10},{3,35},{4,12},{5,37},{6,14},{7,39},{8,16},{9,4... | collective-permute-start | bytes 5419016 | tf_op jit(solution)/shard_map/ppermute | solution.py:90
  47.2 10.3 %collective-permute-done.7.refs_8_ = bf16[336,2688]{1,0:T(8,128)(2,1)S(1)} collective-permute-done((bf16[336,2688]{1,0:T(8,128)(2,1)S(1)}, bf16[336,2688]{1,0:T(8,128)(2,1)S(1)}, u32[]{:S(2)}, u32[]{:S(2)}) %collective-permute-start.7) | collective-permute-done | bytes 1806368 | tf_op jit(solution)/shard_map/ppermute | solution.py:90
  57.5 1.3 copy-done.13
  58.7 6.0 %attend.1 = bf16[2,4,64,512]{3,2,1,0:T(8,128)(2,1)S(1)} custom-call(s32[4]{0:T(128)S(1)} %pad_add_fusion.at_ref.refs_10_.refs_12_.refs_4_, bf16[512,512]{1,0:T(8,128)(2,1)S(1)} %copy-done.4, bf16[512,512]{1,0:T(8,128)(2,1)S(1)} %collective-permute-done.5.kv2_ref, bf16[512,512]{1,0:T(8,128)(2,1)} %collective-permute-done.4.kv1_ref, ...), custom_call_target="tpu_custom_call" | custom-call | bytes 1000 | tf_op jit(solution)/shard_map/attend/pallas_call | solution.py:123
  64.8 1.5 collective-permute-start.8
  67.5 7.3 %project.1 = (bf16[64,5376]{1,0:T(8,128)(2,1)S(1)}, bf16[32,5376]{1,0:T(8,128)(2,1)S(1)}, bf16[32,5376]{1,0:T(8,128)(2,1)S(1)}, bf16[32,5376]{1,0:T(8,128)(2,1)S...) custom-call(bf16[256,512]{1,0:T(8,128)(2,1)S(1)} %bitcast.129, ...), custom_call_target="tpu_custom_call" | custom-call | bytes 1000 | tf_op jit(solution)/shard_map/project/pallas_call | solution.py:147
  74.8 3.2 %collective-permute-start.12 = (bf16[32,5376]{1,0:T(8,128)(2,1)S(1)}, bf16[32,5376]{1,0:T(8,128)(2,1)S(1)}, u32[]{:S(2)}, u32[]{:S(2)}) collective-permute-start(bf16[32,5376]{1,0:T(8,128)(2,1)S(1)} %get-tuple-element.58), channel_id=1, source_target_pairs={{0,2},{2,4},{4,6},{6,0},{1,3},{3,5},{5,7},{7,1},{8,10},{10,12},{12... | collective-permute-start | bytes 1032200 | tf_op jit(solution)/shard_map/ppermute | solution.py:34
  78.0 3.1 %collective-permute-start.13 = (bf16[32,5376]{1,0:T(8,128)(2,1)S(1)}, bf16[32,5376]{1,0:T(8,128)(2,1)S(1)}, u32[]{:S(2)}, u32[]{:S(2)}) collective-permute-start(bf16[32,5376]{1,0:T(8,128)(2,1)S(1)} %get-tuple-element.59), channel_id=1, source_target_pairs={{0,6},{2,0},{4,2},{6,4},{1,7},{3,1},{5,3},{7,5},{8,14},{10,8},{12,... | collective-permute-start | bytes 1032200 | tf_op jit(solution)/shard_map/ppermute | solution.py:34
  81.7 1.5 collective-permute-start.10
  84.4 1.3 collective-permute-done.16.refs_4_
  85.7 3.4 %collective-permute-done.12 = bf16[32,5376]{1,0:T(8,128)(2,1)S(1)} collective-permute-done((bf16[32,5376]{1,0:T(8,128)(2,1)S(1)}, bf16[32,5376]{1,0:T(8,128)(2,1)S(1)}, u32[]{:S(2)}, u32[]{:S(2)}) %collective-permute-start.12) | collective-permute-done | bytes 344096 | tf_op jit(solution)/shard_map/ppermute | solution.py:34
  90.0 1.7 collective-permute-start.24
  91.9 15.4 %collective-permute-done.10.refs_6_ = bf16[336,2688]{1,0:T(8,128)(2,1)S(1)} collective-permute-done((bf16[336,2688]{1,0:T(8,128)(2,1)}, bf16[336,2688]{1,0:T(8,128)(2,1)S(1)}, u32[]{:S(2)}, u32[]{:S(2)}) %collective-permute-start.10) | collective-permute-done | bytes 1806368 | tf_op jit(solution)/shard_map/ppermute | solution.py:90
  107.9 1.3 collective-permute-start.17
  109.2 4.5 %collective-permute-done.19.bt_ref = bf16[32,5376]{1,0:T(8,128)(2,1)S(1)} collective-permute-done((bf16[32,5376]{1,0:T(8,128)(2,1)S(1)}, bf16[32,5376]{1,0:T(8,128)(2,1)S(1)}, u32[]{:S(2)}, u32[]{:S(2)}) %collective-permute-start.19) | collective-permute-done | bytes 344096 | tf_op jit(solution)/shard_map/ppermute | solution.py:34
  113.7 3.8 %collective-permute-done.20.bb_ref = bf16[32,5376]{1,0:T(8,128)(2,1)S(1)} collective-permute-done((bf16[32,5376]{1,0:T(8,128)(2,1)S(1)}, bf16[32,5376]{1,0:T(8,128)(2,1)S(1)}, u32[]{:S(2)}, u32[]{:S(2)}) %collective-permute-start.20) | collective-permute-done | bytes 344096 | tf_op jit(solution)/shard_map/ppermute | solution.py:34
  119.4 1.9 collective-permute-start.22
  121.3 11.8 %collective-permute-start.27 = (bf16[64,5376]{1,0:T(8,128)(2,1)S(1)}, bf16[64,5376]{1,0:T(8,128)(2,1)S(1)}, u32[]{:S(2)}, u32[]{:S(2)}) collective-permute-start(bf16[64,5376]{1,0:T(8,128)(2,1)S(1)} %get-tuple-element.69.refs_0_), channel_id=1, source_target_pairs={{0,1},{1,0},{2,3},{3,2},{4,5},{5,4},{6,7},{7,6},{8,9},{9,8},{10,11... | collective-permute-start | bytes 2064392 | tf_op jit(solution)/shard_map/ppermute | solution.py:34
  133.2 1.8 collective-permute-start.25
  136.0 8.6 %collective-permute-done.25.refs_3_ = bf16[32,5376]{1,0:T(8,128)(2,1)S(1)} collective-permute-done((bf16[32,5376]{1,0:T(8,128)(2,1)S(1)}, bf16[32,5376]{1,0:T(8,128)(2,1)S(1)}, u32[]{:S(2)}, u32[]{:S(2)}) %collective-permute-start.25) | collective-permute-done | bytes 344096 | tf_op jit(solution)/shard_map/ppermute | solution.py:34
  144.6 11.7 %collective-permute-start.30 = (bf16[32,5376]{1,0:T(8,128)(2,1)S(1)}, bf16[32,5376]{1,0:T(8,128)(2,1)S(1)}, u32[]{:S(2)}, u32[]{:S(2)}) collective-permute-start(bf16[32,5376]{1,0:T(8,128)(2,1)S(1)} %collective-permute-done.25.refs_3_), channel_id=1, source_target_pairs={{0,1},{1,0},{2,3},{3,2},{4,5},{5,4},{6,7},{7,6},{8,9},{9,8},{10,11... | collective-permute-start | bytes 1032200 | tf_op jit(solution)/shard_map/ppermute | solution.py:34
  156.3 1.5 collective-permute-start.32
  157.8 1.2 collective-permute-start.33
  160.5 1.3 collective-permute-done.31.refs_9_
  162.1 1.8 collective-permute-done.28.refs_6_
  164.3 1.8 collective-permute-done.29.refs_7_
  166.0 5.1 %order.1.refs_13_.refs_5_ = bf16[512,5632]{1,0:T(8,128)(2,1)S(1)} custom-call(bf16[64,5376]{1,0:T(8,128)(2,1)S(1)} %get-tuple-element.69.refs_0_, bf16[64,5376]{1,0:T(8,128)(2,1)S(1)} %collective-permute-done.21.refs_1_, bf16[64,5376]{1,0:T(8,128)(2,1)S(1)} %collective-permute-done.22.refs_2_, bf16[32,5376]{1,0:T(8,128)(2,1)S(1)} %collective-permute-done.25.refs_3_, ...), custom_call_target="tpu_custom_call" | custom-call | bytes 1000 | tf_op jit(solution)/shard_map/order/pallas_call | solution.py:241
  171.1 2.5 %copy-done = bf16[512,5632]{1,0:T(8,128)(2,1)} copy-done((bf16[512,5632]{1,0:T(8,128)(2,1)}, bf16[512,5632]{1,0:T(8,128)(2,1)S(1)}, u32[]{:S(2)}) %copy-start) | copy-done | bytes 5767192
  173.6 4.9 %collective-permute-done.35.refs_2_ = bf16[336,2688]{1,0:T(8,128)(2,1)S(1)} collective-permute-done((bf16[336,2688]{1,0:T(8,128)(2,1)S(1)}, bf16[336,2688]{1,0:T(8,128)(2,1)S(1)}, u32[]{:S(2)}, u32[]{:S(2)}) %collective-permute-start.35) | collective-permute-done | bytes 1806368 | tf_op jit(solution)/shard_map/ppermute | solution.py:90
  179.7 18.0 %collective-permute-done.33.refs_11_ = bf16[336,2688]{1,0:T(8,128)(2,1)S(1)} collective-permute-done((bf16[336,2688]{1,0:T(8,128)(2,1)S(1)}, bf16[336,2688]{1,0:T(8,128)(2,1)S(1)}, u32[]{:S(2)}, u32[]{:S(2)}) %collective-permute-start.33) | collective-permute-done | bytes 1806368 | tf_op jit(solution)/shard_map/ppermute | solution.py:90
  197.7 1.2 copy-done.20
  199.0 1.2 collective-permute-start.41
  201.8 21.8 %near.1.refs_6_ = f32[512,2688]{1,0:T(8,128)} custom-call(bf16[336,2688]{1,0:T(8,128)(2,1)} %copy-done.1, bf16[336,2688]{1,0:T(8,128)(2,1)} %copy-done.14, bf16[336,2688]{1,0:T(8,128)(2,1)} %collective-permute-done.6.refs_2_, bf16[336,2688]{1,0:T(8,128)(2,1)} %copy-done.16, bf16[336,2688]{1,0:T(8,128)(2,1)} %copy-done.15, ...), custom_call_target="tpu_custom_call" | custom-call | bytes 1000 | tf_op jit(solution)/shard_map/near/pallas_call | solution.py:298
  226.8 1.3 copy-done.11
  228.1 1.2 copy-done.12
  229.3 13.4 %far.1 = bf16[1344,512]{1,0:T(8,128)(2,1)} custom-call(bf16[336,2688]{1,0:T(8,128)(2,1)} %copy-done.10, bf16[336,2688]{1,0:T(8,128)(2,1)} %copy-done.11, bf16[336,2688]{1,0:T(8,128)(2,1)} %copy-done.9, bf16[336,2688]{1,0:T(8,128)(2,1)} %copy-done.12, s32[4]{0:T(128)} %copy-done.7, bf16[512,5632]{1,0:T(8,128)(2,1)} %copy-done, f32[512,2688]{1,0:T(8,128)} %near.1.refs_6_), custom_call_target="tpu_custom_call" | custom-call | flops 3699376128 | bytes 12730368 | tf_op jit(solution)/shard_map/far/pallas_call | solution.py:342
  (139 shorter events, 25.4 us)
Async XLA Ops:
  0.7 66.9 %collective-permute-start.9 = (bf16[512,5376]{1,0:T(8,128)(2,1)}, bf16[512,5376]{1,0:T(8,128)(2,1)}, u32[]{:S(2)}, u32[]{:S(2)}) collective-permute-start(bf16[512,5376]{1,0:T(8,128)(2,1)} %w_ref.1), channel_id=1, source_target_pairs={{0,1},{1,0},{2,3},{3,2},{4,5},{5,4},{6,7},{7,6},{8,9},{9,8},{10,11... | collective-permute-start | bytes 16515080 | tf_op jit(solution)/shard_map/ppermute | solution.py:34
  6.1 8.2 %collective-permute-start = (bf16[4,80,672]{2,1,0:T(8,128)(2,1)}, bf16[4,80,672]{2,1,0:T(8,128)(2,1)}, u32[]{:S(2)}, u32[]{:S(2)}) collective-permute-start(bf16[4,80,672]{2,1,0:T(8,128)(2,1)} %fusion.6), channel_id=1, source_target_pairs={{0,1},{1,0},{2,3},{3,2},{4,5},{5,4},{6,7},{7,6},{8,9},{9,8},{10,11... | collective-permute-start | bytes 1290248 | tf_op jit(solution)/shard_map/ppermute | solution.py:34
  6.3 14.3 %collective-permute-start.4 = (bf16[512,512]{1,0:T(8,128)(2,1)S(1)}, bf16[512,512]{1,0:T(8,128)(2,1)}, u32[]{:S(2)}, u32[]{:S(2)}) collective-permute-start(bf16[512,512]{1,0:T(8,128)(2,1)S(1)} %pair.1.kv0_ref), channel_id=1, source_target_pairs={{0,8},{8,16},{16,24},{24,32},{32,40},{40,48},{48,56},{56,64},{64,7... | collective-permute-start | bytes 1572872 | tf_op jit(solution)/shard_map/ppermute | solution.py:39
  11.9 28.7 %collective-permute-start.6 = (bf16[336,2688]{1,0:T(8,128)(2,1)S(1)}, bf16[336,2688]{1,0:T(8,128)(2,1)}, u32[]{:S(2)}, u32[]{:S(2)}) collective-permute-start(bf16[336,2688]{1,0:T(8,128)(2,1)S(1)} %pack.1.refs_0_), channel_id=1, source_target_pairs={{0,24},{1,97},{2,26},{3,99},{4,28},{5,101},{6,30},{7,103},{8,0},{9... | collective-permute-start | bytes 5419016 | tf_op jit(solution)/shard_map/ppermute | solution.py:90
  14.3 151.7 %copy-start.7 = (s32[4]{0:T(128)}, s32[4]{0:T(128)S(1)}, u32[]{:S(2)}) copy-start(s32[4]{0:T(128)S(1)} %pad_add_fusion.at_ref.refs_10_.refs_12_.refs_4_) | copy-start | bytes 52
  14.3 53.2 %slice-start = ((s8[5505024]{0:T(1024)(128)(4,1)}), s8[4194304]{0:T(1024)(128)(4,1)S(1)}, s32[]{:S(2)}) async-start(s8[5505024]{0:T(1024)(128)(4,1)} %bitcast.124), calls=%async_computation | async-start | bytes 8388608
  16.8 10.8 %collective-permute-start.1 = (bf16[2,80,672]{2,1,0:T(8,128)(2,1)S(1)}, bf16[2,80,672]{2,1,0:T(8,128)(2,1)S(1)}, u32[]{:S(2)}, u32[]{:S(2)}) collective-permute-start(bf16[2,80,672]{2,1,0:T(8,128)(2,1)S(1)} %get-tuple-element.100), channel_id=1, source_target_pairs={{0,6},{2,0},{4,2},{6,4},{1,7},{3,1},{5,3},{7,5},{8,14},{10,8},{12,... | collective-permute-start | bytes 645128 | tf_op jit(solution)/shard_map/ppermute | solution.py:34
  20.6 36.9 %collective-permute-start.7 = (bf16[336,2688]{1,0:T(8,128)(2,1)S(1)}, bf16[336,2688]{1,0:T(8,128)(2,1)S(1)}, u32[]{:S(2)}, u32[]{:S(2)}) collective-permute-start(bf16[336,2688]{1,0:T(8,128)(2,1)S(1)} %pack.1.refs_0_), channel_id=1, source_target_pairs={{0,96},{1,25},{2,98},{3,27},{4,100},{5,29},{6,102},{7,31},{8,104},... | collective-permute-start | bytes 5419016 | tf_op jit(solution)/shard_map/ppermute | solution.py:90
  23.9 7.3 %collective-permute-start.2 = (bf16[2,80,672]{2,1,0:T(8,128)(2,1)S(1)}, bf16[2,80,672]{2,1,0:T(8,128)(2,1)S(1)}, u32[]{:S(2)}, u32[]{:S(2)}) collective-permute-start(bf16[2,80,672]{2,1,0:T(8,128)(2,1)S(1)} %get-tuple-element.99), channel_id=1, source_target_pairs={{0,4},{2,6},{4,0},{6,2},{1,5},{3,7},{5,1},{7,3},{8,12},{10,14},{12... | collective-permute-start | bytes 645128 | tf_op jit(solution)/shard_map/ppermute | solution.py:34
  27.6 10.4 %collective-permute-start.5 = (bf16[512,512]{1,0:T(8,128)(2,1)}, bf16[512,512]{1,0:T(8,128)(2,1)S(1)}, u32[]{:S(2)}, u32[]{:S(2)}) collective-permute-start(bf16[512,512]{1,0:T(8,128)(2,1)} %collective-permute-done.4.kv1_ref), channel_id=1, source_target_pairs={{0,8},{8,16},{16,24},{24,32},{32,40},{40,48},{48,56},{56,64},{64,7... | collective-permute-start | bytes 1572872 | tf_op jit(solution)/shard_map/ppermute | solution.py:39
  31.2 6.8 %collective-permute-start.3 = (bf16[2,80,672]{2,1,0:T(8,128)(2,1)S(1)}, bf16[2,80,672]{2,1,0:T(8,128)(2,1)S(1)}, u32[]{:S(2)}, u32[]{:S(2)}) collective-permute-start(bf16[2,80,672]{2,1,0:T(8,128)(2,1)S(1)} %get-tuple-element.98), channel_id=1, source_target_pairs={{0,2},{2,4},{4,6},{6,0},{1,3},{3,5},{5,7},{7,1},{8,10},{10,12},{12... | collective-permute-start | bytes 645128 | tf_op jit(solution)/shard_map/ppermute | solution.py:34
  40.6 41.1 %collective-permute-start.14 = (bf16[336,2688]{1,0:T(8,128)(2,1)S(1)}, bf16[336,2688]{1,0:T(8,128)(2,1)S(1)}, u32[]{:S(2)}, u32[]{:S(2)}) collective-permute-start(bf16[336,2688]{1,0:T(8,128)(2,1)S(1)} %pack.1.refs_0_), channel_id=1, source_target_pairs={{0,8},{1,33},{2,10},{3,35},{4,12},{5,37},{6,14},{7,39},{8,16},{9,4... | collective-permute-start | bytes 5419016 | tf_op jit(solution)/shard_map/ppermute | solution.py:90
  45.3 40.4 %collective-permute-start.16 = (bf16[336,2688]{1,0:T(8,128)(2,1)S(1)}, bf16[336,2688]{1,0:T(8,128)(2,1)S(1)}, u32[]{:S(2)}, u32[]{:S(2)}) collective-permute-start(bf16[336,2688]{1,0:T(8,128)(2,1)S(1)} %pack.1.refs_0_), channel_id=1, source_target_pairs={{0,32},{1,9},{2,34},{3,11},{4,36},{5,13},{6,38},{7,15},{8,40},{9,1... | collective-permute-start | bytes 5419016 | tf_op jit(solution)/shard_map/ppermute | solution.py:90
  45.8 37.4 %collective-permute-start.15 = (bf16[336,2688]{1,0:T(8,128)(2,1)}, bf16[336,2688]{1,0:T(8,128)(2,1)S(1)}, u32[]{:S(2)}, u32[]{:S(2)}) collective-permute-start(bf16[336,2688]{1,0:T(8,128)(2,1)} %collective-permute-done.6.refs_2_), channel_id=1, source_target_pairs={{0,24},{1,97},{2,26},{3,99},{4,28},{5,101},{6,30},{7,103},{8,0},{9... | collective-permute-start | bytes 5419016 | tf_op jit(solution)/shard_map/ppermute | solution.py:90
  64.8 2.7 %collective-permute-start.8 = (bf16[256,512]{1,0:T(8,128)(2,1)S(1)}, bf16[256,512]{1,0:T(8,128)(2,1)S(1)}, u32[]{:S(2)}, u32[]{:S(2)}) collective-permute-start(bf16[256,512]{1,0:T(8,128)(2,1)S(1)} %bitcast.134), channel_id=1, source_target_pairs={{0,1},{1,0},{2,3},{3,2},{4,5},{5,4},{6,7},{7,6},{8,9},{9,8},{10,11... | collective-permute-start | bytes 786440 | tf_op jit(solution)/shard_map/ppermute | solution.py:34
  74.8 14.3 %collective-permute-start.12 = (bf16[32,5376]{1,0:T(8,128)(2,1)S(1)}, bf16[32,5376]{1,0:T(8,128)(2,1)S(1)}, u32[]{:S(2)}, u32[]{:S(2)}) collective-permute-start(bf16[32,5376]{1,0:T(8,128)(2,1)S(1)} %get-tuple-element.58), channel_id=1, source_target_pairs={{0,2},{2,4},{4,6},{6,0},{1,3},{3,5},{5,7},{7,1},{8,10},{10,12},{12... | collective-permute-start | bytes 1032200 | tf_op jit(solution)/shard_map/ppermute | solution.py:34
  78.0 11.1 %collective-permute-start.13 = (bf16[32,5376]{1,0:T(8,128)(2,1)S(1)}, bf16[32,5376]{1,0:T(8,128)(2,1)S(1)}, u32[]{:S(2)}, u32[]{:S(2)}) collective-permute-start(bf16[32,5376]{1,0:T(8,128)(2,1)S(1)} %get-tuple-element.59), channel_id=1, source_target_pairs={{0,6},{2,0},{4,2},{6,4},{1,7},{3,1},{5,3},{7,5},{8,14},{10,8},{12,... | collective-permute-start | bytes 1032200 | tf_op jit(solution)/shard_map/ppermute | solution.py:34
  81.7 25.6 %collective-permute-start.10 = (bf16[336,2688]{1,0:T(8,128)(2,1)}, bf16[336,2688]{1,0:T(8,128)(2,1)S(1)}, u32[]{:S(2)}, u32[]{:S(2)}) collective-permute-start(bf16[336,2688]{1,0:T(8,128)(2,1)} %collective-permute-done.6.refs_2_), channel_id=1, source_target_pairs={{0,32},{1,9},{2,34},{3,11},{4,36},{5,13},{6,38},{7,15},{8,40},{9,1... | collective-permute-start | bytes 5419016 | tf_op jit(solution)/shard_map/ppermute | solution.py:90
  83.3 74.5 %copy-start.16 = (bf16[336,2688]{1,0:T(8,128)(2,1)}, bf16[336,2688]{1,0:T(8,128)(2,1)S(1)}, u32[]{:S(2)}) copy-start(bf16[336,2688]{1,0:T(8,128)(2,1)S(1)} %collective-permute-done.15.refs_3_) | copy-start | bytes 5419012
  83.3 24.5 %collective-permute-start.11 = (bf16[336,2688]{1,0:T(8,128)(2,1)}, bf16[336,2688]{1,0:T(8,128)(2,1)S(1)}, u32[]{:S(2)}, u32[]{:S(2)}) collective-permute-start(bf16[336,2688]{1,0:T(8,128)(2,1)} %collective-permute-done.6.refs_2_), channel_id=1, source_target_pairs={{0,96},{1,25},{2,98},{3,27},{4,100},{5,29},{6,102},{7,31},{8,104},... | collective-permute-start | bytes 5419016 | tf_op jit(solution)/shard_map/ppermute | solution.py:90
  85.7 73.3 %copy-start.15 = (bf16[336,2688]{1,0:T(8,128)(2,1)}, bf16[336,2688]{1,0:T(8,128)(2,1)S(1)}, u32[]{:S(2)}) copy-start(bf16[336,2688]{1,0:T(8,128)(2,1)S(1)} %collective-permute-done.16.refs_4_) | copy-start | bytes 5419012
  85.7 22.2 %collective-permute-start.18 = (bf16[32,5376]{1,0:T(8,128)(2,1)S(1)}, bf16[32,5376]{1,0:T(8,128)(2,1)S(1)}, u32[]{:S(2)}, u32[]{:S(2)}) collective-permute-start(bf16[32,5376]{1,0:T(8,128)(2,1)S(1)} %get-tuple-element.63), channel_id=1, source_target_pairs={{0,2},{2,4},{4,6},{6,0},{1,3},{3,5},{5,7},{7,1},{8,10},{10,12},{12... | collective-permute-start | bytes 1032200 | tf_op jit(solution)/shard_map/ppermute | solution.py:34
  89.1 44.1 %collective-permute-start.23 = (bf16[336,2688]{1,0:T(8,128)(2,1)S(1)}, bf16[336,2688]{1,0:T(8,128)(2,1)}, u32[]{:S(2)}, u32[]{:S(2)}) collective-permute-start(bf16[336,2688]{1,0:T(8,128)(2,1)S(1)} %collective-permute-done.14.refs_1_), channel_id=1, source_target_pairs={{0,32},{1,9},{2,34},{3,11},{4,36},{5,13},{6,38},{7,15},{8,40},{9,1... | collective-permute-start | bytes 5419016 | tf_op jit(solution)/shard_map/ppermute | solution.py:90
  90.0 43.1 %collective-permute-start.24 = (bf16[336,2688]{1,0:T(8,128)(2,1)S(1)}, bf16[336,2688]{1,0:T(8,128)(2,1)S(1)}, u32[]{:S(2)}, u32[]{:S(2)}) collective-permute-start(bf16[336,2688]{1,0:T(8,128)(2,1)S(1)} %collective-permute-done.14.refs_1_), channel_id=1, source_target_pairs={{0,96},{1,25},{2,98},{3,27},{4,100},{5,29},{6,102},{7,31},{8,104},... | collective-permute-start | bytes 5419016 | tf_op jit(solution)/shard_map/ppermute | solution.py:90
  107.3 51.7 %copy-start.17 = (bf16[336,2688]{1,0:T(8,128)(2,1)}, bf16[336,2688]{1,0:T(8,128)(2,1)S(1)}, u32[]{:S(2)}) copy-start(bf16[336,2688]{1,0:T(8,128)(2,1)S(1)} %collective-permute-done.10.refs_6_) | copy-start | bytes 5419012
  107.3 6.4 %collective-permute-start.19 = (bf16[32,5376]{1,0:T(8,128)(2,1)S(1)}, bf16[32,5376]{1,0:T(8,128)(2,1)S(1)}, u32[]{:S(2)}, u32[]{:S(2)}) collective-permute-start(bf16[32,5376]{1,0:T(8,128)(2,1)S(1)} %get-tuple-element.64), channel_id=1, source_target_pairs={{0,6},{2,0},{4,2},{6,4},{1,7},{3,1},{5,3},{7,5},{8,14},{10,8},{12,... | collective-permute-start | bytes 1032200 | tf_op jit(solution)/shard_map/ppermute | solution.py:34
  107.7 63.4 %copy-start.18 = (bf16[336,2688]{1,0:T(8,128)(2,1)}, bf16[336,2688]{1,0:T(8,128)(2,1)S(1)}, u32[]{:S(2)}) copy-start(bf16[336,2688]{1,0:T(8,128)(2,1)S(1)} %collective-permute-done.11.refs_10_) | copy-start | bytes 5419012
  107.7 9.7 %collective-permute-start.20 = (bf16[32,5376]{1,0:T(8,128)(2,1)S(1)}, bf16[32,5376]{1,0:T(8,128)(2,1)S(1)}, u32[]{:S(2)}, u32[]{:S(2)}) collective-permute-start(bf16[32,5376]{1,0:T(8,128)(2,1)S(1)} %add_convert_fusion), channel_id=1, source_target_pairs={{0,6},{2,0},{4,2},{6,4},{1,7},{3,1},{5,3},{7,5},{8,14},{10,8},{12,... | collective-permute-start | bytes 1032200 | tf_op jit(solution)/shard_map/ppermute | solution.py:34
  107.9 9.6 %collective-permute-start.17 = (bf16[32,5376]{1,0:T(8,128)(2,1)S(1)}, bf16[32,5376]{1,0:T(8,128)(2,1)S(1)}, u32[]{:S(2)}, u32[]{:S(2)}) collective-permute-start(bf16[32,5376]{1,0:T(8,128)(2,1)S(1)} %add_convert_fusion.1), channel_id=1, source_target_pairs={{0,2},{2,4},{4,6},{6,0},{1,3},{3,5},{5,7},{7,1},{8,10},{10,12},{12... | collective-permute-start | bytes 1032200 | tf_op jit(solution)/shard_map/ppermute | solution.py:34
  118.6 14.5 %collective-permute-start.21 = (bf16[64,5376]{1,0:T(8,128)(2,1)S(1)}, bf16[64,5376]{1,0:T(8,128)(2,1)S(1)}, u32[]{:S(2)}, u32[]{:S(2)}) collective-permute-start(bf16[64,5376]{1,0:T(8,128)(2,1)S(1)} %get-tuple-element.69.refs_0_), channel_id=1, source_target_pairs={{0,2},{2,4},{4,6},{6,0},{1,3},{3,5},{5,7},{7,1},{8,10},{10,12},{12... | collective-permute-start | bytes 2064392 | tf_op jit(solution)/shard_map/ppermute | solution.py:34
  119.4 13.7 %collective-permute-start.22 = (bf16[64,5376]{1,0:T(8,128)(2,1)S(1)}, bf16[64,5376]{1,0:T(8,128)(2,1)S(1)}, u32[]{:S(2)}, u32[]{:S(2)}) collective-permute-start(bf16[64,5376]{1,0:T(8,128)(2,1)S(1)} %get-tuple-element.69.refs_0_), channel_id=1, source_target_pairs={{0,6},{2,0},{4,2},{6,4},{1,7},{3,1},{5,3},{7,5},{8,14},{10,8},{12,... | collective-permute-start | bytes 2064392 | tf_op jit(solution)/shard_map/ppermute | solution.py:34
  121.3 36.4 %collective-permute-start.27 = (bf16[64,5376]{1,0:T(8,128)(2,1)S(1)}, bf16[64,5376]{1,0:T(8,128)(2,1)S(1)}, u32[]{:S(2)}, u32[]{:S(2)}) collective-permute-start(bf16[64,5376]{1,0:T(8,128)(2,1)S(1)} %get-tuple-element.69.refs_0_), channel_id=1, source_target_pairs={{0,1},{1,0},{2,3},{3,2},{4,5},{5,4},{6,7},{7,6},{8,9},{9,8},{10,11... | collective-permute-start | bytes 2064392 | tf_op jit(solution)/shard_map/ppermute | solution.py:34
  133.2 11.4 %collective-permute-start.25 = (bf16[32,5376]{1,0:T(8,128)(2,1)S(1)}, bf16[32,5376]{1,0:T(8,128)(2,1)S(1)}, u32[]{:S(2)}, u32[]{:S(2)}) collective-permute-start(bf16[32,5376]{1,0:T(8,128)(2,1)S(1)} %slice.76), channel_id=1, source_target_pairs={{0,2},{2,4},{4,6},{6,0},{1,3},{3,5},{5,7},{7,1},{8,10},{10,12},{12... | collective-permute-start | bytes 1032200 | tf_op jit(solution)/shard_map/ppermute | solution.py:34
  135.0 24.0 %collective-permute-start.26 = (bf16[32,5376]{1,0:T(8,128)(2,1)S(1)}, bf16[32,5376]{1,0:T(8,128)(2,1)S(1)}, u32[]{:S(2)}, u32[]{:S(2)}) collective-permute-start(bf16[32,5376]{1,0:T(8,128)(2,1)S(1)} %slice.77), channel_id=1, source_target_pairs={{0,6},{2,0},{4,2},{6,4},{1,7},{3,1},{5,3},{7,5},{8,14},{10,8},{12,... | collective-permute-start | bytes 1032200 | tf_op jit(solution)/shard_map/ppermute | solution.py:34
  144.6 14.7 %collective-permute-start.30 = (bf16[32,5376]{1,0:T(8,128)(2,1)S(1)}, bf16[32,5376]{1,0:T(8,128)(2,1)S(1)}, u32[]{:S(2)}, u32[]{:S(2)}) collective-permute-start(bf16[32,5376]{1,0:T(8,128)(2,1)S(1)} %collective-permute-done.25.refs_3_), channel_id=1, source_target_pairs={{0,1},{1,0},{2,3},{3,2},{4,5},{5,4},{6,7},{7,6},{8,9},{9,8},{10,11... | collective-permute-start | bytes 1032200 | tf_op jit(solution)/shard_map/ppermute | solution.py:34
  156.3 22.2 %collective-permute-start.35 = (bf16[336,2688]{1,0:T(8,128)(2,1)S(1)}, bf16[336,2688]{1,0:T(8,128)(2,1)S(1)}, u32[]{:S(2)}, u32[]{:S(2)}) collective-permute-start(bf16[336,2688]{1,0:T(8,128)(2,1)S(1)} %collective-permute-done.11.refs_10_), channel_id=1, source_target_pairs={{0,96},{1,25},{2,98},{3,27},{4,100},{5,29},{6,102},{7,31},{8,104},... | collective-permute-start | bytes 5419016 | tf_op jit(solution)/shard_map/ppermute | solution.py:90
  156.3 23.4 %collective-permute-start.32 = (bf16[336,2688]{1,0:T(8,128)(2,1)S(1)}, bf16[336,2688]{1,0:T(8,128)(2,1)}, u32[]{:S(2)}, u32[]{:S(2)}) collective-permute-start(bf16[336,2688]{1,0:T(8,128)(2,1)S(1)} %collective-permute-done.15.refs_3_), channel_id=1, source_target_pairs={{0,32},{1,9},{2,34},{3,11},{4,36},{5,13},{6,38},{7,15},{8,40},{9,1... | collective-permute-start | bytes 5419016 | tf_op jit(solution)/shard_map/ppermute | solution.py:90
  157.8 39.9 %collective-permute-start.33 = (bf16[336,2688]{1,0:T(8,128)(2,1)S(1)}, bf16[336,2688]{1,0:T(8,128)(2,1)S(1)}, u32[]{:S(2)}, u32[]{:S(2)}) collective-permute-start(bf16[336,2688]{1,0:T(8,128)(2,1)S(1)} %collective-permute-done.15.refs_3_), channel_id=1, source_target_pairs={{0,96},{1,25},{2,98},{3,27},{4,100},{5,29},{6,102},{7,31},{8,104},... | collective-permute-start | bytes 5419016 | tf_op jit(solution)/shard_map/ppermute | solution.py:90
  159.0 40.0 %collective-permute-start.34 = (bf16[336,2688]{1,0:T(8,128)(2,1)S(1)}, bf16[336,2688]{1,0:T(8,128)(2,1)S(1)}, u32[]{:S(2)}, u32[]{:S(2)}) collective-permute-start(bf16[336,2688]{1,0:T(8,128)(2,1)S(1)} %collective-permute-done.16.refs_4_), channel_id=1, source_target_pairs={{0,32},{1,9},{2,34},{3,11},{4,36},{5,13},{6,38},{7,15},{8,40},{9,1... | collective-permute-start | bytes 5419016 | tf_op jit(solution)/shard_map/ppermute | solution.py:90
  159.3 2.4 collective-permute-start.31
  161.7 2.1 collective-permute-start.28
  163.9 2.1 collective-permute-start.29
  166.0 60.8 %collective-permute-start.40 = (bf16[336,2688]{1,0:T(8,128)(2,1)}, bf16[336,2688]{1,0:T(8,128)(2,1)S(1)}, u32[]{:S(2)}, u32[]{:S(2)}) collective-permute-start(bf16[336,2688]{1,0:T(8,128)(2,1)} %collective-permute-done.23.refs_5_), channel_id=1, source_target_pairs={{0,32},{1,9},{2,34},{3,11},{4,36},{5,13},{6,38},{7,15},{8,40},{9,1... | collective-permute-start | bytes 5419016 | tf_op jit(solution)/shard_map/ppermute | solution.py:90
  199.0 27.8 %collective-permute-start.41 = (bf16[336,2688]{1,0:T(8,128)(2,1)}, bf16[336,2688]{1,0:T(8,128)(2,1)S(1)}, u32[]{:S(2)}, u32[]{:S(2)}) collective-permute-start(bf16[336,2688]{1,0:T(8,128)(2,1)} %copy-done.20), channel_id=1, source_target_pairs={{0,96},{1,25},{2,98},{3,27},{4,100},{5,29},{6,102},{7,31},{8,104},... | collective-permute-start | bytes 5419016 | tf_op jit(solution)/shard_map/ppermute | solution.py:90
  201.0 22.7 %collective-permute-start.36 = (bf16[4,64,672]{2,1,0:T(8,128)(2,1)}, bf16[4,64,672]{2,1,0:T(8,128)(2,1)}, u32[]{:S(2)}, u32[]{:S(2)}) collective-permute-start(bf16[4,64,672]{2,1,0:T(8,128)(2,1)} %select_bitcast_fusion.2), channel_id=1, source_target_pairs={{0,1},{1,0},{2,3},{3,2},{4,5},{5,4},{6,7},{7,6},{8,9},{9,8},{10,11... | collective-permute-start | bytes 1032200 | tf_op jit(solution)/shard_map/ppermute | solution.py:34
  225.3 17.5 %collective-permute-start.37 = (bf16[2,64,672]{2,1,0:T(8,128)(2,1)S(1)}, bf16[2,64,672]{2,1,0:T(8,128)(2,1)S(1)}, u32[]{:S(2)}, u32[]{:S(2)}) collective-permute-start(bf16[2,64,672]{2,1,0:T(8,128)(2,1)S(1)} %get-tuple-element.103), channel_id=1, source_target_pairs={{0,6},{2,0},{4,2},{6,4},{1,7},{3,1},{5,3},{7,5},{8,14},{10,8},{12,... | collective-permute-start | bytes 516104 | tf_op jit(solution)/shard_map/ppermute | solution.py:34
  225.3 17.4 %collective-permute-start.38 = (bf16[2,64,672]{2,1,0:T(8,128)(2,1)S(1)}, bf16[2,64,672]{2,1,0:T(8,128)(2,1)S(1)}, u32[]{:S(2)}, u32[]{:S(2)}) collective-permute-start(bf16[2,64,672]{2,1,0:T(8,128)(2,1)S(1)} %get-tuple-element.102), channel_id=1, source_target_pairs={{0,4},{2,6},{4,0},{6,2},{1,5},{3,7},{5,1},{7,3},{8,12},{10,14},{12... | collective-permute-start | bytes 516104 | tf_op jit(solution)/shard_map/ppermute | solution.py:34
  226.4 16.3 %collective-permute-start.39 = (bf16[2,64,672]{2,1,0:T(8,128)(2,1)S(1)}, bf16[2,64,672]{2,1,0:T(8,128)(2,1)S(1)}, u32[]{:S(2)}, u32[]{:S(2)}) collective-permute-start(bf16[2,64,672]{2,1,0:T(8,128)(2,1)S(1)} %get-tuple-element.101), channel_id=1, source_target_pairs={{0,2},{2,4},{4,6},{6,0},{1,3},{3,5},{5,7},{7,1},{8,10},{10,12},{12... | collective-permute-start | bytes 516104 | tf_op jit(solution)/shard_map/ppermute | solution.py:34
  (18 other events, 243.4 us)

commit v10 on v7

--- a/solution.py
+++ b/solution.py
@@ -385,15 +385,14 @@
 
     kv0 = pair(keys, values)
     kv1 = behind(kv0)
-    gate_weight, kv0 = lax.optimization_barrier((gate_weight, kv0))
     w = pack(gate_weight, up_weight)
     p = ring(w, -1, 0)
-    kv1, w = lax.optimization_barrier((kv1, w))
+    kv1, w_late = lax.optimization_barrier((kv1, w))
     kv2 = behind(kv1)
-    kv2, w_late, p = lax.optimization_barrier((kv2, w, p))
     m = ring(w_late, 1, 0)
     b = ring(p, -1, 0)
-    prev, following = [ring(w_late, 1, 1)], [ring(w, -1, 1)]
+    w_late, kv2 = lax.optimization_barrier((w_late, kv2))
+    prev, following = [ring(w_late, 1, 1)], [ring(w_late, -1, 1)]
 
     gains = jnp.stack([post_gain, pre_gain])
     high = gains.astype(BF)
@@ -408,20 +407,22 @@
     kid = lax.dynamic_slice_in_dim(padded, start, 3 * TOK, 0)[None, :]
     qid = lax.dynamic_slice_in_dim(doc_ids, start, TOK, 0)[:, None]
 
-    queries, mine, p, following[0] = lax.optimization_barrier((queries, mine, p, following[0]))
+    queries, mine, p = lax.optimization_barrier((queries, mine, p))
     mix = attend(where, queries, kv2, kv1, kv0, qid, kid)
     other_weight = shift(out_weight, "c", 1)
     own, other = mix[0].reshape(256, 512), shift(mix[1].reshape(256, 512), "c", 1)
-    other, m = lax.optimization_barrier((other, m))
+    other, m, following[0] = lax.optimization_barrier((other, m, following[0]))
+    prev += [ring(v, 1, 1) for v in (m, p)]
+    following += [ring(v, -1, 1) for v in (m, p)]
     p0, p1t, p1b, p2t, p2b, p3t, p3b = project(own, other, out_weight, other_weight)
 
     up_t = shift(p2t, "z", 1)
     dn_b = shift(p2b, "z", -1)
     a_b = shift(p1b, "z", 1)
     b_t = shift(p3t, "z", -1)
-    up_t, dn_b, m, b, prev, following = lax.optimization_barrier((up_t, dn_b, m, b, prev, following))
-    prev += [ring(v, 1, 1) for v in (m, p, b)]
-    following += [ring(v, -1, 1) for v in (m, p, b)]
+    up_t, dn_b, b, prev[0] = lax.optimization_barrier((up_t, dn_b, b, prev[0]))
+    prev += [ring(b, 1, 1)]
+    following += [ring(b, -1, 1)]
     add = lambda p, q: (p.astype(F32) + q.astype(F32)).astype(BF)
     a_t = shift(add(p1t, up_t), "z", 1)
     b_b = shift(add(p3b, dn_b), "z", -1)

time: 235 us -> 218 us (0.928)
  starting transfers between devices: 78.1 us -> 58.6 us
  waiting for transfers between devices: 81.1 us -> 84.1 us
    ppermute x25, starting transfers between devices: 52.3 us -> 36.8 us  [shift(): return lax.ppermute(value, axis, [(i, (i + by) % n) for i in range(n)])]
    ppermute x2, waiting for transfers between devices: 3.99 us -> 13.9 us  [behind(): return lax.ppermute(value, ('y', 'x'), [(i, i + 1) for i in range(n - 1)])]
    ppermute x15, waiting for transfers between devices: 40.8 us -> 31.2 us  [ring(): return lax.ppermute(value, ('y', 'x', 'z', 'c'), pairs)]
    ppermute x15, starting transfers between devices: 18.4 us -> 15.5 us  [ring(): return lax.ppermute(value, ('y', 'x', 'z', 'c'), pairs)]
    unnamed x62 -> x58, local copies, waits for them, and re-layouts: 11.9 us -> 9.15 us
    ppermute x25, waiting for transfers between devices: 36.3 us -> 38.9 us  [shift(): return lax.ppermute(value, axis, [(i, (i + by) % n) for i in range(n)])]
  transfers between devices with their start and end apart: 42 -> 42, of which waited for: 14 -> 18; matrix products, arithmetic and copies ran while one was open for 3% -> 5% of each run, Pallas kernels for 24% -> 25%
where the time goes in v10:
time: 218 us; the launch traced here: 217 us
  waiting for transfers between devices  84.1 us (39%)
  starting transfers between devices  58.6 us (27%)
  Pallas kernels  54.7 us (25%)
  local copies, waits for them, and re-layouts  12.2 us (6%)
  other arithmetic  5.83 us (3%)
    ppermute x25, waiting for transfers between devices, shift(): return lax.ppermute(value, axis, [(i, (i + by) % n) for i in range(n)])  38.9 us
    ppermute x25, starting transfers between devices, shift(): return lax.ppermute(value, axis, [(i, (i + by) % n) for i in range(n)])  36.8 us
    ppermute x15, waiting for transfers between devices, ring(): return lax.ppermute(value, ('y', 'x', 'z', 'c'), pairs)  31.2 us
    pallas_call x1, Pallas kernels, near(): pl.pallas_call(body, out_shape=jax.ShapeDtypeStruct((TOK, 2688), F32), gr...  21.9 us
    ppermute x15, starting transfers between devices, ring(): return lax.ppermute(value, ('y', 'x', 'z', 'c'), pairs)  15.5 us
    ppermute x2, waiting for transfers between devices, behind(): return lax.ppermute(value, ('y', 'x'), [(i, i + 1) for i in range(n - 1)])  13.9 us
    pallas_call x1, Pallas kernels, far(): pl.pallas_call(body, out_shape=jax.ShapeDtypeStruct((1344, TOK), BF), gri...  13.4 us
    unnamed x58, local copies, waits for them, and re-layouts  9.15 us
  transfers between devices with their start and end apart: 42, of which 18 were waited for; matrix products, arithmetic and copies ran while one was open for 5% of the time, Pallas kernels for 25%

profile of v10, /device:TPU:1, one launch (start us, length us, event | category | flops | bytes accessed | tf_op | source)
XLA Modules:
  0.0 216.6 jit_solution(18020953286171503002)
XLA Ops:
  0.6 1.5 collective-permute-start.10
  3.5 1.4 copy.22
  7.0 2.9 %collective-permute-start.4 = (bf16[336,2688]{1,0:T(8,128)(2,1)S(1)}, bf16[336,2688]{1,0:T(8,128)(2,1)}, u32[]{:S(2)}, u32[]{:S(2)}) collective-permute-start(bf16[336,2688]{1,0:T(8,128)(2,1)S(1)} %pack.1.refs_0_), channel_id=1, source_target_pairs={{0,24},{1,97},{2,26},{3,99},{4,28},{5,101},{6,30},{7,103},{8,0},{9... | collective-permute-start | bytes 5419016 | tf_op jit(solution)/shard_map/ppermute | solution.py:90
  9.9 3.1 %collective-permute-start.5 = (bf16[512,512]{1,0:T(8,128)(2,1)S(1)}, bf16[512,512]{1,0:T(8,128)(2,1)S(1)}, u32[]{:S(2)}, u32[]{:S(2)}) collective-permute-start(bf16[512,512]{1,0:T(8,128)(2,1)S(1)} %pair.1.kv0_ref), channel_id=1, source_target_pairs={{0,8},{8,16},{16,24},{24,32},{32,40},{40,48},{48,56},{56,64},{64,7... | collective-permute-start | bytes 1572872 | tf_op jit(solution)/shard_map/ppermute | solution.py:39
  13.6 1.8 select_bitcast_fusion
  16.0 3.8 %collective-permute-start.1 = (bf16[2,80,672]{2,1,0:T(8,128)(2,1)S(1)}, bf16[2,80,672]{2,1,0:T(8,128)(2,1)S(1)}, u32[]{:S(2)}, u32[]{:S(2)}) collective-permute-start(bf16[2,80,672]{2,1,0:T(8,128)(2,1)S(1)} %get-tuple-element.108), channel_id=1, source_target_pairs={{0,6},{2,0},{4,2},{6,4},{1,7},{3,1},{5,3},{7,5},{8,14},{10,8},{12,... | collective-permute-start | bytes 645128 | tf_op jit(solution)/shard_map/ppermute | solution.py:34
  19.9 3.4 %collective-permute-done.5.kv1_ref = bf16[512,512]{1,0:T(8,128)(2,1)S(1)} collective-permute-done((bf16[512,512]{1,0:T(8,128)(2,1)S(1)}, bf16[512,512]{1,0:T(8,128)(2,1)S(1)}, u32[]{:S(2)}, u32[]{:S(2)}) %collective-permute-start.5) | collective-permute-done | bytes 524320 | tf_op jit(solution)/shard_map/ppermute | solution.py:39
  23.4 1.6 collective-permute-start.3
  25.0 5.1 %collective-permute-done.1 = bf16[2,80,672]{2,1,0:T(8,128)(2,1)S(1)} collective-permute-done((bf16[2,80,672]{2,1,0:T(8,128)(2,1)S(1)}, bf16[2,80,672]{2,1,0:T(8,128)(2,1)S(1)}, u32[]{:S(2)}, u32[]{:S(2)}) %collective-permute-start.1) | collective-permute-done | bytes 215072 | tf_op jit(solution)/shard_map/ppermute | solution.py:34
  30.1 3.1 %collective-permute-start.6 = (bf16[512,512]{1,0:T(8,128)(2,1)S(1)}, bf16[512,512]{1,0:T(8,128)(2,1)S(1)}, u32[]{:S(2)}, u32[]{:S(2)}) collective-permute-start(bf16[512,512]{1,0:T(8,128)(2,1)S(1)} %collective-permute-done.5.kv1_ref), channel_id=1, source_target_pairs={{0,8},{8,16},{16,24},{24,32},{32,40},{40,48},{48,56},{56,64},{64,7... | collective-permute-start | bytes 1572872 | tf_op jit(solution)/shard_map/ppermute | solution.py:39
  34.3 10.5 %collective-permute-done.6.kv2_ref = bf16[512,512]{1,0:T(8,128)(2,1)S(1)} collective-permute-done((bf16[512,512]{1,0:T(8,128)(2,1)S(1)}, bf16[512,512]{1,0:T(8,128)(2,1)S(1)}, u32[]{:S(2)}, u32[]{:S(2)}) %collective-permute-start.6) | collective-permute-done | bytes 524320 | tf_op jit(solution)/shard_map/ppermute | solution.py:39
  44.8 1.3 collective-permute-start.9
  47.0 5.5 %attend.1 = bf16[2,4,64,512]{3,2,1,0:T(8,128)(2,1)S(1)} custom-call(s32[4]{0:T(128)S(1)} %pad_add_fusion.at_ref.refs_10_.refs_12_.refs_4_, bf16[512,512]{1,0:T(8,128)(2,1)S(1)} %copy-done.4, bf16[512,512]{1,0:T(8,128)(2,1)S(1)} %collective-permute-done.6.kv2_ref, bf16[512,512]{1,0:T(8,128)(2,1)S(1)} %collective-permute-done.5.kv1_ref, ...), custom_call_target="tpu_custom_call" | custom-call | bytes 1000 | tf_op jit(solution)/shard_map/attend/pallas_call | solution.py:123
  52.6 2.6 %collective-permute-start.7 = (bf16[256,512]{1,0:T(8,128)(2,1)S(1)}, bf16[256,512]{1,0:T(8,128)(2,1)S(1)}, u32[]{:S(2)}, u32[]{:S(2)}) collective-permute-start(bf16[256,512]{1,0:T(8,128)(2,1)S(1)} %bitcast.134), channel_id=1, source_target_pairs={{0,1},{1,0},{2,3},{3,2},{4,5},{5,4},{6,7},{7,6},{8,9},{9,8},{10,11... | collective-permute-start | bytes 786440 | tf_op jit(solution)/shard_map/ppermute | solution.py:34
  55.1 1.2 collective-permute-done.7.s
  56.3 2.9 %collective-permute-start.15 = (bf16[336,2688]{1,0:T(8,128)(2,1)}, bf16[336,2688]{1,0:T(8,128)(2,1)S(1)}, u32[]{:S(2)}, u32[]{:S(2)}) collective-permute-start(bf16[336,2688]{1,0:T(8,128)(2,1)} %collective-permute-done.4.refs_2_), channel_id=1, source_target_pairs={{0,24},{1,97},{2,26},{3,99},{4,28},{5,101},{6,30},{7,103},{8,0},{9... | collective-permute-start | bytes 5419016 | tf_op jit(solution)/shard_map/ppermute | solution.py:90
  59.2 19.3 %collective-permute-done.8.refs_1_ = bf16[336,2688]{1,0:T(8,128)(2,1)S(1)} collective-permute-done((bf16[336,2688]{1,0:T(8,128)(2,1)S(1)}, bf16[336,2688]{1,0:T(8,128)(2,1)S(1)}, u32[]{:S(2)}, u32[]{:S(2)}) %collective-permute-start.8) | collective-permute-done | bytes 1806368 | tf_op jit(solution)/shard_map/ppermute | solution.py:90
  78.6 2.7 %collective-permute-start.12 = (bf16[336,2688]{1,0:T(8,128)(2,1)}, bf16[336,2688]{1,0:T(8,128)(2,1)}, u32[]{:S(2)}, u32[]{:S(2)}) collective-permute-start(bf16[336,2688]{1,0:T(8,128)(2,1)} %collective-permute-done.4.refs_2_), channel_id=1, source_target_pairs={{0,96},{1,25},{2,98},{3,27},{4,100},{5,29},{6,102},{7,31},{8,104},... | collective-permute-start | bytes 5419016 | tf_op jit(solution)/shard_map/ppermute | solution.py:90
  81.3 7.3 %project.1 = (bf16[64,5376]{1,0:T(8,128)(2,1)S(1)}, bf16[32,5376]{1,0:T(8,128)(2,1)S(1)}, bf16[32,5376]{1,0:T(8,128)(2,1)S(1)}, bf16[32,5376]{1,0:T(8,128)(2,1)S...) custom-call(bf16[256,512]{1,0:T(8,128)(2,1)S(1)} %bitcast.129, ...), custom_call_target="tpu_custom_call" | custom-call | bytes 1000 | tf_op jit(solution)/shard_map/project/pallas_call | solution.py:147
  88.7 2.8 %collective-permute-start.14 = (bf16[32,5376]{1,0:T(8,128)(2,1)S(1)}, bf16[32,5376]{1,0:T(8,128)(2,1)S(1)}, u32[]{:S(2)}, u32[]{:S(2)}) collective-permute-start(bf16[32,5376]{1,0:T(8,128)(2,1)S(1)} %get-tuple-element.62), channel_id=1, source_target_pairs={{0,6},{2,0},{4,2},{6,4},{1,7},{3,1},{5,3},{7,5},{8,14},{10,8},{12,... | collective-permute-start | bytes 1032200 | tf_op jit(solution)/shard_map/ppermute | solution.py:34
  91.8 4.5 %collective-permute-done.13 = bf16[32,5376]{1,0:T(8,128)(2,1)S(1)} collective-permute-done((bf16[32,5376]{1,0:T(8,128)(2,1)S(1)}, bf16[32,5376]{1,0:T(8,128)(2,1)S(1)}, u32[]{:S(2)}, u32[]{:S(2)}) %collective-permute-start.13) | collective-permute-done | bytes 344096 | tf_op jit(solution)/shard_map/ppermute | solution.py:34
  97.4 6.8 %collective-permute-done.11.refs_6_ = bf16[336,2688]{1,0:T(8,128)(2,1)S(1)} collective-permute-done((bf16[336,2688]{1,0:T(8,128)(2,1)}, bf16[336,2688]{1,0:T(8,128)(2,1)S(1)}, u32[]{:S(2)}, u32[]{:S(2)}) %collective-permute-start.11) | collective-permute-done | bytes 1806368 | tf_op jit(solution)/shard_map/ppermute | solution.py:90
  104.2 3.6 %collective-permute-start.19 = (bf16[32,5376]{1,0:T(8,128)(2,1)S(1)}, bf16[32,5376]{1,0:T(8,128)(2,1)S(1)}, u32[]{:S(2)}, u32[]{:S(2)}) collective-permute-start(bf16[32,5376]{1,0:T(8,128)(2,1)S(1)} %get-tuple-element.65), channel_id=1, source_target_pairs={{0,6},{2,0},{4,2},{6,4},{1,7},{3,1},{5,3},{7,5},{8,14},{10,8},{12,... | collective-permute-start | bytes 1032200 | tf_op jit(solution)/shard_map/ppermute | solution.py:34
  107.7 1.6 collective-permute-start.20
  109.5 3.4 %collective-permute-done.19.bt_ref = bf16[32,5376]{1,0:T(8,128)(2,1)S(1)} collective-permute-done((bf16[32,5376]{1,0:T(8,128)(2,1)S(1)}, bf16[32,5376]{1,0:T(8,128)(2,1)S(1)}, u32[]{:S(2)}, u32[]{:S(2)}) %collective-permute-start.19) | collective-permute-done | bytes 344096 | tf_op jit(solution)/shard_map/ppermute | solution.py:34
  112.9 7.4 %collective-permute-done.20.bb_ref = bf16[32,5376]{1,0:T(8,128)(2,1)S(1)} collective-permute-done((bf16[32,5376]{1,0:T(8,128)(2,1)S(1)}, bf16[32,5376]{1,0:T(8,128)(2,1)S(1)}, u32[]{:S(2)}, u32[]{:S(2)}) %collective-permute-start.20) | collective-permute-done | bytes 344096 | tf_op jit(solution)/shard_map/ppermute | solution.py:34
  120.3 1.1 norm.1
  121.5 2.1 collective-permute-done.23.refs_5_
  123.6 3.6 %collective-permute-start.22 = (bf16[64,5376]{1,0:T(8,128)(2,1)S(1)}, bf16[64,5376]{1,0:T(8,128)(2,1)S(1)}, u32[]{:S(2)}, u32[]{:S(2)}) collective-permute-start(bf16[64,5376]{1,0:T(8,128)(2,1)S(1)} %get-tuple-element.75.refs_0_), channel_id=1, source_target_pairs={{0,6},{2,0},{4,2},{6,4},{1,7},{3,1},{5,3},{7,5},{8,14},{10,8},{12,... | collective-permute-start | bytes 2064392 | tf_op jit(solution)/shard_map/ppermute | solution.py:34
  127.2 2.9 %collective-permute-start.27 = (bf16[64,5376]{1,0:T(8,128)(2,1)S(1)}, bf16[64,5376]{1,0:T(8,128)(2,1)S(1)}, u32[]{:S(2)}, u32[]{:S(2)}) collective-permute-start(bf16[64,5376]{1,0:T(8,128)(2,1)S(1)} %get-tuple-element.75.refs_0_), channel_id=1, source_target_pairs={{0,1},{1,0},{2,3},{3,2},{4,5},{5,4},{6,7},{7,6},{8,9},{9,8},{10,11... | collective-permute-start | bytes 2064392 | tf_op jit(solution)/shard_map/ppermute | solution.py:34
  130.1 6.0 %collective-permute-done.21.refs_1_ = bf16[64,5376]{1,0:T(8,128)(2,1)S(1)} collective-permute-done((bf16[64,5376]{1,0:T(8,128)(2,1)S(1)}, bf16[64,5376]{1,0:T(8,128)(2,1)S(1)}, u32[]{:S(2)}, u32[]{:S(2)}) %collective-permute-start.21) | collective-permute-done | bytes 688160 | tf_op jit(solution)/shard_map/ppermute | solution.py:34
  136.0 3.3 %collective-permute-done.22.refs_2_ = bf16[64,5376]{1,0:T(8,128)(2,1)S(1)} collective-permute-done((bf16[64,5376]{1,0:T(8,128)(2,1)S(1)}, bf16[64,5376]{1,0:T(8,128)(2,1)S(1)}, u32[]{:S(2)}, u32[]{:S(2)}) %collective-permute-start.22) | collective-permute-done | bytes 688160 | tf_op jit(solution)/shard_map/ppermute | solution.py:34
  139.5 3.5 %collective-permute-start.26 = (bf16[32,5376]{1,0:T(8,128)(2,1)S(1)}, bf16[32,5376]{1,0:T(8,128)(2,1)S(1)}, u32[]{:S(2)}, u32[]{:S(2)}) collective-permute-start(bf16[32,5376]{1,0:T(8,128)(2,1)S(1)} %slice.77), channel_id=1, source_target_pairs={{0,6},{2,0},{4,2},{6,4},{1,7},{3,1},{5,3},{7,5},{8,14},{10,8},{12,... | collective-permute-start | bytes 1032200 | tf_op jit(solution)/shard_map/ppermute | solution.py:34
  143.0 4.5 %collective-permute-done.25.refs_3_ = bf16[32,5376]{1,0:T(8,128)(2,1)S(1)} collective-permute-done((bf16[32,5376]{1,0:T(8,128)(2,1)S(1)}, bf16[32,5376]{1,0:T(8,128)(2,1)S(1)}, u32[]{:S(2)}, u32[]{:S(2)}) %collective-permute-start.25) | collective-permute-done | bytes 344096 | tf_op jit(solution)/shard_map/ppermute | solution.py:34
  147.5 4.4 %collective-permute-start.30 = (bf16[32,5376]{1,0:T(8,128)(2,1)S(1)}, bf16[32,5376]{1,0:T(8,128)(2,1)S(1)}, u32[]{:S(2)}, u32[]{:S(2)}) collective-permute-start(bf16[32,5376]{1,0:T(8,128)(2,1)S(1)} %collective-permute-done.25.refs_3_), channel_id=1, source_target_pairs={{0,1},{1,0},{2,3},{3,2},{4,5},{5,4},{6,7},{7,6},{8,9},{9,8},{10,11... | collective-permute-start | bytes 1032200 | tf_op jit(solution)/shard_map/ppermute | solution.py:34
  153.5 2.1 collective-permute-done.31.refs_9_
  157.6 1.2 copy-done.17
  158.9 2.1 collective-permute-start.41
  161.0 5.1 %order.1.refs_13_.refs_5_ = bf16[512,5632]{1,0:T(8,128)(2,1)S(1)} custom-call(bf16[64,5376]{1,0:T(8,128)(2,1)S(1)} %get-tuple-element.75.refs_0_, bf16[64,5376]{1,0:T(8,128)(2,1)S(1)} %collective-permute-done.21.refs_1_, bf16[64,5376]{1,0:T(8,128)(2,1)S(1)} %collective-permute-done.22.refs_2_, bf16[32,5376]{1,0:T(8,128)(2,1)S(1)} %collective-permute-done.25.refs_3_, ...), custom_call_target="tpu_custom_call" | custom-call | bytes 1000 | tf_op jit(solution)/shard_map/order/pallas_call | solution.py:241
  166.1 2.5 %copy-done = bf16[512,5632]{1,0:T(8,128)(2,1)} copy-done((bf16[512,5632]{1,0:T(8,128)(2,1)}, bf16[512,5632]{1,0:T(8,128)(2,1)S(1)}, u32[]{:S(2)}) %copy-start) | copy-done | bytes 5767192
  169.9 21.9 %near.1.refs_6_ = f32[512,2688]{1,0:T(8,128)} custom-call(bf16[336,2688]{1,0:T(8,128)(2,1)} %copy-done.1, bf16[336,2688]{1,0:T(8,128)(2,1)} %copy-done.13, bf16[336,2688]{1,0:T(8,128)(2,1)} %collective-permute-done.4.refs_2_, bf16[336,2688]{1,0:T(8,128)(2,1)} %copy-done.15, bf16[336,2688]{1,0:T(8,128)(2,1)} %collective-permute-done.16.refs_4_, ...), custom_call_target="tpu_custom_call" | custom-call | bytes 1000 | tf_op jit(solution)/shard_map/near/pallas_call | solution.py:298
  191.8 1.1 fusion.10
  194.1 1.7 collective-permute-start.35
  196.8 2.6 %collective-permute-done.39.refs_1_ = bf16[336,2688]{1,0:T(8,128)(2,1)S(1)} collective-permute-done((bf16[336,2688]{1,0:T(8,128)(2,1)}, bf16[336,2688]{1,0:T(8,128)(2,1)S(1)}, u32[]{:S(2)}, u32[]{:S(2)}) %collective-permute-start.39) | collective-permute-done | bytes 1806368 | tf_op jit(solution)/shard_map/ppermute | solution.py:90
  199.4 1.2 copy-done.11
  200.6 1.2 copy-done.12
  201.8 13.4 %far.1 = bf16[1344,512]{1,0:T(8,128)(2,1)} custom-call(bf16[336,2688]{1,0:T(8,128)(2,1)} %copy-done.10, bf16[336,2688]{1,0:T(8,128)(2,1)} %copy-done.11, bf16[336,2688]{1,0:T(8,128)(2,1)} %copy-done.9, bf16[336,2688]{1,0:T(8,128)(2,1)} %copy-done.12, s32[4]{0:T(128)} %copy-done.7, bf16[512,5632]{1,0:T(8,128)(2,1)} %copy-done, f32[512,2688]{1,0:T(8,128)} %near.1.refs_6_), custom_call_target="tpu_custom_call" | custom-call | flops 3699376128 | bytes 12730368 | tf_op jit(solution)/shard_map/far/pallas_call | solution.py:342
  215.5 1.1 copy.34
  (133 shorter events, 15.8 us)
Async XLA Ops:
  0.6 80.6 %collective-permute-start.10 = (bf16[512,5376]{1,0:T(8,128)(2,1)}, bf16[512,5376]{1,0:T(8,128)(2,1)}, u32[]{:S(2)}, u32[]{:S(2)}) collective-permute-start(bf16[512,5376]{1,0:T(8,128)(2,1)} %w_ref.1), channel_id=1, source_target_pairs={{0,1},{1,0},{2,3},{3,2},{4,5},{5,4},{6,7},{7,6},{8,9},{9,8},{10,11... | collective-permute-start | bytes 16515080 | tf_op jit(solution)/shard_map/ppermute | solution.py:34
  6.1 7.4 %collective-permute-start = (bf16[4,80,672]{2,1,0:T(8,128)(2,1)}, bf16[4,80,672]{2,1,0:T(8,128)(2,1)}, u32[]{:S(2)}, u32[]{:S(2)}) collective-permute-start(bf16[4,80,672]{2,1,0:T(8,128)(2,1)} %fusion.6), channel_id=1, source_target_pairs={{0,1},{1,0},{2,3},{3,2},{4,5},{5,4},{6,7},{7,6},{8,9},{9,8},{10,11... | collective-permute-start | bytes 1290248 | tf_op jit(solution)/shard_map/ppermute | solution.py:34
  7.0 39.2 %copy-start.1 = (bf16[336,2688]{1,0:T(8,128)(2,1)}, bf16[336,2688]{1,0:T(8,128)(2,1)S(1)}, u32[]{:S(2)}) copy-start(bf16[336,2688]{1,0:T(8,128)(2,1)S(1)} %pack.1.refs_0_) | copy-start | bytes 5419012
  7.0 40.0 %collective-permute-start.4 = (bf16[336,2688]{1,0:T(8,128)(2,1)S(1)}, bf16[336,2688]{1,0:T(8,128)(2,1)}, u32[]{:S(2)}, u32[]{:S(2)}) collective-permute-start(bf16[336,2688]{1,0:T(8,128)(2,1)S(1)} %pack.1.refs_0_), channel_id=1, source_target_pairs={{0,24},{1,97},{2,26},{3,99},{4,28},{5,101},{6,30},{7,103},{8,0},{9... | collective-permute-start | bytes 5419016 | tf_op jit(solution)/shard_map/ppermute | solution.py:90
  9.9 13.4 %collective-permute-start.5 = (bf16[512,512]{1,0:T(8,128)(2,1)S(1)}, bf16[512,512]{1,0:T(8,128)(2,1)S(1)}, u32[]{:S(2)}, u32[]{:S(2)}) collective-permute-start(bf16[512,512]{1,0:T(8,128)(2,1)S(1)} %pair.1.kv0_ref), channel_id=1, source_target_pairs={{0,8},{8,16},{16,24},{24,32},{32,40},{40,48},{48,56},{56,64},{64,7... | collective-permute-start | bytes 1572872 | tf_op jit(solution)/shard_map/ppermute | solution.py:39
  13.5 147.5 %copy-start.7 = (s32[4]{0:T(128)}, s32[4]{0:T(128)S(1)}, u32[]{:S(2)}) copy-start(s32[4]{0:T(128)S(1)} %pad_add_fusion.at_ref.refs_10_.refs_12_.refs_4_) | copy-start | bytes 52
  13.6 67.7 %slice-start = ((s8[5505024]{0:T(1024)(128)(4,1)}), s8[4194304]{0:T(1024)(128)(4,1)S(1)}, s32[]{:S(2)}) async-start(s8[5505024]{0:T(1024)(128)(4,1)} %bitcast.124), calls=%async_computation | async-start | bytes 8388608
  16.0 14.1 %collective-permute-start.1 = (bf16[2,80,672]{2,1,0:T(8,128)(2,1)S(1)}, bf16[2,80,672]{2,1,0:T(8,128)(2,1)S(1)}, u32[]{:S(2)}, u32[]{:S(2)}) collective-permute-start(bf16[2,80,672]{2,1,0:T(8,128)(2,1)S(1)} %get-tuple-element.108), channel_id=1, source_target_pairs={{0,6},{2,0},{4,2},{6,4},{1,7},{3,1},{5,3},{7,5},{8,14},{10,8},{12,... | collective-permute-start | bytes 645128 | tf_op jit(solution)/shard_map/ppermute | solution.py:34
  19.9 13.4 %collective-permute-start.2 = (bf16[2,80,672]{2,1,0:T(8,128)(2,1)S(1)}, bf16[2,80,672]{2,1,0:T(8,128)(2,1)S(1)}, u32[]{:S(2)}, u32[]{:S(2)}) collective-permute-start(bf16[2,80,672]{2,1,0:T(8,128)(2,1)S(1)} %get-tuple-element.107), channel_id=1, source_target_pairs={{0,4},{2,6},{4,0},{6,2},{1,5},{3,7},{5,1},{7,3},{8,12},{10,14},{12... | collective-permute-start | bytes 645128 | tf_op jit(solution)/shard_map/ppermute | solution.py:34
  23.4 10.7 %collective-permute-start.3 = (bf16[2,80,672]{2,1,0:T(8,128)(2,1)S(1)}, bf16[2,80,672]{2,1,0:T(8,128)(2,1)S(1)}, u32[]{:S(2)}, u32[]{:S(2)}) collective-permute-start(bf16[2,80,672]{2,1,0:T(8,128)(2,1)S(1)} %get-tuple-element.106), channel_id=1, source_target_pairs={{0,2},{2,4},{4,6},{6,0},{1,3},{3,5},{5,7},{7,1},{8,10},{10,12},{12... | collective-permute-start | bytes 645128 | tf_op jit(solution)/shard_map/ppermute | solution.py:34
  30.1 14.7 %collective-permute-start.6 = (bf16[512,512]{1,0:T(8,128)(2,1)S(1)}, bf16[512,512]{1,0:T(8,128)(2,1)S(1)}, u32[]{:S(2)}, u32[]{:S(2)}) collective-permute-start(bf16[512,512]{1,0:T(8,128)(2,1)S(1)} %collective-permute-done.5.kv1_ref), channel_id=1, source_target_pairs={{0,8},{8,16},{16,24},{24,32},{32,40},{40,48},{48,56},{56,64},{64,7... | collective-permute-start | bytes 1572872 | tf_op jit(solution)/shard_map/ppermute | solution.py:39
  33.3 45.3 %collective-permute-start.8 = (bf16[336,2688]{1,0:T(8,128)(2,1)S(1)}, bf16[336,2688]{1,0:T(8,128)(2,1)S(1)}, u32[]{:S(2)}, u32[]{:S(2)}) collective-permute-start(bf16[336,2688]{1,0:T(8,128)(2,1)S(1)} %pack.1.refs_0_), channel_id=1, source_target_pairs={{0,8},{1,33},{2,10},{3,35},{4,12},{5,37},{6,14},{7,39},{8,16},{9,4... | collective-permute-start | bytes 5419016 | tf_op jit(solution)/shard_map/ppermute | solution.py:90
  34.1 47.2 %slice-start.1 = ((s8[5505024]{0:T(1024)(128)(4,1)}), s8[1310720]{0:T(1024)(128)(4,1)S(1)}, s32[]{:S(2)}) async-start(s8[5505024]{0:T(1024)(128)(4,1)} %bitcast.124), calls=%async_computation.1 | async-start | bytes 2621440
  44.8 33.8 %collective-permute-start.9 = (bf16[336,2688]{1,0:T(8,128)(2,1)S(1)}, bf16[336,2688]{1,0:T(8,128)(2,1)S(1)}, u32[]{:S(2)}, u32[]{:S(2)}) collective-permute-start(bf16[336,2688]{1,0:T(8,128)(2,1)S(1)} %pack.1.refs_0_), channel_id=1, source_target_pairs={{0,96},{1,25},{2,98},{3,27},{4,100},{5,29},{6,102},{7,31},{8,104},... | collective-permute-start | bytes 5419016 | tf_op jit(solution)/shard_map/ppermute | solution.py:90
  46.1 42.6 %collective-permute-start.16 = (bf16[336,2688]{1,0:T(8,128)(2,1)S(1)}, bf16[336,2688]{1,0:T(8,128)(2,1)}, u32[]{:S(2)}, u32[]{:S(2)}) collective-permute-start(bf16[336,2688]{1,0:T(8,128)(2,1)S(1)} %pack.1.refs_0_), channel_id=1, source_target_pairs={{0,32},{1,9},{2,34},{3,11},{4,36},{5,13},{6,38},{7,15},{8,40},{9,1... | collective-permute-start | bytes 5419016 | tf_op jit(solution)/shard_map/ppermute | solution.py:90
  52.6 3.7 %collective-permute-start.7 = (bf16[256,512]{1,0:T(8,128)(2,1)S(1)}, bf16[256,512]{1,0:T(8,128)(2,1)S(1)}, u32[]{:S(2)}, u32[]{:S(2)}) collective-permute-start(bf16[256,512]{1,0:T(8,128)(2,1)S(1)} %bitcast.134), channel_id=1, source_target_pairs={{0,1},{1,0},{2,3},{3,2},{4,5},{5,4},{6,7},{7,6},{8,9},{9,8},{10,11... | collective-permute-start | bytes 786440 | tf_op jit(solution)/shard_map/ppermute | solution.py:34
  56.3 35.5 %collective-permute-start.15 = (bf16[336,2688]{1,0:T(8,128)(2,1)}, bf16[336,2688]{1,0:T(8,128)(2,1)S(1)}, u32[]{:S(2)}, u32[]{:S(2)}) collective-permute-start(bf16[336,2688]{1,0:T(8,128)(2,1)} %collective-permute-done.4.refs_2_), channel_id=1, source_target_pairs={{0,24},{1,97},{2,26},{3,99},{4,28},{5,101},{6,30},{7,103},{8,0},{9... | collective-permute-start | bytes 5419016 | tf_op jit(solution)/shard_map/ppermute | solution.py:90
  78.6 17.7 %copy-start.13 = (bf16[336,2688]{1,0:T(8,128)(2,1)}, bf16[336,2688]{1,0:T(8,128)(2,1)S(1)}, u32[]{:S(2)}) copy-start(bf16[336,2688]{1,0:T(8,128)(2,1)S(1)} %collective-permute-done.8.refs_1_) | copy-start | bytes 5419012
  78.6 25.6 %collective-permute-start.11 = (bf16[336,2688]{1,0:T(8,128)(2,1)}, bf16[336,2688]{1,0:T(8,128)(2,1)S(1)}, u32[]{:S(2)}, u32[]{:S(2)}) collective-permute-start(bf16[336,2688]{1,0:T(8,128)(2,1)} %collective-permute-done.4.refs_2_), channel_id=1, source_target_pairs={{0,32},{1,9},{2,34},{3,11},{4,36},{5,13},{6,38},{7,15},{8,40},{9,1... | collective-permute-start | bytes 5419016 | tf_op jit(solution)/shard_map/ppermute | solution.py:90
  78.6 29.1 %collective-permute-start.12 = (bf16[336,2688]{1,0:T(8,128)(2,1)}, bf16[336,2688]{1,0:T(8,128)(2,1)}, u32[]{:S(2)}, u32[]{:S(2)}) collective-permute-start(bf16[336,2688]{1,0:T(8,128)(2,1)} %collective-permute-done.4.refs_2_), channel_id=1, source_target_pairs={{0,96},{1,25},{2,98},{3,27},{4,100},{5,29},{6,102},{7,31},{8,104},... | collective-permute-start | bytes 5419016 | tf_op jit(solution)/shard_map/ppermute | solution.py:90
  88.6 7.7 %collective-permute-start.13 = (bf16[32,5376]{1,0:T(8,128)(2,1)S(1)}, bf16[32,5376]{1,0:T(8,128)(2,1)S(1)}, u32[]{:S(2)}, u32[]{:S(2)}) collective-permute-start(bf16[32,5376]{1,0:T(8,128)(2,1)S(1)} %get-tuple-element.61), channel_id=1, source_target_pairs={{0,2},{2,4},{4,6},{6,0},{1,3},{3,5},{5,7},{7,1},{8,10},{10,12},{12... | collective-permute-start | bytes 1032200 | tf_op jit(solution)/shard_map/ppermute | solution.py:34
  88.7 8.2 %collective-permute-start.14 = (bf16[32,5376]{1,0:T(8,128)(2,1)S(1)}, bf16[32,5376]{1,0:T(8,128)(2,1)S(1)}, u32[]{:S(2)}, u32[]{:S(2)}) collective-permute-start(bf16[32,5376]{1,0:T(8,128)(2,1)S(1)} %get-tuple-element.62), channel_id=1, source_target_pairs={{0,6},{2,0},{4,2},{6,4},{1,7},{3,1},{5,3},{7,5},{8,14},{10,8},{12,... | collective-permute-start | bytes 1032200 | tf_op jit(solution)/shard_map/ppermute | solution.py:34
  91.8 29.6 %copy-start.15 = (bf16[336,2688]{1,0:T(8,128)(2,1)}, bf16[336,2688]{1,0:T(8,128)(2,1)S(1)}, u32[]{:S(2)}) copy-start(bf16[336,2688]{1,0:T(8,128)(2,1)S(1)} %collective-permute-done.15.refs_3_) | copy-start | bytes 5419012
  91.8 31.9 %collective-permute-start.23 = (bf16[336,2688]{1,0:T(8,128)(2,1)S(1)}, bf16[336,2688]{1,0:T(8,128)(2,1)}, u32[]{:S(2)}, u32[]{:S(2)}) collective-permute-start(bf16[336,2688]{1,0:T(8,128)(2,1)S(1)} %collective-permute-done.8.refs_1_), channel_id=1, source_target_pairs={{0,32},{1,9},{2,34},{3,11},{4,36},{5,13},{6,38},{7,15},{8,40},{9,1... | collective-permute-start | bytes 5419016 | tf_op jit(solution)/shard_map/ppermute | solution.py:90
  96.3 30.9 %collective-permute-start.24 = (bf16[336,2688]{1,0:T(8,128)(2,1)S(1)}, bf16[336,2688]{1,0:T(8,128)(2,1)}, u32[]{:S(2)}, u32[]{:S(2)}) collective-permute-start(bf16[336,2688]{1,0:T(8,128)(2,1)S(1)} %collective-permute-done.8.refs_1_), channel_id=1, source_target_pairs={{0,96},{1,25},{2,98},{3,27},{4,100},{5,29},{6,102},{7,31},{8,104},... | collective-permute-start | bytes 5419016 | tf_op jit(solution)/shard_map/ppermute | solution.py:90
  96.9 12.5 %collective-permute-start.18 = (bf16[32,5376]{1,0:T(8,128)(2,1)S(1)}, bf16[32,5376]{1,0:T(8,128)(2,1)S(1)}, u32[]{:S(2)}, u32[]{:S(2)}) collective-permute-start(bf16[32,5376]{1,0:T(8,128)(2,1)S(1)} %get-tuple-element.64), channel_id=1, source_target_pairs={{0,2},{2,4},{4,6},{6,0},{1,3},{3,5},{5,7},{7,1},{8,10},{10,12},{12... | collective-permute-start | bytes 1032200 | tf_op jit(solution)/shard_map/ppermute | solution.py:34
  104.2 8.8 %collective-permute-start.19 = (bf16[32,5376]{1,0:T(8,128)(2,1)S(1)}, bf16[32,5376]{1,0:T(8,128)(2,1)S(1)}, u32[]{:S(2)}, u32[]{:S(2)}) collective-permute-start(bf16[32,5376]{1,0:T(8,128)(2,1)S(1)} %get-tuple-element.65), channel_id=1, source_target_pairs={{0,6},{2,0},{4,2},{6,4},{1,7},{3,1},{5,3},{7,5},{8,14},{10,8},{12,... | collective-permute-start | bytes 1032200 | tf_op jit(solution)/shard_map/ppermute | solution.py:34
  107.7 12.6 %collective-permute-start.20 = (bf16[32,5376]{1,0:T(8,128)(2,1)S(1)}, bf16[32,5376]{1,0:T(8,128)(2,1)S(1)}, u32[]{:S(2)}, u32[]{:S(2)}) collective-permute-start(bf16[32,5376]{1,0:T(8,128)(2,1)S(1)} %add_convert_fusion), channel_id=1, source_target_pairs={{0,6},{2,0},{4,2},{6,4},{1,7},{3,1},{5,3},{7,5},{8,14},{10,8},{12,... | collective-permute-start | bytes 1032200 | tf_op jit(solution)/shard_map/ppermute | solution.py:34
  109.4 10.9 %collective-permute-start.17 = (bf16[32,5376]{1,0:T(8,128)(2,1)S(1)}, bf16[32,5376]{1,0:T(8,128)(2,1)S(1)}, u32[]{:S(2)}, u32[]{:S(2)}) collective-permute-start(bf16[32,5376]{1,0:T(8,128)(2,1)S(1)} %add_convert_fusion.1), channel_id=1, source_target_pairs={{0,2},{2,4},{4,6},{6,0},{1,3},{3,5},{5,7},{7,1},{8,10},{10,12},{12... | collective-permute-start | bytes 1032200 | tf_op jit(solution)/shard_map/ppermute | solution.py:34
  112.9 44.7 %collective-permute-start.32 = (bf16[336,2688]{1,0:T(8,128)(2,1)S(1)}, bf16[336,2688]{1,0:T(8,128)(2,1)S(1)}, u32[]{:S(2)}, u32[]{:S(2)}) collective-permute-start(bf16[336,2688]{1,0:T(8,128)(2,1)S(1)} %collective-permute-done.15.refs_3_), channel_id=1, source_target_pairs={{0,32},{1,9},{2,34},{3,11},{4,36},{5,13},{6,38},{7,15},{8,40},{9,1... | collective-permute-start | bytes 5419016 | tf_op jit(solution)/shard_map/ppermute | solution.py:90
  120.3 37.3 %collective-permute-start.33 = (bf16[336,2688]{1,0:T(8,128)(2,1)S(1)}, bf16[336,2688]{1,0:T(8,128)(2,1)}, u32[]{:S(2)}, u32[]{:S(2)}) collective-permute-start(bf16[336,2688]{1,0:T(8,128)(2,1)S(1)} %collective-permute-done.15.refs_3_), channel_id=1, source_target_pairs={{0,96},{1,25},{2,98},{3,27},{4,100},{5,29},{6,102},{7,31},{8,104},... | collective-permute-start | bytes 5419016 | tf_op jit(solution)/shard_map/ppermute | solution.py:90
  121.4 14.6 %collective-permute-start.21 = (bf16[64,5376]{1,0:T(8,128)(2,1)S(1)}, bf16[64,5376]{1,0:T(8,128)(2,1)S(1)}, u32[]{:S(2)}, u32[]{:S(2)}) collective-permute-start(bf16[64,5376]{1,0:T(8,128)(2,1)S(1)} %get-tuple-element.75.refs_0_), channel_id=1, source_target_pairs={{0,2},{2,4},{4,6},{6,0},{1,3},{3,5},{5,7},{7,1},{8,10},{10,12},{12... | collective-permute-start | bytes 2064392 | tf_op jit(solution)/shard_map/ppermute | solution.py:34
  123.6 15.7 %collective-permute-start.22 = (bf16[64,5376]{1,0:T(8,128)(2,1)S(1)}, bf16[64,5376]{1,0:T(8,128)(2,1)S(1)}, u32[]{:S(2)}, u32[]{:S(2)}) collective-permute-start(bf16[64,5376]{1,0:T(8,128)(2,1)S(1)} %get-tuple-element.75.refs_0_), channel_id=1, source_target_pairs={{0,6},{2,0},{4,2},{6,4},{1,7},{3,1},{5,3},{7,5},{8,14},{10,8},{12,... | collective-permute-start | bytes 2064392 | tf_op jit(solution)/shard_map/ppermute | solution.py:34
  127.2 24.7 %collective-permute-start.27 = (bf16[64,5376]{1,0:T(8,128)(2,1)S(1)}, bf16[64,5376]{1,0:T(8,128)(2,1)S(1)}, u32[]{:S(2)}, u32[]{:S(2)}) collective-permute-start(bf16[64,5376]{1,0:T(8,128)(2,1)S(1)} %get-tuple-element.75.refs_0_), channel_id=1, source_target_pairs={{0,1},{1,0},{2,3},{3,2},{4,5},{5,4},{6,7},{7,6},{8,9},{9,8},{10,11... | collective-permute-start | bytes 2064392 | tf_op jit(solution)/shard_map/ppermute | solution.py:34
  139.4 8.1 %collective-permute-start.25 = (bf16[32,5376]{1,0:T(8,128)(2,1)S(1)}, bf16[32,5376]{1,0:T(8,128)(2,1)S(1)}, u32[]{:S(2)}, u32[]{:S(2)}) collective-permute-start(bf16[32,5376]{1,0:T(8,128)(2,1)S(1)} %slice.76), channel_id=1, source_target_pairs={{0,2},{2,4},{4,6},{6,0},{1,3},{3,5},{5,7},{7,1},{8,10},{10,12},{12... | collective-permute-start | bytes 1032200 | tf_op jit(solution)/shard_map/ppermute | solution.py:34
  139.5 12.4 %collective-permute-start.26 = (bf16[32,5376]{1,0:T(8,128)(2,1)S(1)}, bf16[32,5376]{1,0:T(8,128)(2,1)S(1)}, u32[]{:S(2)}, u32[]{:S(2)}) collective-permute-start(bf16[32,5376]{1,0:T(8,128)(2,1)S(1)} %slice.77), channel_id=1, source_target_pairs={{0,6},{2,0},{4,2},{6,4},{1,7},{3,1},{5,3},{7,5},{8,14},{10,8},{12,... | collective-permute-start | bytes 1032200 | tf_op jit(solution)/shard_map/ppermute | solution.py:34
  147.5 5.7 %collective-permute-start.30 = (bf16[32,5376]{1,0:T(8,128)(2,1)S(1)}, bf16[32,5376]{1,0:T(8,128)(2,1)S(1)}, u32[]{:S(2)}, u32[]{:S(2)}) collective-permute-start(bf16[32,5376]{1,0:T(8,128)(2,1)S(1)} %collective-permute-done.25.refs_3_), channel_id=1, source_target_pairs={{0,1},{1,0},{2,3},{3,2},{4,5},{5,4},{6,7},{7,6},{8,9},{9,8},{10,11... | collective-permute-start | bytes 1032200 | tf_op jit(solution)/shard_map/ppermute | solution.py:34
  151.9 4.7 %collective-permute-start.28 = (bf16[64,5376]{1,0:T(8,128)(2,1)S(1)}, bf16[64,5376]{1,0:T(8,128)(2,1)S(1)}, u32[]{:S(2)}, u32[]{:S(2)}) collective-permute-start(bf16[64,5376]{1,0:T(8,128)(2,1)S(1)} %collective-permute-done.21.refs_1_), channel_id=1, source_target_pairs={{0,1},{1,0},{2,3},{3,2},{4,5},{5,4},{6,7},{7,6},{8,9},{9,8},{10,11... | collective-permute-start | bytes 2064392 | tf_op jit(solution)/shard_map/ppermute | solution.py:34
  151.9 5.2 %collective-permute-start.29 = (bf16[64,5376]{1,0:T(8,128)(2,1)S(1)}, bf16[64,5376]{1,0:T(8,128)(2,1)S(1)}, u32[]{:S(2)}, u32[]{:S(2)}) collective-permute-start(bf16[64,5376]{1,0:T(8,128)(2,1)S(1)} %collective-permute-done.22.refs_2_), channel_id=1, source_target_pairs={{0,1},{1,0},{2,3},{3,2},{4,5},{5,4},{6,7},{7,6},{8,9},{9,8},{10,11... | collective-permute-start | bytes 2064392 | tf_op jit(solution)/shard_map/ppermute | solution.py:34
  153.1 2.5 %collective-permute-start.31 = (bf16[32,5376]{1,0:T(8,128)(2,1)S(1)}, bf16[32,5376]{1,0:T(8,128)(2,1)S(1)}, u32[]{:S(2)}, u32[]{:S(2)}) collective-permute-start(bf16[32,5376]{1,0:T(8,128)(2,1)S(1)} %collective-permute-done.26.refs_4_), channel_id=1, source_target_pairs={{0,1},{1,0},{2,3},{3,2},{4,5},{5,4},{6,7},{7,6},{8,9},{9,8},{10,11... | collective-permute-start | bytes 1032200 | tf_op jit(solution)/shard_map/ppermute | solution.py:34
  155.6 40.2 %collective-permute-start.40 = (bf16[336,2688]{1,0:T(8,128)(2,1)}, bf16[336,2688]{1,0:T(8,128)(2,1)S(1)}, u32[]{:S(2)}, u32[]{:S(2)}) collective-permute-start(bf16[336,2688]{1,0:T(8,128)(2,1)} %collective-permute-done.12.refs_10_), channel_id=1, source_target_pairs={{0,96},{1,25},{2,98},{3,27},{4,100},{5,29},{6,102},{7,31},{8,104},... | collective-permute-start | bytes 5419016 | tf_op jit(solution)/shard_map/ppermute | solution.py:90
  156.5 39.5 %collective-permute-start.38 = (bf16[336,2688]{1,0:T(8,128)(2,1)}, bf16[336,2688]{1,0:T(8,128)(2,1)S(1)}, u32[]{:S(2)}, u32[]{:S(2)}) collective-permute-start(bf16[336,2688]{1,0:T(8,128)(2,1)} %collective-permute-done.16.refs_4_), channel_id=1, source_target_pairs={{0,32},{1,9},{2,34},{3,11},{4,36},{5,13},{6,38},{7,15},{8,40},{9,1... | collective-permute-start | bytes 5419016 | tf_op jit(solution)/shard_map/ppermute | solution.py:90
  157.1 42.3 %collective-permute-start.39 = (bf16[336,2688]{1,0:T(8,128)(2,1)}, bf16[336,2688]{1,0:T(8,128)(2,1)S(1)}, u32[]{:S(2)}, u32[]{:S(2)}) collective-permute-start(bf16[336,2688]{1,0:T(8,128)(2,1)} %collective-permute-done.23.refs_5_), channel_id=1, source_target_pairs={{0,32},{1,9},{2,34},{3,11},{4,36},{5,13},{6,38},{7,15},{8,40},{9,1... | collective-permute-start | bytes 5419016 | tf_op jit(solution)/shard_map/ppermute | solution.py:90
  158.9 40.5 %collective-permute-start.41 = (bf16[336,2688]{1,0:T(8,128)(2,1)}, bf16[336,2688]{1,0:T(8,128)(2,1)S(1)}, u32[]{:S(2)}, u32[]{:S(2)}) collective-permute-start(bf16[336,2688]{1,0:T(8,128)(2,1)} %collective-permute-done.33.refs_11_), channel_id=1, source_target_pairs={{0,96},{1,25},{2,98},{3,27},{4,100},{5,29},{6,102},{7,31},{8,104},... | collective-permute-start | bytes 5419016 | tf_op jit(solution)/shard_map/ppermute | solution.py:90
  169.3 22.5 %collective-permute-start.34 = (bf16[4,64,672]{2,1,0:T(8,128)(2,1)}, bf16[4,64,672]{2,1,0:T(8,128)(2,1)}, u32[]{:S(2)}, u32[]{:S(2)}) collective-permute-start(bf16[4,64,672]{2,1,0:T(8,128)(2,1)} %select_bitcast_fusion.2), channel_id=1, source_target_pairs={{0,1},{1,0},{2,3},{3,2},{4,5},{5,4},{6,7},{7,6},{8,9},{9,8},{10,11... | collective-permute-start | bytes 1032200 | tf_op jit(solution)/shard_map/ppermute | solution.py:34
  194.1 21.2 %collective-permute-start.35 = (bf16[2,64,672]{2,1,0:T(8,128)(2,1)}, bf16[2,64,672]{2,1,0:T(8,128)(2,1)S(1)}, u32[]{:S(2)}, u32[]{:S(2)}) collective-permute-start(bf16[2,64,672]{2,1,0:T(8,128)(2,1)} %get-tuple-element.111), channel_id=1, source_target_pairs={{0,6},{2,0},{4,2},{6,4},{1,7},{3,1},{5,3},{7,5},{8,14},{10,8},{12,... | collective-permute-start | bytes 516104 | tf_op jit(solution)/shard_map/ppermute | solution.py:34
  195.8 19.4 %collective-permute-start.36 = (bf16[2,64,672]{2,1,0:T(8,128)(2,1)}, bf16[2,64,672]{2,1,0:T(8,128)(2,1)S(1)}, u32[]{:S(2)}, u32[]{:S(2)}) collective-permute-start(bf16[2,64,672]{2,1,0:T(8,128)(2,1)} %get-tuple-element.110), channel_id=1, source_target_pairs={{0,4},{2,6},{4,0},{6,2},{1,5},{3,7},{5,1},{7,3},{8,12},{10,14},{12... | collective-permute-start | bytes 516104 | tf_op jit(solution)/shard_map/ppermute | solution.py:34
  196.0 19.3 %collective-permute-start.37 = (bf16[2,64,672]{2,1,0:T(8,128)(2,1)S(1)}, bf16[2,64,672]{2,1,0:T(8,128)(2,1)S(1)}, u32[]{:S(2)}, u32[]{:S(2)}) collective-permute-start(bf16[2,64,672]{2,1,0:T(8,128)(2,1)S(1)} %get-tuple-element.109), channel_id=1, source_target_pairs={{0,2},{2,4},{4,6},{6,0},{1,3},{3,5},{5,7},{7,1},{8,10},{10,12},{12... | collective-permute-start | bytes 516104 | tf_op jit(solution)/shard_map/ppermute | solution.py:34
  (15 other events, 74.8 us)

commit v11 on v10

--- a/solution.py
+++ b/solution.py
@@ -392,7 +392,7 @@
     m = ring(w_late, 1, 0)
     b = ring(p, -1, 0)
     w_late, kv2 = lax.optimization_barrier((w_late, kv2))
-    prev, following = [ring(w_late, 1, 1)], [ring(w_late, -1, 1)]
+    prev, following = [ring(w_late, 1, 1)], [ring(w, -1, 1)]
 
     gains = jnp.stack([post_gain, pre_gain])
     high = gains.astype(BF)

time: 218 us -> 226 us (1.037)
  starting transfers between devices: 58.6 us -> 86.6 us
  waiting for transfers between devices: 84.1 us -> 60.8 us
    ppermute x25, starting transfers between devices: 36.8 us -> 57.2 us  [shift(): return lax.ppermute(value, axis, [(i, (i + by) % n) for i in range(n)])]
    ppermute x25, waiting for transfers between devices: 38.9 us -> 27.4 us  [shift(): return lax.ppermute(value, axis, [(i, (i + by) % n) for i in range(n)])]
    ppermute x2, waiting for transfers between devices: 13.9 us -> 4.76 us  [behind(): return lax.ppermute(value, ('y', 'x'), [(i, i + 1) for i in range(n - 1)])]
    ppermute x15, starting transfers between devices: 15.5 us -> 23.8 us  [ring(): return lax.ppermute(value, ('y', 'x', 'z', 'c'), pairs)]
    ppermute x15, waiting for transfers between devices: 31.2 us -> 28.7 us  [ring(): return lax.ppermute(value, ('y', 'x', 'z', 'c'), pairs)]
    unnamed x58 -> x56, local copies, waits for them, and re-layouts: 9.15 us -> 10 us
  transfers between devices with their start and end apart: 42 -> 42, of which waited for: 18 -> 16; matrix products, arithmetic and copies ran while one was open for 5% -> 5% of each run, Pallas kernels for 25% -> 25%
where the time goes in v11:
time: 226 us; the launch traced here: 223 us
  starting transfers between devices  86.6 us (38%)
  waiting for transfers between devices  60.8 us (27%)
  Pallas kernels  55.3 us (24%)
  local copies, waits for them, and re-layouts  13 us (6%)
  other arithmetic  5.84 us (3%)
    ppermute x25, starting transfers between devices, shift(): return lax.ppermute(value, axis, [(i, (i + by) % n) for i in range(n)])  57.2 us
    ppermute x15, waiting for transfers between devices, ring(): return lax.ppermute(value, ('y', 'x', 'z', 'c'), pairs)  28.7 us
    ppermute x25, waiting for transfers between devices, shift(): return lax.ppermute(value, axis, [(i, (i + by) % n) for i in range(n)])  27.4 us
    ppermute x15, starting transfers between devices, ring(): return lax.ppermute(value, ('y', 'x', 'z', 'c'), pairs)  23.8 us
    pallas_call x1, Pallas kernels, near(): pl.pallas_call(body, out_shape=jax.ShapeDtypeStruct((TOK, 2688), F32), gr...  21.9 us
    pallas_call x1, Pallas kernels, far(): pl.pallas_call(body, out_shape=jax.ShapeDtypeStruct((1344, TOK), BF), gri...  13.4 us
    unnamed x56, local copies, waits for them, and re-layouts  10 us
    pallas_call x1, Pallas kernels, project(): pl.pallas_call(project_kernel, out_shape=[jax.ShapeDtypeStruct((64, D), B...  7.83 us
  transfers between devices with their start and end apart: 42, of which 16 were waited for; matrix products, arithmetic and copies ran while one was open for 5% of the time, Pallas kernels for 25%

profile of v11, /device:TPU:1, one launch (start us, length us, event | category | flops | bytes accessed | tf_op | source)
XLA Modules:
  0.0 222.8 jit_solution(14566916781794305818)
XLA Ops:
  0.6 1.5 collective-permute-start.10
  3.5 1.4 copy.22
  7.0 2.9 %collective-permute-start.4 = (bf16[336,2688]{1,0:T(8,128)(2,1)S(1)}, bf16[336,2688]{1,0:T(8,128)(2,1)}, u32[]{:S(2)}, u32[]{:S(2)}) collective-permute-start(bf16[336,2688]{1,0:T(8,128)(2,1)S(1)} %pack.1.refs_0_), channel_id=1, source_target_pairs={{0,24},{1,97},{2,26},{3,99},{4,28},{5,101},{6,30},{7,103},{8,0},{9... | collective-permute-start | bytes 5419016 | tf_op jit(solution)/shard_map/ppermute | solution.py:90
  9.8 2.5 %collective-permute-start.9 = (bf16[336,2688]{1,0:T(8,128)(2,1)S(1)}, bf16[336,2688]{1,0:T(8,128)(2,1)}, u32[]{:S(2)}, u32[]{:S(2)}) collective-permute-start(bf16[336,2688]{1,0:T(8,128)(2,1)S(1)} %pack.1.refs_0_), channel_id=1, source_target_pairs={{0,96},{1,25},{2,98},{3,27},{4,100},{5,29},{6,102},{7,31},{8,104},... | collective-permute-start | bytes 5419016 | tf_op jit(solution)/shard_map/ppermute | solution.py:90
  12.4 1.3 collective-permute-start.5
  14.2 1.8 select_bitcast_fusion
  16.7 3.8 %collective-permute-start.1 = (bf16[2,80,672]{2,1,0:T(8,128)(2,1)S(1)}, bf16[2,80,672]{2,1,0:T(8,128)(2,1)S(1)}, u32[]{:S(2)}, u32[]{:S(2)}) collective-permute-start(bf16[2,80,672]{2,1,0:T(8,128)(2,1)S(1)} %get-tuple-element.108), channel_id=1, source_target_pairs={{0,6},{2,0},{4,2},{6,4},{1,7},{3,1},{5,3},{7,5},{8,14},{10,8},{12,... | collective-permute-start | bytes 645128 | tf_op jit(solution)/shard_map/ppermute | solution.py:34
  20.5 4.0 %collective-permute-done.5.kv1_ref = bf16[512,512]{1,0:T(8,128)(2,1)S(1)} collective-permute-done((bf16[512,512]{1,0:T(8,128)(2,1)S(1)}, bf16[512,512]{1,0:T(8,128)(2,1)S(1)}, u32[]{:S(2)}, u32[]{:S(2)}) %collective-permute-start.5) | collective-permute-done | bytes 524320 | tf_op jit(solution)/shard_map/ppermute | solution.py:39
  24.5 4.2 %collective-permute-start.6 = (bf16[512,512]{1,0:T(8,128)(2,1)S(1)}, bf16[512,512]{1,0:T(8,128)(2,1)S(1)}, u32[]{:S(2)}, u32[]{:S(2)}) collective-permute-start(bf16[512,512]{1,0:T(8,128)(2,1)S(1)} %collective-permute-done.5.kv1_ref), channel_id=1, source_target_pairs={{0,8},{8,16},{16,24},{24,32},{32,40},{40,48},{48,56},{56,64},{64,7... | collective-permute-start | bytes 1572872 | tf_op jit(solution)/shard_map/ppermute | solution.py:39
  28.8 3.7 %collective-permute-start.2 = (bf16[2,80,672]{2,1,0:T(8,128)(2,1)S(1)}, bf16[2,80,672]{2,1,0:T(8,128)(2,1)S(1)}, u32[]{:S(2)}, u32[]{:S(2)}) collective-permute-start(bf16[2,80,672]{2,1,0:T(8,128)(2,1)S(1)} %get-tuple-element.107), channel_id=1, source_target_pairs={{0,4},{2,6},{4,0},{6,2},{1,5},{3,7},{5,1},{7,3},{8,12},{10,14},{12... | collective-permute-start | bytes 645128 | tf_op jit(solution)/shard_map/ppermute | solution.py:34
  32.5 4.8 %collective-permute-done.2 = bf16[2,80,672]{2,1,0:T(8,128)(2,1)S(1)} collective-permute-done((bf16[2,80,672]{2,1,0:T(8,128)(2,1)S(1)}, bf16[2,80,672]{2,1,0:T(8,128)(2,1)S(1)}, u32[]{:S(2)}, u32[]{:S(2)}) %collective-permute-start.2) | collective-permute-done | bytes 215072 | tf_op jit(solution)/shard_map/ppermute | solution.py:34
  38.7 4.9 %collective-permute-start.8 = (bf16[336,2688]{1,0:T(8,128)(2,1)S(1)}, bf16[336,2688]{1,0:T(8,128)(2,1)S(1)}, u32[]{:S(2)}, u32[]{:S(2)}) collective-permute-start(bf16[336,2688]{1,0:T(8,128)(2,1)S(1)} %pack.1.refs_0_), channel_id=1, source_target_pairs={{0,8},{1,33},{2,10},{3,35},{4,12},{5,37},{6,14},{7,39},{8,16},{9,4... | collective-permute-start | bytes 5419016 | tf_op jit(solution)/shard_map/ppermute | solution.py:90
  43.9 1.7 collective-permute-done.4.refs_2_
  45.6 3.5 %collective-permute-start.15 = (bf16[336,2688]{1,0:T(8,128)(2,1)}, bf16[336,2688]{1,0:T(8,128)(2,1)S(1)}, u32[]{:S(2)}, u32[]{:S(2)}) collective-permute-start(bf16[336,2688]{1,0:T(8,128)(2,1)} %collective-permute-done.4.refs_2_), channel_id=1, source_target_pairs={{0,24},{1,97},{2,26},{3,99},{4,28},{5,101},{6,30},{7,103},{8,0},{9... | collective-permute-start | bytes 5419016 | tf_op jit(solution)/shard_map/ppermute | solution.py:90
  50.2 5.5 %attend.1 = bf16[2,4,64,512]{3,2,1,0:T(8,128)(2,1)S(1)} custom-call(s32[4]{0:T(128)S(1)} %pad_add_fusion.at_ref.refs_10_.refs_12_.refs_4_, bf16[512,512]{1,0:T(8,128)(2,1)S(1)} %copy-done.4, bf16[512,512]{1,0:T(8,128)(2,1)S(1)} %collective-permute-done.6.kv2_ref, bf16[512,512]{1,0:T(8,128)(2,1)S(1)} %collective-permute-done.5.kv1_ref, ...), custom_call_target="tpu_custom_call" | custom-call | bytes 1000 | tf_op jit(solution)/shard_map/attend/pallas_call | solution.py:123
  55.7 3.3 %collective-permute-start.7 = (bf16[256,512]{1,0:T(8,128)(2,1)S(1)}, bf16[256,512]{1,0:T(8,128)(2,1)S(1)}, u32[]{:S(2)}, u32[]{:S(2)}) collective-permute-start(bf16[256,512]{1,0:T(8,128)(2,1)S(1)} %bitcast.134), channel_id=1, source_target_pairs={{0,1},{1,0},{2,3},{3,2},{4,5},{5,4},{6,7},{7,6},{8,9},{9,8},{10,11... | collective-permute-start | bytes 786440 | tf_op jit(solution)/shard_map/ppermute | solution.py:34
  59.1 1.2 collective-permute-done.7.s
  60.8 19.8 %collective-permute-done.8.refs_1_ = bf16[336,2688]{1,0:T(8,128)(2,1)S(1)} collective-permute-done((bf16[336,2688]{1,0:T(8,128)(2,1)S(1)}, bf16[336,2688]{1,0:T(8,128)(2,1)S(1)}, u32[]{:S(2)}, u32[]{:S(2)}) %collective-permute-start.8) | collective-permute-done | bytes 1806368 | tf_op jit(solution)/shard_map/ppermute | solution.py:90
  80.6 7.8 %project.1 = (bf16[64,5376]{1,0:T(8,128)(2,1)S(1)}, bf16[32,5376]{1,0:T(8,128)(2,1)S(1)}, bf16[32,5376]{1,0:T(8,128)(2,1)S(1)}, bf16[32,5376]{1,0:T(8,128)(2,1)S...) custom-call(bf16[256,512]{1,0:T(8,128)(2,1)S(1)} %bitcast.129, ...), custom_call_target="tpu_custom_call" | custom-call | bytes 1000 | tf_op jit(solution)/shard_map/project/pallas_call | solution.py:147
  88.5 3.7 %collective-permute-start.13 = (bf16[32,5376]{1,0:T(8,128)(2,1)S(1)}, bf16[32,5376]{1,0:T(8,128)(2,1)S(1)}, u32[]{:S(2)}, u32[]{:S(2)}) collective-permute-start(bf16[32,5376]{1,0:T(8,128)(2,1)S(1)} %get-tuple-element.60), channel_id=1, source_target_pairs={{0,2},{2,4},{4,6},{6,0},{1,3},{3,5},{5,7},{7,1},{8,10},{10,12},{12... | collective-permute-start | bytes 1032200 | tf_op jit(solution)/shard_map/ppermute | solution.py:34
  92.1 2.2 collective-permute-start.14
  95.3 3.9 %collective-permute-done.13 = bf16[32,5376]{1,0:T(8,128)(2,1)S(1)} collective-permute-done((bf16[32,5376]{1,0:T(8,128)(2,1)S(1)}, bf16[32,5376]{1,0:T(8,128)(2,1)S(1)}, u32[]{:S(2)}, u32[]{:S(2)}) %collective-permute-start.13) | collective-permute-done | bytes 344096 | tf_op jit(solution)/shard_map/ppermute | solution.py:34
  99.2 1.1 collective-permute-start.18
  100.4 3.4 %collective-permute-done.11.refs_6_ = bf16[336,2688]{1,0:T(8,128)(2,1)S(1)} collective-permute-done((bf16[336,2688]{1,0:T(8,128)(2,1)}, bf16[336,2688]{1,0:T(8,128)(2,1)S(1)}, u32[]{:S(2)}, u32[]{:S(2)}) %collective-permute-start.11) | collective-permute-done | bytes 1806368 | tf_op jit(solution)/shard_map/ppermute | solution.py:90
  103.8 3.8 %collective-permute-start.19 = (bf16[32,5376]{1,0:T(8,128)(2,1)S(1)}, bf16[32,5376]{1,0:T(8,128)(2,1)S(1)}, u32[]{:S(2)}, u32[]{:S(2)}) collective-permute-start(bf16[32,5376]{1,0:T(8,128)(2,1)S(1)} %get-tuple-element.65), channel_id=1, source_target_pairs={{0,6},{2,0},{4,2},{6,4},{1,7},{3,1},{5,3},{7,5},{8,14},{10,8},{12,... | collective-permute-start | bytes 1032200 | tf_op jit(solution)/shard_map/ppermute | solution.py:34
  107.5 1.2 collective-permute-start.20
  109.6 2.2 collective-permute-done.19.bt_ref
  112.4 3.1 %collective-permute-done.20.bb_ref = bf16[32,5376]{1,0:T(8,128)(2,1)S(1)} collective-permute-done((bf16[32,5376]{1,0:T(8,128)(2,1)S(1)}, bf16[32,5376]{1,0:T(8,128)(2,1)S(1)}, u32[]{:S(2)}, u32[]{:S(2)}) %collective-permute-start.20) | collective-permute-done | bytes 344096 | tf_op jit(solution)/shard_map/ppermute | solution.py:34
  115.4 3.6 %collective-permute-start.33 = (bf16[336,2688]{1,0:T(8,128)(2,1)S(1)}, bf16[336,2688]{1,0:T(8,128)(2,1)}, u32[]{:S(2)}, u32[]{:S(2)}) collective-permute-start(bf16[336,2688]{1,0:T(8,128)(2,1)S(1)} %collective-permute-done.15.refs_3_), channel_id=1, source_target_pairs={{0,96},{1,25},{2,98},{3,27},{4,100},{5,29},{6,102},{7,31},{8,104},... | collective-permute-start | bytes 5419016 | tf_op jit(solution)/shard_map/ppermute | solution.py:90
  120.3 2.9 %collective-permute-done.23.refs_5_ = bf16[336,2688]{1,0:T(8,128)(2,1)} collective-permute-done((bf16[336,2688]{1,0:T(8,128)(2,1)S(1)}, bf16[336,2688]{1,0:T(8,128)(2,1)}, u32[]{:S(2)}, u32[]{:S(2)}) %collective-permute-start.23) | collective-permute-done | bytes 1806368 | tf_op jit(solution)/shard_map/ppermute | solution.py:90
  123.2 3.8 %collective-permute-start.22 = (bf16[64,5376]{1,0:T(8,128)(2,1)S(1)}, bf16[64,5376]{1,0:T(8,128)(2,1)S(1)}, u32[]{:S(2)}, u32[]{:S(2)}) collective-permute-start(bf16[64,5376]{1,0:T(8,128)(2,1)S(1)} %get-tuple-element.75.refs_0_), channel_id=1, source_target_pairs={{0,6},{2,0},{4,2},{6,4},{1,7},{3,1},{5,3},{7,5},{8,14},{10,8},{12,... | collective-permute-start | bytes 2064392 | tf_op jit(solution)/shard_map/ppermute | solution.py:34
  127.0 10.7 %collective-permute-start.27 = (bf16[64,5376]{1,0:T(8,128)(2,1)S(1)}, bf16[64,5376]{1,0:T(8,128)(2,1)S(1)}, u32[]{:S(2)}, u32[]{:S(2)}) collective-permute-start(bf16[64,5376]{1,0:T(8,128)(2,1)S(1)} %get-tuple-element.75.refs_0_), channel_id=1, source_target_pairs={{0,1},{1,0},{2,3},{3,2},{4,5},{5,4},{6,7},{7,6},{8,9},{9,8},{10,11... | collective-permute-start | bytes 2064392 | tf_op jit(solution)/shard_map/ppermute | solution.py:34
  137.9 2.7 %collective-permute-start.26 = (bf16[32,5376]{1,0:T(8,128)(2,1)S(1)}, bf16[32,5376]{1,0:T(8,128)(2,1)S(1)}, u32[]{:S(2)}, u32[]{:S(2)}) collective-permute-start(bf16[32,5376]{1,0:T(8,128)(2,1)S(1)} %slice.77), channel_id=1, source_target_pairs={{0,6},{2,0},{4,2},{6,4},{1,7},{3,1},{5,3},{7,5},{8,14},{10,8},{12,... | collective-permute-start | bytes 1032200 | tf_op jit(solution)/shard_map/ppermute | solution.py:34
  140.6 8.6 %collective-permute-done.25.refs_3_ = bf16[32,5376]{1,0:T(8,128)(2,1)S(1)} collective-permute-done((bf16[32,5376]{1,0:T(8,128)(2,1)S(1)}, bf16[32,5376]{1,0:T(8,128)(2,1)S(1)}, u32[]{:S(2)}, u32[]{:S(2)}) %collective-permute-start.25) | collective-permute-done | bytes 344096 | tf_op jit(solution)/shard_map/ppermute | solution.py:34
  149.2 9.7 %collective-permute-start.30 = (bf16[32,5376]{1,0:T(8,128)(2,1)S(1)}, bf16[32,5376]{1,0:T(8,128)(2,1)S(1)}, u32[]{:S(2)}, u32[]{:S(2)}) collective-permute-start(bf16[32,5376]{1,0:T(8,128)(2,1)S(1)} %collective-permute-done.25.refs_3_), channel_id=1, source_target_pairs={{0,1},{1,0},{2,3},{3,2},{4,5},{5,4},{6,7},{7,6},{8,9},{9,8},{10,11... | collective-permute-start | bytes 1032200 | tf_op jit(solution)/shard_map/ppermute | solution.py:34
  160.6 2.1 collective-permute-done.31.refs_9_
  162.6 1.5 collective-permute-start.38
  164.2 1.2 copy-done.16
  165.4 2.6 %collective-permute-start.41 = (bf16[336,2688]{1,0:T(8,128)(2,1)}, bf16[336,2688]{1,0:T(8,128)(2,1)S(1)}, u32[]{:S(2)}, u32[]{:S(2)}) collective-permute-start(bf16[336,2688]{1,0:T(8,128)(2,1)} %collective-permute-done.33.refs_11_), channel_id=1, source_target_pairs={{0,96},{1,25},{2,98},{3,27},{4,100},{5,29},{6,102},{7,31},{8,104},... | collective-permute-start | bytes 5419016 | tf_op jit(solution)/shard_map/ppermute | solution.py:90
  168.0 5.1 %order.1.refs_13_.refs_5_ = bf16[512,5632]{1,0:T(8,128)(2,1)S(1)} custom-call(bf16[64,5376]{1,0:T(8,128)(2,1)S(1)} %get-tuple-element.75.refs_0_, bf16[64,5376]{1,0:T(8,128)(2,1)S(1)} %collective-permute-done.21.refs_1_, bf16[64,5376]{1,0:T(8,128)(2,1)S(1)} %collective-permute-done.22.refs_2_, bf16[32,5376]{1,0:T(8,128)(2,1)S(1)} %collective-permute-done.25.refs_3_, ...), custom_call_target="tpu_custom_call" | custom-call | bytes 1000 | tf_op jit(solution)/shard_map/order/pallas_call | solution.py:241
  173.1 2.5 %copy-done = bf16[512,5632]{1,0:T(8,128)(2,1)} copy-done((bf16[512,5632]{1,0:T(8,128)(2,1)}, bf16[512,5632]{1,0:T(8,128)(2,1)S(1)}, u32[]{:S(2)}) %copy-start) | copy-done | bytes 5767192
  176.4 1.3 collective-permute-start.34
  177.7 21.9 %near.1.refs_6_ = f32[512,2688]{1,0:T(8,128)} custom-call(bf16[336,2688]{1,0:T(8,128)(2,1)} %copy-done.1, bf16[336,2688]{1,0:T(8,128)(2,1)} %copy-done.13, bf16[336,2688]{1,0:T(8,128)(2,1)} %collective-permute-done.4.refs_2_, bf16[336,2688]{1,0:T(8,128)(2,1)} %copy-done.14, bf16[336,2688]{1,0:T(8,128)(2,1)} %collective-permute-done.16.refs_4_, ...), custom_call_target="tpu_custom_call" | custom-call | bytes 1000 | tf_op jit(solution)/shard_map/near/pallas_call | solution.py:298
  201.9 1.7 collective-permute-start.35
  205.5 1.2 copy-done.11
  206.7 1.2 copy-done.12
  207.9 13.4 %far.1 = bf16[1344,512]{1,0:T(8,128)(2,1)} custom-call(bf16[336,2688]{1,0:T(8,128)(2,1)} %copy-done.10, bf16[336,2688]{1,0:T(8,128)(2,1)} %copy-done.11, bf16[336,2688]{1,0:T(8,128)(2,1)} %copy-done.9, bf16[336,2688]{1,0:T(8,128)(2,1)} %copy-done.12, s32[4]{0:T(128)} %copy-done.7, bf16[512,5632]{1,0:T(8,128)(2,1)} %copy-done, f32[512,2688]{1,0:T(8,128)} %near.1.refs_6_), custom_call_target="tpu_custom_call" | custom-call | flops 3699376128 | bytes 12730368 | tf_op jit(solution)/shard_map/far/pallas_call | solution.py:342
  221.7 1.1 copy.34
  (131 shorter events, 18.6 us)
Async XLA Ops:
  0.6 80.0 %collective-permute-start.10 = (bf16[512,5376]{1,0:T(8,128)(2,1)}, bf16[512,5376]{1,0:T(8,128)(2,1)}, u32[]{:S(2)}, u32[]{:S(2)}) collective-permute-start(bf16[512,5376]{1,0:T(8,128)(2,1)} %w_ref.1), channel_id=1, source_target_pairs={{0,1},{1,0},{2,3},{3,2},{4,5},{5,4},{6,7},{7,6},{8,9},{9,8},{10,11... | collective-permute-start | bytes 16515080 | tf_op jit(solution)/shard_map/ppermute | solution.py:34
  6.1 8.1 %collective-permute-start = (bf16[4,80,672]{2,1,0:T(8,128)(2,1)}, bf16[4,80,672]{2,1,0:T(8,128)(2,1)}, u32[]{:S(2)}, u32[]{:S(2)}) collective-permute-start(bf16[4,80,672]{2,1,0:T(8,128)(2,1)} %fusion.6), channel_id=1, source_target_pairs={{0,1},{1,0},{2,3},{3,2},{4,5},{5,4},{6,7},{7,6},{8,9},{9,8},{10,11... | collective-permute-start | bytes 1290248 | tf_op jit(solution)/shard_map/ppermute | solution.py:34
  7.0 36.7 %copy-start.1 = (bf16[336,2688]{1,0:T(8,128)(2,1)}, bf16[336,2688]{1,0:T(8,128)(2,1)S(1)}, u32[]{:S(2)}) copy-start(bf16[336,2688]{1,0:T(8,128)(2,1)S(1)} %pack.1.refs_0_) | copy-start | bytes 5419012
  7.0 38.6 %collective-permute-start.4 = (bf16[336,2688]{1,0:T(8,128)(2,1)S(1)}, bf16[336,2688]{1,0:T(8,128)(2,1)}, u32[]{:S(2)}, u32[]{:S(2)}) collective-permute-start(bf16[336,2688]{1,0:T(8,128)(2,1)S(1)} %pack.1.refs_0_), channel_id=1, source_target_pairs={{0,24},{1,97},{2,26},{3,99},{4,28},{5,101},{6,30},{7,103},{8,0},{9... | collective-permute-start | bytes 5419016 | tf_op jit(solution)/shard_map/ppermute | solution.py:90
  9.8 45.9 %collective-permute-start.9 = (bf16[336,2688]{1,0:T(8,128)(2,1)S(1)}, bf16[336,2688]{1,0:T(8,128)(2,1)}, u32[]{:S(2)}, u32[]{:S(2)}) collective-permute-start(bf16[336,2688]{1,0:T(8,128)(2,1)S(1)} %pack.1.refs_0_), channel_id=1, source_target_pairs={{0,96},{1,25},{2,98},{3,27},{4,100},{5,29},{6,102},{7,31},{8,104},... | collective-permute-start | bytes 5419016 | tf_op jit(solution)/shard_map/ppermute | solution.py:90
  12.4 12.1 %collective-permute-start.5 = (bf16[512,512]{1,0:T(8,128)(2,1)S(1)}, bf16[512,512]{1,0:T(8,128)(2,1)S(1)}, u32[]{:S(2)}, u32[]{:S(2)}) collective-permute-start(bf16[512,512]{1,0:T(8,128)(2,1)S(1)} %pair.1.kv0_ref), channel_id=1, source_target_pairs={{0,8},{8,16},{16,24},{24,32},{32,40},{40,48},{48,56},{56,64},{64,7... | collective-permute-start | bytes 1572872 | tf_op jit(solution)/shard_map/ppermute | solution.py:39
  14.2 153.8 %copy-start.7 = (s32[4]{0:T(128)}, s32[4]{0:T(128)S(1)}, u32[]{:S(2)}) copy-start(s32[4]{0:T(128)S(1)} %pad_add_fusion.at_ref.refs_10_.refs_12_.refs_4_) | copy-start | bytes 52
  14.2 66.4 %slice-start = ((s8[5505024]{0:T(1024)(128)(4,1)}), s8[4194304]{0:T(1024)(128)(4,1)S(1)}, s32[]{:S(2)}) async-start(s8[5505024]{0:T(1024)(128)(4,1)} %bitcast.124), calls=%async_computation | async-start | bytes 8388608
  16.7 12.1 %collective-permute-start.1 = (bf16[2,80,672]{2,1,0:T(8,128)(2,1)S(1)}, bf16[2,80,672]{2,1,0:T(8,128)(2,1)S(1)}, u32[]{:S(2)}, u32[]{:S(2)}) collective-permute-start(bf16[2,80,672]{2,1,0:T(8,128)(2,1)S(1)} %get-tuple-element.108), channel_id=1, source_target_pairs={{0,6},{2,0},{4,2},{6,4},{1,7},{3,1},{5,3},{7,5},{8,14},{10,8},{12,... | collective-permute-start | bytes 645128 | tf_op jit(solution)/shard_map/ppermute | solution.py:34
  24.5 14.2 %collective-permute-start.6 = (bf16[512,512]{1,0:T(8,128)(2,1)S(1)}, bf16[512,512]{1,0:T(8,128)(2,1)S(1)}, u32[]{:S(2)}, u32[]{:S(2)}) collective-permute-start(bf16[512,512]{1,0:T(8,128)(2,1)S(1)} %collective-permute-done.5.kv1_ref), channel_id=1, source_target_pairs={{0,8},{8,16},{16,24},{24,32},{32,40},{40,48},{48,56},{56,64},{64,7... | collective-permute-start | bytes 1572872 | tf_op jit(solution)/shard_map/ppermute | solution.py:39
  28.8 8.5 %collective-permute-start.2 = (bf16[2,80,672]{2,1,0:T(8,128)(2,1)S(1)}, bf16[2,80,672]{2,1,0:T(8,128)(2,1)S(1)}, u32[]{:S(2)}, u32[]{:S(2)}) collective-permute-start(bf16[2,80,672]{2,1,0:T(8,128)(2,1)S(1)} %get-tuple-element.107), channel_id=1, source_target_pairs={{0,4},{2,6},{4,0},{6,2},{1,5},{3,7},{5,1},{7,3},{8,12},{10,14},{12... | collective-permute-start | bytes 645128 | tf_op jit(solution)/shard_map/ppermute | solution.py:34
  37.3 6.4 %collective-permute-start.3 = (bf16[2,80,672]{2,1,0:T(8,128)(2,1)S(1)}, bf16[2,80,672]{2,1,0:T(8,128)(2,1)S(1)}, u32[]{:S(2)}, u32[]{:S(2)}) collective-permute-start(bf16[2,80,672]{2,1,0:T(8,128)(2,1)S(1)} %get-tuple-element.106), channel_id=1, source_target_pairs={{0,2},{2,4},{4,6},{6,0},{1,3},{3,5},{5,7},{7,1},{8,10},{10,12},{12... | collective-permute-start | bytes 645128 | tf_op jit(solution)/shard_map/ppermute | solution.py:34
  38.7 41.9 %collective-permute-start.8 = (bf16[336,2688]{1,0:T(8,128)(2,1)S(1)}, bf16[336,2688]{1,0:T(8,128)(2,1)S(1)}, u32[]{:S(2)}, u32[]{:S(2)}) collective-permute-start(bf16[336,2688]{1,0:T(8,128)(2,1)S(1)} %pack.1.refs_0_), channel_id=1, source_target_pairs={{0,8},{1,33},{2,10},{3,35},{4,12},{5,37},{6,14},{7,39},{8,16},{9,4... | collective-permute-start | bytes 5419016 | tf_op jit(solution)/shard_map/ppermute | solution.py:90
  43.7 48.4 %collective-permute-start.16 = (bf16[336,2688]{1,0:T(8,128)(2,1)S(1)}, bf16[336,2688]{1,0:T(8,128)(2,1)}, u32[]{:S(2)}, u32[]{:S(2)}) collective-permute-start(bf16[336,2688]{1,0:T(8,128)(2,1)S(1)} %pack.1.refs_0_), channel_id=1, source_target_pairs={{0,32},{1,9},{2,34},{3,11},{4,36},{5,13},{6,38},{7,15},{8,40},{9,1... | collective-permute-start | bytes 5419016 | tf_op jit(solution)/shard_map/ppermute | solution.py:90
  43.9 36.8 %slice-start.1 = ((s8[5505024]{0:T(1024)(128)(4,1)}), s8[1310720]{0:T(1024)(128)(4,1)S(1)}, s32[]{:S(2)}) async-start(s8[5505024]{0:T(1024)(128)(4,1)} %bitcast.124), calls=%async_computation.1 | async-start | bytes 2621440
  45.6 48.8 %collective-permute-start.15 = (bf16[336,2688]{1,0:T(8,128)(2,1)}, bf16[336,2688]{1,0:T(8,128)(2,1)S(1)}, u32[]{:S(2)}, u32[]{:S(2)}) collective-permute-start(bf16[336,2688]{1,0:T(8,128)(2,1)} %collective-permute-done.4.refs_2_), channel_id=1, source_target_pairs={{0,24},{1,97},{2,26},{3,99},{4,28},{5,101},{6,30},{7,103},{8,0},{9... | collective-permute-start | bytes 5419016 | tf_op jit(solution)/shard_map/ppermute | solution.py:90
  55.7 4.5 %collective-permute-start.7 = (bf16[256,512]{1,0:T(8,128)(2,1)S(1)}, bf16[256,512]{1,0:T(8,128)(2,1)S(1)}, u32[]{:S(2)}, u32[]{:S(2)}) collective-permute-start(bf16[256,512]{1,0:T(8,128)(2,1)S(1)} %bitcast.134), channel_id=1, source_target_pairs={{0,1},{1,0},{2,3},{3,2},{4,5},{5,4},{6,7},{7,6},{8,9},{9,8},{10,11... | collective-permute-start | bytes 786440 | tf_op jit(solution)/shard_map/ppermute | solution.py:34
  60.2 43.6 %collective-permute-start.11 = (bf16[336,2688]{1,0:T(8,128)(2,1)}, bf16[336,2688]{1,0:T(8,128)(2,1)S(1)}, u32[]{:S(2)}, u32[]{:S(2)}) collective-permute-start(bf16[336,2688]{1,0:T(8,128)(2,1)} %collective-permute-done.4.refs_2_), channel_id=1, source_target_pairs={{0,32},{1,9},{2,34},{3,11},{4,36},{5,13},{6,38},{7,15},{8,40},{9,1... | collective-permute-start | bytes 5419016 | tf_op jit(solution)/shard_map/ppermute | solution.py:90
  80.6 18.6 %copy-start.13 = (bf16[336,2688]{1,0:T(8,128)(2,1)}, bf16[336,2688]{1,0:T(8,128)(2,1)S(1)}, u32[]{:S(2)}) copy-start(bf16[336,2688]{1,0:T(8,128)(2,1)S(1)} %collective-permute-done.8.refs_1_) | copy-start | bytes 5419012
  80.6 26.9 %collective-permute-start.12 = (bf16[336,2688]{1,0:T(8,128)(2,1)}, bf16[336,2688]{1,0:T(8,128)(2,1)}, u32[]{:S(2)}, u32[]{:S(2)}) collective-permute-start(bf16[336,2688]{1,0:T(8,128)(2,1)} %collective-permute-done.4.refs_2_), channel_id=1, source_target_pairs={{0,96},{1,25},{2,98},{3,27},{4,100},{5,29},{6,102},{7,31},{8,104},... | collective-permute-start | bytes 5419016 | tf_op jit(solution)/shard_map/ppermute | solution.py:90
  88.5 10.7 %collective-permute-start.13 = (bf16[32,5376]{1,0:T(8,128)(2,1)S(1)}, bf16[32,5376]{1,0:T(8,128)(2,1)S(1)}, u32[]{:S(2)}, u32[]{:S(2)}) collective-permute-start(bf16[32,5376]{1,0:T(8,128)(2,1)S(1)} %get-tuple-element.60), channel_id=1, source_target_pairs={{0,2},{2,4},{4,6},{6,0},{1,3},{3,5},{5,7},{7,1},{8,10},{10,12},{12... | collective-permute-start | bytes 1032200 | tf_op jit(solution)/shard_map/ppermute | solution.py:34
  92.1 7.1 %collective-permute-start.14 = (bf16[32,5376]{1,0:T(8,128)(2,1)S(1)}, bf16[32,5376]{1,0:T(8,128)(2,1)S(1)}, u32[]{:S(2)}, u32[]{:S(2)}) collective-permute-start(bf16[32,5376]{1,0:T(8,128)(2,1)S(1)} %get-tuple-element.61), channel_id=1, source_target_pairs={{0,6},{2,0},{4,2},{6,4},{1,7},{3,1},{5,3},{7,5},{8,14},{10,8},{12,... | collective-permute-start | bytes 1032200 | tf_op jit(solution)/shard_map/ppermute | solution.py:34
  94.4 25.8 %copy-start.14 = (bf16[336,2688]{1,0:T(8,128)(2,1)}, bf16[336,2688]{1,0:T(8,128)(2,1)S(1)}, u32[]{:S(2)}) copy-start(bf16[336,2688]{1,0:T(8,128)(2,1)S(1)} %collective-permute-done.15.refs_3_) | copy-start | bytes 5419012
  94.4 28.9 %collective-permute-start.23 = (bf16[336,2688]{1,0:T(8,128)(2,1)S(1)}, bf16[336,2688]{1,0:T(8,128)(2,1)}, u32[]{:S(2)}, u32[]{:S(2)}) collective-permute-start(bf16[336,2688]{1,0:T(8,128)(2,1)S(1)} %collective-permute-done.8.refs_1_), channel_id=1, source_target_pairs={{0,32},{1,9},{2,34},{3,11},{4,36},{5,13},{6,38},{7,15},{8,40},{9,1... | collective-permute-start | bytes 5419016 | tf_op jit(solution)/shard_map/ppermute | solution.py:90
  99.2 27.8 %collective-permute-start.24 = (bf16[336,2688]{1,0:T(8,128)(2,1)S(1)}, bf16[336,2688]{1,0:T(8,128)(2,1)}, u32[]{:S(2)}, u32[]{:S(2)}) collective-permute-start(bf16[336,2688]{1,0:T(8,128)(2,1)S(1)} %collective-permute-done.8.refs_1_), channel_id=1, source_target_pairs={{0,96},{1,25},{2,98},{3,27},{4,100},{5,29},{6,102},{7,31},{8,104},... | collective-permute-start | bytes 5419016 | tf_op jit(solution)/shard_map/ppermute | solution.py:90
  99.2 10.3 %collective-permute-start.18 = (bf16[32,5376]{1,0:T(8,128)(2,1)S(1)}, bf16[32,5376]{1,0:T(8,128)(2,1)S(1)}, u32[]{:S(2)}, u32[]{:S(2)}) collective-permute-start(bf16[32,5376]{1,0:T(8,128)(2,1)S(1)} %get-tuple-element.64), channel_id=1, source_target_pairs={{0,2},{2,4},{4,6},{6,0},{1,3},{3,5},{5,7},{7,1},{8,10},{10,12},{12... | collective-permute-start | bytes 1032200 | tf_op jit(solution)/shard_map/ppermute | solution.py:34
  103.8 8.0 %collective-permute-start.19 = (bf16[32,5376]{1,0:T(8,128)(2,1)S(1)}, bf16[32,5376]{1,0:T(8,128)(2,1)S(1)}, u32[]{:S(2)}, u32[]{:S(2)}) collective-permute-start(bf16[32,5376]{1,0:T(8,128)(2,1)S(1)} %get-tuple-element.65), channel_id=1, source_target_pairs={{0,6},{2,0},{4,2},{6,4},{1,7},{3,1},{5,3},{7,5},{8,14},{10,8},{12,... | collective-permute-start | bytes 1032200 | tf_op jit(solution)/shard_map/ppermute | solution.py:34
  107.5 7.9 %collective-permute-start.20 = (bf16[32,5376]{1,0:T(8,128)(2,1)S(1)}, bf16[32,5376]{1,0:T(8,128)(2,1)S(1)}, u32[]{:S(2)}, u32[]{:S(2)}) collective-permute-start(bf16[32,5376]{1,0:T(8,128)(2,1)S(1)} %add_convert_fusion), channel_id=1, source_target_pairs={{0,6},{2,0},{4,2},{6,4},{1,7},{3,1},{5,3},{7,5},{8,14},{10,8},{12,... | collective-permute-start | bytes 1032200 | tf_op jit(solution)/shard_map/ppermute | solution.py:34
  109.6 9.5 %collective-permute-start.17 = (bf16[32,5376]{1,0:T(8,128)(2,1)S(1)}, bf16[32,5376]{1,0:T(8,128)(2,1)S(1)}, u32[]{:S(2)}, u32[]{:S(2)}) collective-permute-start(bf16[32,5376]{1,0:T(8,128)(2,1)S(1)} %add_convert_fusion.1), channel_id=1, source_target_pairs={{0,2},{2,4},{4,6},{6,0},{1,3},{3,5},{5,7},{7,1},{8,10},{10,12},{12... | collective-permute-start | bytes 1032200 | tf_op jit(solution)/shard_map/ppermute | solution.py:34
  111.7 52.5 %collective-permute-start.32 = (bf16[336,2688]{1,0:T(8,128)(2,1)S(1)}, bf16[336,2688]{1,0:T(8,128)(2,1)S(1)}, u32[]{:S(2)}, u32[]{:S(2)}) collective-permute-start(bf16[336,2688]{1,0:T(8,128)(2,1)S(1)} %collective-permute-done.15.refs_3_), channel_id=1, source_target_pairs={{0,32},{1,9},{2,34},{3,11},{4,36},{5,13},{6,38},{7,15},{8,40},{9,1... | collective-permute-start | bytes 5419016 | tf_op jit(solution)/shard_map/ppermute | solution.py:90
  115.4 48.8 %collective-permute-start.33 = (bf16[336,2688]{1,0:T(8,128)(2,1)S(1)}, bf16[336,2688]{1,0:T(8,128)(2,1)}, u32[]{:S(2)}, u32[]{:S(2)}) collective-permute-start(bf16[336,2688]{1,0:T(8,128)(2,1)S(1)} %collective-permute-done.15.refs_3_), channel_id=1, source_target_pairs={{0,96},{1,25},{2,98},{3,27},{4,100},{5,29},{6,102},{7,31},{8,104},... | collective-permute-start | bytes 5419016 | tf_op jit(solution)/shard_map/ppermute | solution.py:90
  120.1 17.6 %collective-permute-start.21 = (bf16[64,5376]{1,0:T(8,128)(2,1)S(1)}, bf16[64,5376]{1,0:T(8,128)(2,1)S(1)}, u32[]{:S(2)}, u32[]{:S(2)}) collective-permute-start(bf16[64,5376]{1,0:T(8,128)(2,1)S(1)} %get-tuple-element.75.refs_0_), channel_id=1, source_target_pairs={{0,2},{2,4},{4,6},{6,0},{1,3},{3,5},{5,7},{7,1},{8,10},{10,12},{12... | collective-permute-start | bytes 2064392 | tf_op jit(solution)/shard_map/ppermute | solution.py:34
  123.2 14.5 %collective-permute-start.22 = (bf16[64,5376]{1,0:T(8,128)(2,1)S(1)}, bf16[64,5376]{1,0:T(8,128)(2,1)S(1)}, u32[]{:S(2)}, u32[]{:S(2)}) collective-permute-start(bf16[64,5376]{1,0:T(8,128)(2,1)S(1)} %get-tuple-element.75.refs_0_), channel_id=1, source_target_pairs={{0,6},{2,0},{4,2},{6,4},{1,7},{3,1},{5,3},{7,5},{8,14},{10,8},{12,... | collective-permute-start | bytes 2064392 | tf_op jit(solution)/shard_map/ppermute | solution.py:34
  127.0 31.9 %collective-permute-start.27 = (bf16[64,5376]{1,0:T(8,128)(2,1)S(1)}, bf16[64,5376]{1,0:T(8,128)(2,1)S(1)}, u32[]{:S(2)}, u32[]{:S(2)}) collective-permute-start(bf16[64,5376]{1,0:T(8,128)(2,1)S(1)} %get-tuple-element.75.refs_0_), channel_id=1, source_target_pairs={{0,1},{1,0},{2,3},{3,2},{4,5},{5,4},{6,7},{7,6},{8,9},{9,8},{10,11... | collective-permute-start | bytes 2064392 | tf_op jit(solution)/shard_map/ppermute | solution.py:34
  137.8 11.4 %collective-permute-start.25 = (bf16[32,5376]{1,0:T(8,128)(2,1)S(1)}, bf16[32,5376]{1,0:T(8,128)(2,1)S(1)}, u32[]{:S(2)}, u32[]{:S(2)}) collective-permute-start(bf16[32,5376]{1,0:T(8,128)(2,1)S(1)} %slice.76), channel_id=1, source_target_pairs={{0,2},{2,4},{4,6},{6,0},{1,3},{3,5},{5,7},{7,1},{8,10},{10,12},{12... | collective-permute-start | bytes 1032200 | tf_op jit(solution)/shard_map/ppermute | solution.py:34
  137.9 21.0 %collective-permute-start.26 = (bf16[32,5376]{1,0:T(8,128)(2,1)S(1)}, bf16[32,5376]{1,0:T(8,128)(2,1)S(1)}, u32[]{:S(2)}, u32[]{:S(2)}) collective-permute-start(bf16[32,5376]{1,0:T(8,128)(2,1)S(1)} %slice.77), channel_id=1, source_target_pairs={{0,6},{2,0},{4,2},{6,4},{1,7},{3,1},{5,3},{7,5},{8,14},{10,8},{12,... | collective-permute-start | bytes 1032200 | tf_op jit(solution)/shard_map/ppermute | solution.py:34
  149.2 11.0 %collective-permute-start.30 = (bf16[32,5376]{1,0:T(8,128)(2,1)S(1)}, bf16[32,5376]{1,0:T(8,128)(2,1)S(1)}, u32[]{:S(2)}, u32[]{:S(2)}) collective-permute-start(bf16[32,5376]{1,0:T(8,128)(2,1)S(1)} %collective-permute-done.25.refs_3_), channel_id=1, source_target_pairs={{0,1},{1,0},{2,3},{3,2},{4,5},{5,4},{6,7},{7,6},{8,9},{9,8},{10,11... | collective-permute-start | bytes 1032200 | tf_op jit(solution)/shard_map/ppermute | solution.py:34
  158.9 3.7 %collective-permute-start.28 = (bf16[64,5376]{1,0:T(8,128)(2,1)S(1)}, bf16[64,5376]{1,0:T(8,128)(2,1)S(1)}, u32[]{:S(2)}, u32[]{:S(2)}) collective-permute-start(bf16[64,5376]{1,0:T(8,128)(2,1)S(1)} %collective-permute-done.21.refs_1_), channel_id=1, source_target_pairs={{0,1},{1,0},{2,3},{3,2},{4,5},{5,4},{6,7},{7,6},{8,9},{9,8},{10,11... | collective-permute-start | bytes 2064392 | tf_op jit(solution)/shard_map/ppermute | solution.py:34
  158.9 5.2 %collective-permute-start.29 = (bf16[64,5376]{1,0:T(8,128)(2,1)S(1)}, bf16[64,5376]{1,0:T(8,128)(2,1)S(1)}, u32[]{:S(2)}, u32[]{:S(2)}) collective-permute-start(bf16[64,5376]{1,0:T(8,128)(2,1)S(1)} %collective-permute-done.22.refs_2_), channel_id=1, source_target_pairs={{0,1},{1,0},{2,3},{3,2},{4,5},{5,4},{6,7},{7,6},{8,9},{9,8},{10,11... | collective-permute-start | bytes 2064392 | tf_op jit(solution)/shard_map/ppermute | solution.py:34
  160.2 2.5 %collective-permute-start.31 = (bf16[32,5376]{1,0:T(8,128)(2,1)S(1)}, bf16[32,5376]{1,0:T(8,128)(2,1)S(1)}, u32[]{:S(2)}, u32[]{:S(2)}) collective-permute-start(bf16[32,5376]{1,0:T(8,128)(2,1)S(1)} %collective-permute-done.26.refs_4_), channel_id=1, source_target_pairs={{0,1},{1,0},{2,3},{3,2},{4,5},{5,4},{6,7},{7,6},{8,9},{9,8},{10,11... | collective-permute-start | bytes 1032200 | tf_op jit(solution)/shard_map/ppermute | solution.py:34
  162.6 41.0 %collective-permute-start.40 = (bf16[336,2688]{1,0:T(8,128)(2,1)}, bf16[336,2688]{1,0:T(8,128)(2,1)S(1)}, u32[]{:S(2)}, u32[]{:S(2)}) collective-permute-start(bf16[336,2688]{1,0:T(8,128)(2,1)} %collective-permute-done.12.refs_10_), channel_id=1, source_target_pairs={{0,96},{1,25},{2,98},{3,27},{4,100},{5,29},{6,102},{7,31},{8,104},... | collective-permute-start | bytes 5419016 | tf_op jit(solution)/shard_map/ppermute | solution.py:90
  162.6 41.2 %collective-permute-start.38 = (bf16[336,2688]{1,0:T(8,128)(2,1)}, bf16[336,2688]{1,0:T(8,128)(2,1)S(1)}, u32[]{:S(2)}, u32[]{:S(2)}) collective-permute-start(bf16[336,2688]{1,0:T(8,128)(2,1)} %collective-permute-done.16.refs_4_), channel_id=1, source_target_pairs={{0,32},{1,9},{2,34},{3,11},{4,36},{5,13},{6,38},{7,15},{8,40},{9,1... | collective-permute-start | bytes 5419016 | tf_op jit(solution)/shard_map/ppermute | solution.py:90
  164.1 41.4 %collective-permute-start.39 = (bf16[336,2688]{1,0:T(8,128)(2,1)}, bf16[336,2688]{1,0:T(8,128)(2,1)S(1)}, u32[]{:S(2)}, u32[]{:S(2)}) collective-permute-start(bf16[336,2688]{1,0:T(8,128)(2,1)} %collective-permute-done.23.refs_5_), channel_id=1, source_target_pairs={{0,32},{1,9},{2,34},{3,11},{4,36},{5,13},{6,38},{7,15},{8,40},{9,1... | collective-permute-start | bytes 5419016 | tf_op jit(solution)/shard_map/ppermute | solution.py:90
  165.4 40.1 %collective-permute-start.41 = (bf16[336,2688]{1,0:T(8,128)(2,1)}, bf16[336,2688]{1,0:T(8,128)(2,1)S(1)}, u32[]{:S(2)}, u32[]{:S(2)}) collective-permute-start(bf16[336,2688]{1,0:T(8,128)(2,1)} %collective-permute-done.33.refs_11_), channel_id=1, source_target_pairs={{0,96},{1,25},{2,98},{3,27},{4,100},{5,29},{6,102},{7,31},{8,104},... | collective-permute-start | bytes 5419016 | tf_op jit(solution)/shard_map/ppermute | solution.py:90
  176.4 23.3 %collective-permute-start.34 = (bf16[4,64,672]{2,1,0:T(8,128)(2,1)}, bf16[4,64,672]{2,1,0:T(8,128)(2,1)}, u32[]{:S(2)}, u32[]{:S(2)}) collective-permute-start(bf16[4,64,672]{2,1,0:T(8,128)(2,1)} %select_bitcast_fusion.2), channel_id=1, source_target_pairs={{0,1},{1,0},{2,3},{3,2},{4,5},{5,4},{6,7},{7,6},{8,9},{9,8},{10,11... | collective-permute-start | bytes 1032200 | tf_op jit(solution)/shard_map/ppermute | solution.py:34
  201.9 19.4 %collective-permute-start.35 = (bf16[2,64,672]{2,1,0:T(8,128)(2,1)}, bf16[2,64,672]{2,1,0:T(8,128)(2,1)S(1)}, u32[]{:S(2)}, u32[]{:S(2)}) collective-permute-start(bf16[2,64,672]{2,1,0:T(8,128)(2,1)} %get-tuple-element.111), channel_id=1, source_target_pairs={{0,6},{2,0},{4,2},{6,4},{1,7},{3,1},{5,3},{7,5},{8,14},{10,8},{12,... | collective-permute-start | bytes 516104 | tf_op jit(solution)/shard_map/ppermute | solution.py:34
  203.7 17.7 %collective-permute-start.36 = (bf16[2,64,672]{2,1,0:T(8,128)(2,1)}, bf16[2,64,672]{2,1,0:T(8,128)(2,1)S(1)}, u32[]{:S(2)}, u32[]{:S(2)}) collective-permute-start(bf16[2,64,672]{2,1,0:T(8,128)(2,1)} %get-tuple-element.110), channel_id=1, source_target_pairs={{0,4},{2,6},{4,0},{6,2},{1,5},{3,7},{5,1},{7,3},{8,12},{10,14},{12... | collective-permute-start | bytes 516104 | tf_op jit(solution)/shard_map/ppermute | solution.py:34
  203.8 17.5 %collective-permute-start.37 = (bf16[2,64,672]{2,1,0:T(8,128)(2,1)S(1)}, bf16[2,64,672]{2,1,0:T(8,128)(2,1)S(1)}, u32[]{:S(2)}, u32[]{:S(2)}) collective-permute-start(bf16[2,64,672]{2,1,0:T(8,128)(2,1)S(1)} %get-tuple-element.109), channel_id=1, source_target_pairs={{0,2},{2,4},{4,6},{6,0},{1,3},{3,5},{5,7},{7,1},{8,10},{10,12},{12... | collective-permute-start | bytes 516104 | tf_op jit(solution)/shard_map/ppermute | solution.py:34
  (14 other events, 55.4 us)
